TPU v7x, 512 devices: a whole 4x8x8 slice. The times are simulated.
512 devices in a mesh: lat: 16 (over x_hi, z), lon: 32 (over y, x_lo, core).
Axes of the slice: x: 4 (x_hi: 2, x_lo: 2; x = x_hi * 2 + x_lo), y: 8, z: 8, core: 2. Of those that a mesh axis runs over, the one named last changes fastest.
Arguments:
- fields: bfloat16 [192, 2, 512, 512], P('lat', None, 'lon'), may hold values from -6 to 6
- land_ids: int32 [192, 512], P('lat', 'lon'), may hold values from 0 to 2
- surface_table: bfloat16 [3, 512], replicated, may hold values from -6 to 6
- level_table: bfloat16 [2, 512], replicated, may hold values from -6 to 6
- norm_first: float32 [512], replicated, may hold values from 0.5 to 1.5
- qkv_first: bfloat16 [3, 512, 512], replicated, may hold values from -2 to 2
- out_first: bfloat16 [512, 512], P('lat'), may hold values from -0.25 to 0.25
- norm_merge2: float32 [2048], replicated, may hold values from 0.5 to 1.5
- merge_second: bfloat16 [2048, 1024], P('lat'), may hold values from -0.125 to 0.125
- norm_merge3: float32 [4096], replicated, may hold values from 0.5 to 1.5
- merge_third: bfloat16 [4096, 2048], P(None, 'lat'), may hold values from -0.09375 to 0.09375
- norm_third: float32 [2048], replicated, may hold values from 0.5 to 1.5
- qkv_third: bfloat16 [3, 2048, 1024], P(None, None, 'lat'), may hold values from -2 to 2
- out_third: bfloat16 [1024, 2048], P('lat'), may hold values from -0.1875 to 0.1875
- up_third: bfloat16 [2048, 1024], P('lat'), may hold values from -0.125 to 0.125
- up_second: bfloat16 [1024, 512], P('lat'), may hold values from -0.1875 to 0.1875
Outputs:
- decoded: bfloat16 [192, 2, 512, 512], P('lat', None, 'lon')
All inputs are finite; a program needn't handle non-finite values.
Results may differ from a plain program's by a relative error of at most 0.02.
Values may be sent and summed in bfloat16 or wider, within the bound.
No kernel may reach another device: no remote copies, remote signals or barrier semaphores. Data moves between devices by JAX's collectives and lax.ppermute only.
A program may use at most 64 MiB of HBM per device.

v0:
```python
import jax
import jax.numpy as jnp
from jax import lax
from jax.experimental import pallas as pl
from jax.experimental.pallas import tpu as pltpu
from jax.sharding import PartitionSpec as P

HD = 64


def with_halo(cells, sides, width, ties):
    for (axis, dim), tie in zip(sides, ties):
        cells = after(cells, *tie)
        count = lax.axis_size(axis)
        head = lax.slice_in_dim(cells, 0, width, axis=dim)
        tail = lax.slice_in_dim(cells, cells.shape[dim] - width, cells.shape[dim], axis=dim)
        cells = jnp.concatenate(
            [
                lax.ppermute(tail, axis, [(i, (i + 1) % count) for i in range(count)]),
                cells,
                lax.ppermute(head, axis, [((i + 1) % count, i) for i in range(count)]),
            ],
            axis=dim,
        )
    return cells


def norm_rows(values, gain):
    row_mean = jnp.mean(values, axis=-1, keepdims=True)
    centred = values - row_mean
    spread = jnp.mean(centred * centred, axis=-1, keepdims=True)
    return centred * lax.rsqrt(spread + 1e-05) * gain


def split_quads(cell_grid):
    lat_count, levels, lon_count, feat_dim = cell_grid.shape
    blocks = cell_grid.reshape(lat_count // 2, 2, levels, lon_count // 2, 2, feat_dim)
    return blocks.transpose(0, 2, 3, 1, 4, 5).reshape(
        lat_count // 2, levels, lon_count // 2, 4 * feat_dim
    )


def spread_quads(cell_grid):
    lat_count, levels, lon_count, feat_dim = cell_grid.shape
    widened = jnp.broadcast_to(
        cell_grid[:, None, :, :, None, :], (lat_count, 2, levels, lon_count, 2, feat_dim)
    )
    return widened.reshape(2 * lat_count, levels, 2 * lon_count, feat_dim)


def call_kernel(body, out_shape, operands, scratch=(), flops=0):
    smem = [operand.dtype == jnp.int32 for operand in operands]
    return pl.pallas_call(
        body,
        out_shape=out_shape,
        in_specs=[
            pl.BlockSpec(memory_space=pltpu.SMEM if scalar else pltpu.VMEM) for scalar in smem
        ],
        out_specs=jax.tree.map(lambda _: pl.BlockSpec(memory_space=pltpu.VMEM), out_shape),
        scratch_shapes=list(scratch),
        compiler_params=pltpu.CompilerParams(vmem_limit_bytes=48 * 1024 * 1024),
        cost_estimate=pl.CostEstimate(
            flops=flops,
            bytes_accessed=sum(operand.size * operand.dtype.itemsize for operand in operands),
            transcendentals=0,
        ),
    )(*operands)


def dot_rows(left, right):
    return lax.dot_general(left, right, (((1,), (0,)), ((), ())), preferred_element_type=jnp.float32)


def softmax_rows(scores, keep):
    scores = jnp.where(keep, scores, -1e30)
    weights = jnp.exp(scores - jnp.max(scores, axis=-1, keepdims=True))
    total = jnp.sum(weights, axis=-1, keepdims=True)
    return (weights / total).astype(jnp.bfloat16)


def first_kernel(x_ref, gain_ref, qkv_ref, window_ref, lat_ref, out_ref):
    steps = lat_ref.shape[0]
    group = x_ref.shape[0] // steps
    lane = lax.broadcasted_iota(jnp.int32, (group, 128), 1)
    gain = gain_ref[...]
    for step in range(steps):
        mine = pl.ds(step * group, group)
        normed = norm_rows(x_ref[mine, :].astype(jnp.float32), gain).astype(jnp.bfloat16)
        query = (dot_rows(normed, qkv_ref[0]).astype(jnp.bfloat16) * 0.125).astype(jnp.bfloat16)
        key = dot_rows(normed, qkv_ref[1]).astype(jnp.bfloat16)
        value = dot_rows(normed, qkv_ref[2]).astype(jnp.bfloat16)
        keep = window_ref[...] * lat_ref[step] > 0.0
        for pair in range(query.shape[1] // 128):
            here = slice(pair * 128, pair * 128 + 128)
            parts = []
            for side in range(2):
                picked = (lane < HD) if side == 0 else (lane >= HD)
                key_side = jnp.where(picked, key[:, here], jnp.zeros_like(key[:, here]))
                scores = lax.dot_general(
                    query[:, here],
                    key_side,
                    (((1,), (1,)), ((), ())),
                    preferred_element_type=jnp.float32,
                )
                parts.append(dot_rows(softmax_rows(scores, keep), value[:, here]))
            out_ref[mine, here] = jnp.where(lane < HD, parts[0], parts[1]).astype(jnp.bfloat16)


def third_kernel(core_ref, own_ref, other_ref, gain_ref, qkv_ref, out_ref, normed_ref):
    blocks, sides, line, width = own_ref.shape
    core = core_ref[0]
    half = blocks * width
    count = 1.0 / (2 * half)
    rows = 32
    for side in range(sides):
        for start in range(0, line, rows):
            mine = slice(start, start + rows)
            tiles = [own_ref[z, side, mine, :].astype(jnp.float32) for z in range(blocks)]
            tiles += [other_ref[z, 1 - side, mine, :].astype(jnp.float32) for z in range(blocks)]
            row_mean = jnp.sum(sum(tiles), axis=-1, keepdims=True) * count
            tiles = [tile - row_mean for tile in tiles]
            spread = jnp.sum(sum(tile * tile for tile in tiles), axis=-1, keepdims=True)
            scale = lax.rsqrt(spread * count + 1e-05)
            for place, tile in enumerate(tiles):
                origin = core if place < blocks else 1 - core
                gain = gain_ref[origin * blocks + place % blocks]
                normed_ref[
                    side * line + start : side * line + start + rows,
                    place * width : (place + 1) * width,
                ] = (tile * scale * gain).astype(jnp.bfloat16)
    own_rows = pl.multiple_of(core * half, half)
    other_rows = pl.multiple_of((1 - core) * half, half)
    triple = (
        dot_rows(normed_ref[:, :half], qkv_ref[pl.ds(own_rows, half), :])
        + dot_rows(normed_ref[:, half:], qkv_ref[pl.ds(other_rows, half), :])
    ).astype(jnp.bfloat16)
    query = (triple[:, :HD] * 0.125).astype(jnp.bfloat16)
    key = triple[:, HD : 2 * HD]
    value = triple[:, 2 * HD :]
    token = lax.broadcasted_iota(jnp.int32, (128, 128), 0)
    other = lax.broadcasted_iota(jnp.int32, (128, 128), 1)
    keep = jnp.right_shift(token, 5) == jnp.right_shift(other, 5)
    mixed = []
    for group in range(sides * line // 128):
        mine = slice(group * 128, group * 128 + 128)
        scores = lax.dot_general(
            query[mine], key[mine], (((1,), (1,)), ((), ())), preferred_element_type=jnp.float32
        )
        mixed.append(dot_rows(softmax_rows(scores, keep), value[mine]))
    mixed = jnp.concatenate(mixed, axis=0)
    count = line // blocks
    for z in range(blocks):
        for side in range(sides):
            start = side * line + z * count
            out_ref[z, side] = mixed[start : start + count].astype(jnp.bfloat16)


def heads_kernel(heads_ref, late_ref, own_ref, send_ref):
    total = [None, None]
    for z in range(heads_ref.shape[0]):
        left = jnp.concatenate(
            [heads_ref[z, 0].astype(jnp.float32), heads_ref[z, 1].astype(jnp.float32)], axis=0
        ).astype(jnp.bfloat16)
        for part in range(2):
            right = jnp.concatenate(
                [late_ref[(2 * row + part) * 8 + z, :, 1280:2304] for row in range(4)], axis=0
            )
            product = dot_rows(left, right)
            total[part] = product if z == 0 else total[part] + product
    count = heads_ref.shape[2]
    for part in range(2):
        here = slice(part * 1024, part * 1024 + 1024)
        own_ref[:, here] = total[part][:count]
        send_ref[:, here] = total[part][count:].astype(jnp.bfloat16)


def spread_matrix(lat_count, lon_count):
    fine = (2 * lat_count * lon_count, lat_count * lon_count // 2)
    row = lax.broadcasted_iota(jnp.int32, fine, 0)
    column = lax.broadcasted_iota(jnp.int32, fine, 1)
    bits = lon_count.bit_length() - 1
    lat = jnp.right_shift(row, bits + 2)
    level = jnp.right_shift(row, bits) & 1
    lon = jnp.right_shift(row & (lon_count - 1), 1)
    source = (lat * 2 + level) * (lon_count // 2) + lon
    return jnp.where(source == column, 1.0, 0.0).astype(jnp.float32)


def spread_rows(values, lat_count, lon_count):
    return lax.dot_general(
        spread_matrix(lat_count, lon_count),
        values,
        (((1,), (0,)), ((), ())),
        precision=lax.Precision.HIGHEST,
        preferred_element_type=jnp.float32,
    )


def up_kernel(
    core_ref, own_coarse_ref, other_coarse_ref, part_ref, recv_ref, late_ref, swapped_ref,
    second_ref, skip_ref, out_ref, coarse_ref, lift_ref, level_ref, small_ref,
):
    core = core_ref[0]
    blocks, count, width = own_coarse_ref.shape
    half = blocks * width
    for z in range(blocks):
        for ref, origin in ((own_coarse_ref, core), (other_coarse_ref, 1 - core)):
            coarse_ref[origin * blocks + z] = ref[z].astype(jnp.float32)
    level_three = []
    for place in range(2 * blocks):
        here = slice(place * width, place * width + width)
        level_three.append(
            (coarse_ref[place] + (part_ref[:, here] + recv_ref[:, here].astype(jnp.float32))).astype(
                jnp.bfloat16
            )
        )
    for weights_ref, origin in ((late_ref, core), (swapped_ref, 1 - core)):
        total = None
        for ring in range(2):
            for z in range(8):
                right = jnp.concatenate(
                    [weights_ref[y * 8 + z, :, ring * 640 : ring * 640 + 512] for y in range(8)],
                    axis=0,
                )
                product = dot_rows(level_three[ring * 8 + z], right)
                total = product if total is None else total + product
        lift_ref[origin] = total
    lat_count, lon_count = 6, 8
    for side in range(2):
        here = slice(side * 512, side * 512 + 512)
        level_ref[:, here] = (
            second_ref[:, here].astype(jnp.float32)
            + spread_rows(lift_ref[side], lat_count, lon_count)
        ).astype(jnp.bfloat16)
    for weights_ref, origin in ((late_ref, core), (swapped_ref, 1 - core)):
        total = None
        for ring in range(2):
            for z in range(0, 8, 2):
                right = jnp.concatenate(
                    [
                        jnp.concatenate(
                            [
                                weights_ref[
                                    (2 * row + part) * 8 + zz, :, ring * 640 + 512 : ring * 640 + 640
                                ]
                                for zz in (z, z + 1)
                                for row in range(4)
                            ],
                            axis=0,
                        )
                        for part in range(2)
                    ],
                    axis=1,
                )
                start = (ring * 8 + z) * 64
                product = dot_rows(level_ref[:, start : start + 128], right)
                total = product if total is None else total + product
        small_ref[origin] = total
    for side in range(2):
        here = slice(side * 256, side * 256 + 256)
        out_ref[:, here] = (
            skip_ref[:, here].astype(jnp.float32)
            + spread_rows(small_ref[side], 2 * lat_count, 2 * lon_count)
        ).astype(jnp.bfloat16)


Z_RING = 8
RINGS = [[ring * Z_RING + place for place in range(Z_RING)] for ring in range(2)]


def swap_cores(values):
    count = lax.axis_size("lon")
    return lax.ppermute(values, "lon", [(i, i ^ 1) for i in range(count)])


def swap_rings(values):
    count = lax.axis_size("lat")
    return lax.ppermute(values, "lat", [(i, (i + Z_RING) % count) for i in range(count)])


def swap_shards(values):
    lon_count = lax.axis_size("lon")
    pairs = []
    for lat in range(lax.axis_size("lat")):
        for lon in range(lon_count):
            ring, place = divmod(lat, Z_RING)
            target = (lat, lon)
            if ring != lon % 2:
                target = ((1 - ring) * Z_RING + place, lon ^ 1)
            pairs.append((lat * lon_count + lon, target[0] * lon_count + target[1]))
    return lax.ppermute(values, ("lat", "lon"), pairs)


def ring_scatter(blocks):
    return lax.all_to_all(blocks, "lat", 0, 0, axis_index_groups=RINGS, tiled=True)


def ring_gather(values):
    return ring_scatter(jnp.broadcast_to(values[None], (Z_RING,) + values.shape))


def in_order(flag, own, other, axis):
    return jnp.where(
        flag == 0,
        jnp.concatenate([own, other], axis=axis),
        jnp.concatenate([other, own], axis=axis),
    )


def cut(values, row, rows, column, columns):
    return lax.dynamic_slice(values, (row, column), (rows, columns))


def after(values, *before):
    return lax.optimization_barrier((values,) + before)[0]


def column_gather(values):
    groups = [[4 * y + x for y in range(8)] for x in range(4)]
    return lax.all_to_all(
        jnp.broadcast_to(values[None], (8,) + values.shape),
        "lon",
        0,
        0,
        axis_index_groups=groups,
        tiled=True,
    )


def on_device(
    fields,
    land_ids,
    surface_table,
    level_table,
    norm_first,
    qkv_first,
    out_first,
    norm_merge2,
    merge_second,
    norm_merge3,
    merge_third,
    norm_third,
    qkv_third,
    out_third,
    up_third,
    up_second,
):
    tile_rows, levels, tile_cols, feat_dim = fields.shape
    lat_count = lax.axis_size("lat")
    ring = lax.axis_index("lat") // Z_RING
    core = lax.axis_index("lon") % 2
    column = lax.axis_index("lon") // 4

    own_merge = lax.dynamic_slice_in_dim(merge_second, core * 512, 512, 1)[None]
    both_merge = in_order(ring, own_merge, swap_rings(own_merge), 0)
    merge_half = lax.all_gather(
        both_merge,
        "lat",
        axis=1,
        axis_index_groups=RINGS,
        tiled=True,
    ).reshape(-1, 512)

    own_rest = jnp.concatenate(
        [
            cut(out_first, column // 4 * 16, 16, column % 4 * 128, 128),
            cut(up_third, column * 16, 16, core * 512, 512),
            cut(up_second, column // 2 * 16, 16, core * 256 + column % 2 * 128, 128),
        ],
        axis=1,
    )[None]
    both_rest = in_order(ring, own_rest, swap_rings(own_rest), 0)
    out_first_rows = ring_gather(both_rest[:, :, :128])
    out_first_tiles = column_gather(out_first_rows)
    out_first_all = (
        out_first_tiles.reshape(2, 4, Z_RING, 2, 16, 128)
        .transpose(3, 2, 0, 4, 1, 5)
        .reshape(feat_dim, feat_dim)
    )
    out_third = swap_shards(out_third)

    picks = (land_ids[:, :, None] == jnp.arange(3, dtype=jnp.int32)).astype(jnp.float32)
    surface = jnp.einsum("ijs,sc->ijc", picks, surface_table.astype(jnp.float32))
    hidden = (
        fields.astype(jnp.float32)
        + surface[:, None, :, :]
        + level_table.astype(jnp.float32)[None, :, None, :]
    ).astype(jnp.bfloat16)
    ext_rows = tile_rows + 4
    ext_cols = tile_cols + 4
    grown = with_halo(
        hidden, (("lat", 0), ("lon", 2)), 2, ((both_merge,), (out_first_rows, out_third))
    )
    group = 8 * ext_cols
    token_col = jnp.arange(group) % ext_cols // 4
    same_window = (token_col[:, None] == token_col[None, :]).astype(jnp.float32)
    lat_place = lax.axis_index("lat") * tile_rows + jnp.arange(ext_rows) - 2
    valid_rows = ((lat_place >= 0) & (lat_place < tile_rows * lat_count)).astype(jnp.float32)
    valid_rows = jnp.repeat(valid_rows, 2 * ext_cols).reshape(ext_rows // 4, 1, group)
    attended = call_kernel(
        first_kernel,
        jax.ShapeDtypeStruct((ext_rows * levels * ext_cols, feat_dim), jnp.bfloat16),
        (
            grown.reshape(-1, feat_dim),
            norm_first[None],
            qkv_first,
            same_window,
            valid_rows,
        ),
        flops=2 * 640 * 512 * 1536,
    )
    merge_third = swap_shards(after(merge_third, grown))
    qkv_third = swap_shards(after(qkv_third, grown))
    late = jnp.concatenate(
        [
            both_rest[0, :, 128:],
            both_rest[1, :, 128:],
            cut(out_third, column // 2 * 16, 16, column % 2 * 1024, 1024),
        ],
        axis=1,
    )
    late_rows = ring_gather(after(late, attended))
    attended = attended.reshape(ext_rows, levels, ext_cols, feat_dim)[
        2 : tile_rows + 2, :, 2 : tile_cols + 2, :
    ]
    projected = jnp.dot(
        attended.reshape(-1, feat_dim), out_first_all, preferred_element_type=jnp.float32
    ).reshape(hidden.shape)
    skip_first = (hidden.astype(jnp.float32) + projected).astype(jnp.bfloat16)
    quads = split_quads(skip_first)
    merged_in = norm_rows(quads.astype(jnp.float32), norm_merge2).astype(jnp.bfloat16)
    merged_in = merged_in.reshape(-1, quads.shape[-1])
    merged_pair = jnp.concatenate([merged_in, swap_cores(merged_in)], axis=0)
    second_half = jnp.dot(merged_pair, merge_half, preferred_element_type=jnp.float32).astype(
        jnp.bfloat16
    )
    own_rows = merged_in.shape[0]
    second_grid = in_order(core, second_half[:own_rows], swap_cores(second_half[own_rows:]), 1)

    late = lax.all_gather(
        late_rows,
        "lon",
        axis=0,
        axis_index_groups=[[4 * y + x for y in range(8)] for x in range(4)],
        tiled=True,
    )

    second_cells = second_grid
    second_grid = second_grid.reshape(tile_rows // 2, levels, tile_cols // 2, -1)
    quads_coarse = split_quads(second_grid)
    coarse_in = (
        norm_rows(quads_coarse.astype(jnp.float32), norm_merge3)
        .astype(jnp.bfloat16)
        .reshape(-1, quads_coarse.shape[-1])
    )
    coarse_in = after(coarse_in, late_rows, merge_third, qkv_third)
    own_count = coarse_in.shape[0]
    line = Z_RING * own_count

    ring_tokens = ring_gather(coarse_in).reshape(line, -1)
    column_block = jnp.stack(
        [
            jnp.dot(tokens, merge_third, preferred_element_type=jnp.float32).astype(jnp.bfloat16)
            for tokens in (ring_tokens, swap_cores(ring_tokens))
        ]
    )
    own_columns = ring_gather(column_block)
    other_columns = swap_cores(own_columns)
    blocks, _, _, width = own_columns.shape
    head_feats = qkv_third.shape[2]
    core_id = core.astype(jnp.int32).reshape(1)
    heads_out = call_kernel(
        third_kernel,
        jax.ShapeDtypeStruct((Z_RING, 2, own_count, head_feats), jnp.bfloat16),
        (
            core_id,
            own_columns,
            other_columns,
            norm_third.reshape(2 * blocks, 1, width),
            jnp.concatenate([qkv_third[0], qkv_third[1], qkv_third[2]], axis=1),
        ),
        (pltpu.VMEM((2 * line, 2 * blocks * width), jnp.bfloat16),),
        flops=2 * 384 * 2048 * 192,
    )

    chip_heads = ring_scatter(heads_out)
    own_part, send_part = call_kernel(
        heads_kernel,
        (
            jax.ShapeDtypeStruct((own_count, 2048), jnp.float32),
            jax.ShapeDtypeStruct((own_count, 2048), jnp.bfloat16),
        ),
        (chip_heads, late),
        flops=2 * 48 * 512 * 2048,
    )
    place = lax.axis_index("lat") % Z_RING
    own_coarse, other_coarse = [
        lax.dynamic_slice_in_dim(columns[:, side], place * own_count, own_count, 1)
        for side, columns in enumerate((own_columns, other_columns))
    ]
    decoded = call_kernel(
        up_kernel,
        jax.ShapeDtypeStruct((tile_rows * levels * tile_cols, feat_dim), jnp.bfloat16),
        (
            core_id,
            own_coarse,
            other_coarse,
            own_part,
            swap_cores(send_part),
            late,
            swap_cores(late[:, :, :1280]),
            second_cells,
            skip_first.reshape(-1, feat_dim),
        ),
        (
            pltpu.VMEM((2 * blocks, own_count, width), jnp.float32),
            pltpu.VMEM((2, own_count, 512), jnp.float32),
            pltpu.VMEM((second_cells.shape[0], 1024), jnp.bfloat16),
            pltpu.VMEM((2, second_cells.shape[0], 256), jnp.float32),
        ),
        flops=2 * (24 * 2048 * 1024 + 96 * 1024 * 512),
    )
    return decoded.reshape(fields.shape)


def solution(mesh):
    in_specs = (
        P("lat", None, "lon", None),
        P("lat", "lon"),
        P(),
        P(),
        P(),
        P(),
        P("lat", None),
        P(),
        P("lat", None),
        P(),
        P(None, "lat"),
        P(),
        P(None, None, "lat"),
        P("lat", None),
        P("lat", None),
        P("lat", None),
    )
    out_specs = P("lat", None, "lon", None)
    return jax.shard_map(
        on_device, mesh=mesh, in_specs=in_specs, out_specs=out_specs, check_vma=False
    )
```

profile of v0, /device:TPU:1, one launch (start us, length us, event | category | flops | bytes accessed | tf_op | source)
XLA Modules:
  0.0 243.8 jit_solution(4411863699236502410)
XLA Ops:
  7.5 5.5 %collective-permute-start = (bf16[1,128,512]{2,1,0:T(8,128)(2,1)S(1)}, bf16[1,128,512]{2,1,0:T(8,128)(2,1)S(1)}, u32[]{:S(2)}, u32[]{:S(2)}) collective-permute-start(bf16[1,128,512]{2,1,0:T(8,128)(2,1)S(1)} %dynamic-slice_bitcast_fusion), channel_id=1, source_target_pairs={{0,256},{32,288},{64,320},{96,352},{128,384},{160,416},{192,448},{... | collective-permute-start | bytes 393224 | tf_op jit(solution)/shard_map/ppermute | solution.py:278
  18.3 4.9 %collective-permute-start.3 = (bf16[1,16,768]{2,1,0:T(8,128)(2,1)S(1)}, bf16[1,16,768]{2,1,0:T(8,128)(2,1)S(1)}, u32[]{:S(2)}, u32[]{:S(2)}) collective-permute-start(bf16[1,16,768]{2,1,0:T(8,128)(2,1)S(1)} %maximum_bitcast_fusion), channel_id=1, source_target_pairs={{0,256},{32,288},{64,320},{96,352},{128,384},{160,416},{192,448},{... | collective-permute-start | bytes 73736 | tf_op jit(solution)/shard_map/ppermute | solution.py:278
  23.2 9.5 %collective-permute-start.4 = (bf16[64,2048]{1,0:T(8,128)(2,1)}, bf16[64,2048]{1,0:T(8,128)(2,1)S(1)}, u32[]{:S(2)}, u32[]{:S(2)}) collective-permute-start(bf16[64,2048]{1,0:T(8,128)(2,1)} %param.29), channel_id=1, source_target_pairs={{0,0},{1,256},{2,2},{3,258},{4,4},{5,260},{6,6},{7,262},{8,8},{9,2... | collective-permute-start | bytes 786440 | tf_op jit(solution)/shard_map/ppermute | solution.py:291
  35.4 4.9 %all-to-all-start = ((bf16[8,2,16,128]{3,2,1,0:T(8,128)(2,1)}), bf16[8,2,16,128]{3,2,1,0:T(8,128)(2,1)S(1)}, u32[]{:S(2)}, u32[]{:S(2)}) async-start(bf16[8,2,16,128]{3,2,1,0:T(8,128)(2,1)} %broadcast_in_dim.22), calls=%async_computation | async-start | bytes 131072 | tf_op jit(solution)/shard_map/all_to_all | solution.py:295
  40.4 3.4 %collective-permute-start.1 = (bf16[2,2,16,512]{3,2,1,0:T(8,128)(2,1)S(1)}, bf16[2,2,16,512]{3,2,1,0:T(8,128)(2,1)S(1)}, u32[]{:S(2)}, u32[]{:S(2)}) collective-permute-start(bf16[2,2,16,512]{3,2,1,0:T(8,128)(2,1)S(1)} %get-tuple-element.28), channel_id=1, source_target_pairs={{0,32},{32,64},{64,96},{96,128},{128,160},{160,192},{192,224},{224... | collective-permute-start | bytes 196616 | tf_op jit(solution)/shard_map/ppermute | solution.py:19
  43.8 5.5 %collective-permute-start.2 = (bf16[2,2,16,512]{3,2,1,0:T(8,128)(2,1)S(1)}, bf16[2,2,16,512]{3,2,1,0:T(8,128)(2,1)S(1)}, u32[]{:S(2)}, u32[]{:S(2)}) collective-permute-start(bf16[2,2,16,512]{3,2,1,0:T(8,128)(2,1)S(1)} %get-tuple-element.29), channel_id=1, source_target_pairs={{32,0},{64,32},{96,64},{128,96},{160,128},{192,160},{224,192},{256... | collective-permute-start | bytes 196616 | tf_op jit(solution)/shard_map/ppermute | solution.py:21
  50.2 6.8 %all-to-all-start.1 = ((bf16[8,8,2,16,128]{4,3,2,1,0:T(8,128)(2,1)}), bf16[8,8,2,16,128]{4,3,2,1,0:T(8,128)(2,1)}, u32[]{:S(2)}, u32[]{:S(2)}) async-start(bf16[8,8,2,16,128]{4,3,2,1,0:T(8,128)(2,1)} %broadcast_in_dim.26), calls=%async_computation.1 | async-start | bytes 1048576 | tf_op jit(solution)/shard_map/all_to_all | solution.py:320
  63.6 3.3 %collective-permute-done.6 = bf16[16,2,2,512]{3,2,1,0:T(2,128)(2,1)S(1)} collective-permute-done((bf16[16,2,2,512]{3,2,1,0:T(2,128)(2,1)S(1)}, bf16[16,2,2,512]{3,2,1,0:T(2,128)(2,1)S(1)}, u32[]{:S(2)}, u32[]{:S(2)}) %collective-permute-start.6) | collective-permute-done | bytes 65568 | tf_op jit(solution)/shard_map/ppermute | solution.py:21
  69.5 4.2 %shard_map.154 = bf16[640,512]{1,0:T(8,128)(2,1)S(1)} custom-call(bf16[640,512]{1,0:T(8,128)(2,1)S(1)} %reshape.172.x_ref, f32[1,512]{1,0:T(1,128)S(1)} %bitcast.54, bf16[3,512,512]{2,1,0:T(8,128)(2,1)S(1)} %copy-done.4, f32[160,160]{1,0:T(8,128)S(1)} %compare_convert_fusion.window_ref, f32[4,1,160]{2,1,0:T(1,128)S(1)} %broadcast_in_dim.25.lat_ref), custom_call_target="tpu_custom_call" | custom-call | flops 1006632960 | bytes 2335232 | tf_op jit(solution)/shard_map/pallas_call | solution.py:53
  76.0 4.2 %all-to-all-start.2 = ((bf16[8,16,2304]{2,1,0:T(8,128)(2,1)}), bf16[8,16,2304]{2,1,0:T(8,128)(2,1)S(1)}, u32[]{:S(2)}, u32[]{:S(2)}) async-start(bf16[8,16,2304]{2,1,0:T(8,128)(2,1)} %broadcast_in_dim.27), calls=%async_computation.2 | async-start | bytes 1179648 | tf_op jit(solution)/shard_map/all_to_all | solution.py:295
  85.5 10.3 %all-to-all-done.2 = bf16[8,16,2304]{2,1,0:T(8,128)(2,1)S(1)} async-done(((bf16[8,16,2304]{2,1,0:T(8,128)(2,1)}), bf16[8,16,2304]{2,1,0:T(8,128)(2,1)S(1)}, u32[]{:S(2)}, u32[]{:S(2)}) %all-to-all-start.2) | async-done | bytes 589856 | tf_op jit(solution)/shard_map/all_to_all | solution.py:295
  98.4 6.2 %collective-permute-start.7 = (bf16[96,2048]{1,0:T(8,128)(2,1)S(1)}, bf16[96,2048]{1,0:T(8,128)(2,1)S(1)}, u32[]{:S(2)}, u32[]{:S(2)}) collective-permute-start(bf16[96,2048]{1,0:T(8,128)(2,1)S(1)} %multiply_convert_fusion), channel_id=1, source_target_pairs={{0,1},{1,0},{2,3},{3,2},{4,5},{5,4},{6,7},{7,6},{8,9},{9,8},{10,11... | collective-permute-start | bytes 1179656 | tf_op jit(solution)/shard_map/ppermute | solution.py:273
  110.6 3.6 %collective-permute-start.10 = (bf16[3,2048,64]{1,2,0:T(8,128)(2,1)}, bf16[3,2048,64]{1,2,0:T(8,128)(2,1)S(1)}, u32[]{:S(2)}, u32[]{:S(2)}) collective-permute-start(bf16[3,2048,64]{1,2,0:T(8,128)(2,1)} %param.28), channel_id=1, source_target_pairs={{0,0},{1,256},{2,2},{3,258},{4,4},{5,260},{6,6},{7,262},{8,8},{9,2... | collective-permute-start | bytes 2359304 | tf_op jit(solution)/shard_map/ppermute | solution.py:291
  114.2 3.6 %collective-permute-start.9 = (bf16[4096,128]{1,0:T(8,128)(2,1)}, bf16[4096,128]{1,0:T(8,128)(2,1)S(1)}, u32[]{:S(2)}, u32[]{:S(2)}) collective-permute-start(bf16[4096,128]{1,0:T(8,128)(2,1)} %param.26), channel_id=1, source_target_pairs={{0,0},{1,256},{2,2},{3,258},{4,4},{5,260},{6,6},{7,262},{8,8},{9,2... | collective-permute-start | bytes 3145736 | tf_op jit(solution)/shard_map/ppermute | solution.py:291
  120.0 5.6 %collective-permute-done.10 = bf16[3,2048,64]{1,2,0:T(8,128)(2,1)S(1)} collective-permute-done((bf16[3,2048,64]{1,2,0:T(8,128)(2,1)}, bf16[3,2048,64]{1,2,0:T(8,128)(2,1)S(1)}, u32[]{:S(2)}, u32[]{:S(2)}) %collective-permute-start.10) | collective-permute-done | bytes 786464 | tf_op jit(solution)/shard_map/ppermute | solution.py:291
  125.6 11.5 %collective-permute-done.9 = bf16[4096,128]{1,0:T(8,128)(2,1)S(1)} collective-permute-done((bf16[4096,128]{1,0:T(8,128)(2,1)}, bf16[4096,128]{1,0:T(8,128)(2,1)S(1)}, u32[]{:S(2)}, u32[]{:S(2)}) %collective-permute-start.9) | collective-permute-done | bytes 1048608 | tf_op jit(solution)/shard_map/ppermute | solution.py:291
  137.3 25.8 %all_to_all.30 = bf16[8,24,4096]{2,1,0:T(8,128)(2,1)S(1)} all-to-all(bf16[8,24,4096]{2,1,0:T(8,128)(2,1)S(1)} %broadcast_in_dim.28), channel_id=1, replica_groups={{0,32,64,96,128,160,192,224},{256,288,320,352,384,416,448,480},{1,33,65..., dimensions={0} | all-to-all | bytes 3145728 | tf_op jit(solution)/shard_map/all_to_all | solution.py:295
  165.6 3.5 %slice.75 = bf16[64,16,1280]{2,1,0:T(8,128)(2,1)} slice(bf16[64,16,2304]{2,1,0:T(8,128)(2,1)} %all-gather.5.cloned.1.call-done.late_ref), slice={[0:64], [0:16], [0:1280]} | slice | bytes 5242880 | tf_op jit(solution)/shard_map/slice | solution.py:511
  174.5 3.5 %all-to-all-start.4 = ((bf16[8,2,192,128]{3,2,1,0:T(8,128)(2,1)}), bf16[8,2,192,128]{3,2,1,0:T(8,128)(2,1)S(1)}, u32[]{:S(2)}, u32[]{:S(2)}) async-start(bf16[8,2,192,128]{3,2,1,0:T(8,128)(2,1)} %broadcast_in_dim.29), calls=%async_computation.4 | async-start | bytes 1572864 | tf_op jit(solution)/shard_map/all_to_all | solution.py:295
  178.1 23.6 %all-to-all-done.4.own_ref = bf16[8,2,192,128]{3,2,1,0:T(8,128)(2,1)S(1)} async-done(((bf16[8,2,192,128]{3,2,1,0:T(8,128)(2,1)}), bf16[8,2,192,128]{3,2,1,0:T(8,128)(2,1)S(1)}, u32[]{:S(2)}, u32[]{:S(2)}) %all-to-all-start.4) | async-done | bytes 786464 | tf_op jit(solution)/shard_map/all_to_all | solution.py:295
  213.5 3.3 %all-to-all-start.5 = ((bf16[8,2,1536]{2,1,0:T(2,128)(2,1)}), bf16[8,2,1536]{2,1,0:T(2,128)(2,1)S(1)}, u32[]{:S(2)}, u32[]{:S(2)}) async-start(bf16[8,2,1536]{2,1,0:T(2,128)(2,1)} %reshape.188), calls=%async_computation.5 | async-start | bytes 98304 | tf_op jit(solution)/shard_map/all_to_all | solution.py:295
  216.8 6.9 %all-to-all-done.5 = bf16[8,2,1536]{2,1,0:T(2,128)(2,1)S(1)} async-done(((bf16[8,2,1536]{2,1,0:T(2,128)(2,1)}), bf16[8,2,1536]{2,1,0:T(2,128)(2,1)S(1)}, u32[]{:S(2)}, u32[]{:S(2)}) %all-to-all-start.5) | async-done | bytes 49184 | tf_op jit(solution)/shard_map/all_to_all | solution.py:295
  226.7 3.2 %collective-permute-start.13 = (bf16[24,2048]{1,0:T(8,128)(2,1)S(1)}, bf16[24,2048]{1,0:T(8,128)(2,1)S(1)}, u32[]{:S(2)}, u32[]{:S(2)}) collective-permute-start(bf16[24,2048]{1,0:T(8,128)(2,1)S(1)} %get-tuple-element.20), channel_id=1, source_target_pairs={{0,1},{1,0},{2,3},{3,2},{4,5},{5,4},{6,7},{7,6},{8,9},{9,8},{10,11... | collective-permute-start | bytes 294920 | tf_op jit(solution)/shard_map/ppermute | solution.py:273
  230.9 6.1 %shard_map.157 = bf16[384,512]{1,0:T(8,128)(2,1)} custom-call(s32[1]{0:T(128)} %bitcast.core_ref, bf16[8,24,128]{2,1,0:T(8,128)(2,1)S(1)} %dynamic-slice_bitcast_fusion.2.own_coarse_ref, bf16[8,24,128]{2,1,0:T(8,128)(2,1)S(1)} %dynamic-slice_bitcast_fusion.1.other_coarse_ref, f32[24,2048]{1,0:T(8,128)S(1)} %get-tuple-element.19.part_ref, ...), custom_call_target="tpu_custom_call" | custom-call | flops 201326592 | bytes 8323076 | tf_op jit(solution)/shard_map/pallas_call | solution.py:53
  (136 shorter events, 60.7 us)
Async XLA Ops:
  6.5 27.9 %copy-start.14 = (bf16[12,2,16,512]{3,2,1,0:T(8,128)(2,1)S(1)}, bf16[12,2,16,512]{3,2,1,0:T(8,128)(2,1)}, u32[]{:S(2)}) copy-start(bf16[12,2,16,512]{3,2,1,0:T(8,128)(2,1)} %param.16) | copy-start | bytes 1179652
  6.5 99.4 %all-gather.3.cloned.1.call-start = ((), (), s32[]{:S(2)}) async-start(), calls=%async_computation.6 | async-start | bytes 2359296 | tf_op jit(solution)/shard_map/all_gather | solution.py:356
  7.5 7.8 %collective-permute-start = (bf16[1,128,512]{2,1,0:T(8,128)(2,1)S(1)}, bf16[1,128,512]{2,1,0:T(8,128)(2,1)S(1)}, u32[]{:S(2)}, u32[]{:S(2)}) collective-permute-start(bf16[1,128,512]{2,1,0:T(8,128)(2,1)S(1)} %dynamic-slice_bitcast_fusion), channel_id=1, source_target_pairs={{0,256},{32,288},{64,320},{96,352},{128,384},{160,416},{192,448},{... | collective-permute-start | bytes 393224 | tf_op jit(solution)/shard_map/ppermute | solution.py:278
  18.3 16.5 %collective-permute-start.3 = (bf16[1,16,768]{2,1,0:T(8,128)(2,1)S(1)}, bf16[1,16,768]{2,1,0:T(8,128)(2,1)S(1)}, u32[]{:S(2)}, u32[]{:S(2)}) collective-permute-start(bf16[1,16,768]{2,1,0:T(8,128)(2,1)S(1)} %maximum_bitcast_fusion), channel_id=1, source_target_pairs={{0,256},{32,288},{64,320},{96,352},{128,384},{160,416},{192,448},{... | collective-permute-start | bytes 73736 | tf_op jit(solution)/shard_map/ppermute | solution.py:278
  23.2 34.0 %collective-permute-start.4 = (bf16[64,2048]{1,0:T(8,128)(2,1)}, bf16[64,2048]{1,0:T(8,128)(2,1)S(1)}, u32[]{:S(2)}, u32[]{:S(2)}) collective-permute-start(bf16[64,2048]{1,0:T(8,128)(2,1)} %param.29), channel_id=1, source_target_pairs={{0,0},{1,256},{2,2},{3,258},{4,4},{5,260},{6,6},{7,262},{8,8},{9,2... | collective-permute-start | bytes 786440 | tf_op jit(solution)/shard_map/ppermute | solution.py:291
  34.6 22.5 %copy-start.7 = (bf16[12,2,16,512]{3,2,1,0:T(8,128)(2,1)}, bf16[12,2,16,512]{3,2,1,0:T(8,128)(2,1)S(1)}, u32[]{:S(2)}) copy-start(bf16[12,2,16,512]{3,2,1,0:T(8,128)(2,1)S(1)} %add_convert_fusion) | copy-start | bytes 1179652
  35.4 13.9 %all-to-all-start = ((bf16[8,2,16,128]{3,2,1,0:T(8,128)(2,1)}), bf16[8,2,16,128]{3,2,1,0:T(8,128)(2,1)S(1)}, u32[]{:S(2)}, u32[]{:S(2)}) async-start(bf16[8,2,16,128]{3,2,1,0:T(8,128)(2,1)} %broadcast_in_dim.22), calls=%async_computation | async-start | bytes 131072 | tf_op jit(solution)/shard_map/all_to_all | solution.py:295
  40.4 16.7 %collective-permute-start.1 = (bf16[2,2,16,512]{3,2,1,0:T(8,128)(2,1)S(1)}, bf16[2,2,16,512]{3,2,1,0:T(8,128)(2,1)S(1)}, u32[]{:S(2)}, u32[]{:S(2)}) collective-permute-start(bf16[2,2,16,512]{3,2,1,0:T(8,128)(2,1)S(1)} %get-tuple-element.28), channel_id=1, source_target_pairs={{0,32},{32,64},{64,96},{96,128},{128,160},{160,192},{192,224},{224... | collective-permute-start | bytes 196616 | tf_op jit(solution)/shard_map/ppermute | solution.py:19
  43.8 13.3 %collective-permute-start.2 = (bf16[2,2,16,512]{3,2,1,0:T(8,128)(2,1)S(1)}, bf16[2,2,16,512]{3,2,1,0:T(8,128)(2,1)S(1)}, u32[]{:S(2)}, u32[]{:S(2)}) collective-permute-start(bf16[2,2,16,512]{3,2,1,0:T(8,128)(2,1)S(1)} %get-tuple-element.29), channel_id=1, source_target_pairs={{32,0},{64,32},{96,64},{128,96},{160,128},{192,160},{224,192},{256... | collective-permute-start | bytes 196616 | tf_op jit(solution)/shard_map/ppermute | solution.py:21
  50.2 24.9 %all-to-all-start.1 = ((bf16[8,8,2,16,128]{4,3,2,1,0:T(8,128)(2,1)}), bf16[8,8,2,16,128]{4,3,2,1,0:T(8,128)(2,1)}, u32[]{:S(2)}, u32[]{:S(2)}) async-start(bf16[8,8,2,16,128]{4,3,2,1,0:T(8,128)(2,1)} %broadcast_in_dim.26), calls=%async_computation.1 | async-start | bytes 1048576 | tf_op jit(solution)/shard_map/all_to_all | solution.py:320
  58.0 5.7 %collective-permute-start.5 = (bf16[16,2,2,512]{3,2,1,0:T(2,128)(2,1)S(1)}, bf16[16,2,2,512]{3,2,1,0:T(2,128)(2,1)S(1)}, u32[]{:S(2)}, u32[]{:S(2)}) collective-permute-start(bf16[16,2,2,512]{3,2,1,0:T(2,128)(2,1)S(1)} %get-tuple-element.26), channel_id=1, source_target_pairs={{0,1},{1,2},{2,3},{3,4},{4,5},{5,6},{6,7},{7,8},{8,9},{9,10},{10,1... | collective-permute-start | bytes 196616 | tf_op jit(solution)/shard_map/ppermute | solution.py:19
  60.9 6.0 %collective-permute-start.6 = (bf16[16,2,2,512]{3,2,1,0:T(2,128)(2,1)S(1)}, bf16[16,2,2,512]{3,2,1,0:T(2,128)(2,1)S(1)}, u32[]{:S(2)}, u32[]{:S(2)}) collective-permute-start(bf16[16,2,2,512]{3,2,1,0:T(2,128)(2,1)S(1)} %get-tuple-element.27), channel_id=1, source_target_pairs={{1,0},{2,1},{3,2},{4,3},{5,4},{6,5},{7,6},{8,7},{9,8},{10,9},{11,1... | collective-permute-start | bytes 196616 | tf_op jit(solution)/shard_map/ppermute | solution.py:21
  76.0 19.8 %all-to-all-start.2 = ((bf16[8,16,2304]{2,1,0:T(8,128)(2,1)}), bf16[8,16,2304]{2,1,0:T(8,128)(2,1)S(1)}, u32[]{:S(2)}, u32[]{:S(2)}) async-start(bf16[8,16,2304]{2,1,0:T(8,128)(2,1)} %broadcast_in_dim.27), calls=%async_computation.2 | async-start | bytes 1179648 | tf_op jit(solution)/shard_map/all_to_all | solution.py:295
  80.2 85.4 %all-gather.5.cloned.1.call-start = ((), (), s32[]{:S(2)}) async-start(), calls=%async_computation.7 | async-start | bytes 5308416 | tf_op jit(solution)/shard_map/all_gather | solution.py:440
  98.4 7.5 %collective-permute-start.7 = (bf16[96,2048]{1,0:T(8,128)(2,1)S(1)}, bf16[96,2048]{1,0:T(8,128)(2,1)S(1)}, u32[]{:S(2)}, u32[]{:S(2)}) collective-permute-start(bf16[96,2048]{1,0:T(8,128)(2,1)S(1)} %multiply_convert_fusion), channel_id=1, source_target_pairs={{0,1},{1,0},{2,3},{3,2},{4,5},{5,4},{6,7},{7,6},{8,9},{9,8},{10,11... | collective-permute-start | bytes 1179656 | tf_op jit(solution)/shard_map/ppermute | solution.py:273
  108.1 9.8 %collective-permute-start.8 = (bf16[96,512]{1,0:T(8,128)(2,1)S(1)}, bf16[96,512]{1,0:T(8,128)(2,1)S(1)}, u32[]{:S(2)}, u32[]{:S(2)}) collective-permute-start(bf16[96,512]{1,0:T(8,128)(2,1)S(1)} %get-tuple-element.32), channel_id=1, source_target_pairs={{0,1},{1,0},{2,3},{3,2},{4,5},{5,4},{6,7},{7,6},{8,9},{9,8},{10,11... | collective-permute-start | bytes 294920 | tf_op jit(solution)/shard_map/ppermute | solution.py:273
  110.6 15.1 %collective-permute-start.10 = (bf16[3,2048,64]{1,2,0:T(8,128)(2,1)}, bf16[3,2048,64]{1,2,0:T(8,128)(2,1)S(1)}, u32[]{:S(2)}, u32[]{:S(2)}) collective-permute-start(bf16[3,2048,64]{1,2,0:T(8,128)(2,1)} %param.28), channel_id=1, source_target_pairs={{0,0},{1,256},{2,2},{3,258},{4,4},{5,260},{6,6},{7,262},{8,8},{9,2... | collective-permute-start | bytes 2359304 | tf_op jit(solution)/shard_map/ppermute | solution.py:291
  114.2 22.9 %collective-permute-start.9 = (bf16[4096,128]{1,0:T(8,128)(2,1)}, bf16[4096,128]{1,0:T(8,128)(2,1)S(1)}, u32[]{:S(2)}, u32[]{:S(2)}) collective-permute-start(bf16[4096,128]{1,0:T(8,128)(2,1)} %param.26), channel_id=1, source_target_pairs={{0,0},{1,256},{2,2},{3,258},{4,4},{5,260},{6,6},{7,262},{8,8},{9,2... | collective-permute-start | bytes 3145736 | tf_op jit(solution)/shard_map/ppermute | solution.py:291
  163.1 8.4 %collective-permute-start.11 = (bf16[192,4096]{1,0:T(8,128)(2,1)S(1)}, bf16[192,4096]{1,0:T(8,128)(2,1)}, u32[]{:S(2)}, u32[]{:S(2)}) collective-permute-start(bf16[192,4096]{1,0:T(8,128)(2,1)S(1)} %bitcast.55), channel_id=1, source_target_pairs={{0,1},{1,0},{2,3},{3,2},{4,5},{5,4},{6,7},{7,6},{8,9},{9,8},{10,11... | collective-permute-start | bytes 4718600 | tf_op jit(solution)/shard_map/ppermute | solution.py:273
  169.1 61.8 %collective-permute-start.14 = (bf16[64,16,1280]{2,1,0:T(8,128)(2,1)}, bf16[64,16,1280]{2,1,0:T(8,128)(2,1)}, u32[]{:S(2)}, u32[]{:S(2)}) collective-permute-start(bf16[64,16,1280]{2,1,0:T(8,128)(2,1)} %slice.75), channel_id=1, source_target_pairs={{0,1},{1,0},{2,3},{3,2},{4,5},{5,4},{6,7},{7,6},{8,9},{9,8},{10,11... | collective-permute-start | bytes 7864328 | tf_op jit(solution)/shard_map/ppermute | solution.py:273
  174.5 27.1 %all-to-all-start.4 = ((bf16[8,2,192,128]{3,2,1,0:T(8,128)(2,1)}), bf16[8,2,192,128]{3,2,1,0:T(8,128)(2,1)S(1)}, u32[]{:S(2)}, u32[]{:S(2)}) async-start(bf16[8,2,192,128]{3,2,1,0:T(8,128)(2,1)} %broadcast_in_dim.29), calls=%async_computation.4 | async-start | bytes 1572864 | tf_op jit(solution)/shard_map/all_to_all | solution.py:295
  201.7 8.5 %collective-permute-start.12 = (bf16[8,2,192,128]{3,2,1,0:T(8,128)(2,1)S(1)}, bf16[8,2,192,128]{3,2,1,0:T(8,128)(2,1)S(1)}, u32[]{:S(2)}, u32[]{:S(2)}) collective-permute-start(bf16[8,2,192,128]{3,2,1,0:T(8,128)(2,1)S(1)} %all-to-all-done.4.own_ref), channel_id=1, source_target_pairs={{0,1},{1,0},{2,3},{3,2},{4,5},{5,4},{6,7},{7,6},{8,9},{9,8},{10,11... | collective-permute-start | bytes 2359304 | tf_op jit(solution)/shard_map/ppermute | solution.py:273
  213.5 10.3 %all-to-all-start.5 = ((bf16[8,2,1536]{2,1,0:T(2,128)(2,1)}), bf16[8,2,1536]{2,1,0:T(2,128)(2,1)S(1)}, u32[]{:S(2)}, u32[]{:S(2)}) async-start(bf16[8,2,1536]{2,1,0:T(2,128)(2,1)} %reshape.188), calls=%async_computation.5 | async-start | bytes 98304 | tf_op jit(solution)/shard_map/all_to_all | solution.py:295
  226.7 4.2 %collective-permute-start.13 = (bf16[24,2048]{1,0:T(8,128)(2,1)S(1)}, bf16[24,2048]{1,0:T(8,128)(2,1)S(1)}, u32[]{:S(2)}, u32[]{:S(2)}) collective-permute-start(bf16[24,2048]{1,0:T(8,128)(2,1)S(1)} %get-tuple-element.20), channel_id=1, source_target_pairs={{0,1},{1,0},{2,3},{3,2},{4,5},{5,4},{6,7},{7,6},{8,9},{9,8},{10,11... | collective-permute-start | bytes 294920 | tf_op jit(solution)/shard_map/ppermute | solution.py:273
  (17 other events, 93.0 us)
Sparse Core Ops, SparseCore 0:
  16.2 50.2 all-gather.2
  96.8 60.6 all-gather.4
where the time goes:
time: 245 us; the launch traced here: 244 us
  starting transfers between devices  82.2 us (34%)
  waiting for transfers between devices  67 us (27%)
  local copies, waits for them, and re-layouts  26.6 us (11%)
  blocking collectives  25.8 us (11%)
  between operations  14.2 us (6%)
  Pallas kernels  13.4 us (5%)
  other arithmetic  7.39 us (3%)
  matrix products  7.1 us (3%)
    all_to_all x4, waiting for transfers between devices, ring_scatter(): lax.all_to_all(blocks, 'lat', 0, 0, axis_index_groups=RINGS, tiled=True)  40.7 us
    all_to_all x1, blocking collectives, ring_scatter(): lax.all_to_all(blocks, 'lat', 0, 0, axis_index_groups=RINGS, tiled=True)  25.8 us
    ppermute x6, starting transfers between devices, swap_cores(): return lax.ppermute(values, 'lon', [(i, i ^ 1) for i in range(count)])  18.5 us
    ppermute x3, waiting for transfers between devices, swap_shards(): return lax.ppermute(values, ('lat', 'lon'), pairs)  17.1 us
    ppermute x3, starting transfers between devices, swap_shards(): return lax.ppermute(values, ('lat', 'lon'), pairs)  16.8 us
    all_to_all x4, starting transfers between devices, ring_scatter(): lax.all_to_all(blocks, 'lat', 0, 0, axis_index_groups=RINGS, tiled=True)  16.1 us
    pallas_call x4, Pallas kernels, call_kernel(): pl.pallas_call(body, out_shape=out_shape, in_specs=[pl.BlockSpec(memory_s...  13.4 us
    ppermute x2, starting transfers between devices, swap_rings(): lax.ppermute(values, 'lat', [(i, (i + Z_RING) % count) for i in range(cou...  10.3 us
  transfers between devices with their start and end apart: 22, of which 10 were waited for; matrix products, arithmetic and copies ran while one was open for 15% of the time, Pallas kernels for 3%

commit v1 on v0

--- a/solution.py
+++ b/solution.py
@@ -8,44 +8,11 @@
 HD = 64
 
 
-def with_halo(cells, sides, width, ties):
-    for (axis, dim), tie in zip(sides, ties):
-        cells = after(cells, *tie)
-        count = lax.axis_size(axis)
-        head = lax.slice_in_dim(cells, 0, width, axis=dim)
-        tail = lax.slice_in_dim(cells, cells.shape[dim] - width, cells.shape[dim], axis=dim)
-        cells = jnp.concatenate(
-            [
-                lax.ppermute(tail, axis, [(i, (i + 1) % count) for i in range(count)]),
-                cells,
-                lax.ppermute(head, axis, [((i + 1) % count, i) for i in range(count)]),
-            ],
-            axis=dim,
-        )
-    return cells
-
-
 def norm_rows(values, gain):
     row_mean = jnp.mean(values, axis=-1, keepdims=True)
     centred = values - row_mean
     spread = jnp.mean(centred * centred, axis=-1, keepdims=True)
     return centred * lax.rsqrt(spread + 1e-05) * gain
-
-
-def split_quads(cell_grid):
-    lat_count, levels, lon_count, feat_dim = cell_grid.shape
-    blocks = cell_grid.reshape(lat_count // 2, 2, levels, lon_count // 2, 2, feat_dim)
-    return blocks.transpose(0, 2, 3, 1, 4, 5).reshape(
-        lat_count // 2, levels, lon_count // 2, 4 * feat_dim
-    )
-
-
-def spread_quads(cell_grid):
-    lat_count, levels, lon_count, feat_dim = cell_grid.shape
-    widened = jnp.broadcast_to(
-        cell_grid[:, None, :, :, None, :], (lat_count, 2, levels, lon_count, 2, feat_dim)
-    )
-    return widened.reshape(2 * lat_count, levels, 2 * lon_count, feat_dim)
 
 
 def call_kernel(body, out_shape, operands, scratch=(), flops=0):
@@ -78,23 +45,35 @@
     return (weights / total).astype(jnp.bfloat16)
 
 
-def first_kernel(x_ref, gain_ref, qkv_ref, window_ref, lat_ref, out_ref):
+def first_kernel(x_ref, left_ref, right_ref, gain_ref, qkv_ref, window_ref, lat_ref, out_ref):
     steps = lat_ref.shape[0]
-    group = x_ref.shape[0] // steps
-    lane = lax.broadcasted_iota(jnp.int32, (group, 128), 1)
+    own, side = x_ref.shape[0] // steps, left_ref.shape[0] // steps
+    lane = lax.broadcasted_iota(jnp.int32, (own, 128), 1)
+    key_lane = lax.broadcasted_iota(jnp.int32, (own + 2 * side, 128), 1)
     gain = gain_ref[...]
     for step in range(steps):
-        mine = pl.ds(step * group, group)
-        normed = norm_rows(x_ref[mine, :].astype(jnp.float32), gain).astype(jnp.bfloat16)
-        query = (dot_rows(normed, qkv_ref[0]).astype(jnp.bfloat16) * 0.125).astype(jnp.bfloat16)
+        rows = jnp.concatenate(
+            [
+                x_ref[step * own : (step + 1) * own, :],
+                left_ref[step * side : (step + 1) * side, :],
+                right_ref[step * side : (step + 1) * side, :],
+            ],
+            axis=0,
+        )
+        normed = norm_rows(rows.astype(jnp.float32), gain).astype(jnp.bfloat16)
+        query = dot_rows(normed[:own], qkv_ref[0]).astype(jnp.bfloat16)
+        query = (query * 0.125).astype(jnp.bfloat16)
         key = dot_rows(normed, qkv_ref[1]).astype(jnp.bfloat16)
         value = dot_rows(normed, qkv_ref[2]).astype(jnp.bfloat16)
         keep = window_ref[...] * lat_ref[step] > 0.0
+        first = own // 2 if step == 0 else 0
+        last = own // 2 if step == steps - 1 else own
+        start = step * own - own // 2 + first
         for pair in range(query.shape[1] // 128):
             here = slice(pair * 128, pair * 128 + 128)
             parts = []
-            for side in range(2):
-                picked = (lane < HD) if side == 0 else (lane >= HD)
+            for odd in range(2):
+                picked = (key_lane < HD) if odd == 0 else (key_lane >= HD)
                 key_side = jnp.where(picked, key[:, here], jnp.zeros_like(key[:, here]))
                 scores = lax.dot_general(
                     query[:, here],
@@ -103,10 +82,77 @@
                     preferred_element_type=jnp.float32,
                 )
                 parts.append(dot_rows(softmax_rows(scores, keep), value[:, here]))
-            out_ref[mine, here] = jnp.where(lane < HD, parts[0], parts[1]).astype(jnp.bfloat16)
-
-
-def third_kernel(core_ref, own_ref, other_ref, gain_ref, qkv_ref, out_ref, normed_ref):
+            mixed = jnp.where(lane < HD, parts[0], parts[1]).astype(jnp.bfloat16)
+            out_ref[start : start + last - first, here] = mixed[first:last]
+
+
+def pick_matrix(lat_count, lon_count, lat_side, lon_side):
+    shape = (2 * lat_count * lon_count, 8 * lat_count * lon_count)
+    row = lax.broadcasted_iota(jnp.int32, shape, 0)
+    column = lax.broadcasted_iota(jnp.int32, shape, 1)
+    bits = lon_count.bit_length() - 1
+    lon = row & (lon_count - 1)
+    level = jnp.right_shift(row, bits) & 1
+    lat = jnp.right_shift(row, bits + 1)
+    source = ((2 * lat + lat_side) * 2 + level) * (2 * lon_count) + 2 * lon + lon_side
+    return jnp.where(source == column, 1.0, 0.0).astype(jnp.bfloat16)
+
+
+def join_quads(cells, lat_count, lon_count, gain_ref, out_ref):
+    width = cells.shape[1]
+    parts = [
+        dot_rows(pick_matrix(lat_count, lon_count, lat_side, lon_side), cells)
+        for lat_side in range(2)
+        for lon_side in range(2)
+    ]
+    count = 1.0 / (4 * width)
+    row_mean = sum(jnp.sum(part, axis=-1, keepdims=True) for part in parts) * count
+    parts = [part - row_mean for part in parts]
+    spread = sum(jnp.sum(part * part, axis=-1, keepdims=True) for part in parts) * count
+    scale = lax.rsqrt(spread + 1e-05)
+    for place, part in enumerate(parts):
+        here = slice(place * width, place * width + width)
+        out_ref[:, here] = (part * scale * gain_ref[:, here]).astype(jnp.bfloat16)
+
+
+def skip_kernel(attended_ref, hidden_ref, tiles_ref, gain_ref, skip_ref, merged_ref):
+    total = None
+    for ring in range(2):
+        for z in range(0, 8, 4):
+            right = jnp.concatenate(
+                [
+                    jnp.concatenate(
+                        [
+                            tiles_ref[row * 4 + part, zz, ring]
+                            for zz in range(z, z + 4)
+                            for row in range(2)
+                        ],
+                        axis=0,
+                    )
+                    for part in range(4)
+                ],
+                axis=1,
+            )
+            start = (ring * 8 + z) * 32
+            product = dot_rows(attended_ref[:, start : start + 128], right)
+            total = product if total is None else total + product
+    skip = (hidden_ref[...].astype(jnp.float32) + total).astype(jnp.bfloat16)
+    skip_ref[...] = skip
+    join_quads(skip, 6, 8, gain_ref, merged_ref)
+
+
+def join_kernel(core_ref, own_ref, recv_ref, gain_ref, second_ref, coarse_ref, halves_ref):
+    core = core_ref[0]
+    halves_ref[core] = own_ref[...]
+    halves_ref[1 - core] = recv_ref[...]
+    second = jnp.concatenate([halves_ref[0], halves_ref[1]], axis=1)
+    second_ref[...] = second
+    join_quads(second, 3, 4, gain_ref, coarse_ref)
+
+
+def third_kernel(
+    core_ref, own_ref, other_ref, gain_ref, qkv_ref, out_ref, coarse_ref, normed_ref, raw_ref
+):
     blocks, sides, line, width = own_ref.shape
     core = core_ref[0]
     half = blocks * width
@@ -117,6 +163,9 @@
             mine = slice(start, start + rows)
             tiles = [own_ref[z, side, mine, :].astype(jnp.float32) for z in range(blocks)]
             tiles += [other_ref[z, 1 - side, mine, :].astype(jnp.float32) for z in range(blocks)]
+            if side == 0:
+                for place, tile in enumerate(tiles):
+                    raw_ref[mine, place * width : (place + 1) * width] = tile
             row_mean = jnp.sum(sum(tiles), axis=-1, keepdims=True) * count
             tiles = [tile - row_mean for tile in tiles]
             spread = jnp.sum(sum(tile * tile for tile in tiles), axis=-1, keepdims=True)
@@ -128,6 +177,8 @@
                     side * line + start : side * line + start + rows,
                     place * width : (place + 1) * width,
                 ] = (tile * scale * gain).astype(jnp.bfloat16)
+    tokens = line // blocks
+    coarse_ref[...] = raw_ref[pl.ds(pl.multiple_of(core_ref[1] * tokens, 8), tokens), :]
     own_rows = pl.multiple_of(core * half, half)
     other_rows = pl.multiple_of((1 - core) * half, half)
     triple = (
@@ -148,11 +199,10 @@
         )
         mixed.append(dot_rows(softmax_rows(scores, keep), value[mine]))
     mixed = jnp.concatenate(mixed, axis=0)
-    count = line // blocks
     for z in range(blocks):
         for side in range(sides):
-            start = side * line + z * count
-            out_ref[z, side] = mixed[start : start + count].astype(jnp.bfloat16)
+            start = side * line + z * tokens
+            out_ref[z, side] = mixed[start : start + tokens].astype(jnp.bfloat16)
 
 
 def heads_kernel(heads_ref, late_ref, own_ref, send_ref):
@@ -197,15 +247,14 @@
 
 
 def up_kernel(
-    core_ref, own_coarse_ref, other_coarse_ref, part_ref, recv_ref, late_ref, swapped_ref,
+    core_ref, own_coarse_ref, part_ref, recv_ref, late_ref, swapped_ref,
     second_ref, skip_ref, out_ref, coarse_ref, lift_ref, level_ref, small_ref,
 ):
     core = core_ref[0]
-    blocks, count, width = own_coarse_ref.shape
-    half = blocks * width
+    blocks, width = 8, 128
     for z in range(blocks):
-        for ref, origin in ((own_coarse_ref, core), (other_coarse_ref, 1 - core)):
-            coarse_ref[origin * blocks + z] = ref[z].astype(jnp.float32)
+        for place, origin in ((z, core), (blocks + z, 1 - core)):
+            coarse_ref[origin * blocks + z] = own_coarse_ref[:, place * width : (place + 1) * width]
     level_three = []
     for place in range(2 * blocks):
         here = slice(place * width, place * width + width)
@@ -268,6 +317,13 @@
 RINGS = [[ring * Z_RING + place for place in range(Z_RING)] for ring in range(2)]
 
 
+def neighbours(first, last, axis):
+    count = lax.axis_size(axis)
+    before = lax.ppermute(last, axis, [(i, (i + 1) % count) for i in range(count)])
+    behind = lax.ppermute(first, axis, [((i + 1) % count, i) for i in range(count)])
+    return before, behind
+
+
 def swap_cores(values):
     count = lax.axis_size("lon")
     return lax.ppermute(values, "lon", [(i, i ^ 1) for i in range(count)])
@@ -370,14 +426,10 @@
         axis=1,
     )[None]
     both_rest = in_order(ring, own_rest, swap_rings(own_rest), 0)
-    out_first_rows = ring_gather(both_rest[:, :, :128])
-    out_first_tiles = column_gather(out_first_rows)
-    out_first_all = (
-        out_first_tiles.reshape(2, 4, Z_RING, 2, 16, 128)
-        .transpose(3, 2, 0, 4, 1, 5)
-        .reshape(feat_dim, feat_dim)
-    )
+    core_place = jnp.stack([core, lax.axis_index("lat") % Z_RING]).astype(jnp.int32)
     out_third = swap_shards(out_third)
+    merge_third = swap_shards(merge_third)
+    qkv_third = swap_shards(qkv_third)
 
     picks = (land_ids[:, :, None] == jnp.arange(3, dtype=jnp.int32)).astype(jnp.float32)
     surface = jnp.einsum("ijs,sc->ijc", picks, surface_table.astype(jnp.float32))
@@ -386,31 +438,41 @@
         + surface[:, None, :, :]
         + level_table.astype(jnp.float32)[None, :, None, :]
     ).astype(jnp.bfloat16)
+    hidden = after(hidden, both_merge)
+    above, below = neighbours(hidden[:2], hidden[-2:], "lat")
+    cells = jnp.concatenate([above, hidden, below], axis=0)
+    cells = after(cells, both_rest)
+    left, right = neighbours(cells[:, :, :2], cells[:, :, -2:], "lon")
+    out_first_rows = ring_gather(after(both_rest, cells)[:, :, :128])
+    left = after(left, out_first_rows, out_third, merge_third, qkv_third)
+    out_first_tiles = column_gather(out_first_rows).reshape(8, Z_RING, 2, 16, 128)
+
     ext_rows = tile_rows + 4
-    ext_cols = tile_cols + 4
-    grown = with_halo(
-        hidden, (("lat", 0), ("lon", 2)), 2, ((both_merge,), (out_first_rows, out_third))
-    )
-    group = 8 * ext_cols
-    token_col = jnp.arange(group) % ext_cols // 4
-    same_window = (token_col[:, None] == token_col[None, :]).astype(jnp.float32)
+    own_window = (jnp.arange(32 * 4) % tile_cols + 2) // 4
+    key_window = jnp.concatenate(
+        [own_window, jnp.zeros((16,), jnp.int32), jnp.full((16,), tile_cols // 4, jnp.int32)]
+    )
+    same_window = (own_window[:, None] == key_window[None, :]).astype(jnp.float32)
     lat_place = lax.axis_index("lat") * tile_rows + jnp.arange(ext_rows) - 2
     valid_rows = ((lat_place >= 0) & (lat_place < tile_rows * lat_count)).astype(jnp.float32)
-    valid_rows = jnp.repeat(valid_rows, 2 * ext_cols).reshape(ext_rows // 4, 1, group)
+    valid_rows = valid_rows.reshape(ext_rows // 4, 1, 4)
+    valid_keys = jnp.concatenate(
+        [jnp.repeat(valid_rows, 2 * count, axis=2) for count in (tile_cols, 2, 2)], axis=2
+    )
     attended = call_kernel(
         first_kernel,
-        jax.ShapeDtypeStruct((ext_rows * levels * ext_cols, feat_dim), jnp.bfloat16),
-        (
-            grown.reshape(-1, feat_dim),
+        jax.ShapeDtypeStruct((tile_rows * levels * tile_cols, feat_dim), jnp.bfloat16),
+        (
+            cells.reshape(-1, feat_dim),
+            left.reshape(-1, feat_dim),
+            right.reshape(-1, feat_dim),
             norm_first[None],
             qkv_first,
             same_window,
-            valid_rows,
+            valid_keys,
         ),
         flops=2 * 640 * 512 * 1536,
     )
-    merge_third = swap_shards(after(merge_third, grown))
-    qkv_third = swap_shards(after(qkv_third, grown))
     late = jnp.concatenate(
         [
             both_rest[0, :, 128:],
@@ -420,23 +482,32 @@
         axis=1,
     )
     late_rows = ring_gather(after(late, attended))
-    attended = attended.reshape(ext_rows, levels, ext_cols, feat_dim)[
-        2 : tile_rows + 2, :, 2 : tile_cols + 2, :
-    ]
-    projected = jnp.dot(
-        attended.reshape(-1, feat_dim), out_first_all, preferred_element_type=jnp.float32
-    ).reshape(hidden.shape)
-    skip_first = (hidden.astype(jnp.float32) + projected).astype(jnp.bfloat16)
-    quads = split_quads(skip_first)
-    merged_in = norm_rows(quads.astype(jnp.float32), norm_merge2).astype(jnp.bfloat16)
-    merged_in = merged_in.reshape(-1, quads.shape[-1])
+    tokens = attended.shape[0]
+    skip_first, merged_in = call_kernel(
+        skip_kernel,
+        (
+            jax.ShapeDtypeStruct((tokens, feat_dim), jnp.bfloat16),
+            jax.ShapeDtypeStruct((tokens // 4, 4 * feat_dim), jnp.bfloat16),
+        ),
+        (attended, hidden.reshape(-1, feat_dim), out_first_tiles, norm_merge2[None]),
+        flops=2 * 384 * 512 * 512,
+    )
     merged_pair = jnp.concatenate([merged_in, swap_cores(merged_in)], axis=0)
     second_half = jnp.dot(merged_pair, merge_half, preferred_element_type=jnp.float32).astype(
         jnp.bfloat16
     )
     own_rows = merged_in.shape[0]
-    second_grid = in_order(core, second_half[:own_rows], swap_cores(second_half[own_rows:]), 1)
-
+    second_cells, coarse_in = call_kernel(
+        join_kernel,
+        (
+            jax.ShapeDtypeStruct((own_rows, 1024), jnp.bfloat16),
+            jax.ShapeDtypeStruct((own_rows // 4, 4096), jnp.bfloat16),
+        ),
+        (core_place, second_half[:own_rows], swap_cores(second_half[own_rows:]), norm_merge3[None]),
+        (pltpu.VMEM((2, own_rows, 512), jnp.bfloat16),),
+        flops=2 * 96 * 96 * 1024,
+    )
+    late_rows = after(late_rows, second_half)
     late = lax.all_gather(
         late_rows,
         "lon",
@@ -445,15 +516,8 @@
         tiled=True,
     )
 
-    second_cells = second_grid
-    second_grid = second_grid.reshape(tile_rows // 2, levels, tile_cols // 2, -1)
-    quads_coarse = split_quads(second_grid)
-    coarse_in = (
-        norm_rows(quads_coarse.astype(jnp.float32), norm_merge3)
-        .astype(jnp.bfloat16)
-        .reshape(-1, quads_coarse.shape[-1])
-    )
-    coarse_in = after(coarse_in, late_rows, merge_third, qkv_third)
+    qkv_joined = jnp.concatenate([qkv_third[0], qkv_third[1], qkv_third[2]], axis=1)
+    coarse_in = after(coarse_in, late_rows, qkv_joined)
     own_count = coarse_in.shape[0]
     line = Z_RING * own_count
 
@@ -468,18 +532,23 @@
     other_columns = swap_cores(own_columns)
     blocks, _, _, width = own_columns.shape
     head_feats = qkv_third.shape[2]
-    core_id = core.astype(jnp.int32).reshape(1)
-    heads_out = call_kernel(
+    heads_out, own_coarse = call_kernel(
         third_kernel,
-        jax.ShapeDtypeStruct((Z_RING, 2, own_count, head_feats), jnp.bfloat16),
-        (
-            core_id,
+        (
+            jax.ShapeDtypeStruct((Z_RING, 2, own_count, head_feats), jnp.bfloat16),
+            jax.ShapeDtypeStruct((own_count, 2 * blocks * width), jnp.float32),
+        ),
+        (
+            core_place,
             own_columns,
             other_columns,
             norm_third.reshape(2 * blocks, 1, width),
-            jnp.concatenate([qkv_third[0], qkv_third[1], qkv_third[2]], axis=1),
-        ),
-        (pltpu.VMEM((2 * line, 2 * blocks * width), jnp.bfloat16),),
+            qkv_joined,
+        ),
+        (
+            pltpu.VMEM((2 * line, 2 * blocks * width), jnp.bfloat16),
+            pltpu.VMEM((line, 2 * blocks * width), jnp.float32),
+        ),
         flops=2 * 384 * 2048 * 192,
     )
 
@@ -493,24 +562,19 @@
         (chip_heads, late),
         flops=2 * 48 * 512 * 2048,
     )
-    place = lax.axis_index("lat") % Z_RING
-    own_coarse, other_coarse = [
-        lax.dynamic_slice_in_dim(columns[:, side], place * own_count, own_count, 1)
-        for side, columns in enumerate((own_columns, other_columns))
-    ]
+    late_swapped = swap_cores(after(late, heads_out))
     decoded = call_kernel(
         up_kernel,
         jax.ShapeDtypeStruct((tile_rows * levels * tile_cols, feat_dim), jnp.bfloat16),
         (
-            core_id,
+            core_place,
             own_coarse,
-            other_coarse,
             own_part,
             swap_cores(send_part),
             late,
-            swap_cores(late[:, :, :1280]),
+            late_swapped,
             second_cells,
-            skip_first.reshape(-1, feat_dim),
+            skip_first,
         ),
         (
             pltpu.VMEM((2 * blocks, own_count, width), jnp.float32),

time: 245 us -> 246 us (level)
  blocking collectives: 25.8 us -> 78.2 us
  waiting for transfers between devices: 67 us -> 21.2 us
  local copies, waits for them, and re-layouts: 26.6 us -> 13.3 us
  Pallas kernels: 13.4 us -> 22.3 us
  starting transfers between devices: 82.2 us -> 87.2 us
  other arithmetic: 7.39 us -> 2.48 us
    all_to_all x1 -> x3, blocking collectives: 25.8 us -> 78.2 us  [ring_scatter(): lax.all_to_all(blocks, 'lat', 0, 0, axis_index_groups=RINGS, tiled=True)]
    all_to_all x4 -> x2, waiting for transfers between devices: 40.7 us -> 7.75 us  [ring_scatter(): lax.all_to_all(blocks, 'lat', 0, 0, axis_index_groups=RINGS, tiled=True)]
    ppermute x3, waiting for transfers between devices: 17.1 us -> 0.01 us  [swap_shards(): return lax.ppermute(values, ('lat', 'lon'), pairs)]
    ppermute x6, starting transfers between devices: 18.5 us -> 27.5 us  [swap_cores(): return lax.ppermute(values, 'lon', [(i, i ^ 1) for i in range(count)])]
    pallas_call x4 -> x6, Pallas kernels: 13.4 us -> 22.3 us  [call_kernel(): pl.pallas_call(body, out_shape=out_shape, in_specs=[pl.BlockSpec(memory_s...]
    all_to_all x4 -> x2, starting transfers between devices: 16.1 us -> 7.88 us  [ring_scatter(): lax.all_to_all(blocks, 'lat', 0, 0, axis_index_groups=RINGS, tiled=True)]
    ppermute x6, waiting for transfers between devices: 2.23 us -> 6.8 us  [swap_cores(): return lax.ppermute(values, 'lon', [(i, i ^ 1) for i in range(count)])]
    ppermute x4, starting transfers between devices: 13.8 us -> 17.3 us  [the longest x2 13.2 us: neighbours(): lax.ppermute(first, axis, [((i + 1) % count, i) for i in range(count)])]
  transfers between devices with their start and end apart: 22 -> 20, of which waited for: 10 -> 11; matrix products, arithmetic and copies ran while one was open for 15% -> 6% of each run, Pallas kernels for 3% -> 7%
where the time goes in v1:
time: 246 us; the launch traced here: 244 us
  starting transfers between devices  87.2 us (35%)
  blocking collectives  78.2 us (32%)
  Pallas kernels  22.3 us (9%)
  waiting for transfers between devices  21.2 us (9%)
  between operations  14 us (6%)
  local copies, waits for them, and re-layouts  13.3 us (5%)
  matrix products  4.93 us (2%)
  other arithmetic  2.48 us (1%)
    all_to_all x3, blocking collectives, ring_scatter(): lax.all_to_all(blocks, 'lat', 0, 0, axis_index_groups=RINGS, tiled=True)  78.2 us
    ppermute x6, starting transfers between devices, swap_cores(): return lax.ppermute(values, 'lon', [(i, i ^ 1) for i in range(count)])  27.5 us
    pallas_call x6, Pallas kernels, call_kernel(): pl.pallas_call(body, out_shape=out_shape, in_specs=[pl.BlockSpec(memory_s...  22.3 us
    ppermute x3, starting transfers between devices, swap_shards(): return lax.ppermute(values, ('lat', 'lon'), pairs)  16.6 us
    ppermute x2, starting transfers between devices, neighbours(): lax.ppermute(first, axis, [((i + 1) % count, i) for i in range(count)])  13.2 us
    ppermute x2, starting transfers between devices, swap_rings(): lax.ppermute(values, 'lat', [(i, (i + Z_RING) % count) for i in range(cou...  10.3 us
    all_to_all x2, starting transfers between devices, ring_scatter(): lax.all_to_all(blocks, 'lat', 0, 0, axis_index_groups=RINGS, tiled=True)  7.88 us
    all_to_all x2, waiting for transfers between devices, ring_scatter(): lax.all_to_all(blocks, 'lat', 0, 0, axis_index_groups=RINGS, tiled=True)  7.75 us
  transfers between devices with their start and end apart: 20, of which 11 were waited for; matrix products, arithmetic and copies ran while one was open for 6% of the time, Pallas kernels for 7%

profile of v1, /device:TPU:1, one launch (start us, length us, event | category | flops | bytes accessed | tf_op | source)
XLA Modules:
  0.0 243.6 jit_solution(16672263153253859959)
XLA Ops:
  7.5 5.5 %collective-permute-start = (bf16[1,128,512]{2,1,0:T(8,128)(2,1)S(1)}, bf16[1,128,512]{2,1,0:T(8,128)(2,1)S(1)}, u32[]{:S(2)}, u32[]{:S(2)}) collective-permute-start(bf16[1,128,512]{2,1,0:T(8,128)(2,1)S(1)} %dynamic-slice_bitcast_fusion), channel_id=1, source_target_pairs={{0,256},{32,288},{64,320},{96,352},{128,384},{160,416},{192,448},{... | collective-permute-start | bytes 393224 | tf_op jit(solution)/shard_map/ppermute | solution.py:334
  13.0 2.3 collective-permute-done
  18.3 4.9 %collective-permute-start.3 = (bf16[1,16,768]{2,1,0:T(8,128)(2,1)S(1)}, bf16[1,16,768]{2,1,0:T(8,128)(2,1)S(1)}, u32[]{:S(2)}, u32[]{:S(2)}) collective-permute-start(bf16[1,16,768]{2,1,0:T(8,128)(2,1)S(1)} %maximum_bitcast_fusion), channel_id=1, source_target_pairs={{0,256},{32,288},{64,320},{96,352},{128,384},{160,416},{192,448},{... | collective-permute-start | bytes 73736 | tf_op jit(solution)/shard_map/ppermute | solution.py:334
  23.1 9.5 %collective-permute-start.5 = (bf16[64,2048]{1,0:T(8,128)(2,1)}, bf16[64,2048]{1,0:T(8,128)(2,1)S(1)}, u32[]{:S(2)}, u32[]{:S(2)}) collective-permute-start(bf16[64,2048]{1,0:T(8,128)(2,1)} %param.29), channel_id=1, source_target_pairs={{0,0},{1,256},{2,2},{3,258},{4,4},{5,260},{6,6},{7,262},{8,8},{9,2... | collective-permute-start | bytes 786440 | tf_op jit(solution)/shard_map/ppermute | solution.py:347
  34.6 5.1 %collective-permute-start.6 = (bf16[4096,128]{1,0:T(8,128)(2,1)}, bf16[4096,128]{1,0:T(8,128)(2,1)S(1)}, u32[]{:S(2)}, u32[]{:S(2)}) collective-permute-start(bf16[4096,128]{1,0:T(8,128)(2,1)} %param.26), channel_id=1, source_target_pairs={{0,0},{1,256},{2,2},{3,258},{4,4},{5,260},{6,6},{7,262},{8,8},{9,2... | collective-permute-start | bytes 3145736 | tf_op jit(solution)/shard_map/ppermute | solution.py:347
  43.9 7.0 %collective-permute-start.2 = (bf16[2,2,16,512]{3,2,1,0:T(8,128)(2,1)S(1)}, bf16[2,2,16,512]{3,2,1,0:T(8,128)(2,1)S(1)}, u32[]{:S(2)}, u32[]{:S(2)}) collective-permute-start(bf16[2,2,16,512]{3,2,1,0:T(8,128)(2,1)S(1)} %get-tuple-element.43), channel_id=1, source_target_pairs={{32,0},{64,32},{96,64},{128,96},{160,128},{192,160},{224,192},{256... | collective-permute-start | bytes 196616 | tf_op jit(solution)/shard_map/ppermute | solution.py:323
  54.7 3.7 %all-to-all-start = ((bf16[8,2,16,128]{3,2,1,0:T(8,128)(2,1)}), bf16[8,2,16,128]{3,2,1,0:T(8,128)(2,1)S(1)}, u32[]{:S(2)}, u32[]{:S(2)}) async-start(bf16[8,2,16,128]{3,2,1,0:T(8,128)(2,1)} %broadcast_in_dim.30), calls=%async_computation | async-start | bytes 131072 | tf_op jit(solution)/shard_map/all_to_all | solution.py:351
  58.5 7.7 %all-to-all-done = bf16[8,2,16,128]{3,2,1,0:T(8,128)(2,1)S(1)} async-done(((bf16[8,2,16,128]{3,2,1,0:T(8,128)(2,1)}), bf16[8,2,16,128]{3,2,1,0:T(8,128)(2,1)S(1)}, u32[]{:S(2)}, u32[]{:S(2)}) %all-to-all-start) | async-done | bytes 65568 | tf_op jit(solution)/shard_map/all_to_all | solution.py:351
  67.1 7.6 %all-to-all-start.1 = ((bf16[8,8,2,16,128]{4,3,2,1,0:T(8,128)(2,1)}), bf16[8,8,2,16,128]{4,3,2,1,0:T(8,128)(2,1)S(1)}, u32[]{:S(2)}, u32[]{:S(2)}) async-start(bf16[8,8,2,16,128]{4,3,2,1,0:T(8,128)(2,1)} %broadcast_in_dim.70), calls=%async_computation.1 | async-start | bytes 1048576 | tf_op jit(solution)/shard_map/all_to_all | solution.py:376
  74.9 6.2 %collective-permute-start.8 = (bf16[16,2,2,512]{3,2,1,0:T(2,128)(2,1)S(1)}, bf16[16,2,2,512]{3,2,1,0:T(2,128)(2,1)S(1)}, u32[]{:S(2)}, u32[]{:S(2)}) collective-permute-start(bf16[16,2,2,512]{3,2,1,0:T(2,128)(2,1)S(1)} %get-tuple-element.40), channel_id=1, source_target_pairs={{1,0},{2,1},{3,2},{4,3},{5,4},{6,5},{7,6},{8,7},{9,8},{10,9},{11,1... | collective-permute-start | bytes 196616 | tf_op jit(solution)/shard_map/ppermute | solution.py:323
  86.0 11.2 %shard_map.154.attended_ref = bf16[384,512]{1,0:T(8,128)(2,1)S(1)} custom-call(bf16[512,512]{1,0:T(8,128)(2,1)S(1)} %bitcast.37, bf16[64,512]{1,0:T(8,128)(2,1)S(1)} %reshape.74.left_ref, bf16[64,512]{1,0:T(8,128)(2,1)S(1)} %reshape.75.right_ref, f32[1,512]{1,0:T(1,128)S(1)} %bitcast.41, bf16[3,512,512]{2,1,0:T(8,128)(2,1)S(1)} %copy-done.5, ...), custom_call_target="tpu_custom_call" | custom-call | flops 1006632960 | bytes 2314752 | tf_op jit(solution)/shard_map/pallas_call | solution.py:20
  98.2 4.2 %all-to-all-start.2 = ((bf16[8,16,2304]{2,1,0:T(8,128)(2,1)}), bf16[8,16,2304]{2,1,0:T(8,128)(2,1)}, u32[]{:S(2)}, u32[]{:S(2)}) async-start(bf16[8,16,2304]{2,1,0:T(8,128)(2,1)} %broadcast_in_dim.73), calls=%async_computation.2 | async-start | bytes 1179648 | tf_op jit(solution)/shard_map/all_to_all | solution.py:351
  103.6 8.5 %collective-permute-start.9 = (bf16[96,2048]{1,0:T(8,128)(2,1)S(1)}, bf16[96,2048]{1,0:T(8,128)(2,1)S(1)}, u32[]{:S(2)}, u32[]{:S(2)}) collective-permute-start(bf16[96,2048]{1,0:T(8,128)(2,1)S(1)} %get-tuple-element.25), channel_id=1, source_target_pairs={{0,1},{1,0},{2,3},{3,2},{4,5},{5,4},{6,7},{7,6},{8,9},{9,8},{10,11... | collective-permute-start | bytes 1179656 | tf_op jit(solution)/shard_map/ppermute | solution.py:329
  113.5 2.9 %convolution_convert_fusion = bf16[192,512]{1,0:T(8,128)(2,1)} fusion(bf16[2048,512]{1,0:T(8,128)(2,1)} %bitcast.48, bf16[96,2048]{1,0:T(8,128)(2,1)S(1)} %collective-permute-done.9, bf16[96,2048]{1,0:T(8,128)(2,1)S(1)} %get-tuple-element.25), kind=kOutput, calls=%fused_computation | convolution fusion | flops 404324352 | bytes 3080192 | tf_op jit(solution)/shard_map/dot_general | solution.py:496
  119.5 8.5 %collective-permute-start.10 = (bf16[96,512]{1,0:T(8,128)(2,1)S(1)}, bf16[96,512]{1,0:T(8,128)(2,1)S(1)}, u32[]{:S(2)}, u32[]{:S(2)}) collective-permute-start(bf16[96,512]{1,0:T(8,128)(2,1)S(1)} %get-tuple-element.44), channel_id=1, source_target_pairs={{0,1},{1,0},{2,3},{3,2},{4,5},{5,4},{6,7},{7,6},{8,9},{9,8},{10,11... | collective-permute-start | bytes 294920 | tf_op jit(solution)/shard_map/ppermute | solution.py:329
  130.2 42.9 %all_to_all.30 = bf16[8,24,4096]{2,1,0:T(8,128)(2,1)S(1)} all-to-all(bf16[8,24,4096]{2,1,0:T(8,128)(2,1)S(1)} %broadcast_in_dim.74), channel_id=1, replica_groups={{0,32,64,96,128,160,192,224},{256,288,320,352,384,416,448,480},{1,33,65..., dimensions={0} | all-to-all | bytes 3145728 | tf_op jit(solution)/shard_map/all_to_all | solution.py:351
  173.1 2.5 %collective-permute-start.11 = (bf16[192,4096]{1,0:T(8,128)(2,1)S(1)}, bf16[192,4096]{1,0:T(8,128)(2,1)S(1)}, u32[]{:S(2)}, u32[]{:S(2)}) collective-permute-start(bf16[192,4096]{1,0:T(8,128)(2,1)S(1)} %bitcast.42), channel_id=1, source_target_pairs={{0,1},{1,0},{2,3},{3,2},{4,5},{5,4},{6,7},{7,6},{8,9},{9,8},{10,11... | collective-permute-start | bytes 4718600 | tf_op jit(solution)/shard_map/ppermute | solution.py:329
  179.2 26.0 %all_to_all.31.own_ref = bf16[8,2,192,128]{3,2,1,0:T(8,128)(2,1)S(1)} all-to-all(bf16[8,2,192,128]{3,2,1,0:T(8,128)(2,1)S(1)} %broadcast_in_dim.75), channel_id=1, replica_groups={{0,32,64,96,128,160,192,224},{256,288,320,352,384,416,448,480},{1,33,65..., dimensions={0} | all-to-all | bytes 1572864 | tf_op jit(solution)/shard_map/all_to_all | solution.py:351
  205.2 2.4 collective-permute-start.12
  209.5 3.1 %shard_map.157 = (bf16[8,2,24,64]{3,2,1,0:T(8,128)(2,1)S(1)}, f32[24,2048]{1,0:T(8,128)S(1)}) custom-call(s32[2]{0:T(128)S(1)} %pad_add_fusion.1.core_ref, bf16[8,2,192,128]{3,2,1,0:T(8,128)(2,1)S(1)} %all_to_all.31.own_ref, bf16[8,2,192,128]{3,2,1,0:T(8,128)(2,1)S(1)} %collective-permute-done.12.other_ref, f32[16,1,128]{2,1,0:T(1,128)S(1)} %bitcast.40, ...), custom_call_target="tpu_custom_call" | custom-call | flops 301989888 | bytes 2367496 | tf_op jit(solution)/shard_map/pallas_call | solution.py:20
  215.0 9.4 %all_to_all.32 = bf16[8,2,1536]{2,1,0:T(2,128)(2,1)S(1)} all-to-all(bf16[8,2,1536]{2,1,0:T(2,128)(2,1)S(1)} %reshape.82), channel_id=1, replica_groups={{0,32,64,96,128,160,192,224},{256,288,320,352,384,416,448,480},{1,33,65..., dimensions={0} | all-to-all | bytes 98304 | tf_op jit(solution)/shard_map/all_to_all | solution.py:351
  224.5 2.3 copy-done.1
  227.4 3.3 %collective-permute-start.13 = (bf16[24,2048]{1,0:T(8,128)(2,1)S(1)}, bf16[24,2048]{1,0:T(8,128)(2,1)S(1)}, u32[]{:S(2)}, u32[]{:S(2)}) collective-permute-start(bf16[24,2048]{1,0:T(8,128)(2,1)S(1)} %get-tuple-element.33), channel_id=1, source_target_pairs={{0,1},{1,0},{2,3},{3,2},{4,5},{5,4},{6,7},{7,6},{8,9},{9,8},{10,11... | collective-permute-start | bytes 294920 | tf_op jit(solution)/shard_map/ppermute | solution.py:329
  231.6 5.2 %shard_map.159 = bf16[384,512]{1,0:T(8,128)(2,1)} custom-call(s32[2]{0:T(128)S(1)} %pad_add_fusion.1.core_ref, f32[24,2048]{1,0:T(8,128)S(1)} %get-tuple-element.30.own_coarse_ref, f32[24,2048]{1,0:T(8,128)S(1)} %get-tuple-element.32.part_ref, bf16[24,2048]{1,0:T(8,128)(2,1)S(1)} %collective-permute-done.13.recv_ref, bf16[64,16,2304]{2,1,0:T(8,128)(2,1)S(1)} %copy-done.1, ...), custom_call_target="tpu_custom_call" | custom-call | flops 201326592 | bytes 10518536 | tf_op jit(solution)/shard_map/pallas_call | solution.py:20
  (91 shorter events, 37.8 us)
Async XLA Ops:
  6.5 35.3 %copy-start.7 = (bf16[12,2,16,512]{3,2,1,0:T(8,128)(2,1)S(1)}, bf16[12,2,16,512]{3,2,1,0:T(8,128)(2,1)}, u32[]{:S(2)}) copy-start(bf16[12,2,16,512]{3,2,1,0:T(8,128)(2,1)} %param.16) | copy-start | bytes 1179652
  6.5 107.0 %all-gather.3.cloned.1.call-start = ((), (), s32[]{:S(2)}) async-start(), calls=%async_computation.6 | async-start | bytes 2359296 | tf_op jit(solution)/shard_map/all_gather | solution.py:412
  7.5 7.8 %collective-permute-start = (bf16[1,128,512]{2,1,0:T(8,128)(2,1)S(1)}, bf16[1,128,512]{2,1,0:T(8,128)(2,1)S(1)}, u32[]{:S(2)}, u32[]{:S(2)}) collective-permute-start(bf16[1,128,512]{2,1,0:T(8,128)(2,1)S(1)} %dynamic-slice_bitcast_fusion), channel_id=1, source_target_pairs={{0,256},{32,288},{64,320},{96,352},{128,384},{160,416},{192,448},{... | collective-permute-start | bytes 393224 | tf_op jit(solution)/shard_map/ppermute | solution.py:334
  18.3 25.6 %collective-permute-start.3 = (bf16[1,16,768]{2,1,0:T(8,128)(2,1)S(1)}, bf16[1,16,768]{2,1,0:T(8,128)(2,1)S(1)}, u32[]{:S(2)}, u32[]{:S(2)}) collective-permute-start(bf16[1,16,768]{2,1,0:T(8,128)(2,1)S(1)} %maximum_bitcast_fusion), channel_id=1, source_target_pairs={{0,256},{32,288},{64,320},{96,352},{128,384},{160,416},{192,448},{... | collective-permute-start | bytes 73736 | tf_op jit(solution)/shard_map/ppermute | solution.py:334
  23.1 60.1 %collective-permute-start.5 = (bf16[64,2048]{1,0:T(8,128)(2,1)}, bf16[64,2048]{1,0:T(8,128)(2,1)S(1)}, u32[]{:S(2)}, u32[]{:S(2)}) collective-permute-start(bf16[64,2048]{1,0:T(8,128)(2,1)} %param.29), channel_id=1, source_target_pairs={{0,0},{1,256},{2,2},{3,258},{4,4},{5,260},{6,6},{7,262},{8,8},{9,2... | collective-permute-start | bytes 786440 | tf_op jit(solution)/shard_map/ppermute | solution.py:347
  32.7 51.9 %collective-permute-start.7 = (bf16[3,2048,64]{1,2,0:T(8,128)(2,1)}, bf16[3,2048,64]{1,2,0:T(8,128)(2,1)}, u32[]{:S(2)}, u32[]{:S(2)}) collective-permute-start(bf16[3,2048,64]{1,2,0:T(8,128)(2,1)} %param.28), channel_id=1, source_target_pairs={{0,0},{1,256},{2,2},{3,258},{4,4},{5,260},{6,6},{7,262},{8,8},{9,2... | collective-permute-start | bytes 2359304 | tf_op jit(solution)/shard_map/ppermute | solution.py:347
  34.6 50.0 %collective-permute-start.6 = (bf16[4096,128]{1,0:T(8,128)(2,1)}, bf16[4096,128]{1,0:T(8,128)(2,1)S(1)}, u32[]{:S(2)}, u32[]{:S(2)}) collective-permute-start(bf16[4096,128]{1,0:T(8,128)(2,1)} %param.26), channel_id=1, source_target_pairs={{0,0},{1,256},{2,2},{3,258},{4,4},{5,260},{6,6},{7,262},{8,8},{9,2... | collective-permute-start | bytes 3145736 | tf_op jit(solution)/shard_map/ppermute | solution.py:347
  42.0 10.5 %collective-permute-start.1 = (bf16[2,2,16,512]{3,2,1,0:T(8,128)(2,1)S(1)}, bf16[2,2,16,512]{3,2,1,0:T(8,128)(2,1)S(1)}, u32[]{:S(2)}, u32[]{:S(2)}) collective-permute-start(bf16[2,2,16,512]{3,2,1,0:T(8,128)(2,1)S(1)} %get-tuple-element.42), channel_id=1, source_target_pairs={{0,32},{32,64},{64,96},{96,128},{128,160},{160,192},{192,224},{224... | collective-permute-start | bytes 196616 | tf_op jit(solution)/shard_map/ppermute | solution.py:322
  43.9 10.1 %collective-permute-start.2 = (bf16[2,2,16,512]{3,2,1,0:T(8,128)(2,1)S(1)}, bf16[2,2,16,512]{3,2,1,0:T(8,128)(2,1)S(1)}, u32[]{:S(2)}, u32[]{:S(2)}) collective-permute-start(bf16[2,2,16,512]{3,2,1,0:T(8,128)(2,1)S(1)} %get-tuple-element.43), channel_id=1, source_target_pairs={{32,0},{64,32},{96,64},{128,96},{160,128},{192,160},{224,192},{256... | collective-permute-start | bytes 196616 | tf_op jit(solution)/shard_map/ppermute | solution.py:323
  54.0 30.6 %copy-start.6 = (f32[512]{0:T(512)S(1)}, f32[512]{0:T(512)}, u32[]{:S(2)}) copy-start(f32[512]{0:T(512)} %param.20) | copy-start | bytes 6148
  54.7 11.5 %all-to-all-start = ((bf16[8,2,16,128]{3,2,1,0:T(8,128)(2,1)}), bf16[8,2,16,128]{3,2,1,0:T(8,128)(2,1)S(1)}, u32[]{:S(2)}, u32[]{:S(2)}) async-start(bf16[8,2,16,128]{3,2,1,0:T(8,128)(2,1)} %broadcast_in_dim.30), calls=%async_computation | async-start | bytes 131072 | tf_op jit(solution)/shard_map/all_to_all | solution.py:351
  67.1 30.2 %all-to-all-start.1 = ((bf16[8,8,2,16,128]{4,3,2,1,0:T(8,128)(2,1)}), bf16[8,8,2,16,128]{4,3,2,1,0:T(8,128)(2,1)S(1)}, u32[]{:S(2)}, u32[]{:S(2)}) async-start(bf16[8,8,2,16,128]{4,3,2,1,0:T(8,128)(2,1)} %broadcast_in_dim.70), calls=%async_computation.1 | async-start | bytes 1048576 | tf_op jit(solution)/shard_map/all_to_all | solution.py:376
  74.9 8.7 %collective-permute-start.8 = (bf16[16,2,2,512]{3,2,1,0:T(2,128)(2,1)S(1)}, bf16[16,2,2,512]{3,2,1,0:T(2,128)(2,1)S(1)}, u32[]{:S(2)}, u32[]{:S(2)}) collective-permute-start(bf16[16,2,2,512]{3,2,1,0:T(2,128)(2,1)S(1)} %get-tuple-element.40), channel_id=1, source_target_pairs={{1,0},{2,1},{3,2},{4,3},{5,4},{6,5},{7,6},{8,7},{9,8},{10,9},{11,1... | collective-permute-start | bytes 196616 | tf_op jit(solution)/shard_map/ppermute | solution.py:323
  81.1 3.5 %collective-permute-start.4 = (bf16[16,2,2,512]{3,2,1,0:T(2,128)(2,1)S(1)}, bf16[16,2,2,512]{3,2,1,0:T(2,128)(2,1)S(1)}, u32[]{:S(2)}, u32[]{:S(2)}) collective-permute-start(bf16[16,2,2,512]{3,2,1,0:T(2,128)(2,1)S(1)} %get-tuple-element.41), channel_id=1, source_target_pairs={{0,1},{1,2},{2,3},{3,4},{4,5},{5,6},{6,7},{7,8},{8,9},{9,10},{10,1... | collective-permute-start | bytes 196616 | tf_op jit(solution)/shard_map/ppermute | solution.py:322
  98.2 18.2 %all-to-all-start.2 = ((bf16[8,16,2304]{2,1,0:T(8,128)(2,1)}), bf16[8,16,2304]{2,1,0:T(8,128)(2,1)}, u32[]{:S(2)}, u32[]{:S(2)}) async-start(bf16[8,16,2304]{2,1,0:T(8,128)(2,1)} %broadcast_in_dim.73), calls=%async_computation.2 | async-start | bytes 1179648 | tf_op jit(solution)/shard_map/all_to_all | solution.py:351
  102.4 110.2 %all-gather.5.cloned.1.call-start = ((), (), s32[]{:S(2)}) async-start(), calls=%async_computation.7 | async-start | bytes 5308416 | tf_op jit(solution)/shard_map/all_gather | solution.py:511
  103.6 9.9 %collective-permute-start.9 = (bf16[96,2048]{1,0:T(8,128)(2,1)S(1)}, bf16[96,2048]{1,0:T(8,128)(2,1)S(1)}, u32[]{:S(2)}, u32[]{:S(2)}) collective-permute-start(bf16[96,2048]{1,0:T(8,128)(2,1)S(1)} %get-tuple-element.25), channel_id=1, source_target_pairs={{0,1},{1,0},{2,3},{3,2},{4,5},{5,4},{6,7},{7,6},{8,9},{9,8},{10,11... | collective-permute-start | bytes 1179656 | tf_op jit(solution)/shard_map/ppermute | solution.py:329
  118.5 10.4 %copy-start.2 = (f32[4096]{0:T(1024)S(1)}, f32[4096]{0:T(1024)}, u32[]{:S(2)}) copy-start(f32[4096]{0:T(1024)} %param.25) | copy-start | bytes 49156
  119.5 9.4 %collective-permute-start.10 = (bf16[96,512]{1,0:T(8,128)(2,1)S(1)}, bf16[96,512]{1,0:T(8,128)(2,1)S(1)}, u32[]{:S(2)}, u32[]{:S(2)}) collective-permute-start(bf16[96,512]{1,0:T(8,128)(2,1)S(1)} %get-tuple-element.44), channel_id=1, source_target_pairs={{0,1},{1,0},{2,3},{3,2},{4,5},{5,4},{6,7},{7,6},{8,9},{9,8},{10,11... | collective-permute-start | bytes 294920 | tf_op jit(solution)/shard_map/ppermute | solution.py:329
  173.1 5.4 %collective-permute-start.11 = (bf16[192,4096]{1,0:T(8,128)(2,1)S(1)}, bf16[192,4096]{1,0:T(8,128)(2,1)S(1)}, u32[]{:S(2)}, u32[]{:S(2)}) collective-permute-start(bf16[192,4096]{1,0:T(8,128)(2,1)S(1)} %bitcast.42), channel_id=1, source_target_pairs={{0,1},{1,0},{2,3},{3,2},{4,5},{5,4},{6,7},{7,6},{8,9},{9,8},{10,11... | collective-permute-start | bytes 4718600 | tf_op jit(solution)/shard_map/ppermute | solution.py:329
  179.0 30.5 %copy-start.4 = (f32[2048]{0:T(1024)S(1)}, f32[2048]{0:T(1024)}, u32[]{:S(2)}) copy-start(f32[2048]{0:T(1024)} %param.27) | copy-start | bytes 24580
  205.2 4.3 %collective-permute-start.12 = (bf16[8,2,192,128]{3,2,1,0:T(8,128)(2,1)S(1)}, bf16[8,2,192,128]{3,2,1,0:T(8,128)(2,1)S(1)}, u32[]{:S(2)}, u32[]{:S(2)}) collective-permute-start(bf16[8,2,192,128]{3,2,1,0:T(8,128)(2,1)S(1)} %all_to_all.31.own_ref), channel_id=1, source_target_pairs={{0,1},{1,0},{2,3},{3,2},{4,5},{5,4},{6,7},{7,6},{8,9},{9,8},{10,11... | collective-permute-start | bytes 2359304 | tf_op jit(solution)/shard_map/ppermute | solution.py:329
  212.6 19.0 %collective-permute-start.14 = (bf16[64,16,2304]{2,1,0:T(8,128)(2,1)}, bf16[64,16,2304]{2,1,0:T(8,128)(2,1)}, u32[]{:S(2)}, u32[]{:S(2)}) collective-permute-start(bf16[64,16,2304]{2,1,0:T(8,128)(2,1)} %all-gather.5.cloned.1.call-done.late_ref), channel_id=1, source_target_pairs={{0,1},{1,0},{2,3},{3,2},{4,5},{5,4},{6,7},{7,6},{8,9},{9,8},{10,11... | collective-permute-start | bytes 14155784 | tf_op jit(solution)/shard_map/ppermute | solution.py:329
  227.4 4.2 %collective-permute-start.13 = (bf16[24,2048]{1,0:T(8,128)(2,1)S(1)}, bf16[24,2048]{1,0:T(8,128)(2,1)S(1)}, u32[]{:S(2)}, u32[]{:S(2)}) collective-permute-start(bf16[24,2048]{1,0:T(8,128)(2,1)S(1)} %get-tuple-element.33), channel_id=1, source_target_pairs={{0,1},{1,0},{2,3},{3,2},{4,5},{5,4},{6,7},{7,6},{8,9},{9,8},{10,11... | collective-permute-start | bytes 294920 | tf_op jit(solution)/shard_map/ppermute | solution.py:329
  (4 other events, 9.8 us)
Sparse Core Ops, SparseCore 0:
  16.2 49.6 all-gather.2
  116.5 63.2 all-gather.4

commit v2 on v1

--- a/solution.py
+++ b/solution.py
@@ -38,11 +38,16 @@
     return lax.dot_general(left, right, (((1,), (0,)), ((), ())), preferred_element_type=jnp.float32)
 
 
-def softmax_rows(scores, keep):
+def mix_tokens(query, key, value, keep):
+    scores = lax.dot_general(
+        key, query, (((1,), (1,)), ((), ())), preferred_element_type=jnp.float32
+    )
     scores = jnp.where(keep, scores, -1e30)
-    weights = jnp.exp(scores - jnp.max(scores, axis=-1, keepdims=True))
-    total = jnp.sum(weights, axis=-1, keepdims=True)
-    return (weights / total).astype(jnp.bfloat16)
+    weights = jnp.exp(scores - jnp.max(scores, axis=0, keepdims=True))
+    weights = (weights / jnp.sum(weights, axis=0, keepdims=True)).astype(jnp.bfloat16)
+    return lax.dot_general(
+        weights, value, (((0,), (0,)), ((), ())), preferred_element_type=jnp.float32
+    )
 
 
 def first_kernel(x_ref, left_ref, right_ref, gain_ref, qkv_ref, window_ref, lat_ref, out_ref):
@@ -75,13 +80,7 @@
             for odd in range(2):
                 picked = (key_lane < HD) if odd == 0 else (key_lane >= HD)
                 key_side = jnp.where(picked, key[:, here], jnp.zeros_like(key[:, here]))
-                scores = lax.dot_general(
-                    query[:, here],
-                    key_side,
-                    (((1,), (1,)), ((), ())),
-                    preferred_element_type=jnp.float32,
-                )
-                parts.append(dot_rows(softmax_rows(scores, keep), value[:, here]))
+                parts.append(mix_tokens(query[:, here], key_side, value[:, here], keep))
             mixed = jnp.where(lane < HD, parts[0], parts[1]).astype(jnp.bfloat16)
             out_ref[start : start + last - first, here] = mixed[first:last]
 
@@ -115,23 +114,13 @@
         out_ref[:, here] = (part * scale * gain_ref[:, here]).astype(jnp.bfloat16)
 
 
-def skip_kernel(attended_ref, hidden_ref, tiles_ref, gain_ref, skip_ref, merged_ref):
+def skip_kernel(attended_ref, hidden_ref, weights_ref, gain_ref, skip_ref, merged_ref):
     total = None
     for ring in range(2):
         for z in range(0, 8, 4):
             right = jnp.concatenate(
-                [
-                    jnp.concatenate(
-                        [
-                            tiles_ref[row * 4 + part, zz, ring]
-                            for zz in range(z, z + 4)
-                            for row in range(2)
-                        ],
-                        axis=0,
-                    )
-                    for part in range(4)
-                ],
-                axis=1,
+                [weights_ref[ring, zz * 160 + 128 : zz * 160 + 160, :] for zz in range(z, z + 4)],
+                axis=0,
             )
             start = (ring * 8 + z) * 32
             product = dot_rows(attended_ref[:, start : start + 128], right)
@@ -141,6 +130,22 @@
     join_quads(skip, 6, 8, gain_ref, merged_ref)
 
 
+def merge_kernel(own_ref, other_ref, weights_ref, own_out_ref, send_ref):
+    left = jnp.concatenate([own_ref[...], other_ref[...]], axis=0)
+    total = None
+    for ring in range(2):
+        for z in range(0, 8, 2):
+            right = jnp.concatenate(
+                [weights_ref[ring, zz * 160 : zz * 160 + 128, :] for zz in (z, z + 1)], axis=0
+            )
+            start = (ring * 8 + z) * 128
+            product = dot_rows(left[:, start : start + 256], right)
+            total = product if total is None else total + product
+    rows = own_ref.shape[0]
+    own_out_ref[...] = total[:rows].astype(jnp.bfloat16)
+    send_ref[...] = total[rows:].astype(jnp.bfloat16)
+
+
 def join_kernel(core_ref, own_ref, recv_ref, gain_ref, second_ref, coarse_ref, halves_ref):
     core = core_ref[0]
     halves_ref[core] = own_ref[...]
@@ -148,6 +153,21 @@
     second = jnp.concatenate([halves_ref[0], halves_ref[1]], axis=1)
     second_ref[...] = second
     join_quads(second, 3, 4, gain_ref, coarse_ref)
+
+
+RING_ORDER = (0, -1, 1, -2, 2, -3, 3, 4)
+
+
+def columns_kernel(place_ref, near_ref, far_ref, near_other_ref, far_other_ref, weights_ref, out_ref):
+    for side, refs in enumerate(((near_ref, far_ref), (near_other_ref, far_other_ref))):
+        places = iter(RING_ORDER)
+        for ref in refs:
+            count, rows, width = ref.shape
+            left = jnp.concatenate([ref[at].astype(jnp.float32) for at in range(count)], axis=0)
+            product = dot_rows(left.astype(jnp.bfloat16), weights_ref[...])
+            for at in range(count):
+                place = jnp.bitwise_and(place_ref[1] + (next(places) + 8), 7)
+                out_ref[side, place] = product[at * rows : (at + 1) * rows].astype(jnp.bfloat16)
 
 
 def third_kernel(
@@ -194,10 +214,7 @@
     mixed = []
     for group in range(sides * line // 128):
         mine = slice(group * 128, group * 128 + 128)
-        scores = lax.dot_general(
-            query[mine], key[mine], (((1,), (1,)), ((), ())), preferred_element_type=jnp.float32
-        )
-        mixed.append(dot_rows(softmax_rows(scores, keep), value[mine]))
+        mixed.append(mix_tokens(query[mine], key[mine], value[mine], keep))
     mixed = jnp.concatenate(mixed, axis=0)
     for z in range(blocks):
         for side in range(sides):
@@ -351,6 +368,11 @@
     return lax.all_to_all(blocks, "lat", 0, 0, axis_index_groups=RINGS, tiled=True)
 
 
+def ring_shift(values, step):
+    pairs = [(at, at // Z_RING * Z_RING + (at + step) % Z_RING) for at in range(2 * Z_RING)]
+    return lax.ppermute(values, "lat", pairs)
+
+
 def ring_gather(values):
     return ring_scatter(jnp.broadcast_to(values[None], (Z_RING,) + values.shape))
 
@@ -369,18 +391,6 @@
 
 def after(values, *before):
     return lax.optimization_barrier((values,) + before)[0]
-
-
-def column_gather(values):
-    groups = [[4 * y + x for y in range(8)] for x in range(4)]
-    return lax.all_to_all(
-        jnp.broadcast_to(values[None], (8,) + values.shape),
-        "lon",
-        0,
-        0,
-        axis_index_groups=groups,
-        tiled=True,
-    )
 
 
 def on_device(
@@ -407,30 +417,14 @@
     core = lax.axis_index("lon") % 2
     column = lax.axis_index("lon") // 4
 
-    own_merge = lax.dynamic_slice_in_dim(merge_second, core * 512, 512, 1)[None]
+    own_merge = jnp.concatenate(
+        [lax.dynamic_slice_in_dim(merge_second, core * 512, 512, 1), out_first], axis=0
+    )[None]
     both_merge = in_order(ring, own_merge, swap_rings(own_merge), 0)
-    merge_half = lax.all_gather(
-        both_merge,
-        "lat",
-        axis=1,
-        axis_index_groups=RINGS,
-        tiled=True,
-    ).reshape(-1, 512)
-
-    own_rest = jnp.concatenate(
-        [
-            cut(out_first, column // 4 * 16, 16, column % 4 * 128, 128),
-            cut(up_third, column * 16, 16, core * 512, 512),
-            cut(up_second, column // 2 * 16, 16, core * 256 + column % 2 * 128, 128),
-        ],
-        axis=1,
-    )[None]
-    both_rest = in_order(ring, own_rest, swap_rings(own_rest), 0)
+    merge_weights = lax.all_gather(
+        both_merge, "lat", axis=1, axis_index_groups=RINGS, tiled=True
+    )
     core_place = jnp.stack([core, lax.axis_index("lat") % Z_RING]).astype(jnp.int32)
-    out_third = swap_shards(out_third)
-    merge_third = swap_shards(merge_third)
-    qkv_third = swap_shards(qkv_third)
-
     picks = (land_ids[:, :, None] == jnp.arange(3, dtype=jnp.int32)).astype(jnp.float32)
     surface = jnp.einsum("ijs,sc->ijc", picks, surface_table.astype(jnp.float32))
     hidden = (
@@ -441,23 +435,43 @@
     hidden = after(hidden, both_merge)
     above, below = neighbours(hidden[:2], hidden[-2:], "lat")
     cells = jnp.concatenate([above, hidden, below], axis=0)
-    cells = after(cells, both_rest)
     left, right = neighbours(cells[:, :, :2], cells[:, :, -2:], "lon")
-    out_first_rows = ring_gather(after(both_rest, cells)[:, :, :128])
-    left = after(left, out_first_rows, out_third, merge_third, qkv_third)
-    out_first_tiles = column_gather(out_first_rows).reshape(8, Z_RING, 2, 16, 128)
+
+    out_third, merge_third, qkv_third, up_third, up_second, _, _ = lax.optimization_barrier(
+        (out_third, merge_third, qkv_third, up_third, up_second, left, right)
+    )
+    own_rest = jnp.concatenate(
+        [
+            cut(up_third, column * 16, 16, core * 512, 512),
+            cut(up_second, column // 2 * 16, 16, core * 256 + column % 2 * 128, 128),
+        ],
+        axis=1,
+    )[None]
+    both_rest = in_order(ring, own_rest, swap_rings(own_rest), 0)
+    out_third = swap_shards(out_third)
+    merge_third = swap_shards(merge_third)
+    qkv_third = swap_shards(qkv_third)
+    late = jnp.concatenate(
+        [
+            both_rest[0],
+            both_rest[1],
+            cut(out_third, column // 2 * 16, 16, column % 2 * 1024, 1024),
+        ],
+        axis=1,
+    )
+    qkv_joined = jnp.concatenate([qkv_third[0], qkv_third[1], qkv_third[2]], axis=1)
 
     ext_rows = tile_rows + 4
     own_window = (jnp.arange(32 * 4) % tile_cols + 2) // 4
     key_window = jnp.concatenate(
         [own_window, jnp.zeros((16,), jnp.int32), jnp.full((16,), tile_cols // 4, jnp.int32)]
     )
-    same_window = (own_window[:, None] == key_window[None, :]).astype(jnp.float32)
+    same_window = (key_window[:, None] == own_window[None, :]).astype(jnp.float32)
     lat_place = lax.axis_index("lat") * tile_rows + jnp.arange(ext_rows) - 2
     valid_rows = ((lat_place >= 0) & (lat_place < tile_rows * lat_count)).astype(jnp.float32)
-    valid_rows = valid_rows.reshape(ext_rows // 4, 1, 4)
+    valid_rows = valid_rows.reshape(ext_rows // 4, 4, 1)
     valid_keys = jnp.concatenate(
-        [jnp.repeat(valid_rows, 2 * count, axis=2) for count in (tile_cols, 2, 2)], axis=2
+        [jnp.repeat(valid_rows, 2 * count, axis=1) for count in (tile_cols, 2, 2)], axis=1
     )
     attended = call_kernel(
         first_kernel,
@@ -473,15 +487,7 @@
         ),
         flops=2 * 640 * 512 * 1536,
     )
-    late = jnp.concatenate(
-        [
-            both_rest[0, :, 128:],
-            both_rest[1, :, 128:],
-            cut(out_third, column // 2 * 16, 16, column % 2 * 1024, 1024),
-        ],
-        axis=1,
-    )
-    late_rows = ring_gather(after(late, attended))
+    attended = after(attended, late, merge_third, qkv_joined)
     tokens = attended.shape[0]
     skip_first, merged_in = call_kernel(
         skip_kernel,
@@ -489,25 +495,29 @@
             jax.ShapeDtypeStruct((tokens, feat_dim), jnp.bfloat16),
             jax.ShapeDtypeStruct((tokens // 4, 4 * feat_dim), jnp.bfloat16),
         ),
-        (attended, hidden.reshape(-1, feat_dim), out_first_tiles, norm_merge2[None]),
+        (attended, hidden.reshape(-1, feat_dim), merge_weights, norm_merge2[None]),
         flops=2 * 384 * 512 * 512,
     )
-    merged_pair = jnp.concatenate([merged_in, swap_cores(merged_in)], axis=0)
-    second_half = jnp.dot(merged_pair, merge_half, preferred_element_type=jnp.float32).astype(
-        jnp.bfloat16
-    )
+    late_rows = ring_gather(after(late, merged_in))
     own_rows = merged_in.shape[0]
+    half_shape = jax.ShapeDtypeStruct((own_rows, 512), jnp.bfloat16)
+    second_half, second_send = call_kernel(
+        merge_kernel,
+        (half_shape, half_shape),
+        (merged_in, swap_cores(merged_in), merge_weights),
+        flops=2 * 192 * 2048 * 512,
+    )
     second_cells, coarse_in = call_kernel(
         join_kernel,
         (
             jax.ShapeDtypeStruct((own_rows, 1024), jnp.bfloat16),
             jax.ShapeDtypeStruct((own_rows // 4, 4096), jnp.bfloat16),
         ),
-        (core_place, second_half[:own_rows], swap_cores(second_half[own_rows:]), norm_merge3[None]),
+        (core_place, second_half, swap_cores(second_send), norm_merge3[None]),
         (pltpu.VMEM((2, own_rows, 512), jnp.bfloat16),),
         flops=2 * 96 * 96 * 1024,
     )
-    late_rows = after(late_rows, second_half)
+    late_rows = after(late_rows, coarse_in)
     late = lax.all_gather(
         late_rows,
         "lon",
@@ -516,18 +526,26 @@
         tiled=True,
     )
 
-    qkv_joined = jnp.concatenate([qkv_third[0], qkv_third[1], qkv_third[2]], axis=1)
-    coarse_in = after(coarse_in, late_rows, qkv_joined)
     own_count = coarse_in.shape[0]
     line = Z_RING * own_count
 
-    ring_tokens = ring_gather(coarse_in).reshape(line, -1)
-    column_block = jnp.stack(
-        [
-            jnp.dot(tokens, merge_third, preferred_element_type=jnp.float32).astype(jnp.bfloat16)
-            for tokens in (ring_tokens, swap_cores(ring_tokens))
-        ]
-    )
+    pieces, forth, back = [coarse_in], coarse_in, coarse_in
+    for _ in range(3):
+        forth, back = ring_shift(forth, 1), ring_shift(back, -1)
+        pieces += [forth, back]
+    half_feats = coarse_in.shape[1] // 2
+    pieces.append(
+        jnp.concatenate(
+            [ring_shift(forth[:, :half_feats], 1), ring_shift(back[:, half_feats:], -1)], axis=1
+        )
+    )
+    near, far = jnp.stack(pieces[:5]), jnp.stack(pieces[5:])
+    column_block = call_kernel(
+        columns_kernel,
+        jax.ShapeDtypeStruct((2, Z_RING, own_count, 128), jnp.bfloat16),
+        (core_place, near, far, swap_cores(near), swap_cores(far), merge_third),
+        flops=2 * 384 * 4096 * 128,
+    ).reshape(2, line, 128)
     own_columns = ring_gather(column_block)
     other_columns = swap_cores(own_columns)
     blocks, _, _, width = own_columns.shape

time: 246 us -> 224 us (0.911)
  blocking collectives: 78.2 us -> 37.7 us
  starting transfers between devices: 87.2 us -> 103 us
  Pallas kernels: 22.3 us -> 17.2 us
  waiting for transfers between devices: 21.2 us -> 25.3 us
  matrix products: 4.93 us -> 0.96 us
  local copies, waits for them, and re-layouts: 13.3 us -> 16.2 us
    all_to_all x3 -> x2, blocking collectives: 78.2 us -> 37.7 us  [ring_scatter(): lax.all_to_all(blocks, 'lat', 0, 0, axis_index_groups=RINGS, tiled=True)]
    ppermute x0 -> x8, starting transfers between devices: none -> 27.8 us  [ring_shift(): return lax.ppermute(values, 'lat', pairs)]
    all_to_all x2 -> x1, waiting for transfers between devices: 7.75 us -> 0.01 us  [ring_scatter(): lax.all_to_all(blocks, 'lat', 0, 0, axis_index_groups=RINGS, tiled=True)]
    all_to_all x1 -> x0, starting transfers between devices: 7.57 us -> none  [column_gather(): lax.all_to_all(jnp.broadcast_to(values[None], (8,) + values.shape), 'lon'...]
    ppermute x0 -> x8, waiting for transfers between devices: none -> 7.07 us  [ring_shift(): return lax.ppermute(values, 'lat', pairs)]
    unnamed x21 -> x53, local copies, waits for them, and re-layouts: 5.84 us -> 11.8 us
    ppermute x2, starting transfers between devices: 4.06 us -> 9.62 us  [neighbours(): lax.ppermute(last, axis, [(i, (i + 1) % count) for i in range(count)])]
    pallas_call x6 -> x8, Pallas kernels: 22.3 us -> 17.2 us  [call_kernel(): pl.pallas_call(body, out_shape=out_shape, in_specs=[pl.BlockSpec(memory_s...]
  transfers between devices with their start and end apart: 20 -> 27, of which waited for: 11 -> 13; matrix products, arithmetic and copies ran while one was open for 6% -> 4% of each run, Pallas kernels for 7% -> 5%
where the time goes in v2:
time: 224 us; the launch traced here: 220 us
  starting transfers between devices  103 us (46%)
  blocking collectives  37.7 us (17%)
  waiting for transfers between devices  25.3 us (11%)
  Pallas kernels  17.2 us (8%)
  local copies, waits for them, and re-layouts  16.2 us (7%)
  between operations  14.2 us (6%)
  other arithmetic  4.91 us (2%)
    all_to_all x2, blocking collectives, ring_scatter(): lax.all_to_all(blocks, 'lat', 0, 0, axis_index_groups=RINGS, tiled=True)  37.7 us
    ppermute x8, starting transfers between devices, ring_shift(): return lax.ppermute(values, 'lat', pairs)  27.8 us
    ppermute x7, starting transfers between devices, swap_cores(): return lax.ppermute(values, 'lon', [(i, i ^ 1) for i in range(count)])  23.8 us
    pallas_call x8, Pallas kernels, call_kernel(): pl.pallas_call(body, out_shape=out_shape, in_specs=[pl.BlockSpec(memory_s...  17.2 us
    ppermute x2, starting transfers between devices, neighbours(): lax.ppermute(first, axis, [((i + 1) % count, i) for i in range(count)])  13.1 us
    ppermute x3, starting transfers between devices, swap_shards(): return lax.ppermute(values, ('lat', 'lon'), pairs)  12.2 us
    unnamed x53, local copies, waits for them, and re-layouts  11.8 us
    ppermute x2, starting transfers between devices, swap_rings(): lax.ppermute(values, 'lat', [(i, (i + Z_RING) % count) for i in range(cou...  9.74 us
  transfers between devices with their start and end apart: 27, of which 13 were waited for; matrix products, arithmetic and copies ran while one was open for 4% of the time, Pallas kernels for 5%

profile of v2, /device:TPU:1, one launch (start us, length us, event | category | flops | bytes accessed | tf_op | source)
XLA Modules:
  0.0 219.6 jit_solution(18420868848122670615)
XLA Ops:
  8.3 5.5 %collective-permute-start = (bf16[1,160,512]{2,1,0:T(8,128)(2,1)S(1)}, bf16[1,160,512]{2,1,0:T(8,128)(2,1)S(1)}, u32[]{:S(2)}, u32[]{:S(2)}) collective-permute-start(bf16[1,160,512]{2,1,0:T(8,128)(2,1)S(1)} %maximum_bitcast_fusion.1), channel_id=1, source_target_pairs={{0,256},{32,288},{64,320},{96,352},{128,384},{160,416},{192,448},{... | collective-permute-start | bytes 491528 | tf_op jit(solution)/shard_map/ppermute | solution.py:351
  19.3 5.1 %collective-permute-start.1 = (bf16[2,2,16,512]{3,2,1,0:T(8,128)(2,1)S(1)}, bf16[2,2,16,512]{3,2,1,0:T(8,128)(2,1)S(1)}, u32[]{:S(2)}, u32[]{:S(2)}) collective-permute-start(bf16[2,2,16,512]{3,2,1,0:T(8,128)(2,1)S(1)} %get-tuple-element.51), channel_id=1, source_target_pairs={{0,32},{32,64},{64,96},{96,128},{128,160},{160,192},{192,224},{224... | collective-permute-start | bytes 196616 | tf_op jit(solution)/shard_map/ppermute | solution.py:339
  24.8 11.0 %collective-permute-start.2 = (bf16[2,2,16,512]{3,2,1,0:T(8,128)(2,1)S(1)}, bf16[2,2,16,512]{3,2,1,0:T(8,128)(2,1)S(1)}, u32[]{:S(2)}, u32[]{:S(2)}) collective-permute-start(bf16[2,2,16,512]{3,2,1,0:T(8,128)(2,1)S(1)} %get-tuple-element.50), channel_id=1, source_target_pairs={{32,0},{64,32},{96,64},{128,96},{160,128},{192,160},{224,192},{256... | collective-permute-start | bytes 196616 | tf_op jit(solution)/shard_map/ppermute | solution.py:340
  37.2 4.5 %collective-permute-start.3 = (bf16[16,2,2,512]{3,2,1,0:T(2,128)(2,1)S(1)}, bf16[16,2,2,512]{3,2,1,0:T(2,128)(2,1)S(1)}, u32[]{:S(2)}, u32[]{:S(2)}) collective-permute-start(bf16[16,2,2,512]{3,2,1,0:T(2,128)(2,1)S(1)} %get-tuple-element.49), channel_id=1, source_target_pairs={{0,1},{1,2},{2,3},{3,4},{4,5},{5,6},{6,7},{7,8},{8,9},{9,10},{10,1... | collective-permute-start | bytes 196616 | tf_op jit(solution)/shard_map/ppermute | solution.py:339
  44.2 3.9 %collective-permute-done.4 = bf16[16,2,2,512]{3,2,1,0:T(2,128)(2,1)S(1)} collective-permute-done((bf16[16,2,2,512]{3,2,1,0:T(2,128)(2,1)S(1)}, bf16[16,2,2,512]{3,2,1,0:T(2,128)(2,1)S(1)}, u32[]{:S(2)}, u32[]{:S(2)}) %collective-permute-start.4) | collective-permute-done | bytes 65568 | tf_op jit(solution)/shard_map/ppermute | solution.py:340
  51.2 4.0 %collective-permute-start.8 = (bf16[3,2048,64]{1,2,0:T(8,128)(2,1)}, bf16[3,2048,64]{1,2,0:T(8,128)(2,1)}, u32[]{:S(2)}, u32[]{:S(2)}) collective-permute-start(bf16[3,2048,64]{1,2,0:T(8,128)(2,1)} %param.28), channel_id=1, source_target_pairs={{0,0},{1,256},{2,2},{3,258},{4,4},{5,260},{6,6},{7,262},{8,8},{9,2... | collective-permute-start | bytes 2359304 | tf_op jit(solution)/shard_map/ppermute | solution.py:364
  56.6 4.3 %collective-permute-start.5 = (bf16[1,16,640]{2,1,0:T(8,128)(2,1)S(1)}, bf16[1,16,640]{2,1,0:T(8,128)(2,1)S(1)}, u32[]{:S(2)}, u32[]{:S(2)}) collective-permute-start(bf16[1,16,640]{2,1,0:T(8,128)(2,1)S(1)} %maximum_bitcast_fusion.2), channel_id=1, source_target_pairs={{0,256},{32,288},{64,320},{96,352},{128,384},{160,416},{192,448},{... | collective-permute-start | bytes 61448 | tf_op jit(solution)/shard_map/ppermute | solution.py:351
  60.9 5.2 %collective-permute-start.7 = (bf16[4096,128]{1,0:T(8,128)(2,1)}, bf16[4096,128]{1,0:T(8,128)(2,1)S(1)}, u32[]{:S(2)}, u32[]{:S(2)}) collective-permute-start(bf16[4096,128]{1,0:T(8,128)(2,1)} %param.26), channel_id=1, source_target_pairs={{0,0},{1,256},{2,2},{3,258},{4,4},{5,260},{6,6},{7,262},{8,8},{9,2... | collective-permute-start | bytes 3145736 | tf_op jit(solution)/shard_map/ppermute | solution.py:364
  67.5 3.2 %shard_map.154.attended_ref = bf16[384,512]{1,0:T(8,128)(2,1)S(1)} custom-call(bf16[512,512]{1,0:T(8,128)(2,1)S(1)} %bitcast.40, bf16[64,512]{1,0:T(8,128)(2,1)S(1)} %reshape.65.left_ref, bf16[64,512]{1,0:T(8,128)(2,1)S(1)} %reshape.66.right_ref, f32[1,512]{1,0:T(1,128)S(1)} %bitcast.44, bf16[3,512,512]{2,1,0:T(8,128)(2,1)S(1)} %copy-done.16, ...), custom_call_target="tpu_custom_call" | custom-call | flops 1006632960 | bytes 2314752 | tf_op jit(solution)/shard_map/pallas_call | solution.py:20
  86.0 6.9 %all-to-all-start.2 = ((bf16[8,16,2304]{2,1,0:T(8,128)(2,1)}), bf16[8,16,2304]{2,1,0:T(8,128)(2,1)}, u32[]{:S(2)}, u32[]{:S(2)}) async-start(bf16[8,16,2304]{2,1,0:T(8,128)(2,1)} %broadcast_in_dim.56), calls=%async_computation.2 | async-start | bytes 1179648 | tf_op jit(solution)/shard_map/all_to_all | solution.py:368
  102.7 3.3 %collective-permute-start.11 = (bf16[24,4096]{1,0:T(8,128)(2,1)S(1)}, bf16[24,4096]{1,0:T(8,128)(2,1)S(1)}, u32[]{:S(2)}, u32[]{:S(2)}) collective-permute-start(bf16[24,4096]{1,0:T(8,128)(2,1)S(1)} %get-tuple-element.35), channel_id=1, source_target_pairs={{0,32},{32,64},{64,96},{96,128},{128,160},{160,192},{192,224},{224... | collective-permute-start | bytes 589832 | tf_op jit(solution)/shard_map/ppermute | solution.py:373
  106.0 3.4 %collective-permute-start.12 = (bf16[24,4096]{1,0:T(8,128)(2,1)S(1)}, bf16[24,4096]{1,0:T(8,128)(2,1)S(1)}, u32[]{:S(2)}, u32[]{:S(2)}) collective-permute-start(bf16[24,4096]{1,0:T(8,128)(2,1)S(1)} %get-tuple-element.35), channel_id=1, source_target_pairs={{0,224},{32,0},{64,32},{96,64},{128,96},{160,128},{192,160},{224,1... | collective-permute-start | bytes 589832 | tf_op jit(solution)/shard_map/ppermute | solution.py:373
  109.5 3.1 %collective-permute-done.11 = bf16[24,4096]{1,0:T(8,128)(2,1)S(1)} collective-permute-done((bf16[24,4096]{1,0:T(8,128)(2,1)S(1)}, bf16[24,4096]{1,0:T(8,128)(2,1)S(1)}, u32[]{:S(2)}, u32[]{:S(2)}) %collective-permute-start.11) | collective-permute-done | bytes 196640 | tf_op jit(solution)/shard_map/ppermute | solution.py:373
  114.6 4.6 %collective-permute-start.14 = (bf16[24,4096]{1,0:T(8,128)(2,1)S(1)}, bf16[24,4096]{1,0:T(8,128)(2,1)S(1)}, u32[]{:S(2)}, u32[]{:S(2)}) collective-permute-start(bf16[24,4096]{1,0:T(8,128)(2,1)S(1)} %collective-permute-done.12), channel_id=1, source_target_pairs={{0,224},{32,0},{64,32},{96,64},{128,96},{160,128},{192,160},{224,1... | collective-permute-start | bytes 589832 | tf_op jit(solution)/shard_map/ppermute | solution.py:373
  119.2 3.1 %collective-permute-done.14 = bf16[24,4096]{1,0:T(8,128)(2,1)S(1)} collective-permute-done((bf16[24,4096]{1,0:T(8,128)(2,1)S(1)}, bf16[24,4096]{1,0:T(8,128)(2,1)S(1)}, u32[]{:S(2)}, u32[]{:S(2)}) %collective-permute-start.14) | collective-permute-done | bytes 196640 | tf_op jit(solution)/shard_map/ppermute | solution.py:373
  122.3 5.3 %collective-permute-start.16 = (bf16[24,4096]{1,0:T(8,128)(2,1)S(1)}, bf16[24,4096]{1,0:T(8,128)(2,1)S(1)}, u32[]{:S(2)}, u32[]{:S(2)}) collective-permute-start(bf16[24,4096]{1,0:T(8,128)(2,1)S(1)} %collective-permute-done.14), channel_id=1, source_target_pairs={{0,224},{32,0},{64,32},{96,64},{128,96},{160,128},{192,160},{224,1... | collective-permute-start | bytes 589832 | tf_op jit(solution)/shard_map/ppermute | solution.py:373
  130.3 5.4 %collective-permute-start.18 = (bf16[24,2048]{1,0:T(8,128)(2,1)S(1)}, bf16[24,2048]{1,0:T(8,128)(2,1)S(1)}, u32[]{:S(2)}, u32[]{:S(2)}) collective-permute-start(bf16[24,2048]{1,0:T(8,128)(2,1)S(1)} %slice.52), channel_id=1, source_target_pairs={{0,224},{32,0},{64,32},{96,64},{128,96},{160,128},{192,160},{224,1... | collective-permute-start | bytes 294920 | tf_op jit(solution)/shard_map/ppermute | solution.py:373
  137.7 4.8 %collective-permute-start.19 = (bf16[5,24,4096]{2,1,0:T(8,128)(2,1)S(1)}, bf16[5,24,4096]{2,1,0:T(8,128)(2,1)S(1)}, u32[]{:S(2)}, u32[]{:S(2)}) collective-permute-start(bf16[5,24,4096]{2,1,0:T(8,128)(2,1)S(1)} %bitcast_dynamic-update-slice_fusion.near_ref), channel_id=1, source_target_pairs={{0,1},{1,0},{2,3},{3,2},{4,5},{5,4},{6,7},{7,6},{8,9},{9,8},{10,11... | collective-permute-start | bytes 2949128 | tf_op jit(solution)/shard_map/ppermute | solution.py:346
  142.8 5.6 %collective-permute-start.20 = (bf16[3,24,4096]{2,1,0:T(8,128)(2,1)S(1)}, bf16[3,24,4096]{2,1,0:T(8,128)(2,1)S(1)}, u32[]{:S(2)}, u32[]{:S(2)}) collective-permute-start(bf16[3,24,4096]{2,1,0:T(8,128)(2,1)S(1)} %pad_maximum_fusion.1.far_ref), channel_id=1, source_target_pairs={{0,1},{1,0},{2,3},{3,2},{4,5},{5,4},{6,7},{7,6},{8,9},{9,8},{10,11... | collective-permute-start | bytes 1769480 | tf_op jit(solution)/shard_map/ppermute | solution.py:346
  151.8 28.4 %all_to_all.15.own_ref = bf16[8,2,192,128]{3,2,1,0:T(8,128)(2,1)S(1)} all-to-all(bf16[8,2,192,128]{3,2,1,0:T(8,128)(2,1)S(1)} %broadcast_in_dim.55), channel_id=1, replica_groups={{0,32,64,96,128,160,192,224},{256,288,320,352,384,416,448,480},{1,33,65..., dimensions={0} | all-to-all | bytes 1572864 | tf_op jit(solution)/shard_map/all_to_all | solution.py:368
  180.2 3.8 %collective-permute-start.21 = (bf16[8,2,192,128]{3,2,1,0:T(8,128)(2,1)S(1)}, bf16[8,2,192,128]{3,2,1,0:T(8,128)(2,1)S(1)}, u32[]{:S(2)}, u32[]{:S(2)}) collective-permute-start(bf16[8,2,192,128]{3,2,1,0:T(8,128)(2,1)S(1)} %all_to_all.15.own_ref), channel_id=1, source_target_pairs={{0,1},{1,0},{2,3},{3,2},{4,5},{5,4},{6,7},{7,6},{8,9},{9,8},{10,11... | collective-permute-start | bytes 2359304 | tf_op jit(solution)/shard_map/ppermute | solution.py:346
  191.0 9.4 %all_to_all.16 = bf16[8,2,1536]{2,1,0:T(2,128)(2,1)S(1)} all-to-all(bf16[8,2,1536]{2,1,0:T(2,128)(2,1)S(1)} %reshape.71), channel_id=1, replica_groups={{0,32,64,96,128,160,192,224},{256,288,320,352,384,416,448,480},{1,33,65..., dimensions={0} | all-to-all | bytes 98304 | tf_op jit(solution)/shard_map/all_to_all | solution.py:368
  203.4 3.3 %collective-permute-start.22 = (bf16[24,2048]{1,0:T(8,128)(2,1)S(1)}, bf16[24,2048]{1,0:T(8,128)(2,1)S(1)}, u32[]{:S(2)}, u32[]{:S(2)}) collective-permute-start(bf16[24,2048]{1,0:T(8,128)(2,1)S(1)} %get-tuple-element.41), channel_id=1, source_target_pairs={{0,1},{1,0},{2,3},{3,2},{4,5},{5,4},{6,7},{7,6},{8,9},{9,8},{10,11... | collective-permute-start | bytes 294920 | tf_op jit(solution)/shard_map/ppermute | solution.py:346
  207.6 5.2 %shard_map.161 = bf16[384,512]{1,0:T(8,128)(2,1)} custom-call(s32[2]{0:T(128)S(1)} %pad_add_fusion.1.core_ref.place_ref, f32[24,2048]{1,0:T(8,128)S(1)} %get-tuple-element.36.own_coarse_ref, f32[24,2048]{1,0:T(8,128)S(1)} %get-tuple-element.40.part_ref, bf16[24,2048]{1,0:T(8,128)(2,1)S(1)} %collective-permute-done.22.recv_ref, ...), custom_call_target="tpu_custom_call" | custom-call | flops 201326592 | bytes 10518536 | tf_op jit(solution)/shard_map/pallas_call | solution.py:20
  (135 shorter events, 63.2 us)
Async XLA Ops:
  6.5 73.1 %all-gather.3.cloned.1.call-start = ((), (), s32[]{:S(2)}) async-start(), calls=%async_computation.3 | async-start | bytes 2949120 | tf_op jit(solution)/shard_map/all_gather | solution.py:424
  8.3 8.2 %collective-permute-start = (bf16[1,160,512]{2,1,0:T(8,128)(2,1)S(1)}, bf16[1,160,512]{2,1,0:T(8,128)(2,1)S(1)}, u32[]{:S(2)}, u32[]{:S(2)}) collective-permute-start(bf16[1,160,512]{2,1,0:T(8,128)(2,1)S(1)} %maximum_bitcast_fusion.1), channel_id=1, source_target_pairs={{0,256},{32,288},{64,320},{96,352},{128,384},{160,416},{192,448},{... | collective-permute-start | bytes 491528 | tf_op jit(solution)/shard_map/ppermute | solution.py:351
  19.3 16.5 %collective-permute-start.1 = (bf16[2,2,16,512]{3,2,1,0:T(8,128)(2,1)S(1)}, bf16[2,2,16,512]{3,2,1,0:T(8,128)(2,1)S(1)}, u32[]{:S(2)}, u32[]{:S(2)}) collective-permute-start(bf16[2,2,16,512]{3,2,1,0:T(8,128)(2,1)S(1)} %get-tuple-element.51), channel_id=1, source_target_pairs={{0,32},{32,64},{64,96},{96,128},{128,160},{160,192},{192,224},{224... | collective-permute-start | bytes 196616 | tf_op jit(solution)/shard_map/ppermute | solution.py:339
  24.8 12.4 %collective-permute-start.2 = (bf16[2,2,16,512]{3,2,1,0:T(8,128)(2,1)S(1)}, bf16[2,2,16,512]{3,2,1,0:T(8,128)(2,1)S(1)}, u32[]{:S(2)}, u32[]{:S(2)}) collective-permute-start(bf16[2,2,16,512]{3,2,1,0:T(8,128)(2,1)S(1)} %get-tuple-element.50), channel_id=1, source_target_pairs={{32,0},{64,32},{96,64},{128,96},{160,128},{192,160},{224,192},{256... | collective-permute-start | bytes 196616 | tf_op jit(solution)/shard_map/ppermute | solution.py:340
  37.2 6.9 %collective-permute-start.3 = (bf16[16,2,2,512]{3,2,1,0:T(2,128)(2,1)S(1)}, bf16[16,2,2,512]{3,2,1,0:T(2,128)(2,1)S(1)}, u32[]{:S(2)}, u32[]{:S(2)}) collective-permute-start(bf16[16,2,2,512]{3,2,1,0:T(2,128)(2,1)S(1)} %get-tuple-element.49), channel_id=1, source_target_pairs={{0,1},{1,2},{2,3},{3,4},{4,5},{5,6},{6,7},{7,8},{8,9},{9,10},{10,1... | collective-permute-start | bytes 196616 | tf_op jit(solution)/shard_map/ppermute | solution.py:339
  41.7 6.4 %collective-permute-start.4 = (bf16[16,2,2,512]{3,2,1,0:T(2,128)(2,1)S(1)}, bf16[16,2,2,512]{3,2,1,0:T(2,128)(2,1)S(1)}, u32[]{:S(2)}, u32[]{:S(2)}) collective-permute-start(bf16[16,2,2,512]{3,2,1,0:T(2,128)(2,1)S(1)} %get-tuple-element.48), channel_id=1, source_target_pairs={{1,0},{2,1},{3,2},{4,3},{5,4},{6,5},{7,6},{8,7},{9,8},{10,9},{11,1... | collective-permute-start | bytes 196616 | tf_op jit(solution)/shard_map/ppermute | solution.py:340
  48.1 23.4 %collective-permute-start.6 = (bf16[64,2048]{1,0:T(8,128)(2,1)S(1)}, bf16[64,2048]{1,0:T(8,128)(2,1)S(1)}, u32[]{:S(2)}, u32[]{:S(2)}) collective-permute-start(bf16[64,2048]{1,0:T(8,128)(2,1)S(1)} %copy-done.20), channel_id=1, source_target_pairs={{0,0},{1,256},{2,2},{3,258},{4,4},{5,260},{6,6},{7,262},{8,8},{9,2... | collective-permute-start | bytes 786440 | tf_op jit(solution)/shard_map/ppermute | solution.py:364
  51.2 21.0 %collective-permute-start.8 = (bf16[3,2048,64]{1,2,0:T(8,128)(2,1)}, bf16[3,2048,64]{1,2,0:T(8,128)(2,1)}, u32[]{:S(2)}, u32[]{:S(2)}) collective-permute-start(bf16[3,2048,64]{1,2,0:T(8,128)(2,1)} %param.28), channel_id=1, source_target_pairs={{0,0},{1,256},{2,2},{3,258},{4,4},{5,260},{6,6},{7,262},{8,8},{9,2... | collective-permute-start | bytes 2359304 | tf_op jit(solution)/shard_map/ppermute | solution.py:364
  56.6 14.9 %collective-permute-start.5 = (bf16[1,16,640]{2,1,0:T(8,128)(2,1)S(1)}, bf16[1,16,640]{2,1,0:T(8,128)(2,1)S(1)}, u32[]{:S(2)}, u32[]{:S(2)}) collective-permute-start(bf16[1,16,640]{2,1,0:T(8,128)(2,1)S(1)} %maximum_bitcast_fusion.2), channel_id=1, source_target_pairs={{0,256},{32,288},{64,320},{96,352},{128,384},{160,416},{192,448},{... | collective-permute-start | bytes 61448 | tf_op jit(solution)/shard_map/ppermute | solution.py:351
  60.9 17.8 %collective-permute-start.7 = (bf16[4096,128]{1,0:T(8,128)(2,1)}, bf16[4096,128]{1,0:T(8,128)(2,1)S(1)}, u32[]{:S(2)}, u32[]{:S(2)}) collective-permute-start(bf16[4096,128]{1,0:T(8,128)(2,1)} %param.26), channel_id=1, source_target_pairs={{0,0},{1,256},{2,2},{3,258},{4,4},{5,260},{6,6},{7,262},{8,8},{9,2... | collective-permute-start | bytes 3145736 | tf_op jit(solution)/shard_map/ppermute | solution.py:364
  86.0 23.4 %all-to-all-start.2 = ((bf16[8,16,2304]{2,1,0:T(8,128)(2,1)}), bf16[8,16,2304]{2,1,0:T(8,128)(2,1)}, u32[]{:S(2)}, u32[]{:S(2)}) async-start(bf16[8,16,2304]{2,1,0:T(8,128)(2,1)} %broadcast_in_dim.56), calls=%async_computation.2 | async-start | bytes 1179648 | tf_op jit(solution)/shard_map/all_to_all | solution.py:368
  92.9 95.7 %all-gather.5.cloned.1.call-start = ((), (), s32[]{:S(2)}) async-start(), calls=%async_computation.4 | async-start | bytes 5308416 | tf_op jit(solution)/shard_map/all_gather | solution.py:521
  102.7 9.9 %collective-permute-start.11 = (bf16[24,4096]{1,0:T(8,128)(2,1)S(1)}, bf16[24,4096]{1,0:T(8,128)(2,1)S(1)}, u32[]{:S(2)}, u32[]{:S(2)}) collective-permute-start(bf16[24,4096]{1,0:T(8,128)(2,1)S(1)} %get-tuple-element.35), channel_id=1, source_target_pairs={{0,32},{32,64},{64,96},{96,128},{128,160},{160,192},{192,224},{224... | collective-permute-start | bytes 589832 | tf_op jit(solution)/shard_map/ppermute | solution.py:373
  106.0 8.5 %collective-permute-start.12 = (bf16[24,4096]{1,0:T(8,128)(2,1)S(1)}, bf16[24,4096]{1,0:T(8,128)(2,1)S(1)}, u32[]{:S(2)}, u32[]{:S(2)}) collective-permute-start(bf16[24,4096]{1,0:T(8,128)(2,1)S(1)} %get-tuple-element.35), channel_id=1, source_target_pairs={{0,224},{32,0},{64,32},{96,64},{128,96},{160,128},{192,160},{224,1... | collective-permute-start | bytes 589832 | tf_op jit(solution)/shard_map/ppermute | solution.py:373
  112.6 15.0 %collective-permute-start.13 = (bf16[24,4096]{1,0:T(8,128)(2,1)S(1)}, bf16[24,4096]{1,0:T(8,128)(2,1)S(1)}, u32[]{:S(2)}, u32[]{:S(2)}) collective-permute-start(bf16[24,4096]{1,0:T(8,128)(2,1)S(1)} %collective-permute-done.11), channel_id=1, source_target_pairs={{0,32},{32,64},{64,96},{96,128},{128,160},{160,192},{192,224},{224... | collective-permute-start | bytes 589832 | tf_op jit(solution)/shard_map/ppermute | solution.py:373
  114.6 7.8 %collective-permute-start.14 = (bf16[24,4096]{1,0:T(8,128)(2,1)S(1)}, bf16[24,4096]{1,0:T(8,128)(2,1)S(1)}, u32[]{:S(2)}, u32[]{:S(2)}) collective-permute-start(bf16[24,4096]{1,0:T(8,128)(2,1)S(1)} %collective-permute-done.12), channel_id=1, source_target_pairs={{0,224},{32,0},{64,32},{96,64},{128,96},{160,128},{192,160},{224,1... | collective-permute-start | bytes 589832 | tf_op jit(solution)/shard_map/ppermute | solution.py:373
  122.3 7.9 %collective-permute-start.16 = (bf16[24,4096]{1,0:T(8,128)(2,1)S(1)}, bf16[24,4096]{1,0:T(8,128)(2,1)S(1)}, u32[]{:S(2)}, u32[]{:S(2)}) collective-permute-start(bf16[24,4096]{1,0:T(8,128)(2,1)S(1)} %collective-permute-done.14), channel_id=1, source_target_pairs={{0,224},{32,0},{64,32},{96,64},{128,96},{160,128},{192,160},{224,1... | collective-permute-start | bytes 589832 | tf_op jit(solution)/shard_map/ppermute | solution.py:373
  127.7 8.0 %collective-permute-start.15 = (bf16[24,4096]{1,0:T(8,128)(2,1)S(1)}, bf16[24,4096]{1,0:T(8,128)(2,1)S(1)}, u32[]{:S(2)}, u32[]{:S(2)}) collective-permute-start(bf16[24,4096]{1,0:T(8,128)(2,1)S(1)} %collective-permute-done.13), channel_id=1, source_target_pairs={{0,32},{32,64},{64,96},{96,128},{128,160},{160,192},{192,224},{224... | collective-permute-start | bytes 589832 | tf_op jit(solution)/shard_map/ppermute | solution.py:373
  130.3 12.3 %collective-permute-start.18 = (bf16[24,2048]{1,0:T(8,128)(2,1)S(1)}, bf16[24,2048]{1,0:T(8,128)(2,1)S(1)}, u32[]{:S(2)}, u32[]{:S(2)}) collective-permute-start(bf16[24,2048]{1,0:T(8,128)(2,1)S(1)} %slice.52), channel_id=1, source_target_pairs={{0,224},{32,0},{64,32},{96,64},{128,96},{160,128},{192,160},{224,1... | collective-permute-start | bytes 294920 | tf_op jit(solution)/shard_map/ppermute | solution.py:373
  135.7 7.0 %collective-permute-start.17 = (bf16[24,2048]{1,0:T(8,128)(2,1)S(1)}, bf16[24,2048]{1,0:T(8,128)(2,1)S(1)}, u32[]{:S(2)}, u32[]{:S(2)}) collective-permute-start(bf16[24,2048]{1,0:T(8,128)(2,1)S(1)} %slice.51), channel_id=1, source_target_pairs={{0,32},{32,64},{64,96},{96,128},{128,160},{160,192},{192,224},{224... | collective-permute-start | bytes 294920 | tf_op jit(solution)/shard_map/ppermute | solution.py:373
  137.7 12.3 %collective-permute-start.19 = (bf16[5,24,4096]{2,1,0:T(8,128)(2,1)S(1)}, bf16[5,24,4096]{2,1,0:T(8,128)(2,1)S(1)}, u32[]{:S(2)}, u32[]{:S(2)}) collective-permute-start(bf16[5,24,4096]{2,1,0:T(8,128)(2,1)S(1)} %bitcast_dynamic-update-slice_fusion.near_ref), channel_id=1, source_target_pairs={{0,1},{1,0},{2,3},{3,2},{4,5},{5,4},{6,7},{7,6},{8,9},{9,8},{10,11... | collective-permute-start | bytes 2949128 | tf_op jit(solution)/shard_map/ppermute | solution.py:346
  142.8 7.2 %collective-permute-start.20 = (bf16[3,24,4096]{2,1,0:T(8,128)(2,1)S(1)}, bf16[3,24,4096]{2,1,0:T(8,128)(2,1)S(1)}, u32[]{:S(2)}, u32[]{:S(2)}) collective-permute-start(bf16[3,24,4096]{2,1,0:T(8,128)(2,1)S(1)} %pad_maximum_fusion.1.far_ref), channel_id=1, source_target_pairs={{0,1},{1,0},{2,3},{3,2},{4,5},{5,4},{6,7},{7,6},{8,9},{9,8},{10,11... | collective-permute-start | bytes 1769480 | tf_op jit(solution)/shard_map/ppermute | solution.py:346
  180.2 5.5 %collective-permute-start.21 = (bf16[8,2,192,128]{3,2,1,0:T(8,128)(2,1)S(1)}, bf16[8,2,192,128]{3,2,1,0:T(8,128)(2,1)S(1)}, u32[]{:S(2)}, u32[]{:S(2)}) collective-permute-start(bf16[8,2,192,128]{3,2,1,0:T(8,128)(2,1)S(1)} %all_to_all.15.own_ref), channel_id=1, source_target_pairs={{0,1},{1,0},{2,3},{3,2},{4,5},{5,4},{6,7},{7,6},{8,9},{9,8},{10,11... | collective-permute-start | bytes 2359304 | tf_op jit(solution)/shard_map/ppermute | solution.py:346
  188.6 19.0 %collective-permute-start.23 = (bf16[64,16,2304]{2,1,0:T(8,128)(2,1)}, bf16[64,16,2304]{2,1,0:T(8,128)(2,1)}, u32[]{:S(2)}, u32[]{:S(2)}) collective-permute-start(bf16[64,16,2304]{2,1,0:T(8,128)(2,1)} %all-gather.5.cloned.1.call-done.late_ref), channel_id=1, source_target_pairs={{0,1},{1,0},{2,3},{3,2},{4,5},{5,4},{6,7},{7,6},{8,9},{9,8},{10,11... | collective-permute-start | bytes 14155784 | tf_op jit(solution)/shard_map/ppermute | solution.py:346
  (24 other events, 286.6 us)
Sparse Core Ops, SparseCore 0:
  17.4 49.3 all-gather.2
  109.6 62.6 all-gather.4

commit v3 on v2

--- a/solution.py
+++ b/solution.py
@@ -159,15 +159,15 @@
 
 
 def columns_kernel(place_ref, near_ref, far_ref, near_other_ref, far_other_ref, weights_ref, out_ref):
-    for side, refs in enumerate(((near_ref, far_ref), (near_other_ref, far_other_ref))):
-        places = iter(RING_ORDER)
-        for ref in refs:
-            count, rows, width = ref.shape
-            left = jnp.concatenate([ref[at].astype(jnp.float32) for at in range(count)], axis=0)
-            product = dot_rows(left.astype(jnp.bfloat16), weights_ref[...])
-            for at in range(count):
-                place = jnp.bitwise_and(place_ref[1] + (next(places) + 8), 7)
-                out_ref[side, place] = product[at * rows : (at + 1) * rows].astype(jnp.bfloat16)
+    for side, (near, far) in enumerate(((near_ref, far_ref), (near_other_ref, far_other_ref))):
+        count, rows, width = near.shape
+        tiles = [near[at].astype(jnp.float32) for at in range(count)]
+        tiles.append(far[...].astype(jnp.float32))
+        left = jnp.concatenate(tiles, axis=0).astype(jnp.bfloat16)
+        product = dot_rows(left, weights_ref[...])
+        for at, offset in enumerate(RING_ORDER):
+            place = jnp.bitwise_and(place_ref[1] + (offset + 8), 7)
+            out_ref[side, place] = product[at * rows : (at + 1) * rows].astype(jnp.bfloat16)
 
 
 def third_kernel(
@@ -199,12 +199,17 @@
                 ] = (tile * scale * gain).astype(jnp.bfloat16)
     tokens = line // blocks
     coarse_ref[...] = raw_ref[pl.ds(pl.multiple_of(core_ref[1] * tokens, 8), tokens), :]
-    own_rows = pl.multiple_of(core * half, half)
-    other_rows = pl.multiple_of((1 - core) * half, half)
-    triple = (
-        dot_rows(normed_ref[:, :half], qkv_ref[pl.ds(own_rows, half), :])
-        + dot_rows(normed_ref[:, half:], qkv_ref[pl.ds(other_rows, half), :])
-    ).astype(jnp.bfloat16)
+    triple = None
+    for place, origin in ((0, core), (half, 1 - core)):
+        columns = pl.ds(pl.multiple_of(origin * half, half), half)
+        product = lax.dot_general(
+            normed_ref[:, place : place + half],
+            qkv_ref[:, columns],
+            (((1,), (1,)), ((), ())),
+            preferred_element_type=jnp.float32,
+        )
+        triple = product if triple is None else triple + product
+    triple = triple.astype(jnp.bfloat16)
     query = (triple[:, :HD] * 0.125).astype(jnp.bfloat16)
     key = triple[:, HD : 2 * HD]
     value = triple[:, 2 * HD :]
@@ -250,17 +255,16 @@
     level = jnp.right_shift(row, bits) & 1
     lon = jnp.right_shift(row & (lon_count - 1), 1)
     source = (lat * 2 + level) * (lon_count // 2) + lon
-    return jnp.where(source == column, 1.0, 0.0).astype(jnp.float32)
+    return jnp.where(source == column, 1.0, 0.0).astype(jnp.bfloat16)
 
 
 def spread_rows(values, lat_count, lon_count):
-    return lax.dot_general(
-        spread_matrix(lat_count, lon_count),
-        values,
-        (((1,), (0,)), ((), ())),
-        precision=lax.Precision.HIGHEST,
-        preferred_element_type=jnp.float32,
-    )
+    matrix = spread_matrix(lat_count, lon_count)
+    high = values.astype(jnp.bfloat16)
+    rest = values - high.astype(jnp.float32)
+    middle = rest.astype(jnp.bfloat16)
+    low = (rest - middle.astype(jnp.float32)).astype(jnp.bfloat16)
+    return dot_rows(matrix, high) + (dot_rows(matrix, middle) + dot_rows(matrix, low))
 
 
 def up_kernel(
@@ -368,9 +372,14 @@
     return lax.all_to_all(blocks, "lat", 0, 0, axis_index_groups=RINGS, tiled=True)
 
 
-def ring_shift(values, step):
-    pairs = [(at, at // Z_RING * Z_RING + (at + step) % Z_RING) for at in range(2 * Z_RING)]
-    return lax.ppermute(values, "lat", pairs)
+def ring_shift(values, step, flip=0):
+    lon_count = lax.axis_size("lon")
+    pairs = []
+    for lat in range(lax.axis_size("lat")):
+        target = lat // Z_RING * Z_RING + (lat + step) % Z_RING
+        for lon in range(lon_count):
+            pairs.append((lat * lon_count + lon, target * lon_count + (lon ^ flip)))
+    return lax.ppermute(values, ("lat", "lon"), pairs)
 
 
 def ring_gather(values):
@@ -435,11 +444,12 @@
     hidden = after(hidden, both_merge)
     above, below = neighbours(hidden[:2], hidden[-2:], "lat")
     cells = jnp.concatenate([above, hidden, below], axis=0)
+    qkv_third = qkv_third.transpose(0, 2, 1).reshape(-1, qkv_third.shape[1])
+
+    out_third, merge_third, qkv_third, up_third, up_second, cells = lax.optimization_barrier(
+        (out_third, merge_third, qkv_third, up_third, up_second, cells)
+    )
     left, right = neighbours(cells[:, :, :2], cells[:, :, -2:], "lon")
-
-    out_third, merge_third, qkv_third, up_third, up_second, _, _ = lax.optimization_barrier(
-        (out_third, merge_third, qkv_third, up_third, up_second, left, right)
-    )
     own_rest = jnp.concatenate(
         [
             cut(up_third, column * 16, 16, core * 512, 512),
@@ -459,7 +469,6 @@
         ],
         axis=1,
     )
-    qkv_joined = jnp.concatenate([qkv_third[0], qkv_third[1], qkv_third[2]], axis=1)
 
     ext_rows = tile_rows + 4
     own_window = (jnp.arange(32 * 4) % tile_cols + 2) // 4
@@ -487,7 +496,9 @@
         ),
         flops=2 * 640 * 512 * 1536,
     )
-    attended = after(attended, late, merge_third, qkv_joined)
+    late = after(late, attended)
+    late_rows = ring_gather(late)
+    attended = after(attended, late, merge_third, qkv_third)
     tokens = attended.shape[0]
     skip_first, merged_in = call_kernel(
         skip_kernel,
@@ -498,7 +509,6 @@
         (attended, hidden.reshape(-1, feat_dim), merge_weights, norm_merge2[None]),
         flops=2 * 384 * 512 * 512,
     )
-    late_rows = ring_gather(after(late, merged_in))
     own_rows = merged_in.shape[0]
     half_shape = jax.ShapeDtypeStruct((own_rows, 512), jnp.bfloat16)
     second_half, second_send = call_kernel(
@@ -533,23 +543,18 @@
     for _ in range(3):
         forth, back = ring_shift(forth, 1), ring_shift(back, -1)
         pieces += [forth, back]
-    half_feats = coarse_in.shape[1] // 2
-    pieces.append(
-        jnp.concatenate(
-            [ring_shift(forth[:, :half_feats], 1), ring_shift(back[:, half_feats:], -1)], axis=1
-        )
-    )
-    near, far = jnp.stack(pieces[:5]), jnp.stack(pieces[5:])
+    near = jnp.stack(pieces)
+    far, far_other = ring_shift(forth, 1), ring_shift(back, -1, 1)
     column_block = call_kernel(
         columns_kernel,
         jax.ShapeDtypeStruct((2, Z_RING, own_count, 128), jnp.bfloat16),
-        (core_place, near, far, swap_cores(near), swap_cores(far), merge_third),
+        (core_place, near, far, swap_cores(near), far_other, merge_third),
         flops=2 * 384 * 4096 * 128,
     ).reshape(2, line, 128)
     own_columns = ring_gather(column_block)
     other_columns = swap_cores(own_columns)
     blocks, _, _, width = own_columns.shape
-    head_feats = qkv_third.shape[2]
+    head_feats = HD
     heads_out, own_coarse = call_kernel(
         third_kernel,
         (
@@ -561,7 +566,7 @@
             own_columns,
             other_columns,
             norm_third.reshape(2 * blocks, 1, width),
-            qkv_joined,
+            qkv_third,
         ),
         (
             pltpu.VMEM((2 * line, 2 * blocks * width), jnp.bfloat16),

time: 224 us -> 216 us (0.964)
  starting transfers between devices: 103 us -> 92.6 us
  waiting for transfers between devices: 25.3 us -> 31.1 us
  other arithmetic: 4.91 us -> 2.06 us
    ppermute x2, waiting for transfers between devices: 0.01 us -> 8.54 us  [neighbours(): lax.ppermute(last, axis, [(i, (i + 1) % count) for i in range(count)])]
    all_to_all x1, waiting for transfers between devices: 0.01 us -> 6.12 us  [ring_scatter(): lax.all_to_all(blocks, 'lat', 0, 0, axis_index_groups=RINGS, tiled=True)]
    ppermute x7 -> x6, starting transfers between devices: 23.8 us -> 17.7 us  [swap_cores(): return lax.ppermute(values, 'lon', [(i, i ^ 1) for i in range(count)])]
    ppermute x2, waiting for transfers between devices: 5.2 us -> 0.32 us  [neighbours(): lax.ppermute(first, axis, [((i + 1) % count, i) for i in range(count)])]
    ppermute x7 -> x6, waiting for transfers between devices: 7.33 us -> 3.66 us  [swap_cores(): return lax.ppermute(values, 'lon', [(i, i ^ 1) for i in range(count)])]
    ppermute x3, waiting for transfers between devices: 2.99 us -> 0.01 us  [swap_shards(): return lax.ppermute(values, ('lat', 'lon'), pairs)]
    ppermute x8, waiting for transfers between devices: 7.07 us -> 9.7 us  [ring_shift(): return lax.ppermute(values, ('lat', 'lon'), pairs)]
    ppermute x2, starting transfers between devices: 9.62 us -> 7.03 us  [neighbours(): lax.ppermute(last, axis, [(i, (i + 1) % count) for i in range(count)])]
  transfers between devices with their start and end apart: 27 -> 26, of which waited for: 13 -> 13; matrix products, arithmetic and copies ran while one was open for 4% -> 3% of each run, Pallas kernels for 5% -> 5%
where the time goes in v3:
time: 216 us; the launch traced here: 213 us
  starting transfers between devices  92.6 us (43%)
  blocking collectives  39 us (18%)
  waiting for transfers between devices  31.1 us (14%)
  Pallas kernels  17.6 us (8%)
  local copies, waits for them, and re-layouts  16.7 us (8%)
  between operations  14.1 us (7%)
    all_to_all x2, blocking collectives, ring_scatter(): lax.all_to_all(blocks, 'lat', 0, 0, axis_index_groups=RINGS, tiled=True)  39 us
    ppermute x8, starting transfers between devices, ring_shift(): return lax.ppermute(values, ('lat', 'lon'), pairs)  26.8 us
    ppermute x6, starting transfers between devices, swap_cores(): return lax.ppermute(values, 'lon', [(i, i ^ 1) for i in range(count)])  17.7 us
    pallas_call x8, Pallas kernels, call_kernel(): pl.pallas_call(body, out_shape=out_shape, in_specs=[pl.BlockSpec(memory_s...  17.6 us
    ppermute x2, starting transfers between devices, neighbours(): lax.ppermute(first, axis, [((i + 1) % count, i) for i in range(count)])  15 us
    unnamed x52, local copies, waits for them, and re-layouts  12.1 us
    ppermute x3, starting transfers between devices, swap_shards(): return lax.ppermute(values, ('lat', 'lon'), pairs)  11.5 us
    ppermute x8, waiting for transfers between devices, ring_shift(): return lax.ppermute(values, ('lat', 'lon'), pairs)  9.7 us
  transfers between devices with their start and end apart: 26, of which 13 were waited for; matrix products, arithmetic and copies ran while one was open for 3% of the time, Pallas kernels for 5%

profile of v3, /device:TPU:1, one launch (start us, length us, event | category | flops | bytes accessed | tf_op | source)
XLA Modules:
  0.0 213.4 jit_solution(13019729727131665469)
XLA Ops:
  8.3 5.5 %collective-permute-start = (bf16[1,160,512]{2,1,0:T(8,128)(2,1)S(1)}, bf16[1,160,512]{2,1,0:T(8,128)(2,1)S(1)}, u32[]{:S(2)}, u32[]{:S(2)}) collective-permute-start(bf16[1,160,512]{2,1,0:T(8,128)(2,1)S(1)} %maximum_bitcast_fusion), channel_id=1, source_target_pairs={{0,256},{32,288},{64,320},{96,352},{128,384},{160,416},{192,448},{... | collective-permute-start | bytes 491528 | tf_op jit(solution)/shard_map/ppermute | solution.py:355
  13.8 2.7 %collective-permute-done = bf16[1,160,512]{2,1,0:T(8,128)(2,1)S(1)} collective-permute-done((bf16[1,160,512]{2,1,0:T(8,128)(2,1)S(1)}, bf16[1,160,512]{2,1,0:T(8,128)(2,1)S(1)}, u32[]{:S(2)}, u32[]{:S(2)}) %collective-permute-start) | collective-permute-done | bytes 163872 | tf_op jit(solution)/shard_map/ppermute | solution.py:355
  18.3 5.1 %collective-permute-start.1 = (bf16[2,2,16,512]{3,2,1,0:T(8,128)(2,1)S(1)}, bf16[2,2,16,512]{3,2,1,0:T(8,128)(2,1)S(1)}, u32[]{:S(2)}, u32[]{:S(2)}) collective-permute-start(bf16[2,2,16,512]{3,2,1,0:T(8,128)(2,1)S(1)} %get-tuple-element.49), channel_id=1, source_target_pairs={{0,32},{32,64},{64,96},{96,128},{128,160},{160,192},{192,224},{224... | collective-permute-start | bytes 196616 | tf_op jit(solution)/shard_map/ppermute | solution.py:343
  23.4 11.0 %collective-permute-start.2 = (bf16[2,2,16,512]{3,2,1,0:T(8,128)(2,1)S(1)}, bf16[2,2,16,512]{3,2,1,0:T(8,128)(2,1)S(1)}, u32[]{:S(2)}, u32[]{:S(2)}) collective-permute-start(bf16[2,2,16,512]{3,2,1,0:T(8,128)(2,1)S(1)} %get-tuple-element.50), channel_id=1, source_target_pairs={{32,0},{64,32},{96,64},{128,96},{160,128},{192,160},{224,192},{256... | collective-permute-start | bytes 196616 | tf_op jit(solution)/shard_map/ppermute | solution.py:344
  35.8 4.4 %collective-permute-start.7 = (bf16[4096,128]{1,0:T(8,128)(2,1)}, bf16[4096,128]{1,0:T(8,128)(2,1)S(1)}, u32[]{:S(2)}, u32[]{:S(2)}) collective-permute-start(bf16[4096,128]{1,0:T(8,128)(2,1)} %param.26), channel_id=1, source_target_pairs={{0,0},{1,256},{2,2},{3,258},{4,4},{5,260},{6,6},{7,262},{8,8},{9,2... | collective-permute-start | bytes 3145736 | tf_op jit(solution)/shard_map/ppermute | solution.py:368
  43.6 4.9 %collective-permute-start.6 = (bf16[64,2048]{1,0:T(8,128)(2,1)}, bf16[64,2048]{1,0:T(8,128)(2,1)}, u32[]{:S(2)}, u32[]{:S(2)}) collective-permute-start(bf16[64,2048]{1,0:T(8,128)(2,1)} %param.29), channel_id=1, source_target_pairs={{0,0},{1,256},{2,2},{3,258},{4,4},{5,260},{6,6},{7,262},{8,8},{9,2... | collective-permute-start | bytes 786440 | tf_op jit(solution)/shard_map/ppermute | solution.py:368
  52.7 4.0 %collective-permute-start.4 = (bf16[16,2,2,512]{3,2,1,0:T(2,128)(2,1)S(1)}, bf16[16,2,2,512]{3,2,1,0:T(2,128)(2,1)S(1)}, u32[]{:S(2)}, u32[]{:S(2)}) collective-permute-start(bf16[16,2,2,512]{3,2,1,0:T(2,128)(2,1)S(1)} %get-tuple-element.47), channel_id=1, source_target_pairs={{1,0},{2,1},{3,2},{4,3},{5,4},{6,5},{7,6},{8,7},{9,8},{10,9},{11,1... | collective-permute-start | bytes 196616 | tf_op jit(solution)/shard_map/ppermute | solution.py:344
  56.7 8.5 %collective-permute-done.3 = bf16[16,2,2,512]{3,2,1,0:T(2,128)(2,1)S(1)} collective-permute-done((bf16[16,2,2,512]{3,2,1,0:T(2,128)(2,1)S(1)}, bf16[16,2,2,512]{3,2,1,0:T(2,128)(2,1)S(1)}, u32[]{:S(2)}, u32[]{:S(2)}) %collective-permute-start.3) | collective-permute-done | bytes 65568 | tf_op jit(solution)/shard_map/ppermute | solution.py:343
  67.8 3.2 %shard_map.154.attended_ref = bf16[384,512]{1,0:T(8,128)(2,1)S(1)} custom-call(bf16[512,512]{1,0:T(8,128)(2,1)S(1)} %bitcast.39, bf16[64,512]{1,0:T(8,128)(2,1)S(1)} %reshape.69.left_ref, bf16[64,512]{1,0:T(8,128)(2,1)S(1)} %reshape.70.right_ref, f32[1,512]{1,0:T(1,128)S(1)} %bitcast.44, bf16[3,512,512]{2,1,0:T(8,128)(2,1)S(1)} %copy-done.16, ...), custom_call_target="tpu_custom_call" | custom-call | flops 1006632960 | bytes 2314752 | tf_op jit(solution)/shard_map/pallas_call | solution.py:20
  82.7 7.0 %all-to-all-start.2 = ((bf16[8,16,2304]{2,1,0:T(8,128)(2,1)}), bf16[8,16,2304]{2,1,0:T(8,128)(2,1)}, u32[]{:S(2)}, u32[]{:S(2)}) async-start(bf16[8,16,2304]{2,1,0:T(8,128)(2,1)} %broadcast_in_dim.56), calls=%async_computation.2 | async-start | bytes 1179648 | tf_op jit(solution)/shard_map/all_to_all | solution.py:372
  91.4 2.7 %collective-permute-start.10 = (bf16[96,512]{1,0:T(8,128)(2,1)S(1)}, bf16[96,512]{1,0:T(8,128)(2,1)S(1)}, u32[]{:S(2)}, u32[]{:S(2)}) collective-permute-start(bf16[96,512]{1,0:T(8,128)(2,1)S(1)} %get-tuple-element.37), channel_id=1, source_target_pairs={{0,1},{1,0},{2,3},{3,2},{4,5},{5,4},{6,7},{7,6},{8,9},{9,8},{10,11... | collective-permute-start | bytes 294920 | tf_op jit(solution)/shard_map/ppermute | solution.py:350
  96.0 3.6 %collective-permute-start.11 = (bf16[24,4096]{1,0:T(8,128)(2,1)S(1)}, bf16[24,4096]{1,0:T(8,128)(2,1)S(1)}, u32[]{:S(2)}, u32[]{:S(2)}) collective-permute-start(bf16[24,4096]{1,0:T(8,128)(2,1)S(1)} %get-tuple-element.38), channel_id=1, source_target_pairs={{0,32},{1,33},{2,34},{3,35},{4,36},{5,37},{6,38},{7,39},{8,40},{9,... | collective-permute-start | bytes 589832 | tf_op jit(solution)/shard_map/ppermute | solution.py:382
  99.7 3.1 %collective-permute-start.12 = (bf16[24,4096]{1,0:T(8,128)(2,1)S(1)}, bf16[24,4096]{1,0:T(8,128)(2,1)S(1)}, u32[]{:S(2)}, u32[]{:S(2)}) collective-permute-start(bf16[24,4096]{1,0:T(8,128)(2,1)S(1)} %get-tuple-element.38), channel_id=1, source_target_pairs={{0,224},{1,225},{2,226},{3,227},{4,228},{5,229},{6,230},{7,231},{8... | collective-permute-start | bytes 589832 | tf_op jit(solution)/shard_map/ppermute | solution.py:382
  102.8 6.1 %all-to-all-done.2 = bf16[8,16,2304]{2,1,0:T(8,128)(2,1)} async-done(((bf16[8,16,2304]{2,1,0:T(8,128)(2,1)}), bf16[8,16,2304]{2,1,0:T(8,128)(2,1)}, u32[]{:S(2)}, u32[]{:S(2)}) %all-to-all-start.2) | async-done | bytes 589856 | tf_op jit(solution)/shard_map/all_to_all | solution.py:372
  111.9 4.6 %collective-permute-start.14 = (bf16[24,4096]{1,0:T(8,128)(2,1)S(1)}, bf16[24,4096]{1,0:T(8,128)(2,1)S(1)}, u32[]{:S(2)}, u32[]{:S(2)}) collective-permute-start(bf16[24,4096]{1,0:T(8,128)(2,1)S(1)} %collective-permute-done.12), channel_id=1, source_target_pairs={{0,224},{1,225},{2,226},{3,227},{4,228},{5,229},{6,230},{7,231},{8... | collective-permute-start | bytes 589832 | tf_op jit(solution)/shard_map/ppermute | solution.py:382
  120.1 4.6 %collective-permute-start.16 = (bf16[24,4096]{1,0:T(8,128)(2,1)S(1)}, bf16[24,4096]{1,0:T(8,128)(2,1)S(1)}, u32[]{:S(2)}, u32[]{:S(2)}) collective-permute-start(bf16[24,4096]{1,0:T(8,128)(2,1)S(1)} %collective-permute-done.14), channel_id=1, source_target_pairs={{0,224},{1,225},{2,226},{3,227},{4,228},{5,229},{6,230},{7,231},{8... | collective-permute-start | bytes 589832 | tf_op jit(solution)/shard_map/ppermute | solution.py:382
  127.3 5.2 %collective-permute-start.18 = (bf16[7,24,4096]{2,1,0:T(8,128)(2,1)S(1)}, bf16[7,24,4096]{2,1,0:T(8,128)(2,1)S(1)}, u32[]{:S(2)}, u32[]{:S(2)}) collective-permute-start(bf16[7,24,4096]{2,1,0:T(8,128)(2,1)S(1)} %bitcast_dynamic-update-slice_fusion.near_ref), channel_id=1, source_target_pairs={{0,1},{1,0},{2,3},{3,2},{4,5},{5,4},{6,7},{7,6},{8,9},{9,8},{10,11... | collective-permute-start | bytes 4128776 | tf_op jit(solution)/shard_map/ppermute | solution.py:350
  134.5 5.2 %collective-permute-start.19 = (bf16[24,4096]{1,0:T(8,128)(2,1)S(1)}, bf16[24,4096]{1,0:T(8,128)(2,1)S(1)}, u32[]{:S(2)}, u32[]{:S(2)}) collective-permute-start(bf16[24,4096]{1,0:T(8,128)(2,1)S(1)} %collective-permute-done.16), channel_id=1, source_target_pairs={{0,225},{1,224},{2,227},{3,226},{4,229},{5,228},{6,231},{7,230},{8... | collective-permute-start | bytes 589832 | tf_op jit(solution)/shard_map/ppermute | solution.py:382
  139.7 3.5 %collective-permute-done.17.far_ref = bf16[24,4096]{1,0:T(8,128)(2,1)S(1)} collective-permute-done((bf16[24,4096]{1,0:T(8,128)(2,1)S(1)}, bf16[24,4096]{1,0:T(8,128)(2,1)S(1)}, u32[]{:S(2)}, u32[]{:S(2)}) %collective-permute-start.17) | collective-permute-done | bytes 196640 | tf_op jit(solution)/shard_map/ppermute | solution.py:382
  145.9 29.6 %all_to_all.15.own_ref = bf16[8,2,192,128]{3,2,1,0:T(8,128)(2,1)S(1)} all-to-all(bf16[8,2,192,128]{3,2,1,0:T(8,128)(2,1)S(1)} %broadcast_in_dim.55), channel_id=1, replica_groups={{0,32,64,96,128,160,192,224},{256,288,320,352,384,416,448,480},{1,33,65..., dimensions={0} | all-to-all | bytes 1572864 | tf_op jit(solution)/shard_map/all_to_all | solution.py:372
  179.8 2.9 %shard_map.159 = (bf16[8,2,24,64]{3,2,1,0:T(8,128)(2,1)S(1)}, f32[24,2048]{1,0:T(8,128)S(1)}) custom-call(s32[2]{0:T(128)S(1)} %pad_add_fusion.1.core_ref.place_ref, bf16[8,2,192,128]{3,2,1,0:T(8,128)(2,1)S(1)} %all_to_all.15.own_ref, bf16[8,2,192,128]{3,2,1,0:T(8,128)(2,1)S(1)} %collective-permute-done.20.other_ref, f32[16,1,128]{2,1,0:T(1,128)S(1)} %bitcast.43, ...), custom_call_target="tpu_custom_call" | custom-call | flops 301989888 | bytes 2367496 | tf_op jit(solution)/shard_map/pallas_call | solution.py:20
  185.1 9.4 %all_to_all.16 = bf16[8,2,1536]{2,1,0:T(2,128)(2,1)S(1)} all-to-all(bf16[8,2,1536]{2,1,0:T(2,128)(2,1)S(1)} %reshape.75), channel_id=1, replica_groups={{0,32,64,96,128,160,192,224},{256,288,320,352,384,416,448,480},{1,33,65..., dimensions={0} | all-to-all | bytes 98304 | tf_op jit(solution)/shard_map/all_to_all | solution.py:372
  197.5 3.3 %collective-permute-start.21 = (bf16[24,2048]{1,0:T(8,128)(2,1)S(1)}, bf16[24,2048]{1,0:T(8,128)(2,1)S(1)}, u32[]{:S(2)}, u32[]{:S(2)}) collective-permute-start(bf16[24,2048]{1,0:T(8,128)(2,1)S(1)} %get-tuple-element.43), channel_id=1, source_target_pairs={{0,1},{1,0},{2,3},{3,2},{4,5},{5,4},{6,7},{7,6},{8,9},{9,8},{10,11... | collective-permute-start | bytes 294920 | tf_op jit(solution)/shard_map/ppermute | solution.py:350
  201.7 4.8 %shard_map.161 = bf16[384,512]{1,0:T(8,128)(2,1)} custom-call(s32[2]{0:T(128)S(1)} %pad_add_fusion.1.core_ref.place_ref, f32[24,2048]{1,0:T(8,128)S(1)} %get-tuple-element.39.own_coarse_ref, f32[24,2048]{1,0:T(8,128)S(1)} %get-tuple-element.42.part_ref, bf16[24,2048]{1,0:T(8,128)(2,1)S(1)} %collective-permute-done.21.recv_ref, ...), custom_call_target="tpu_custom_call" | custom-call | flops 201326592 | bytes 10518536 | tf_op jit(solution)/shard_map/pallas_call | solution.py:20
  (126 shorter events, 54.2 us)
Async XLA Ops:
  6.5 67.9 %all-gather.3.cloned.1.call-start = ((), (), s32[]{:S(2)}) async-start(), calls=%async_computation.3 | async-start | bytes 2949120 | tf_op jit(solution)/shard_map/all_gather | solution.py:433
  8.3 8.2 %collective-permute-start = (bf16[1,160,512]{2,1,0:T(8,128)(2,1)S(1)}, bf16[1,160,512]{2,1,0:T(8,128)(2,1)S(1)}, u32[]{:S(2)}, u32[]{:S(2)}) collective-permute-start(bf16[1,160,512]{2,1,0:T(8,128)(2,1)S(1)} %maximum_bitcast_fusion), channel_id=1, source_target_pairs={{0,256},{32,288},{64,320},{96,352},{128,384},{160,416},{192,448},{... | collective-permute-start | bytes 491528 | tf_op jit(solution)/shard_map/ppermute | solution.py:355
  18.3 17.2 %collective-permute-start.1 = (bf16[2,2,16,512]{3,2,1,0:T(8,128)(2,1)S(1)}, bf16[2,2,16,512]{3,2,1,0:T(8,128)(2,1)S(1)}, u32[]{:S(2)}, u32[]{:S(2)}) collective-permute-start(bf16[2,2,16,512]{3,2,1,0:T(8,128)(2,1)S(1)} %get-tuple-element.49), channel_id=1, source_target_pairs={{0,32},{32,64},{64,96},{96,128},{128,160},{160,192},{192,224},{224... | collective-permute-start | bytes 196616 | tf_op jit(solution)/shard_map/ppermute | solution.py:343
  23.4 12.4 %collective-permute-start.2 = (bf16[2,2,16,512]{3,2,1,0:T(8,128)(2,1)S(1)}, bf16[2,2,16,512]{3,2,1,0:T(8,128)(2,1)S(1)}, u32[]{:S(2)}, u32[]{:S(2)}) collective-permute-start(bf16[2,2,16,512]{3,2,1,0:T(8,128)(2,1)S(1)} %get-tuple-element.50), channel_id=1, source_target_pairs={{32,0},{64,32},{96,64},{128,96},{160,128},{192,160},{224,192},{256... | collective-permute-start | bytes 196616 | tf_op jit(solution)/shard_map/ppermute | solution.py:344
  35.8 37.6 %collective-permute-start.7 = (bf16[4096,128]{1,0:T(8,128)(2,1)}, bf16[4096,128]{1,0:T(8,128)(2,1)S(1)}, u32[]{:S(2)}, u32[]{:S(2)}) collective-permute-start(bf16[4096,128]{1,0:T(8,128)(2,1)} %param.26), channel_id=1, source_target_pairs={{0,0},{1,256},{2,2},{3,258},{4,4},{5,260},{6,6},{7,262},{8,8},{9,2... | collective-permute-start | bytes 3145736 | tf_op jit(solution)/shard_map/ppermute | solution.py:368
  41.7 11.0 %collective-permute-start.5 = (bf16[1,16,640]{2,1,0:T(8,128)(2,1)S(1)}, bf16[1,16,640]{2,1,0:T(8,128)(2,1)S(1)}, u32[]{:S(2)}, u32[]{:S(2)}) collective-permute-start(bf16[1,16,640]{2,1,0:T(8,128)(2,1)S(1)} %maximum_bitcast_fusion.1), channel_id=1, source_target_pairs={{0,256},{32,288},{64,320},{96,352},{128,384},{160,416},{192,448},{... | collective-permute-start | bytes 61448 | tf_op jit(solution)/shard_map/ppermute | solution.py:355
  43.6 28.1 %collective-permute-start.6 = (bf16[64,2048]{1,0:T(8,128)(2,1)}, bf16[64,2048]{1,0:T(8,128)(2,1)}, u32[]{:S(2)}, u32[]{:S(2)}) collective-permute-start(bf16[64,2048]{1,0:T(8,128)(2,1)} %param.29), channel_id=1, source_target_pairs={{0,0},{1,256},{2,2},{3,258},{4,4},{5,260},{6,6},{7,262},{8,8},{9,2... | collective-permute-start | bytes 786440 | tf_op jit(solution)/shard_map/ppermute | solution.py:368
  48.5 24.0 %collective-permute-start.8 = (bf16[192,2048]{1,0:T(8,128)(2,1)}, bf16[192,2048]{1,0:T(8,128)(2,1)S(1)}, u32[]{:S(2)}, u32[]{:S(2)}) collective-permute-start(bf16[192,2048]{1,0:T(8,128)(2,1)} %bitcast.45), channel_id=1, source_target_pairs={{0,0},{1,256},{2,2},{3,258},{4,4},{5,260},{6,6},{7,262},{8,8},{9,2... | collective-permute-start | bytes 2359304 | tf_op jit(solution)/shard_map/ppermute | solution.py:368
  50.8 14.5 %collective-permute-start.3 = (bf16[16,2,2,512]{3,2,1,0:T(2,128)(2,1)S(1)}, bf16[16,2,2,512]{3,2,1,0:T(2,128)(2,1)S(1)}, u32[]{:S(2)}, u32[]{:S(2)}) collective-permute-start(bf16[16,2,2,512]{3,2,1,0:T(2,128)(2,1)S(1)} %get-tuple-element.48), channel_id=1, source_target_pairs={{0,1},{1,2},{2,3},{3,4},{4,5},{5,6},{6,7},{7,8},{8,9},{9,10},{10,1... | collective-permute-start | bytes 196616 | tf_op jit(solution)/shard_map/ppermute | solution.py:343
  52.7 12.6 %collective-permute-start.4 = (bf16[16,2,2,512]{3,2,1,0:T(2,128)(2,1)S(1)}, bf16[16,2,2,512]{3,2,1,0:T(2,128)(2,1)S(1)}, u32[]{:S(2)}, u32[]{:S(2)}) collective-permute-start(bf16[16,2,2,512]{3,2,1,0:T(2,128)(2,1)S(1)} %get-tuple-element.47), channel_id=1, source_target_pairs={{1,0},{2,1},{3,2},{4,3},{5,4},{6,5},{7,6},{8,7},{9,8},{10,9},{11,1... | collective-permute-start | bytes 196616 | tf_op jit(solution)/shard_map/ppermute | solution.py:344
  79.9 9.9 %collective-permute-start.9 = (bf16[96,2048]{1,0:T(8,128)(2,1)}, bf16[96,2048]{1,0:T(8,128)(2,1)S(1)}, u32[]{:S(2)}, u32[]{:S(2)}) collective-permute-start(bf16[96,2048]{1,0:T(8,128)(2,1)} %get-tuple-element.35.own_ref), channel_id=1, source_target_pairs={{0,1},{1,0},{2,3},{3,2},{4,5},{5,4},{6,7},{7,6},{8,9},{9,8},{10,11... | collective-permute-start | bytes 1179656 | tf_op jit(solution)/shard_map/ppermute | solution.py:350
  82.7 26.2 %all-to-all-start.2 = ((bf16[8,16,2304]{2,1,0:T(8,128)(2,1)}), bf16[8,16,2304]{2,1,0:T(8,128)(2,1)}, u32[]{:S(2)}, u32[]{:S(2)}) async-start(bf16[8,16,2304]{2,1,0:T(8,128)(2,1)} %broadcast_in_dim.56), calls=%async_computation.2 | async-start | bytes 1179648 | tf_op jit(solution)/shard_map/all_to_all | solution.py:372
  89.7 93.0 %all-gather.5.cloned.1.call-start = ((), (), s32[]{:S(2)}) async-start(), calls=%async_computation.4 | async-start | bytes 5308416 | tf_op jit(solution)/shard_map/all_gather | solution.py:531
  96.0 13.9 %collective-permute-start.11 = (bf16[24,4096]{1,0:T(8,128)(2,1)S(1)}, bf16[24,4096]{1,0:T(8,128)(2,1)S(1)}, u32[]{:S(2)}, u32[]{:S(2)}) collective-permute-start(bf16[24,4096]{1,0:T(8,128)(2,1)S(1)} %get-tuple-element.38), channel_id=1, source_target_pairs={{0,32},{1,33},{2,34},{3,35},{4,36},{5,37},{6,38},{7,39},{8,40},{9,... | collective-permute-start | bytes 589832 | tf_op jit(solution)/shard_map/ppermute | solution.py:382
  99.7 12.2 %collective-permute-start.12 = (bf16[24,4096]{1,0:T(8,128)(2,1)S(1)}, bf16[24,4096]{1,0:T(8,128)(2,1)S(1)}, u32[]{:S(2)}, u32[]{:S(2)}) collective-permute-start(bf16[24,4096]{1,0:T(8,128)(2,1)S(1)} %get-tuple-element.38), channel_id=1, source_target_pairs={{0,224},{1,225},{2,226},{3,227},{4,228},{5,229},{6,230},{7,231},{8... | collective-permute-start | bytes 589832 | tf_op jit(solution)/shard_map/ppermute | solution.py:382
  110.0 8.2 %collective-permute-start.13 = (bf16[24,4096]{1,0:T(8,128)(2,1)S(1)}, bf16[24,4096]{1,0:T(8,128)(2,1)S(1)}, u32[]{:S(2)}, u32[]{:S(2)}) collective-permute-start(bf16[24,4096]{1,0:T(8,128)(2,1)S(1)} %collective-permute-done.11), channel_id=1, source_target_pairs={{0,32},{1,33},{2,34},{3,35},{4,36},{5,37},{6,38},{7,39},{8,40},{9,... | collective-permute-start | bytes 589832 | tf_op jit(solution)/shard_map/ppermute | solution.py:382
  111.9 8.2 %collective-permute-start.14 = (bf16[24,4096]{1,0:T(8,128)(2,1)S(1)}, bf16[24,4096]{1,0:T(8,128)(2,1)S(1)}, u32[]{:S(2)}, u32[]{:S(2)}) collective-permute-start(bf16[24,4096]{1,0:T(8,128)(2,1)S(1)} %collective-permute-done.12), channel_id=1, source_target_pairs={{0,224},{1,225},{2,226},{3,227},{4,228},{5,229},{6,230},{7,231},{8... | collective-permute-start | bytes 589832 | tf_op jit(solution)/shard_map/ppermute | solution.py:382
  118.2 8.0 %collective-permute-start.15 = (bf16[24,4096]{1,0:T(8,128)(2,1)S(1)}, bf16[24,4096]{1,0:T(8,128)(2,1)S(1)}, u32[]{:S(2)}, u32[]{:S(2)}) collective-permute-start(bf16[24,4096]{1,0:T(8,128)(2,1)S(1)} %collective-permute-done.13), channel_id=1, source_target_pairs={{0,32},{1,33},{2,34},{3,35},{4,36},{5,37},{6,38},{7,39},{8,40},{9,... | collective-permute-start | bytes 589832 | tf_op jit(solution)/shard_map/ppermute | solution.py:382
  120.1 7.2 %collective-permute-start.16 = (bf16[24,4096]{1,0:T(8,128)(2,1)S(1)}, bf16[24,4096]{1,0:T(8,128)(2,1)S(1)}, u32[]{:S(2)}, u32[]{:S(2)}) collective-permute-start(bf16[24,4096]{1,0:T(8,128)(2,1)S(1)} %collective-permute-done.14), channel_id=1, source_target_pairs={{0,224},{1,225},{2,226},{3,227},{4,228},{5,229},{6,230},{7,231},{8... | collective-permute-start | bytes 589832 | tf_op jit(solution)/shard_map/ppermute | solution.py:382
  127.3 16.9 %collective-permute-start.18 = (bf16[7,24,4096]{2,1,0:T(8,128)(2,1)S(1)}, bf16[7,24,4096]{2,1,0:T(8,128)(2,1)S(1)}, u32[]{:S(2)}, u32[]{:S(2)}) collective-permute-start(bf16[7,24,4096]{2,1,0:T(8,128)(2,1)S(1)} %bitcast_dynamic-update-slice_fusion.near_ref), channel_id=1, source_target_pairs={{0,1},{1,0},{2,3},{3,2},{4,5},{5,4},{6,7},{7,6},{8,9},{9,8},{10,11... | collective-permute-start | bytes 4128776 | tf_op jit(solution)/shard_map/ppermute | solution.py:350
  132.5 10.7 %collective-permute-start.17 = (bf16[24,4096]{1,0:T(8,128)(2,1)S(1)}, bf16[24,4096]{1,0:T(8,128)(2,1)S(1)}, u32[]{:S(2)}, u32[]{:S(2)}) collective-permute-start(bf16[24,4096]{1,0:T(8,128)(2,1)S(1)} %collective-permute-done.15), channel_id=1, source_target_pairs={{0,32},{1,33},{2,34},{3,35},{4,36},{5,37},{6,38},{7,39},{8,40},{9,... | collective-permute-start | bytes 589832 | tf_op jit(solution)/shard_map/ppermute | solution.py:382
  134.5 9.7 %collective-permute-start.19 = (bf16[24,4096]{1,0:T(8,128)(2,1)S(1)}, bf16[24,4096]{1,0:T(8,128)(2,1)S(1)}, u32[]{:S(2)}, u32[]{:S(2)}) collective-permute-start(bf16[24,4096]{1,0:T(8,128)(2,1)S(1)} %collective-permute-done.16), channel_id=1, source_target_pairs={{0,225},{1,224},{2,227},{3,226},{4,229},{5,228},{6,231},{7,230},{8... | collective-permute-start | bytes 589832 | tf_op jit(solution)/shard_map/ppermute | solution.py:382
  175.5 4.2 %collective-permute-start.20 = (bf16[8,2,192,128]{3,2,1,0:T(8,128)(2,1)S(1)}, bf16[8,2,192,128]{3,2,1,0:T(8,128)(2,1)S(1)}, u32[]{:S(2)}, u32[]{:S(2)}) collective-permute-start(bf16[8,2,192,128]{3,2,1,0:T(8,128)(2,1)S(1)} %all_to_all.15.own_ref), channel_id=1, source_target_pairs={{0,1},{1,0},{2,3},{3,2},{4,5},{5,4},{6,7},{7,6},{8,9},{9,8},{10,11... | collective-permute-start | bytes 2359304 | tf_op jit(solution)/shard_map/ppermute | solution.py:350
  182.7 19.0 %collective-permute-start.22 = (bf16[64,16,2304]{2,1,0:T(8,128)(2,1)}, bf16[64,16,2304]{2,1,0:T(8,128)(2,1)}, u32[]{:S(2)}, u32[]{:S(2)}) collective-permute-start(bf16[64,16,2304]{2,1,0:T(8,128)(2,1)} %all-gather.5.cloned.1.call-done.late_ref), channel_id=1, source_target_pairs={{0,1},{1,0},{2,3},{3,2},{4,5},{5,4},{6,7},{7,6},{8,9},{9,8},{10,11... | collective-permute-start | bytes 14155784 | tf_op jit(solution)/shard_map/ppermute | solution.py:350
  (24 other events, 244.3 us)
Sparse Core Ops, SparseCore 0:
  17.4 49.1 all-gather.2
  109.1 58.8 all-gather.4

commit v4 on v3

--- a/solution.py
+++ b/solution.py
@@ -155,95 +155,69 @@
     join_quads(second, 3, 4, gain_ref, coarse_ref)
 
 
-RING_ORDER = (0, -1, 1, -2, 2, -3, 3, 4)
-
-
-def columns_kernel(place_ref, near_ref, far_ref, near_other_ref, far_other_ref, weights_ref, out_ref):
-    for side, (near, far) in enumerate(((near_ref, far_ref), (near_other_ref, far_other_ref))):
-        count, rows, width = near.shape
-        tiles = [near[at].astype(jnp.float32) for at in range(count)]
-        tiles.append(far[...].astype(jnp.float32))
-        left = jnp.concatenate(tiles, axis=0).astype(jnp.bfloat16)
-        product = dot_rows(left, weights_ref[...])
+RING_ORDER = (0, -1, 1, -2, 2, -3, 3)
+
+
+def columns_kernel(place_ref, *refs):
+    near, (far_low, far_high), (own_ref, other_ref, out_ref) = refs[:7], refs[7:9], refs[9:]
+    rows, half = far_low.shape
+    left = jnp.concatenate([ref[...].astype(jnp.float32) for ref in near], axis=0)
+    left = left.astype(jnp.bfloat16)
+    ring = place_ref[2]
+    for weights, shard in ((own_ref, ring), (other_ref, 1 - ring)):
+        product = dot_rows(left, weights[...])
         for at, offset in enumerate(RING_ORDER):
             place = jnp.bitwise_and(place_ref[1] + (offset + 8), 7)
-            out_ref[side, place] = product[at * rows : (at + 1) * rows].astype(jnp.bfloat16)
-
-
-def third_kernel(
-    core_ref, own_ref, other_ref, gain_ref, qkv_ref, out_ref, coarse_ref, normed_ref, raw_ref
-):
-    blocks, sides, line, width = own_ref.shape
-    core = core_ref[0]
-    half = blocks * width
-    count = 1.0 / (2 * half)
-    rows = 32
-    for side in range(sides):
-        for start in range(0, line, rows):
-            mine = slice(start, start + rows)
-            tiles = [own_ref[z, side, mine, :].astype(jnp.float32) for z in range(blocks)]
-            tiles += [other_ref[z, 1 - side, mine, :].astype(jnp.float32) for z in range(blocks)]
-            if side == 0:
-                for place, tile in enumerate(tiles):
-                    raw_ref[mine, place * width : (place + 1) * width] = tile
-            row_mean = jnp.sum(sum(tiles), axis=-1, keepdims=True) * count
-            tiles = [tile - row_mean for tile in tiles]
-            spread = jnp.sum(sum(tile * tile for tile in tiles), axis=-1, keepdims=True)
-            scale = lax.rsqrt(spread * count + 1e-05)
-            for place, tile in enumerate(tiles):
-                origin = core if place < blocks else 1 - core
-                gain = gain_ref[origin * blocks + place % blocks]
-                normed_ref[
-                    side * line + start : side * line + start + rows,
-                    place * width : (place + 1) * width,
-                ] = (tile * scale * gain).astype(jnp.bfloat16)
-    tokens = line // blocks
-    coarse_ref[...] = raw_ref[pl.ds(pl.multiple_of(core_ref[1] * tokens, 8), tokens), :]
-    triple = None
-    for place, origin in ((0, core), (half, 1 - core)):
-        columns = pl.ds(pl.multiple_of(origin * half, half), half)
-        product = lax.dot_general(
-            normed_ref[:, place : place + half],
-            qkv_ref[:, columns],
+            out_ref[place, shard] = product[at * rows : (at + 1) * rows].astype(jnp.bfloat16)
+        far = dot_rows(far_low[...], weights[:half, :]) + dot_rows(far_high[...], weights[half:, :])
+        out_ref[jnp.bitwise_and(place_ref[1] + 4, 7), shard] = far.astype(jnp.bfloat16)
+
+
+def third_kernel(place_ref, x_ref, gain_ref, own_ref, other_ref, out_ref, coarse_ref, normed_ref):
+    blocks, places, shards, rows, width = x_ref.shape
+    count = 1.0 / (blocks * shards * width)
+    order = [(z, shard) for shard in range(shards) for z in range(blocks)]
+    for first in range(0, places, 2):
+        tiles = [
+            jnp.concatenate(
+                [x_ref[z, first + at, shard].astype(jnp.float32) for at in range(2)], axis=0
+            )
+            for z, shard in order
+        ]
+        row_mean = jnp.sum(sum(tiles), axis=-1, keepdims=True) * count
+        tiles = [tile - row_mean for tile in tiles]
+        spread = jnp.sum(sum(tile * tile for tile in tiles), axis=-1, keepdims=True)
+        scale = lax.rsqrt(spread * count + 1e-05)
+        for at, tile in enumerate(tiles):
+            here = slice(at * width, (at + 1) * width)
+            normed_ref[first * rows : (first + 2) * rows, here] = (
+                tile * scale * gain_ref[:, here]
+            ).astype(jnp.bfloat16)
+    for at, (z, shard) in enumerate(order):
+        coarse_ref[:, at * width : (at + 1) * width] = x_ref[z, place_ref[1], shard].astype(
+            jnp.float32
+        )
+    token = lax.broadcasted_iota(jnp.int32, (96, 96), 0)
+    other = lax.broadcasted_iota(jnp.int32, (96, 96), 1)
+    keep = jnp.right_shift(token, 5) == jnp.right_shift(other, 5)
+    ring = place_ref[2]
+    for weights, shard in ((own_ref, ring), (other_ref, 1 - ring)):
+        triple = lax.dot_general(
+            normed_ref[...],
+            weights[...],
             (((1,), (1,)), ((), ())),
             preferred_element_type=jnp.float32,
-        )
-        triple = product if triple is None else triple + product
-    triple = triple.astype(jnp.bfloat16)
-    query = (triple[:, :HD] * 0.125).astype(jnp.bfloat16)
-    key = triple[:, HD : 2 * HD]
-    value = triple[:, 2 * HD :]
-    token = lax.broadcasted_iota(jnp.int32, (128, 128), 0)
-    other = lax.broadcasted_iota(jnp.int32, (128, 128), 1)
-    keep = jnp.right_shift(token, 5) == jnp.right_shift(other, 5)
-    mixed = []
-    for group in range(sides * line // 128):
-        mine = slice(group * 128, group * 128 + 128)
-        mixed.append(mix_tokens(query[mine], key[mine], value[mine], keep))
-    mixed = jnp.concatenate(mixed, axis=0)
-    for z in range(blocks):
-        for side in range(sides):
-            start = side * line + z * tokens
-            out_ref[z, side] = mixed[start : start + tokens].astype(jnp.bfloat16)
-
-
-def heads_kernel(heads_ref, late_ref, own_ref, send_ref):
-    total = [None, None]
-    for z in range(heads_ref.shape[0]):
-        left = jnp.concatenate(
-            [heads_ref[z, 0].astype(jnp.float32), heads_ref[z, 1].astype(jnp.float32)], axis=0
         ).astype(jnp.bfloat16)
-        for part in range(2):
-            right = jnp.concatenate(
-                [late_ref[(2 * row + part) * 8 + z, :, 1280:2304] for row in range(4)], axis=0
-            )
-            product = dot_rows(left, right)
-            total[part] = product if z == 0 else total[part] + product
-    count = heads_ref.shape[2]
-    for part in range(2):
-        here = slice(part * 1024, part * 1024 + 1024)
-        own_ref[:, here] = total[part][:count]
-        send_ref[:, here] = total[part][count:].astype(jnp.bfloat16)
+        query = (triple[:, :HD] * 0.125).astype(jnp.bfloat16)
+        key = triple[:, HD : 2 * HD]
+        value = triple[:, 2 * HD :]
+        for group in range(places * rows // 96):
+            mine = slice(group * 96, group * 96 + 96)
+            mixed = mix_tokens(query[mine], key[mine], value[mine], keep)
+            for at in range(96 // rows):
+                out_ref[group * (96 // rows) + at, shard] = mixed[
+                    at * rows : (at + 1) * rows
+                ].astype(jnp.bfloat16)
 
 
 def spread_matrix(lat_count, lon_count):
@@ -268,28 +242,49 @@
 
 
 def up_kernel(
-    core_ref, own_coarse_ref, part_ref, recv_ref, late_ref, swapped_ref,
-    second_ref, skip_ref, out_ref, coarse_ref, lift_ref, level_ref, small_ref,
+    core_ref, heads_ref, own_coarse_ref, late_ref, swapped_ref, second_ref, skip_ref, out_ref,
+    third_ref, lift_ref, level_ref, small_ref,
 ):
     core = core_ref[0]
-    blocks, width = 8, 128
-    for z in range(blocks):
-        for place, origin in ((z, core), (blocks + z, 1 - core)):
-            coarse_ref[origin * blocks + z] = own_coarse_ref[:, place * width : (place + 1) * width]
+    pairs = []
+    for ring in range(2):
+        for z in range(0, 8, 2):
+            pairs.append(
+                jnp.concatenate(
+                    [heads_ref[z, ring].astype(jnp.float32), heads_ref[z + 1, ring].astype(jnp.float32)],
+                    axis=1,
+                ).astype(jnp.bfloat16)
+            )
+    for weights_ref, origin in ((late_ref, core), (swapped_ref, 1 - core)):
+        for part in range(2):
+            total = None
+            for ring in range(2):
+                for z in range(0, 8, 2):
+                    right = jnp.concatenate(
+                        [
+                            weights_ref[
+                                (2 * row + part) * 8 + zz, :, ring * 1152 + 640 : ring * 1152 + 1152
+                            ]
+                            for zz in (z, z + 1)
+                            for row in range(4)
+                        ],
+                        axis=0,
+                    )
+                    product = dot_rows(pairs[ring * 4 + z // 2], right)
+                    total = product if total is None else total + product
+            third_ref[part, origin] = total
     level_three = []
-    for place in range(2 * blocks):
-        here = slice(place * width, place * width + width)
-        level_three.append(
-            (coarse_ref[place] + (part_ref[:, here] + recv_ref[:, here].astype(jnp.float32))).astype(
-                jnp.bfloat16
-            )
-        )
+    for place in range(16):
+        here = slice(place * 128, place * 128 + 128)
+        quarter = place // 4
+        update = third_ref[quarter // 2, quarter % 2][:, place % 4 * 128 : place % 4 * 128 + 128]
+        level_three.append((own_coarse_ref[:, here] + update).astype(jnp.bfloat16))
     for weights_ref, origin in ((late_ref, core), (swapped_ref, 1 - core)):
         total = None
         for ring in range(2):
             for z in range(8):
                 right = jnp.concatenate(
-                    [weights_ref[y * 8 + z, :, ring * 640 : ring * 640 + 512] for y in range(8)],
+                    [weights_ref[y * 8 + z, :, ring * 1152 : ring * 1152 + 512] for y in range(8)],
                     axis=0,
                 )
                 product = dot_rows(level_three[ring * 8 + z], right)
@@ -311,7 +306,7 @@
                         jnp.concatenate(
                             [
                                 weights_ref[
-                                    (2 * row + part) * 8 + zz, :, ring * 640 + 512 : ring * 640 + 640
+                                    (2 * row + part) * 8 + zz, :, ring * 1152 + 512 : ring * 1152 + 640
                                 ]
                                 for zz in (z, z + 1)
                                 for row in range(4)
@@ -355,31 +350,13 @@
     return lax.ppermute(values, "lat", [(i, (i + Z_RING) % count) for i in range(count)])
 
 
-def swap_shards(values):
-    lon_count = lax.axis_size("lon")
-    pairs = []
-    for lat in range(lax.axis_size("lat")):
-        for lon in range(lon_count):
-            ring, place = divmod(lat, Z_RING)
-            target = (lat, lon)
-            if ring != lon % 2:
-                target = ((1 - ring) * Z_RING + place, lon ^ 1)
-            pairs.append((lat * lon_count + lon, target[0] * lon_count + target[1]))
-    return lax.ppermute(values, ("lat", "lon"), pairs)
-
-
 def ring_scatter(blocks):
     return lax.all_to_all(blocks, "lat", 0, 0, axis_index_groups=RINGS, tiled=True)
 
 
-def ring_shift(values, step, flip=0):
-    lon_count = lax.axis_size("lon")
-    pairs = []
-    for lat in range(lax.axis_size("lat")):
-        target = lat // Z_RING * Z_RING + (lat + step) % Z_RING
-        for lon in range(lon_count):
-            pairs.append((lat * lon_count + lon, target * lon_count + (lon ^ flip)))
-    return lax.ppermute(values, ("lat", "lon"), pairs)
+def ring_shift(values, step):
+    pairs = [(at, at // Z_RING * Z_RING + (at + step) % Z_RING) for at in range(2 * Z_RING)]
+    return lax.ppermute(values, "lat", pairs)
 
 
 def ring_gather(values):
@@ -433,7 +410,18 @@
     merge_weights = lax.all_gather(
         both_merge, "lat", axis=1, axis_index_groups=RINGS, tiled=True
     )
-    core_place = jnp.stack([core, lax.axis_index("lat") % Z_RING]).astype(jnp.int32)
+    core_place = jnp.stack([core, lax.axis_index("lat") % Z_RING, ring]).astype(jnp.int32)
+    own_rest = jnp.concatenate(
+        [
+            cut(up_third, column * 16, 16, core * 512, 512),
+            cut(up_second, column // 2 * 16, 16, core * 256 + column % 2 * 128, 128),
+            cut(out_third, column // 2 * 16, 16, column % 2 * 1024 + core * 512, 512),
+        ],
+        axis=1,
+    )
+    other_rest = swap_rings(own_rest)
+    late = in_order(ring, own_rest, other_rest, 1)
+
     picks = (land_ids[:, :, None] == jnp.arange(3, dtype=jnp.int32)).astype(jnp.float32)
     surface = jnp.einsum("ijs,sc->ijc", picks, surface_table.astype(jnp.float32))
     hidden = (
@@ -441,34 +429,17 @@
         + surface[:, None, :, :]
         + level_table.astype(jnp.float32)[None, :, None, :]
     ).astype(jnp.bfloat16)
-    hidden = after(hidden, both_merge)
+    hidden = after(hidden, both_merge, other_rest)
     above, below = neighbours(hidden[:2], hidden[-2:], "lat")
     cells = jnp.concatenate([above, hidden, below], axis=0)
     qkv_third = qkv_third.transpose(0, 2, 1).reshape(-1, qkv_third.shape[1])
 
-    out_third, merge_third, qkv_third, up_third, up_second, cells = lax.optimization_barrier(
-        (out_third, merge_third, qkv_third, up_third, up_second, cells)
-    )
+    merge_third, qkv_third, cells = lax.optimization_barrier((merge_third, qkv_third, cells))
     left, right = neighbours(cells[:, :, :2], cells[:, :, -2:], "lon")
-    own_rest = jnp.concatenate(
-        [
-            cut(up_third, column * 16, 16, core * 512, 512),
-            cut(up_second, column // 2 * 16, 16, core * 256 + column % 2 * 128, 128),
-        ],
-        axis=1,
-    )[None]
-    both_rest = in_order(ring, own_rest, swap_rings(own_rest), 0)
-    out_third = swap_shards(out_third)
-    merge_third = swap_shards(merge_third)
-    qkv_third = swap_shards(qkv_third)
-    late = jnp.concatenate(
-        [
-            both_rest[0],
-            both_rest[1],
-            cut(out_third, column // 2 * 16, 16, column % 2 * 1024, 1024),
-        ],
-        axis=1,
-    )
+    merge_other = swap_rings(merge_third)
+    qkv_other = swap_rings(qkv_third)
+    late, left = lax.optimization_barrier((late, left))
+    late_rows = ring_gather(late)
 
     ext_rows = tile_rows + 4
     own_window = (jnp.arange(32 * 4) % tile_cols + 2) // 4
@@ -496,9 +467,7 @@
         ),
         flops=2 * 640 * 512 * 1536,
     )
-    late = after(late, attended)
-    late_rows = ring_gather(late)
-    attended = after(attended, late, merge_third, qkv_third)
+    attended = after(attended, merge_other, late_rows)
     tokens = attended.shape[0]
     skip_first, merged_in = call_kernel(
         skip_kernel,
@@ -514,7 +483,7 @@
     second_half, second_send = call_kernel(
         merge_kernel,
         (half_shape, half_shape),
-        (merged_in, swap_cores(merged_in), merge_weights),
+        (merged_in, after(swap_cores(merged_in), qkv_other), merge_weights),
         flops=2 * 192 * 2048 * 512,
     )
     second_cells, coarse_in = call_kernel(
@@ -527,85 +496,59 @@
         (pltpu.VMEM((2, own_rows, 512), jnp.bfloat16),),
         flops=2 * 96 * 96 * 1024,
     )
-    late_rows = after(late_rows, coarse_in)
     late = lax.all_gather(
-        late_rows,
+        after(late_rows, coarse_in),
         "lon",
         axis=0,
         axis_index_groups=[[4 * y + x for y in range(8)] for x in range(4)],
         tiled=True,
-    )
+    ).reshape(64, 16, -1)
 
     own_count = coarse_in.shape[0]
-    line = Z_RING * own_count
 
     pieces, forth, back = [coarse_in], coarse_in, coarse_in
     for _ in range(3):
         forth, back = ring_shift(forth, 1), ring_shift(back, -1)
         pieces += [forth, back]
-    near = jnp.stack(pieces)
-    far, far_other = ring_shift(forth, 1), ring_shift(back, -1, 1)
+    half_feats = coarse_in.shape[1] // 2
+    pieces += [ring_shift(forth[:, :half_feats], 1), ring_shift(back[:, half_feats:], -1)]
     column_block = call_kernel(
         columns_kernel,
-        jax.ShapeDtypeStruct((2, Z_RING, own_count, 128), jnp.bfloat16),
-        (core_place, near, far, swap_cores(near), far_other, merge_third),
-        flops=2 * 384 * 4096 * 128,
-    ).reshape(2, line, 128)
-    own_columns = ring_gather(column_block)
-    other_columns = swap_cores(own_columns)
-    blocks, _, _, width = own_columns.shape
-    head_feats = HD
+        jax.ShapeDtypeStruct((Z_RING, 2, own_count, 128), jnp.bfloat16),
+        (core_place, *pieces, merge_third, merge_other),
+        flops=2 * 192 * 4096 * 256,
+    )
     heads_out, own_coarse = call_kernel(
         third_kernel,
         (
-            jax.ShapeDtypeStruct((Z_RING, 2, own_count, head_feats), jnp.bfloat16),
-            jax.ShapeDtypeStruct((own_count, 2 * blocks * width), jnp.float32),
-        ),
-        (
-            core_place,
-            own_columns,
-            other_columns,
-            norm_third.reshape(2 * blocks, 1, width),
-            qkv_third,
-        ),
-        (
-            pltpu.VMEM((2 * line, 2 * blocks * width), jnp.bfloat16),
-            pltpu.VMEM((line, 2 * blocks * width), jnp.float32),
-        ),
-        flops=2 * 384 * 2048 * 192,
-    )
-
-    chip_heads = ring_scatter(heads_out)
-    own_part, send_part = call_kernel(
-        heads_kernel,
-        (
+            jax.ShapeDtypeStruct((Z_RING, 2, own_count, HD), jnp.bfloat16),
             jax.ShapeDtypeStruct((own_count, 2048), jnp.float32),
-            jax.ShapeDtypeStruct((own_count, 2048), jnp.bfloat16),
-        ),
-        (chip_heads, late),
-        flops=2 * 48 * 512 * 2048,
-    )
+        ),
+        (core_place, ring_gather(column_block), norm_third[None], qkv_third, qkv_other),
+        (pltpu.VMEM((Z_RING * own_count, 2048), jnp.bfloat16),),
+        flops=2 * 192 * 2048 * 384,
+    )
+
     late_swapped = swap_cores(after(late, heads_out))
     decoded = call_kernel(
         up_kernel,
         jax.ShapeDtypeStruct((tile_rows * levels * tile_cols, feat_dim), jnp.bfloat16),
         (
             core_place,
+            ring_scatter(heads_out),
             own_coarse,
-            own_part,
-            swap_cores(send_part),
             late,
             late_swapped,
             second_cells,
             skip_first,
         ),
         (
-            pltpu.VMEM((2 * blocks, own_count, width), jnp.float32),
+            pltpu.VMEM((2, 2, own_count, 512), jnp.float32),
             pltpu.VMEM((2, own_count, 512), jnp.float32),
             pltpu.VMEM((second_cells.shape[0], 1024), jnp.bfloat16),
             pltpu.VMEM((2, second_cells.shape[0], 256), jnp.float32),
         ),
-        flops=2 * (24 * 2048 * 1024 + 96 * 1024 * 512),
+        flops=2 * (24 * 1024 * 2048 + 24 * 2048 * 1024 + 96 * 1024 * 512),
     )
     return decoded.reshape(fields.shape)
 

time: 216 us -> 221 us (1.023)
  waiting for transfers between devices: 31.1 us -> 41.4 us
  blocking collectives: 39 us -> 30.6 us
  local copies, waits for them, and re-layouts: 16.7 us -> 19.6 us
  starting transfers between devices: 92.6 us -> 90.1 us
    ppermute x2, waiting for transfers between devices: 0.32 us -> 26.6 us  [neighbours(): lax.ppermute(first, axis, [((i + 1) % count, i) for i in range(count)])]
    ppermute x11 -> x8, starting transfers between devices: 38.3 us -> 29.6 us  [ring_shift(): return lax.ppermute(values, 'lat', pairs)]
    ppermute x2 -> x4, starting transfers between devices: 7.39 us -> 16.1 us  [swap_rings(): lax.ppermute(values, 'lat', [(i, (i + Z_RING) % count) for i in range(cou...]
    ppermute x2, waiting for transfers between devices: 8.54 us -> 0.01 us  [neighbours(): lax.ppermute(last, axis, [(i, (i + 1) % count) for i in range(count)])]
    all_to_all x2, blocking collectives: 39 us -> 30.6 us  [ring_scatter(): lax.all_to_all(blocks, 'lat', 0, 0, axis_index_groups=RINGS, tiled=True)]
    ppermute x6 -> x3, starting transfers between devices: 17.7 us -> 11.6 us  [swap_cores(): return lax.ppermute(values, 'lon', [(i, i ^ 1) for i in range(count)])]
    all_to_all x1, waiting for transfers between devices: 6.12 us -> 0.01 us  [ring_scatter(): lax.all_to_all(blocks, 'lat', 0, 0, axis_index_groups=RINGS, tiled=True)]
    ppermute x2, starting transfers between devices: 7.03 us -> 11 us  [neighbours(): lax.ppermute(last, axis, [(i, (i + 1) % count) for i in range(count)])]
  transfers between devices with their start and end apart: 26 -> 22, of which waited for: 13 -> 9; matrix products, arithmetic and copies ran while one was open for 3% -> 4% of each run, Pallas kernels for 5% -> 5%
where the time goes in v4:
time: 221 us; the launch traced here: 219 us
  starting transfers between devices  90.1 us (41%)
  waiting for transfers between devices  41.4 us (19%)
  blocking collectives  30.6 us (14%)
  local copies, waits for them, and re-layouts  19.6 us (9%)
  Pallas kernels  18.8 us (9%)
  between operations  14 us (6%)
  other arithmetic  3.75 us (2%)
    all_to_all x2, blocking collectives, ring_scatter(): lax.all_to_all(blocks, 'lat', 0, 0, axis_index_groups=RINGS, tiled=True)  30.6 us
    ppermute x8, starting transfers between devices, ring_shift(): return lax.ppermute(values, 'lat', pairs)  29.6 us
    ppermute x2, waiting for transfers between devices, neighbours(): lax.ppermute(first, axis, [((i + 1) % count, i) for i in range(count)])  26.6 us
    pallas_call x7, Pallas kernels, call_kernel(): pl.pallas_call(body, out_shape=out_shape, in_specs=[pl.BlockSpec(memory_s...  18.8 us
    ppermute x4, starting transfers between devices, swap_rings(): lax.ppermute(values, 'lat', [(i, (i + Z_RING) % count) for i in range(cou...  16.1 us
    ppermute x2, starting transfers between devices, neighbours(): lax.ppermute(first, axis, [((i + 1) % count, i) for i in range(count)])  15.4 us
    unnamed x40, local copies, waits for them, and re-layouts  13.6 us
    ppermute x3, starting transfers between devices, swap_cores(): return lax.ppermute(values, 'lon', [(i, i ^ 1) for i in range(count)])  11.6 us
  transfers between devices with their start and end apart: 22, of which 9 were waited for; matrix products, arithmetic and copies ran while one was open for 4% of the time, Pallas kernels for 5%

profile of v4, /device:TPU:1, one launch (start us, length us, event | category | flops | bytes accessed | tf_op | source)
XLA Modules:
  0.0 219.2 jit_solution(9400647055911117279)
XLA Ops:
  8.3 5.5 %collective-permute-start = (bf16[1,160,512]{2,1,0:T(8,128)(2,1)S(1)}, bf16[1,160,512]{2,1,0:T(8,128)(2,1)S(1)}, u32[]{:S(2)}, u32[]{:S(2)}) collective-permute-start(bf16[1,160,512]{2,1,0:T(8,128)(2,1)S(1)} %maximum_bitcast_fusion), channel_id=1, source_target_pairs={{0,256},{32,288},{64,320},{96,352},{128,384},{160,416},{192,448},{... | collective-permute-start | bytes 491528 | tf_op jit(solution)/shard_map/ppermute | solution.py:350
  13.8 2.7 %collective-permute-done = bf16[1,160,512]{2,1,0:T(8,128)(2,1)S(1)} collective-permute-done((bf16[1,160,512]{2,1,0:T(8,128)(2,1)S(1)}, bf16[1,160,512]{2,1,0:T(8,128)(2,1)S(1)}, u32[]{:S(2)}, u32[]{:S(2)}) %collective-permute-start) | collective-permute-done | bytes 163872 | tf_op jit(solution)/shard_map/ppermute | solution.py:350
  19.4 4.9 %collective-permute-start.1 = (bf16[16,1152]{1,0:T(8,128)(2,1)S(1)}, bf16[16,1152]{1,0:T(8,128)(2,1)S(1)}, u32[]{:S(2)}, u32[]{:S(2)}) collective-permute-start(bf16[16,1152]{1,0:T(8,128)(2,1)S(1)} %pad_maximum_fusion.1), channel_id=1, source_target_pairs={{0,256},{32,288},{64,320},{96,352},{128,384},{160,416},{192,448},{... | collective-permute-start | bytes 110600 | tf_op jit(solution)/shard_map/ppermute | solution.py:350
  27.1 4.9 %collective-permute-start.2 = (bf16[2,2,16,512]{3,2,1,0:T(8,128)(2,1)S(1)}, bf16[2,2,16,512]{3,2,1,0:T(8,128)(2,1)S(1)}, u32[]{:S(2)}, u32[]{:S(2)}) collective-permute-start(bf16[2,2,16,512]{3,2,1,0:T(8,128)(2,1)S(1)} %get-tuple-element.43), channel_id=1, source_target_pairs={{0,32},{32,64},{64,96},{96,128},{128,160},{160,192},{192,224},{224... | collective-permute-start | bytes 196616 | tf_op jit(solution)/shard_map/ppermute | solution.py:338
  32.0 9.8 %collective-permute-start.3 = (bf16[2,2,16,512]{3,2,1,0:T(8,128)(2,1)S(1)}, bf16[2,2,16,512]{3,2,1,0:T(8,128)(2,1)S(1)}, u32[]{:S(2)}, u32[]{:S(2)}) collective-permute-start(bf16[2,2,16,512]{3,2,1,0:T(8,128)(2,1)S(1)} %get-tuple-element.44), channel_id=1, source_target_pairs={{32,0},{64,32},{96,64},{128,96},{160,128},{192,160},{224,192},{256... | collective-permute-start | bytes 196616 | tf_op jit(solution)/shard_map/ppermute | solution.py:339
  43.9 6.1 %collective-permute-start.4 = (bf16[16,2,2,512]{3,2,1,0:T(2,128)(2,1)S(1)}, bf16[16,2,2,512]{3,2,1,0:T(2,128)(2,1)S(1)}, u32[]{:S(2)}, u32[]{:S(2)}) collective-permute-start(bf16[16,2,2,512]{3,2,1,0:T(2,128)(2,1)S(1)} %get-tuple-element.42), channel_id=1, source_target_pairs={{0,1},{1,2},{2,3},{3,4},{4,5},{5,6},{6,7},{7,8},{8,9},{9,10},{10,1... | collective-permute-start | bytes 196616 | tf_op jit(solution)/shard_map/ppermute | solution.py:338
  50.1 3.5 %collective-permute-start.6 = (bf16[4096,128]{1,0:T(8,128)(2,1)S(1)}, bf16[4096,128]{1,0:T(8,128)(2,1)S(1)}, u32[]{:S(2)}, u32[]{:S(2)}) collective-permute-start(bf16[4096,128]{1,0:T(8,128)(2,1)S(1)} %copy-done.4), channel_id=1, source_target_pairs={{0,256},{32,288},{64,320},{96,352},{128,384},{160,416},{192,448},{... | collective-permute-start | bytes 3145736 | tf_op jit(solution)/shard_map/ppermute | solution.py:350
  54.5 6.4 %all-to-all-start = ((bf16[8,16,2304]{2,1,0:T(8,128)(2,1)}), bf16[8,16,2304]{2,1,0:T(8,128)(2,1)}, u32[]{:S(2)}, u32[]{:S(2)}) async-start(bf16[8,16,2304]{2,1,0:T(8,128)(2,1)} %broadcast_in_dim.50), calls=%async_computation | async-start | bytes 1179648 | tf_op jit(solution)/shard_map/all_to_all | solution.py:354
  61.3 2.3 %collective-permute-start.8 = (bf16[192,2048]{1,0:T(8,128)(2,1)}, bf16[192,2048]{1,0:T(8,128)(2,1)}, u32[]{:S(2)}, u32[]{:S(2)}) collective-permute-start(bf16[192,2048]{1,0:T(8,128)(2,1)} %bitcast.20), channel_id=1, source_target_pairs={{0,256},{32,288},{64,320},{96,352},{128,384},{160,416},{192,448},{... | collective-permute-start | bytes 2359304 | tf_op jit(solution)/shard_map/ppermute | solution.py:350
  63.7 5.6 %collective-permute-start.5 = (bf16[16,2,2,512]{3,2,1,0:T(2,128)(2,1)}, bf16[16,2,2,512]{3,2,1,0:T(2,128)(2,1)}, u32[]{:S(2)}, u32[]{:S(2)}) collective-permute-start(bf16[16,2,2,512]{3,2,1,0:T(2,128)(2,1)} %get-tuple-element.41), channel_id=1, source_target_pairs={{1,0},{2,1},{3,2},{4,3},{5,4},{6,5},{7,6},{8,7},{9,8},{10,9},{11,1... | collective-permute-start | bytes 196616 | tf_op jit(solution)/shard_map/ppermute | solution.py:339
  70.3 25.3 %collective-permute-done.5 = bf16[16,2,2,512]{3,2,1,0:T(2,128)(2,1)} collective-permute-done((bf16[16,2,2,512]{3,2,1,0:T(2,128)(2,1)}, bf16[16,2,2,512]{3,2,1,0:T(2,128)(2,1)}, u32[]{:S(2)}, u32[]{:S(2)}) %collective-permute-start.5) | collective-permute-done | bytes 65568 | tf_op jit(solution)/shard_map/ppermute | solution.py:339
  98.9 3.2 %shard_map.154.attended_ref = bf16[384,512]{1,0:T(8,128)(2,1)S(1)} custom-call(bf16[512,512]{1,0:T(8,128)(2,1)S(1)} %bitcast.19, bf16[64,512]{1,0:T(8,128)(2,1)S(1)} %reshape.66.left_ref, bf16[64,512]{1,0:T(8,128)(2,1)S(1)} %reshape.67.right_ref, f32[1,512]{1,0:T(1,128)S(1)} %bitcast.25, bf16[3,512,512]{2,1,0:T(8,128)(2,1)S(1)} %copy-done.17, ...), custom_call_target="tpu_custom_call" | custom-call | flops 1006632960 | bytes 2314752 | tf_op jit(solution)/shard_map/pallas_call | solution.py:20
  119.1 5.7 %collective-permute-start.11 = (bf16[24,4096]{1,0:T(8,128)(2,1)S(1)}, bf16[24,4096]{1,0:T(8,128)(2,1)S(1)}, u32[]{:S(2)}, u32[]{:S(2)}) collective-permute-start(bf16[24,4096]{1,0:T(8,128)(2,1)S(1)} %get-tuple-element.34.refs_0_), channel_id=1, source_target_pairs={{0,224},{32,0},{64,32},{96,64},{128,96},{160,128},{192,160},{224,1... | collective-permute-start | bytes 589832 | tf_op jit(solution)/shard_map/ppermute | solution.py:359
  126.8 2.2 %collective-permute-done.11.refs_2_ = bf16[24,4096]{1,0:T(8,128)(2,1)S(1)} collective-permute-done((bf16[24,4096]{1,0:T(8,128)(2,1)S(1)}, bf16[24,4096]{1,0:T(8,128)(2,1)S(1)}, u32[]{:S(2)}, u32[]{:S(2)}) %collective-permute-start.11) | collective-permute-done | bytes 196640 | tf_op jit(solution)/shard_map/ppermute | solution.py:359
  129.0 5.3 %collective-permute-start.13 = (bf16[24,4096]{1,0:T(8,128)(2,1)S(1)}, bf16[24,4096]{1,0:T(8,128)(2,1)S(1)}, u32[]{:S(2)}, u32[]{:S(2)}) collective-permute-start(bf16[24,4096]{1,0:T(8,128)(2,1)S(1)} %collective-permute-done.11.refs_2_), channel_id=1, source_target_pairs={{0,224},{32,0},{64,32},{96,64},{128,96},{160,128},{192,160},{224,1... | collective-permute-start | bytes 589832 | tf_op jit(solution)/shard_map/ppermute | solution.py:359
  137.6 5.4 %collective-permute-start.15 = (bf16[24,4096]{1,0:T(8,128)(2,1)S(1)}, bf16[24,4096]{1,0:T(8,128)(2,1)S(1)}, u32[]{:S(2)}, u32[]{:S(2)}) collective-permute-start(bf16[24,4096]{1,0:T(8,128)(2,1)S(1)} %collective-permute-done.13.refs_4_), channel_id=1, source_target_pairs={{0,224},{32,0},{64,32},{96,64},{128,96},{160,128},{192,160},{224,1... | collective-permute-start | bytes 589832 | tf_op jit(solution)/shard_map/ppermute | solution.py:359
  145.6 5.4 %collective-permute-start.17 = (bf16[24,2048]{1,0:T(8,128)(2,1)S(1)}, bf16[24,2048]{1,0:T(8,128)(2,1)S(1)}, u32[]{:S(2)}, u32[]{:S(2)}) collective-permute-start(bf16[24,2048]{1,0:T(8,128)(2,1)S(1)} %slice.25), channel_id=1, source_target_pairs={{0,224},{32,0},{64,32},{96,64},{128,96},{160,128},{192,160},{224,1... | collective-permute-start | bytes 294920 | tf_op jit(solution)/shard_map/ppermute | solution.py:359
  153.0 5.0 %collective-permute-done.16.refs_7_ = bf16[24,2048]{1,0:T(8,128)(2,1)S(1)} collective-permute-done((bf16[24,2048]{1,0:T(8,128)(2,1)S(1)}, bf16[24,2048]{1,0:T(8,128)(2,1)S(1)}, u32[]{:S(2)}, u32[]{:S(2)}) %collective-permute-start.16) | collective-permute-done | bytes 98336 | tf_op jit(solution)/shard_map/ppermute | solution.py:359
  162.3 21.3 %all_to_all.15.x_ref = bf16[8,8,2,24,128]{4,3,2,1,0:T(8,128)(2,1)S(1)} all-to-all(bf16[8,8,2,24,128]{4,3,2,1,0:T(8,128)(2,1)S(1)} %broadcast_in_dim.53), channel_id=1, replica_groups={{0,32,64,96,128,160,192,224},{256,288,320,352,384,416,448,480},{1,33,65..., dimensions={0} | all-to-all | bytes 1572864 | tf_op jit(solution)/shard_map/all_to_all | solution.py:354
  183.6 3.8 %shard_map.159 = (bf16[8,2,24,64]{3,2,1,0:T(8,128)(2,1)S(1)}, f32[24,2048]{1,0:T(8,128)S(1)}) custom-call(s32[3]{0:T(128)S(1)} %pad_add_fusion.1.core_ref.place_ref, bf16[8,8,2,24,128]{4,3,2,1,0:T(8,128)(2,1)S(1)} %all_to_all.15.x_ref, f32[1,2048]{1,0:T(1,128)S(1)} %bitcast.24, bf16[192,2048]{1,0:T(8,128)(2,1)S(1)} %bitcast.21, ...), custom_call_target="tpu_custom_call" | custom-call | flops 301989888 | bytes 2367500 | tf_op jit(solution)/shard_map/pallas_call | solution.py:20
  187.4 7.5 %collective-permute-start.18 = (bf16[64,16,2304]{2,1,0:T(8,128)(2,1)}, bf16[64,16,2304]{2,1,0:T(8,128)(2,1)}, u32[]{:S(2)}, u32[]{:S(2)}) collective-permute-start(bf16[64,16,2304]{2,1,0:T(8,128)(2,1)} %all-gather.5.cloned.1.call-done.late_ref), channel_id=1, source_target_pairs={{0,1},{1,0},{2,3},{3,2},{4,5},{5,4},{6,7},{7,6},{8,9},{9,8},{10,11... | collective-permute-start | bytes 14155784 | tf_op jit(solution)/shard_map/ppermute | solution.py:345
  195.0 9.4 %all_to_all.16 = bf16[8,2,1536]{2,1,0:T(2,128)(2,1)S(1)} all-to-all(bf16[8,2,1536]{2,1,0:T(2,128)(2,1)S(1)} %reshape.71), channel_id=1, replica_groups={{0,32,64,96,128,160,192,224},{256,288,320,352,384,416,448,480},{1,33,65..., dimensions={0} | all-to-all | bytes 98304 | tf_op jit(solution)/shard_map/all_to_all | solution.py:354
  204.5 2.3 %copy-done.3 = bf16[64,16,2304]{2,1,0:T(8,128)(2,1)S(1)} copy-done((bf16[64,16,2304]{2,1,0:T(8,128)(2,1)S(1)}, bf16[64,16,2304]{2,1,0:T(8,128)(2,1)}, u32[]{:S(2)}) %copy-start.3) | copy-done | bytes 4718616
  206.9 5.5 %shard_map.160 = bf16[384,512]{1,0:T(8,128)(2,1)} custom-call(s32[3]{0:T(128)S(1)} %pad_add_fusion.1.core_ref.place_ref, bf16[8,2,24,64]{3,2,1,0:T(8,128)(2,1)S(1)} %reshape.72.heads_ref, f32[24,2048]{1,0:T(8,128)S(1)} %get-tuple-element.36.own_coarse_ref, bf16[64,16,2304]{2,1,0:T(8,128)(2,1)S(1)} %copy-done.3, ...), custom_call_target="tpu_custom_call" | custom-call | flops 301989888 | bytes 10272780 | tf_op jit(solution)/shard_map/pallas_call | solution.py:20
  (104 shorter events, 46.3 us)
Async XLA Ops:
  6.5 90.0 %copy-start.18 = (f32[512]{0:T(512)S(1)}, f32[512]{0:T(512)}, u32[]{:S(2)}) copy-start(f32[512]{0:T(512)} %param.20) | copy-start | bytes 6148
  6.5 97.3 %all-gather.3.cloned.1.call-start = ((), (), s32[]{:S(2)}) async-start(), calls=%async_computation.3 | async-start | bytes 2949120 | tf_op jit(solution)/shard_map/all_gather | solution.py:410
  8.3 8.2 %collective-permute-start = (bf16[1,160,512]{2,1,0:T(8,128)(2,1)S(1)}, bf16[1,160,512]{2,1,0:T(8,128)(2,1)S(1)}, u32[]{:S(2)}, u32[]{:S(2)}) collective-permute-start(bf16[1,160,512]{2,1,0:T(8,128)(2,1)S(1)} %maximum_bitcast_fusion), channel_id=1, source_target_pairs={{0,256},{32,288},{64,320},{96,352},{128,384},{160,416},{192,448},{... | collective-permute-start | bytes 491528 | tf_op jit(solution)/shard_map/ppermute | solution.py:350
  19.4 7.7 %collective-permute-start.1 = (bf16[16,1152]{1,0:T(8,128)(2,1)S(1)}, bf16[16,1152]{1,0:T(8,128)(2,1)S(1)}, u32[]{:S(2)}, u32[]{:S(2)}) collective-permute-start(bf16[16,1152]{1,0:T(8,128)(2,1)S(1)} %pad_maximum_fusion.1), channel_id=1, source_target_pairs={{0,256},{32,288},{64,320},{96,352},{128,384},{160,416},{192,448},{... | collective-permute-start | bytes 110600 | tf_op jit(solution)/shard_map/ppermute | solution.py:350
  27.1 14.7 %collective-permute-start.2 = (bf16[2,2,16,512]{3,2,1,0:T(8,128)(2,1)S(1)}, bf16[2,2,16,512]{3,2,1,0:T(8,128)(2,1)S(1)}, u32[]{:S(2)}, u32[]{:S(2)}) collective-permute-start(bf16[2,2,16,512]{3,2,1,0:T(8,128)(2,1)S(1)} %get-tuple-element.43), channel_id=1, source_target_pairs={{0,32},{32,64},{64,96},{96,128},{128,160},{160,192},{192,224},{224... | collective-permute-start | bytes 196616 | tf_op jit(solution)/shard_map/ppermute | solution.py:338
  32.0 11.1 %collective-permute-start.3 = (bf16[2,2,16,512]{3,2,1,0:T(8,128)(2,1)S(1)}, bf16[2,2,16,512]{3,2,1,0:T(8,128)(2,1)S(1)}, u32[]{:S(2)}, u32[]{:S(2)}) collective-permute-start(bf16[2,2,16,512]{3,2,1,0:T(8,128)(2,1)S(1)} %get-tuple-element.44), channel_id=1, source_target_pairs={{32,0},{64,32},{96,64},{128,96},{160,128},{192,160},{224,192},{256... | collective-permute-start | bytes 196616 | tf_op jit(solution)/shard_map/ppermute | solution.py:339
  43.9 9.7 %collective-permute-start.4 = (bf16[16,2,2,512]{3,2,1,0:T(2,128)(2,1)S(1)}, bf16[16,2,2,512]{3,2,1,0:T(2,128)(2,1)S(1)}, u32[]{:S(2)}, u32[]{:S(2)}) collective-permute-start(bf16[16,2,2,512]{3,2,1,0:T(2,128)(2,1)S(1)} %get-tuple-element.42), channel_id=1, source_target_pairs={{0,1},{1,2},{2,3},{3,4},{4,5},{5,6},{6,7},{7,8},{8,9},{9,10},{10,1... | collective-permute-start | bytes 196616 | tf_op jit(solution)/shard_map/ppermute | solution.py:338
  50.1 52.8 %collective-permute-start.6 = (bf16[4096,128]{1,0:T(8,128)(2,1)S(1)}, bf16[4096,128]{1,0:T(8,128)(2,1)S(1)}, u32[]{:S(2)}, u32[]{:S(2)}) collective-permute-start(bf16[4096,128]{1,0:T(8,128)(2,1)S(1)} %copy-done.4), channel_id=1, source_target_pairs={{0,256},{32,288},{64,320},{96,352},{128,384},{160,416},{192,448},{... | collective-permute-start | bytes 3145736 | tf_op jit(solution)/shard_map/ppermute | solution.py:350
  54.5 49.4 %all-to-all-start = ((bf16[8,16,2304]{2,1,0:T(8,128)(2,1)}), bf16[8,16,2304]{2,1,0:T(8,128)(2,1)}, u32[]{:S(2)}, u32[]{:S(2)}) async-start(bf16[8,16,2304]{2,1,0:T(8,128)(2,1)} %broadcast_in_dim.50), calls=%async_computation | async-start | bytes 1179648 | tf_op jit(solution)/shard_map/all_to_all | solution.py:354
  60.9 126.6 %all-gather.5.cloned.1.call-start = ((), (), s32[]{:S(2)}) async-start(), calls=%async_computation.4 | async-start | bytes 5308416 | tf_op jit(solution)/shard_map/all_gather | solution.py:499
  61.3 49.9 %collective-permute-start.8 = (bf16[192,2048]{1,0:T(8,128)(2,1)}, bf16[192,2048]{1,0:T(8,128)(2,1)}, u32[]{:S(2)}, u32[]{:S(2)}) collective-permute-start(bf16[192,2048]{1,0:T(8,128)(2,1)} %bitcast.20), channel_id=1, source_target_pairs={{0,256},{32,288},{64,320},{96,352},{128,384},{160,416},{192,448},{... | collective-permute-start | bytes 2359304 | tf_op jit(solution)/shard_map/ppermute | solution.py:350
  63.7 31.9 %collective-permute-start.5 = (bf16[16,2,2,512]{3,2,1,0:T(2,128)(2,1)}, bf16[16,2,2,512]{3,2,1,0:T(2,128)(2,1)}, u32[]{:S(2)}, u32[]{:S(2)}) collective-permute-start(bf16[16,2,2,512]{3,2,1,0:T(2,128)(2,1)} %get-tuple-element.41), channel_id=1, source_target_pairs={{1,0},{2,1},{3,2},{4,3},{5,4},{6,5},{7,6},{8,7},{9,8},{10,9},{11,1... | collective-permute-start | bytes 196616 | tf_op jit(solution)/shard_map/ppermute | solution.py:339
  109.3 3.8 %collective-permute-start.7 = (bf16[96,2048]{1,0:T(8,128)(2,1)}, bf16[96,2048]{1,0:T(8,128)(2,1)S(1)}, u32[]{:S(2)}, u32[]{:S(2)}) collective-permute-start(bf16[96,2048]{1,0:T(8,128)(2,1)} %get-tuple-element.29.own_ref), channel_id=1, source_target_pairs={{0,1},{1,0},{2,3},{3,2},{4,5},{5,4},{6,7},{7,6},{8,9},{9,8},{10,11... | collective-permute-start | bytes 1179656 | tf_op jit(solution)/shard_map/ppermute | solution.py:345
  114.7 3.3 %collective-permute-start.9 = (bf16[96,512]{1,0:T(8,128)(2,1)S(1)}, bf16[96,512]{1,0:T(8,128)(2,1)S(1)}, u32[]{:S(2)}, u32[]{:S(2)}) collective-permute-start(bf16[96,512]{1,0:T(8,128)(2,1)S(1)} %get-tuple-element.33), channel_id=1, source_target_pairs={{0,1},{1,0},{2,3},{3,2},{4,5},{5,4},{6,7},{7,6},{8,9},{9,8},{10,11... | collective-permute-start | bytes 294920 | tf_op jit(solution)/shard_map/ppermute | solution.py:345
  119.1 85.4 %copy-start.10 = (bf16[384,512]{1,0:T(8,128)(2,1)S(1)}, bf16[384,512]{1,0:T(8,128)(2,1)}, u32[]{:S(2)}) copy-start(bf16[384,512]{1,0:T(8,128)(2,1)} %copy-done.9) | copy-start | bytes 1179652
  119.1 9.9 %collective-permute-start.11 = (bf16[24,4096]{1,0:T(8,128)(2,1)S(1)}, bf16[24,4096]{1,0:T(8,128)(2,1)S(1)}, u32[]{:S(2)}, u32[]{:S(2)}) collective-permute-start(bf16[24,4096]{1,0:T(8,128)(2,1)S(1)} %get-tuple-element.34.refs_0_), channel_id=1, source_target_pairs={{0,224},{32,0},{64,32},{96,64},{128,96},{160,128},{192,160},{224,1... | collective-permute-start | bytes 589832 | tf_op jit(solution)/shard_map/ppermute | solution.py:359
  124.9 9.5 %collective-permute-start.10 = (bf16[24,4096]{1,0:T(8,128)(2,1)S(1)}, bf16[24,4096]{1,0:T(8,128)(2,1)S(1)}, u32[]{:S(2)}, u32[]{:S(2)}) collective-permute-start(bf16[24,4096]{1,0:T(8,128)(2,1)S(1)} %get-tuple-element.34.refs_0_), channel_id=1, source_target_pairs={{0,32},{32,64},{64,96},{96,128},{128,160},{160,192},{192,224},{224... | collective-permute-start | bytes 589832 | tf_op jit(solution)/shard_map/ppermute | solution.py:359
  129.0 8.5 %collective-permute-start.13 = (bf16[24,4096]{1,0:T(8,128)(2,1)S(1)}, bf16[24,4096]{1,0:T(8,128)(2,1)S(1)}, u32[]{:S(2)}, u32[]{:S(2)}) collective-permute-start(bf16[24,4096]{1,0:T(8,128)(2,1)S(1)} %collective-permute-done.11.refs_2_), channel_id=1, source_target_pairs={{0,224},{32,0},{64,32},{96,64},{128,96},{160,128},{192,160},{224,1... | collective-permute-start | bytes 589832 | tf_op jit(solution)/shard_map/ppermute | solution.py:359
  134.3 8.6 %collective-permute-start.12 = (bf16[24,4096]{1,0:T(8,128)(2,1)S(1)}, bf16[24,4096]{1,0:T(8,128)(2,1)S(1)}, u32[]{:S(2)}, u32[]{:S(2)}) collective-permute-start(bf16[24,4096]{1,0:T(8,128)(2,1)S(1)} %collective-permute-done.10.refs_1_), channel_id=1, source_target_pairs={{0,32},{32,64},{64,96},{96,128},{128,160},{160,192},{192,224},{224... | collective-permute-start | bytes 589832 | tf_op jit(solution)/shard_map/ppermute | solution.py:359
  137.6 8.0 %collective-permute-start.15 = (bf16[24,4096]{1,0:T(8,128)(2,1)S(1)}, bf16[24,4096]{1,0:T(8,128)(2,1)S(1)}, u32[]{:S(2)}, u32[]{:S(2)}) collective-permute-start(bf16[24,4096]{1,0:T(8,128)(2,1)S(1)} %collective-permute-done.13.refs_4_), channel_id=1, source_target_pairs={{0,224},{32,0},{64,32},{96,64},{128,96},{160,128},{192,160},{224,1... | collective-permute-start | bytes 589832 | tf_op jit(solution)/shard_map/ppermute | solution.py:359
  143.0 8.0 %collective-permute-start.14 = (bf16[24,4096]{1,0:T(8,128)(2,1)S(1)}, bf16[24,4096]{1,0:T(8,128)(2,1)S(1)}, u32[]{:S(2)}, u32[]{:S(2)}) collective-permute-start(bf16[24,4096]{1,0:T(8,128)(2,1)S(1)} %collective-permute-done.12.refs_3_), channel_id=1, source_target_pairs={{0,32},{32,64},{64,96},{96,128},{128,160},{160,192},{192,224},{224... | collective-permute-start | bytes 589832 | tf_op jit(solution)/shard_map/ppermute | solution.py:359
  145.6 7.4 %collective-permute-start.17 = (bf16[24,2048]{1,0:T(8,128)(2,1)S(1)}, bf16[24,2048]{1,0:T(8,128)(2,1)S(1)}, u32[]{:S(2)}, u32[]{:S(2)}) collective-permute-start(bf16[24,2048]{1,0:T(8,128)(2,1)S(1)} %slice.25), channel_id=1, source_target_pairs={{0,224},{32,0},{64,32},{96,64},{128,96},{160,128},{192,160},{224,1... | collective-permute-start | bytes 294920 | tf_op jit(solution)/shard_map/ppermute | solution.py:359
  151.0 7.0 %collective-permute-start.16 = (bf16[24,2048]{1,0:T(8,128)(2,1)S(1)}, bf16[24,2048]{1,0:T(8,128)(2,1)S(1)}, u32[]{:S(2)}, u32[]{:S(2)}) collective-permute-start(bf16[24,2048]{1,0:T(8,128)(2,1)S(1)} %slice.24), channel_id=1, source_target_pairs={{0,32},{32,64},{64,96},{96,128},{128,160},{160,192},{192,224},{224... | collective-permute-start | bytes 294920 | tf_op jit(solution)/shard_map/ppermute | solution.py:359
  187.4 17.1 %collective-permute-start.18 = (bf16[64,16,2304]{2,1,0:T(8,128)(2,1)}, bf16[64,16,2304]{2,1,0:T(8,128)(2,1)}, u32[]{:S(2)}, u32[]{:S(2)}) collective-permute-start(bf16[64,16,2304]{2,1,0:T(8,128)(2,1)} %all-gather.5.cloned.1.call-done.late_ref), channel_id=1, source_target_pairs={{0,1},{1,0},{2,3},{3,2},{4,5},{5,4},{6,7},{7,6},{8,9},{9,8},{10,11... | collective-permute-start | bytes 14155784 | tf_op jit(solution)/shard_map/ppermute | solution.py:345
  (17 other events, 302.7 us)
Sparse Core Ops, SparseCore 0:
  17.4 56.9 all-gather.2
  119.3 61.0 all-gather.4

commit v5 on v4

--- a/solution.py
+++ b/solution.py
@@ -158,22 +158,33 @@
 RING_ORDER = (0, -1, 1, -2, 2, -3, 3)
 
 
+def halves_in_order(core, mine_ref, partner_ref):
+    mine, partner = mine_ref[...], partner_ref[...]
+    first = core == 0
+    return jnp.concatenate(
+        [jnp.where(first, mine, partner), jnp.where(first, partner, mine)], axis=0
+    )
+
+
 def columns_kernel(place_ref, *refs):
-    near, (far_low, far_high), (own_ref, other_ref, out_ref) = refs[:7], refs[7:9], refs[9:]
+    near, (far_low, far_high), (own_ref, *halves, out_ref) = refs[:7], refs[7:9], refs[9:]
     rows, half = far_low.shape
     left = jnp.concatenate([ref[...].astype(jnp.float32) for ref in near], axis=0)
     left = left.astype(jnp.bfloat16)
     ring = place_ref[2]
-    for weights, shard in ((own_ref, ring), (other_ref, 1 - ring)):
-        product = dot_rows(left, weights[...])
+    own = own_ref[...]
+    for weights, shard in ((own, ring), (halves_in_order(place_ref[0], *halves), 1 - ring)):
+        product = dot_rows(left, weights)
         for at, offset in enumerate(RING_ORDER):
             place = jnp.bitwise_and(place_ref[1] + (offset + 8), 7)
             out_ref[place, shard] = product[at * rows : (at + 1) * rows].astype(jnp.bfloat16)
-        far = dot_rows(far_low[...], weights[:half, :]) + dot_rows(far_high[...], weights[half:, :])
+        far = dot_rows(far_low[...], weights[:half]) + dot_rows(far_high[...], weights[half:])
         out_ref[jnp.bitwise_and(place_ref[1] + 4, 7), shard] = far.astype(jnp.bfloat16)
 
 
-def third_kernel(place_ref, x_ref, gain_ref, own_ref, other_ref, out_ref, coarse_ref, normed_ref):
+def third_kernel(
+    place_ref, x_ref, gain_ref, own_ref, mine_ref, partner_ref, out_ref, coarse_ref, normed_ref
+):
     blocks, places, shards, rows, width = x_ref.shape
     count = 1.0 / (blocks * shards * width)
     order = [(z, shard) for shard in range(shards) for z in range(blocks)]
@@ -197,14 +208,15 @@
         coarse_ref[:, at * width : (at + 1) * width] = x_ref[z, place_ref[1], shard].astype(
             jnp.float32
         )
-    token = lax.broadcasted_iota(jnp.int32, (96, 96), 0)
-    other = lax.broadcasted_iota(jnp.int32, (96, 96), 1)
-    keep = jnp.right_shift(token, 5) == jnp.right_shift(other, 5)
+    query_token = lax.broadcasted_iota(jnp.int32, (96, 96), 0)
+    key_token = lax.broadcasted_iota(jnp.int32, (96, 96), 1)
+    keep = jnp.right_shift(query_token, 5) == jnp.right_shift(key_token, 5)
     ring = place_ref[2]
-    for weights, shard in ((own_ref, ring), (other_ref, 1 - ring)):
+    other = halves_in_order(place_ref[0], mine_ref, partner_ref)
+    for weights, shard in ((own_ref[...], ring), (other, 1 - ring)):
         triple = lax.dot_general(
             normed_ref[...],
-            weights[...],
+            weights,
             (((1,), (1,)), ((), ())),
             preferred_element_type=jnp.float32,
         ).astype(jnp.bfloat16)
@@ -411,6 +423,28 @@
         both_merge, "lat", axis=1, axis_index_groups=RINGS, tiled=True
     )
     core_place = jnp.stack([core, lax.axis_index("lat") % Z_RING, ring]).astype(jnp.int32)
+    picks = (land_ids[:, :, None] == jnp.arange(3, dtype=jnp.int32)).astype(jnp.float32)
+    surface = jnp.einsum("ijs,sc->ijc", picks, surface_table.astype(jnp.float32))
+    hidden = (
+        fields.astype(jnp.float32)
+        + surface[:, None, :, :]
+        + level_table.astype(jnp.float32)[None, :, None, :]
+    ).astype(jnp.bfloat16)
+    hidden = after(hidden, both_merge)
+    above, below = neighbours(hidden[:2], hidden[-2:], "lat")
+    cells = jnp.concatenate([above, hidden, below], axis=0)
+    qkv_third = qkv_third.transpose(0, 2, 1).reshape(-1, qkv_third.shape[1])
+
+    merge_third, qkv_third, up_third, up_second, out_third, cells = lax.optimization_barrier(
+        (merge_third, qkv_third, up_third, up_second, out_third, cells)
+    )
+    left, right = neighbours(cells[:, :, :2], cells[:, :, -2:], "lon")
+
+    merge_mine, qkv_mine = [
+        swap_rings(lax.dynamic_slice_in_dim(table, core * (table.shape[0] // 2), table.shape[0] // 2))
+        for table in (merge_third, qkv_third)
+    ]
+
     own_rest = jnp.concatenate(
         [
             cut(up_third, column * 16, 16, core * 512, 512),
@@ -422,24 +456,10 @@
     other_rest = swap_rings(own_rest)
     late = in_order(ring, own_rest, other_rest, 1)
 
-    picks = (land_ids[:, :, None] == jnp.arange(3, dtype=jnp.int32)).astype(jnp.float32)
-    surface = jnp.einsum("ijs,sc->ijc", picks, surface_table.astype(jnp.float32))
-    hidden = (
-        fields.astype(jnp.float32)
-        + surface[:, None, :, :]
-        + level_table.astype(jnp.float32)[None, :, None, :]
-    ).astype(jnp.bfloat16)
-    hidden = after(hidden, both_merge, other_rest)
-    above, below = neighbours(hidden[:2], hidden[-2:], "lat")
-    cells = jnp.concatenate([above, hidden, below], axis=0)
-    qkv_third = qkv_third.transpose(0, 2, 1).reshape(-1, qkv_third.shape[1])
-
-    merge_third, qkv_third, cells = lax.optimization_barrier((merge_third, qkv_third, cells))
-    left, right = neighbours(cells[:, :, :2], cells[:, :, -2:], "lon")
-    merge_other = swap_rings(merge_third)
-    qkv_other = swap_rings(qkv_third)
-    late, left = lax.optimization_barrier((late, left))
-    late_rows = ring_gather(late)
+    padded = jnp.pad(late, ((0, 0), (0, 4096 - late.shape[1])))
+    late_rows = lax.all_gather(
+        padded, "lat", axis=0, axis_index_groups=RINGS, tiled=True
+    )
 
     ext_rows = tile_rows + 4
     own_window = (jnp.arange(32 * 4) % tile_cols + 2) // 4
@@ -467,7 +487,7 @@
         ),
         flops=2 * 640 * 512 * 1536,
     )
-    attended = after(attended, merge_other, late_rows)
+    attended = after(attended, merge_mine, qkv_mine, padded)
     tokens = attended.shape[0]
     skip_first, merged_in = call_kernel(
         skip_kernel,
@@ -480,10 +500,11 @@
     )
     own_rows = merged_in.shape[0]
     half_shape = jax.ShapeDtypeStruct((own_rows, 512), jnp.bfloat16)
+    merge_partner, qkv_partner = swap_cores(merge_mine), swap_cores(qkv_mine)
     second_half, second_send = call_kernel(
         merge_kernel,
         (half_shape, half_shape),
-        (merged_in, after(swap_cores(merged_in), qkv_other), merge_weights),
+        (merged_in, after(swap_cores(merged_in), merge_partner, qkv_partner), merge_weights),
         flops=2 * 192 * 2048 * 512,
     )
     second_cells, coarse_in = call_kernel(
@@ -496,26 +517,25 @@
         (pltpu.VMEM((2, own_rows, 512), jnp.bfloat16),),
         flops=2 * 96 * 96 * 1024,
     )
+    own_count = coarse_in.shape[0]
+
+    pieces, forth, back = [coarse_in], coarse_in, coarse_in
+    for _ in range(3):
+        forth, back = ring_shift(forth, 1), ring_shift(back, -1)
+        pieces += [forth, back]
     late = lax.all_gather(
-        after(late_rows, coarse_in),
+        after(late_rows, pieces[1])[:, : late.shape[1]],
         "lon",
         axis=0,
         axis_index_groups=[[4 * y + x for y in range(8)] for x in range(4)],
         tiled=True,
     ).reshape(64, 16, -1)
-
-    own_count = coarse_in.shape[0]
-
-    pieces, forth, back = [coarse_in], coarse_in, coarse_in
-    for _ in range(3):
-        forth, back = ring_shift(forth, 1), ring_shift(back, -1)
-        pieces += [forth, back]
     half_feats = coarse_in.shape[1] // 2
     pieces += [ring_shift(forth[:, :half_feats], 1), ring_shift(back[:, half_feats:], -1)]
     column_block = call_kernel(
         columns_kernel,
         jax.ShapeDtypeStruct((Z_RING, 2, own_count, 128), jnp.bfloat16),
-        (core_place, *pieces, merge_third, merge_other),
+        (core_place, *pieces, merge_third, merge_mine, merge_partner),
         flops=2 * 192 * 4096 * 256,
     )
     heads_out, own_coarse = call_kernel(
@@ -524,7 +544,7 @@
             jax.ShapeDtypeStruct((Z_RING, 2, own_count, HD), jnp.bfloat16),
             jax.ShapeDtypeStruct((own_count, 2048), jnp.float32),
         ),
-        (core_place, ring_gather(column_block), norm_third[None], qkv_third, qkv_other),
+        (core_place, ring_gather(column_block), norm_third[None], qkv_third, qkv_mine, qkv_partner),
         (pltpu.VMEM((Z_RING * own_count, 2048), jnp.bfloat16),),
         flops=2 * 192 * 2048 * 384,
     )

time: 221 us -> 211 us (0.955)
  waiting for transfers between devices: 41.4 us -> 37.3 us
  local copies, waits for them, and re-layouts: 19.6 us -> 16.8 us
    ppermute x2, waiting for transfers between devices: 26.6 us -> 1.57 us  [neighbours(): lax.ppermute(first, axis, [((i + 1) % count, i) for i in range(count)])]
    ppermute x3 -> x5, starting transfers between devices: 11.6 us -> 26.6 us  [swap_cores(): return lax.ppermute(values, 'lon', [(i, i ^ 1) for i in range(count)])]
    all_gather x1 -> x2, waiting for transfers between devices: 0.02 us -> 12.2 us  [the longest x1 10 us: on_device(): lax.all_gather(padded, 'lat', axis=0, axis_index_groups=RINGS, tiled=True)]
    ppermute x8, starting transfers between devices: 29.6 us -> 22.9 us  [ring_shift(): return lax.ppermute(values, 'lat', pairs)]
    all_to_all x1 -> x0, starting transfers between devices: 6.39 us -> none  [ring_scatter(): lax.all_to_all(blocks, 'lat', 0, 0, axis_index_groups=RINGS, tiled=True)]
    ppermute x8, waiting for transfers between devices: 9.19 us -> 14.4 us  [ring_shift(): return lax.ppermute(values, 'lat', pairs)]
    ppermute x4, waiting for transfers between devices: 2.68 us -> 6.7 us  [swap_rings(): lax.ppermute(values, 'lat', [(i, (i + Z_RING) % count) for i in range(cou...]
    ppermute x2, starting transfers between devices: 11 us -> 7.22 us  [neighbours(): lax.ppermute(last, axis, [(i, (i + 1) % count) for i in range(count)])]
  transfers between devices with their start and end apart: 22 -> 24, of which waited for: 9 -> 15; matrix products, arithmetic and copies ran while one was open for 4% -> 4% of each run, Pallas kernels for 5% -> 7%
where the time goes in v5:
time: 211 us; the launch traced here: 210 us
  starting transfers between devices  88.9 us (42%)
  waiting for transfers between devices  37.3 us (18%)
  blocking collectives  28.8 us (14%)
  Pallas kernels  19.5 us (9%)
  local copies, waits for them, and re-layouts  16.8 us (8%)
  between operations  13.7 us (6%)
  other arithmetic  3.76 us (2%)
    all_to_all x2, blocking collectives, ring_scatter(): lax.all_to_all(blocks, 'lat', 0, 0, axis_index_groups=RINGS, tiled=True)  28.8 us
    ppermute x5, starting transfers between devices, swap_cores(): return lax.ppermute(values, 'lon', [(i, i ^ 1) for i in range(count)])  26.6 us
    ppermute x8, starting transfers between devices, ring_shift(): return lax.ppermute(values, 'lat', pairs)  22.9 us
    pallas_call x7, Pallas kernels, call_kernel(): pl.pallas_call(body, out_shape=out_shape, in_specs=[pl.BlockSpec(memory_s...  19.5 us
    ppermute x2, starting transfers between devices, neighbours(): lax.ppermute(first, axis, [((i + 1) % count, i) for i in range(count)])  17.8 us
    ppermute x8, waiting for transfers between devices, ring_shift(): return lax.ppermute(values, 'lat', pairs)  14.4 us
    ppermute x4, starting transfers between devices, swap_rings(): lax.ppermute(values, 'lat', [(i, (i + Z_RING) % count) for i in range(cou...  14.4 us
    unnamed x36, local copies, waits for them, and re-layouts  10.4 us
  transfers between devices with their start and end apart: 24, of which 15 were waited for; matrix products, arithmetic and copies ran while one was open for 4% of the time, Pallas kernels for 7%

profile of v5, /device:TPU:1, one launch (start us, length us, event | category | flops | bytes accessed | tf_op | source)
XLA Modules:
  0.0 209.8 jit_solution(8806778609941485292)
XLA Ops:
  8.3 5.5 %collective-permute-start = (bf16[1,160,512]{2,1,0:T(8,128)(2,1)S(1)}, bf16[1,160,512]{2,1,0:T(8,128)(2,1)S(1)}, u32[]{:S(2)}, u32[]{:S(2)}) collective-permute-start(bf16[1,160,512]{2,1,0:T(8,128)(2,1)S(1)} %maximum_bitcast_fusion), channel_id=1, source_target_pairs={{0,256},{32,288},{64,320},{96,352},{128,384},{160,416},{192,448},{... | collective-permute-start | bytes 491528 | tf_op jit(solution)/shard_map/ppermute | solution.py:362
  13.8 2.7 %collective-permute-done = bf16[1,160,512]{2,1,0:T(8,128)(2,1)S(1)} collective-permute-done((bf16[1,160,512]{2,1,0:T(8,128)(2,1)S(1)}, bf16[1,160,512]{2,1,0:T(8,128)(2,1)S(1)}, u32[]{:S(2)}, u32[]{:S(2)}) %collective-permute-start) | collective-permute-done | bytes 163872 | tf_op jit(solution)/shard_map/ppermute | solution.py:362
  20.2 5.1 %collective-permute-start.1 = (bf16[2,2,16,512]{3,2,1,0:T(8,128)(2,1)S(1)}, bf16[2,2,16,512]{3,2,1,0:T(8,128)(2,1)S(1)}, u32[]{:S(2)}, u32[]{:S(2)}) collective-permute-start(bf16[2,2,16,512]{3,2,1,0:T(8,128)(2,1)S(1)} %get-tuple-element.45), channel_id=1, source_target_pairs={{0,32},{32,64},{64,96},{96,128},{128,160},{160,192},{192,224},{224... | collective-permute-start | bytes 196616 | tf_op jit(solution)/shard_map/ppermute | solution.py:350
  25.3 11.0 %collective-permute-start.2 = (bf16[2,2,16,512]{3,2,1,0:T(8,128)(2,1)S(1)}, bf16[2,2,16,512]{3,2,1,0:T(8,128)(2,1)S(1)}, u32[]{:S(2)}, u32[]{:S(2)}) collective-permute-start(bf16[2,2,16,512]{3,2,1,0:T(8,128)(2,1)S(1)} %get-tuple-element.46), channel_id=1, source_target_pairs={{32,0},{64,32},{96,64},{128,96},{160,128},{192,160},{224,192},{256... | collective-permute-start | bytes 196616 | tf_op jit(solution)/shard_map/ppermute | solution.py:351
  42.1 4.0 %collective-permute-done.7 = bf16[16,1152]{1,0:T(8,128)(2,1)S(1)} collective-permute-done((bf16[16,1152]{1,0:T(8,128)(2,1)S(1)}, bf16[16,1152]{1,0:T(8,128)(2,1)S(1)}, u32[]{:S(2)}, u32[]{:S(2)}) %collective-permute-start.7) | collective-permute-done | bytes 36896 | tf_op jit(solution)/shard_map/ppermute | solution.py:362
  47.8 2.5 %collective-permute-start.5 = (bf16[2048,128]{1,0:T(8,128)(2,1)}, bf16[2048,128]{1,0:T(8,128)(2,1)}, u32[]{:S(2)}, u32[]{:S(2)}) collective-permute-start(bf16[2048,128]{1,0:T(8,128)(2,1)} %constant_dynamic-slice_fusion.1), channel_id=1, source_target_pairs={{0,256},{32,288},{64,320},{96,352},{128,384},{160,416},{192,448},{... | collective-permute-start | bytes 1572872 | tf_op jit(solution)/shard_map/ppermute | solution.py:362
  50.7 4.3 %collective-permute-start.6 = (bf16[96,2048]{1,0:T(8,128)(2,1)S(1)}, bf16[96,2048]{1,0:T(8,128)(2,1)}, u32[]{:S(2)}, u32[]{:S(2)}) collective-permute-start(bf16[96,2048]{1,0:T(8,128)(2,1)S(1)} %constant_dynamic-slice_fusion), channel_id=1, source_target_pairs={{0,256},{32,288},{64,320},{96,352},{128,384},{160,416},{192,448},{... | collective-permute-start | bytes 1179656 | tf_op jit(solution)/shard_map/ppermute | solution.py:362
  55.1 6.7 %collective-permute-start.4 = (bf16[16,2,2,512]{3,2,1,0:T(2,128)(2,1)S(1)}, bf16[16,2,2,512]{3,2,1,0:T(2,128)(2,1)S(1)}, u32[]{:S(2)}, u32[]{:S(2)}) collective-permute-start(bf16[16,2,2,512]{3,2,1,0:T(2,128)(2,1)S(1)} %get-tuple-element.43), channel_id=1, source_target_pairs={{1,0},{2,1},{3,2},{4,3},{5,4},{6,5},{7,6},{8,7},{9,8},{10,9},{11,1... | collective-permute-start | bytes 196616 | tf_op jit(solution)/shard_map/ppermute | solution.py:351
  64.0 9.3 %collective-permute-start.9 = (bf16[2048,128]{1,0:T(8,128)(2,1)}, bf16[2048,128]{1,0:T(8,128)(2,1)}, u32[]{:S(2)}, u32[]{:S(2)}) collective-permute-start(bf16[2048,128]{1,0:T(8,128)(2,1)} %collective-permute-done.5.refs_10_), channel_id=1, source_target_pairs={{0,1},{1,0},{2,3},{3,2},{4,5},{5,4},{6,7},{7,6},{8,9},{9,8},{10,11... | collective-permute-start | bytes 1572872 | tf_op jit(solution)/shard_map/ppermute | solution.py:357
  75.3 3.2 %shard_map.154.attended_ref = bf16[384,512]{1,0:T(8,128)(2,1)S(1)} custom-call(bf16[512,512]{1,0:T(8,128)(2,1)S(1)} %bitcast.24, bf16[64,512]{1,0:T(8,128)(2,1)S(1)} %reshape.68.left_ref, bf16[64,512]{1,0:T(8,128)(2,1)S(1)} %reshape.69.right_ref, f32[1,512]{1,0:T(1,128)S(1)} %bitcast.28, bf16[3,512,512]{2,1,0:T(8,128)(2,1)S(1)} %copy-done.15, ...), custom_call_target="tpu_custom_call" | custom-call | flops 1006632960 | bytes 2314752 | tf_op jit(solution)/shard_map/pallas_call | solution.py:20
  86.7 2.4 %collective-permute-start.8 = (bf16[96,2048]{1,0:T(8,128)(2,1)}, bf16[96,2048]{1,0:T(8,128)(2,1)S(1)}, u32[]{:S(2)}, u32[]{:S(2)}) collective-permute-start(bf16[96,2048]{1,0:T(8,128)(2,1)} %get-tuple-element.32.own_ref), channel_id=1, source_target_pairs={{0,1},{1,0},{2,3},{3,2},{4,5},{5,4},{6,7},{7,6},{8,9},{9,8},{10,11... | collective-permute-start | bytes 1179656 | tf_op jit(solution)/shard_map/ppermute | solution.py:357
  92.2 2.4 %collective-permute-start.11 = (bf16[96,512]{1,0:T(8,128)(2,1)S(1)}, bf16[96,512]{1,0:T(8,128)(2,1)S(1)}, u32[]{:S(2)}, u32[]{:S(2)}) collective-permute-start(bf16[96,512]{1,0:T(8,128)(2,1)S(1)} %get-tuple-element.35), channel_id=1, source_target_pairs={{0,1},{1,0},{2,3},{3,2},{4,5},{5,4},{6,7},{7,6},{8,9},{9,8},{10,11... | collective-permute-start | bytes 294920 | tf_op jit(solution)/shard_map/ppermute | solution.py:357
  98.5 10.0 %all-gather.6.cloned.1.call-done = bf16[128,4096]{1,0:T(8,128)(2,1)} async-done(((bf16[16,4096]{1,0:T(8,128)(2,1)}), bf16[128,4096]{1,0:T(8,128)(2,1)}) %all-gather.6.cloned.1.call-update) | async-done | bytes 1048592 | tf_op jit(solution)/shard_map/all_gather | solution.py:460
  114.5 4.5 %collective-permute-done.13.refs_2_ = bf16[24,4096]{1,0:T(8,128)(2,1)S(1)} collective-permute-done((bf16[24,4096]{1,0:T(8,128)(2,1)S(1)}, bf16[24,4096]{1,0:T(8,128)(2,1)S(1)}, u32[]{:S(2)}, u32[]{:S(2)}) %collective-permute-start.13) | collective-permute-done | bytes 196640 | tf_op jit(solution)/shard_map/ppermute | solution.py:371
  119.0 3.1 %collective-permute-start.15 = (bf16[24,4096]{1,0:T(8,128)(2,1)S(1)}, bf16[24,4096]{1,0:T(8,128)(2,1)S(1)}, u32[]{:S(2)}, u32[]{:S(2)}) collective-permute-start(bf16[24,4096]{1,0:T(8,128)(2,1)S(1)} %collective-permute-done.13.refs_2_), channel_id=1, source_target_pairs={{0,224},{32,0},{64,32},{96,64},{128,96},{160,128},{192,160},{224,1... | collective-permute-start | bytes 589832 | tf_op jit(solution)/shard_map/ppermute | solution.py:371
  125.4 4.4 %collective-permute-start.17 = (bf16[24,4096]{1,0:T(8,128)(2,1)S(1)}, bf16[24,4096]{1,0:T(8,128)(2,1)S(1)}, u32[]{:S(2)}, u32[]{:S(2)}) collective-permute-start(bf16[24,4096]{1,0:T(8,128)(2,1)S(1)} %collective-permute-done.15.refs_4_), channel_id=1, source_target_pairs={{0,224},{32,0},{64,32},{96,64},{128,96},{160,128},{192,160},{224,1... | collective-permute-start | bytes 589832 | tf_op jit(solution)/shard_map/ppermute | solution.py:371
  132.4 5.4 %collective-permute-start.19 = (bf16[24,2048]{1,0:T(8,128)(2,1)S(1)}, bf16[24,2048]{1,0:T(8,128)(2,1)S(1)}, u32[]{:S(2)}, u32[]{:S(2)}) collective-permute-start(bf16[24,2048]{1,0:T(8,128)(2,1)S(1)} %slice.29), channel_id=1, source_target_pairs={{0,224},{32,0},{64,32},{96,64},{128,96},{160,128},{192,160},{224,1... | collective-permute-start | bytes 294920 | tf_op jit(solution)/shard_map/ppermute | solution.py:371
  140.1 5.9 %collective-permute-done.18.refs_7_ = bf16[24,2048]{1,0:T(8,128)(2,1)S(1)} collective-permute-done((bf16[24,2048]{1,0:T(8,128)(2,1)S(1)}, bf16[24,2048]{1,0:T(8,128)(2,1)S(1)}, u32[]{:S(2)}, u32[]{:S(2)}) %collective-permute-start.18) | collective-permute-done | bytes 98336 | tf_op jit(solution)/shard_map/ppermute | solution.py:371
  147.2 2.4 %shard_map.158 = bf16[8,2,24,128]{3,2,1,0:T(8,128)(2,1)S(1)} custom-call(s32[3]{0:T(128)S(1)} %pad_add_fusion.1.core_ref.place_ref, bf16[24,4096]{1,0:T(8,128)(2,1)S(1)} %get-tuple-element.36.refs_0_, bf16[24,4096]{1,0:T(8,128)(2,1)S(1)} %collective-permute-done.12.refs_1_, bf16[24,4096]{1,0:T(8,128)(2,1)S(1)} %collective-permute-done.13.refs_2_, ...), custom_call_target="tpu_custom_call" | custom-call | flops 402653184 | bytes 3670028 | tf_op jit(solution)/shard_map/pallas_call | solution.py:20
  149.8 19.4 %all_to_all.10.x_ref = bf16[8,8,2,24,128]{4,3,2,1,0:T(8,128)(2,1)S(1)} all-to-all(bf16[8,8,2,24,128]{4,3,2,1,0:T(8,128)(2,1)S(1)} %broadcast_in_dim.46), channel_id=1, replica_groups={{0,32,64,96,128,160,192,224},{256,288,320,352,384,416,448,480},{1,33,65..., dimensions={0} | all-to-all | bytes 1572864 | tf_op jit(solution)/shard_map/all_to_all | solution.py:366
  169.2 3.8 %shard_map.159 = (bf16[8,2,24,64]{3,2,1,0:T(8,128)(2,1)S(1)}, f32[24,2048]{1,0:T(8,128)S(1)}) custom-call(s32[3]{0:T(128)S(1)} %pad_add_fusion.1.core_ref.place_ref, bf16[8,8,2,24,128]{4,3,2,1,0:T(8,128)(2,1)S(1)} %all_to_all.10.x_ref, f32[1,2048]{1,0:T(1,128)S(1)} %bitcast.27, bf16[192,2048]{1,0:T(8,128)(2,1)S(1)} %bitcast.23, ...), custom_call_target="tpu_custom_call" | custom-call | flops 301989888 | bytes 2367500 | tf_op jit(solution)/shard_map/pallas_call | solution.py:20
  175.2 10.6 %collective-permute-start.20 = (bf16[64,16,2304]{2,1,0:T(8,128)(2,1)}, bf16[64,16,2304]{2,1,0:T(8,128)(2,1)}, u32[]{:S(2)}, u32[]{:S(2)}) collective-permute-start(bf16[64,16,2304]{2,1,0:T(8,128)(2,1)} %bitcast.19), channel_id=1, source_target_pairs={{0,1},{1,0},{2,3},{3,2},{4,5},{5,4},{6,7},{7,6},{8,9},{9,8},{10,11... | collective-permute-start | bytes 14155784 | tf_op jit(solution)/shard_map/ppermute | solution.py:357
  185.9 9.4 %all_to_all.11 = bf16[8,2,1536]{2,1,0:T(2,128)(2,1)S(1)} all-to-all(bf16[8,2,1536]{2,1,0:T(2,128)(2,1)S(1)} %reshape.74), channel_id=1, replica_groups={{0,32,64,96,128,160,192,224},{256,288,320,352,384,416,448,480},{1,33,65..., dimensions={0} | all-to-all | bytes 98304 | tf_op jit(solution)/shard_map/all_to_all | solution.py:366
  197.7 5.5 %shard_map.160 = bf16[384,512]{1,0:T(8,128)(2,1)} custom-call(s32[3]{0:T(128)S(1)} %pad_add_fusion.1.core_ref.place_ref, bf16[8,2,24,64]{3,2,1,0:T(8,128)(2,1)S(1)} %reshape.75.heads_ref, f32[24,2048]{1,0:T(8,128)S(1)} %get-tuple-element.38.own_coarse_ref, bf16[64,16,2304]{2,1,0:T(8,128)(2,1)S(1)} %bitcast.20, ...), custom_call_target="tpu_custom_call" | custom-call | flops 301989888 | bytes 10272780 | tf_op jit(solution)/shard_map/pallas_call | solution.py:20
  (108 shorter events, 52.5 us)
Async XLA Ops:
  6.5 74.6 %all-gather.4.cloned.1.call-start = ((), (), s32[]{:S(2)}) async-start(), calls=%async_computation.2 | async-start | bytes 2949120 | tf_op jit(solution)/shard_map/all_gather | solution.py:422
  8.3 8.2 %collective-permute-start = (bf16[1,160,512]{2,1,0:T(8,128)(2,1)S(1)}, bf16[1,160,512]{2,1,0:T(8,128)(2,1)S(1)}, u32[]{:S(2)}, u32[]{:S(2)}) collective-permute-start(bf16[1,160,512]{2,1,0:T(8,128)(2,1)S(1)} %maximum_bitcast_fusion), channel_id=1, source_target_pairs={{0,256},{32,288},{64,320},{96,352},{128,384},{160,416},{192,448},{... | collective-permute-start | bytes 491528 | tf_op jit(solution)/shard_map/ppermute | solution.py:362
  17.2 91.3 %all-gather.6.cloned.1.call-start = ((), (), s32[]{:S(2)}) async-start(), calls=%async_computation.3 | async-start | bytes 1179648 | tf_op jit(solution)/shard_map/all_gather | solution.py:460
  20.2 16.2 %collective-permute-start.1 = (bf16[2,2,16,512]{3,2,1,0:T(8,128)(2,1)S(1)}, bf16[2,2,16,512]{3,2,1,0:T(8,128)(2,1)S(1)}, u32[]{:S(2)}, u32[]{:S(2)}) collective-permute-start(bf16[2,2,16,512]{3,2,1,0:T(8,128)(2,1)S(1)} %get-tuple-element.45), channel_id=1, source_target_pairs={{0,32},{32,64},{64,96},{96,128},{128,160},{160,192},{192,224},{224... | collective-permute-start | bytes 196616 | tf_op jit(solution)/shard_map/ppermute | solution.py:350
  25.3 12.4 %collective-permute-start.2 = (bf16[2,2,16,512]{3,2,1,0:T(8,128)(2,1)S(1)}, bf16[2,2,16,512]{3,2,1,0:T(8,128)(2,1)S(1)}, u32[]{:S(2)}, u32[]{:S(2)}) collective-permute-start(bf16[2,2,16,512]{3,2,1,0:T(8,128)(2,1)S(1)} %get-tuple-element.46), channel_id=1, source_target_pairs={{32,0},{64,32},{96,64},{128,96},{160,128},{192,160},{224,192},{256... | collective-permute-start | bytes 196616 | tf_op jit(solution)/shard_map/ppermute | solution.py:351
  39.9 6.2 %collective-permute-start.7 = (bf16[16,1152]{1,0:T(8,128)(2,1)S(1)}, bf16[16,1152]{1,0:T(8,128)(2,1)S(1)}, u32[]{:S(2)}, u32[]{:S(2)}) collective-permute-start(bf16[16,1152]{1,0:T(8,128)(2,1)S(1)} %pad_maximum_fusion.1), channel_id=1, source_target_pairs={{0,256},{32,288},{64,320},{96,352},{128,384},{160,416},{192,448},{... | collective-permute-start | bytes 110600 | tf_op jit(solution)/shard_map/ppermute | solution.py:362
  46.8 128.3 %all-gather.8.cloned.1.call-start = ((), (), s32[]{:S(2)}) async-start(), calls=%async_computation.4 | async-start | bytes 5308416 | tf_op jit(solution)/shard_map/all_gather | solution.py:526
  47.8 16.1 %collective-permute-start.5 = (bf16[2048,128]{1,0:T(8,128)(2,1)}, bf16[2048,128]{1,0:T(8,128)(2,1)}, u32[]{:S(2)}, u32[]{:S(2)}) collective-permute-start(bf16[2048,128]{1,0:T(8,128)(2,1)} %constant_dynamic-slice_fusion.1), channel_id=1, source_target_pairs={{0,256},{32,288},{64,320},{96,352},{128,384},{160,416},{192,448},{... | collective-permute-start | bytes 1572872 | tf_op jit(solution)/shard_map/ppermute | solution.py:362
  50.7 28.6 %collective-permute-start.6 = (bf16[96,2048]{1,0:T(8,128)(2,1)S(1)}, bf16[96,2048]{1,0:T(8,128)(2,1)}, u32[]{:S(2)}, u32[]{:S(2)}) collective-permute-start(bf16[96,2048]{1,0:T(8,128)(2,1)S(1)} %constant_dynamic-slice_fusion), channel_id=1, source_target_pairs={{0,256},{32,288},{64,320},{96,352},{128,384},{160,416},{192,448},{... | collective-permute-start | bytes 1179656 | tf_op jit(solution)/shard_map/ppermute | solution.py:362
  55.1 18.7 %collective-permute-start.4 = (bf16[16,2,2,512]{3,2,1,0:T(2,128)(2,1)S(1)}, bf16[16,2,2,512]{3,2,1,0:T(2,128)(2,1)S(1)}, u32[]{:S(2)}, u32[]{:S(2)}) collective-permute-start(bf16[16,2,2,512]{3,2,1,0:T(2,128)(2,1)S(1)} %get-tuple-element.43), channel_id=1, source_target_pairs={{1,0},{2,1},{3,2},{4,3},{5,4},{6,5},{7,6},{8,7},{9,8},{10,9},{11,1... | collective-permute-start | bytes 196616 | tf_op jit(solution)/shard_map/ppermute | solution.py:351
  61.8 12.0 %collective-permute-start.3 = (bf16[16,2,2,512]{3,2,1,0:T(2,128)(2,1)S(1)}, bf16[16,2,2,512]{3,2,1,0:T(2,128)(2,1)S(1)}, u32[]{:S(2)}, u32[]{:S(2)}) collective-permute-start(bf16[16,2,2,512]{3,2,1,0:T(2,128)(2,1)S(1)} %get-tuple-element.44), channel_id=1, source_target_pairs={{0,1},{1,2},{2,3},{3,4},{4,5},{5,6},{6,7},{7,8},{8,9},{9,10},{10,1... | collective-permute-start | bytes 196616 | tf_op jit(solution)/shard_map/ppermute | solution.py:350
  64.0 25.1 %collective-permute-start.9 = (bf16[2048,128]{1,0:T(8,128)(2,1)}, bf16[2048,128]{1,0:T(8,128)(2,1)}, u32[]{:S(2)}, u32[]{:S(2)}) collective-permute-start(bf16[2048,128]{1,0:T(8,128)(2,1)} %collective-permute-done.5.refs_10_), channel_id=1, source_target_pairs={{0,1},{1,0},{2,3},{3,2},{4,5},{5,4},{6,7},{7,6},{8,9},{9,8},{10,11... | collective-permute-start | bytes 1572872 | tf_op jit(solution)/shard_map/ppermute | solution.py:357
  79.3 9.8 %collective-permute-start.10 = (bf16[96,2048]{1,0:T(8,128)(2,1)}, bf16[96,2048]{1,0:T(8,128)(2,1)}, u32[]{:S(2)}, u32[]{:S(2)}) collective-permute-start(bf16[96,2048]{1,0:T(8,128)(2,1)} %collective-permute-done.6.mine_ref), channel_id=1, source_target_pairs={{0,1},{1,0},{2,3},{3,2},{4,5},{5,4},{6,7},{7,6},{8,9},{9,8},{10,11... | collective-permute-start | bytes 1179656 | tf_op jit(solution)/shard_map/ppermute | solution.py:357
  86.7 3.9 %collective-permute-start.8 = (bf16[96,2048]{1,0:T(8,128)(2,1)}, bf16[96,2048]{1,0:T(8,128)(2,1)S(1)}, u32[]{:S(2)}, u32[]{:S(2)}) collective-permute-start(bf16[96,2048]{1,0:T(8,128)(2,1)} %get-tuple-element.32.own_ref), channel_id=1, source_target_pairs={{0,1},{1,0},{2,3},{3,2},{4,5},{5,4},{6,7},{7,6},{8,9},{9,8},{10,11... | collective-permute-start | bytes 1179656 | tf_op jit(solution)/shard_map/ppermute | solution.py:357
  92.2 3.4 %collective-permute-start.11 = (bf16[96,512]{1,0:T(8,128)(2,1)S(1)}, bf16[96,512]{1,0:T(8,128)(2,1)S(1)}, u32[]{:S(2)}, u32[]{:S(2)}) collective-permute-start(bf16[96,512]{1,0:T(8,128)(2,1)S(1)} %get-tuple-element.35), channel_id=1, source_target_pairs={{0,1},{1,0},{2,3},{3,2},{4,5},{5,4},{6,7},{7,6},{8,9},{9,8},{10,11... | collective-permute-start | bytes 294920 | tf_op jit(solution)/shard_map/ppermute | solution.py:357
  96.6 13.8 %collective-permute-start.12 = (bf16[24,4096]{1,0:T(8,128)(2,1)S(1)}, bf16[24,4096]{1,0:T(8,128)(2,1)S(1)}, u32[]{:S(2)}, u32[]{:S(2)}) collective-permute-start(bf16[24,4096]{1,0:T(8,128)(2,1)S(1)} %get-tuple-element.36.refs_0_), channel_id=1, source_target_pairs={{0,32},{32,64},{64,96},{96,128},{128,160},{160,192},{192,224},{224... | collective-permute-start | bytes 589832 | tf_op jit(solution)/shard_map/ppermute | solution.py:371
  112.4 6.5 %collective-permute-start.13 = (bf16[24,4096]{1,0:T(8,128)(2,1)S(1)}, bf16[24,4096]{1,0:T(8,128)(2,1)S(1)}, u32[]{:S(2)}, u32[]{:S(2)}) collective-permute-start(bf16[24,4096]{1,0:T(8,128)(2,1)S(1)} %get-tuple-element.36.refs_0_), channel_id=1, source_target_pairs={{0,224},{32,0},{64,32},{96,64},{128,96},{160,128},{192,160},{224,1... | collective-permute-start | bytes 589832 | tf_op jit(solution)/shard_map/ppermute | solution.py:371
  119.0 6.4 %collective-permute-start.15 = (bf16[24,4096]{1,0:T(8,128)(2,1)S(1)}, bf16[24,4096]{1,0:T(8,128)(2,1)S(1)}, u32[]{:S(2)}, u32[]{:S(2)}) collective-permute-start(bf16[24,4096]{1,0:T(8,128)(2,1)S(1)} %collective-permute-done.13.refs_2_), channel_id=1, source_target_pairs={{0,224},{32,0},{64,32},{96,64},{128,96},{160,128},{192,160},{224,1... | collective-permute-start | bytes 589832 | tf_op jit(solution)/shard_map/ppermute | solution.py:371
  122.1 7.6 %collective-permute-start.14 = (bf16[24,4096]{1,0:T(8,128)(2,1)S(1)}, bf16[24,4096]{1,0:T(8,128)(2,1)S(1)}, u32[]{:S(2)}, u32[]{:S(2)}) collective-permute-start(bf16[24,4096]{1,0:T(8,128)(2,1)S(1)} %collective-permute-done.12.refs_1_), channel_id=1, source_target_pairs={{0,32},{32,64},{64,96},{96,128},{128,160},{160,192},{192,224},{224... | collective-permute-start | bytes 589832 | tf_op jit(solution)/shard_map/ppermute | solution.py:371
  125.4 7.0 %collective-permute-start.17 = (bf16[24,4096]{1,0:T(8,128)(2,1)S(1)}, bf16[24,4096]{1,0:T(8,128)(2,1)S(1)}, u32[]{:S(2)}, u32[]{:S(2)}) collective-permute-start(bf16[24,4096]{1,0:T(8,128)(2,1)S(1)} %collective-permute-done.15.refs_4_), channel_id=1, source_target_pairs={{0,224},{32,0},{64,32},{96,64},{128,96},{160,128},{192,160},{224,1... | collective-permute-start | bytes 589832 | tf_op jit(solution)/shard_map/ppermute | solution.py:371
  129.7 8.3 %collective-permute-start.16 = (bf16[24,4096]{1,0:T(8,128)(2,1)S(1)}, bf16[24,4096]{1,0:T(8,128)(2,1)S(1)}, u32[]{:S(2)}, u32[]{:S(2)}) collective-permute-start(bf16[24,4096]{1,0:T(8,128)(2,1)S(1)} %collective-permute-done.14.refs_3_), channel_id=1, source_target_pairs={{0,32},{32,64},{64,96},{96,128},{128,160},{160,192},{192,224},{224... | collective-permute-start | bytes 589832 | tf_op jit(solution)/shard_map/ppermute | solution.py:371
  132.4 7.7 %collective-permute-start.19 = (bf16[24,2048]{1,0:T(8,128)(2,1)S(1)}, bf16[24,2048]{1,0:T(8,128)(2,1)S(1)}, u32[]{:S(2)}, u32[]{:S(2)}) collective-permute-start(bf16[24,2048]{1,0:T(8,128)(2,1)S(1)} %slice.29), channel_id=1, source_target_pairs={{0,224},{32,0},{64,32},{96,64},{128,96},{160,128},{192,160},{224,1... | collective-permute-start | bytes 294920 | tf_op jit(solution)/shard_map/ppermute | solution.py:371
  138.1 7.9 %collective-permute-start.18 = (bf16[24,2048]{1,0:T(8,128)(2,1)S(1)}, bf16[24,2048]{1,0:T(8,128)(2,1)S(1)}, u32[]{:S(2)}, u32[]{:S(2)}) collective-permute-start(bf16[24,2048]{1,0:T(8,128)(2,1)S(1)} %slice.28), channel_id=1, source_target_pairs={{0,32},{32,64},{64,96},{96,128},{128,160},{160,192},{192,224},{224... | collective-permute-start | bytes 294920 | tf_op jit(solution)/shard_map/ppermute | solution.py:371
  175.2 20.2 %collective-permute-start.20 = (bf16[64,16,2304]{2,1,0:T(8,128)(2,1)}, bf16[64,16,2304]{2,1,0:T(8,128)(2,1)}, u32[]{:S(2)}, u32[]{:S(2)}) collective-permute-start(bf16[64,16,2304]{2,1,0:T(8,128)(2,1)} %bitcast.19), channel_id=1, source_target_pairs={{0,1},{1,0},{2,3},{3,2},{4,5},{5,4},{6,7},{7,6},{8,9},{9,8},{10,11... | collective-permute-start | bytes 14155784 | tf_op jit(solution)/shard_map/ppermute | solution.py:357
  (17 other events, 488.1 us)
Sparse Core Ops, SparseCore 0:
  17.4 49.4 all-gather.3
  68.9 39.5 all-gather.5
  112.5 62.5 all-gather.7

commit v6 on v5

--- a/solution.py
+++ b/solution.py
@@ -48,6 +48,24 @@
     return lax.dot_general(
         weights, value, (((0,), (0,)), ((), ())), preferred_element_type=jnp.float32
     )
+
+
+def pack_kernel(place_ref, merge_ref, first_ref, up_third_ref, up_second_ref, out_third_ref, out_ref):
+    core, column = place_ref[0], place_ref[1]
+    out_ref[:128, :512] = merge_ref[:, pl.ds(pl.multiple_of(core * 512, 128), 512)]
+    out_ref[128:, :512] = first_ref[...]
+    high, low = jnp.right_shift(column, 1), jnp.bitwise_and(column, 1)
+    rows = pl.ds(pl.multiple_of(high * 16, 16), 16)
+    for tile in range(4):
+        start = pl.multiple_of(core * 512 + tile * 128, 128)
+        out_ref[tile * 16 : tile * 16 + 16, 512:] = up_third_ref[
+            pl.ds(pl.multiple_of(column * 16, 16), 16), pl.ds(start, 128)
+        ]
+        start = pl.multiple_of(low * 1024 + core * 512 + tile * 128, 128)
+        out_ref[64 + tile * 16 : 80 + tile * 16, 512:] = out_third_ref[rows, pl.ds(start, 128)]
+    last = up_second_ref[rows, pl.ds(pl.multiple_of(core * 256 + low * 128, 128), 128)]
+    out_ref[128:144, 512:] = last
+    out_ref[144:, 512:] = last
 
 
 def first_kernel(x_ref, left_ref, right_ref, gain_ref, qkv_ref, window_ref, lat_ref, out_ref):
@@ -119,7 +137,7 @@
     for ring in range(2):
         for z in range(0, 8, 4):
             right = jnp.concatenate(
-                [weights_ref[ring, zz * 160 + 128 : zz * 160 + 160, :] for zz in range(z, z + 4)],
+                [weights_ref[ring, zz * 160 + 128 : zz * 160 + 160, :512] for zz in range(z, z + 4)],
                 axis=0,
             )
             start = (ring * 8 + z) * 32
@@ -136,7 +154,7 @@
     for ring in range(2):
         for z in range(0, 8, 2):
             right = jnp.concatenate(
-                [weights_ref[ring, zz * 160 : zz * 160 + 128, :] for zz in (z, z + 1)], axis=0
+                [weights_ref[ring, zz * 160 : zz * 160 + 128, :512] for zz in (z, z + 1)], axis=0
             )
             start = (ring * 8 + z) * 128
             product = dot_rows(left[:, start : start + 256], right)
@@ -253,6 +271,14 @@
     return dot_rows(matrix, high) + (dot_rows(matrix, middle) + dot_rows(matrix, low))
 
 
+def late_tile(ref, column, ring, z, tile):
+    return ref[((column * 2 + ring) * 8 + z) * 9 + tile]
+
+
+def late_row(ref, column, ring, z, first):
+    return jnp.concatenate([late_tile(ref, column, ring, z, first + at) for at in range(4)], axis=1)
+
+
 def up_kernel(
     core_ref, heads_ref, own_coarse_ref, late_ref, swapped_ref, second_ref, skip_ref, out_ref,
     third_ref, lift_ref, level_ref, small_ref,
@@ -274,9 +300,7 @@
                 for z in range(0, 8, 2):
                     right = jnp.concatenate(
                         [
-                            weights_ref[
-                                (2 * row + part) * 8 + zz, :, ring * 1152 + 640 : ring * 1152 + 1152
-                            ]
+                            late_row(weights_ref, 2 * row + part, ring, zz, 4)
                             for zz in (z, z + 1)
                             for row in range(4)
                         ],
@@ -296,7 +320,7 @@
         for ring in range(2):
             for z in range(8):
                 right = jnp.concatenate(
-                    [weights_ref[y * 8 + z, :, ring * 1152 : ring * 1152 + 512] for y in range(8)],
+                    [late_row(weights_ref, y, ring, z, 0) for y in range(8)],
                     axis=0,
                 )
                 product = dot_rows(level_three[ring * 8 + z], right)
@@ -317,9 +341,7 @@
                     [
                         jnp.concatenate(
                             [
-                                weights_ref[
-                                    (2 * row + part) * 8 + zz, :, ring * 1152 + 512 : ring * 1152 + 640
-                                ]
+                                late_tile(weights_ref, 2 * row + part, ring, zz, 8)
                                 for zz in (z, z + 1)
                                 for row in range(4)
                             ],
@@ -381,10 +403,6 @@
         jnp.concatenate([own, other], axis=axis),
         jnp.concatenate([other, own], axis=axis),
     )
-
-
-def cut(values, row, rows, column, columns):
-    return lax.dynamic_slice(values, (row, column), (rows, columns))
 
 
 def after(values, *before):
@@ -415,8 +433,17 @@
     core = lax.axis_index("lon") % 2
     column = lax.axis_index("lon") // 4
 
-    own_merge = jnp.concatenate(
-        [lax.dynamic_slice_in_dim(merge_second, core * 512, 512, 1), out_first], axis=0
+    own_merge = call_kernel(
+        pack_kernel,
+        jax.ShapeDtypeStruct((160, 640), jnp.bfloat16),
+        (
+            jnp.stack([core, column]).astype(jnp.int32),
+            merge_second,
+            out_first,
+            up_third,
+            up_second,
+            out_third,
+        ),
     )[None]
     both_merge = in_order(ring, own_merge, swap_rings(own_merge), 0)
     merge_weights = lax.all_gather(
@@ -435,31 +462,15 @@
     cells = jnp.concatenate([above, hidden, below], axis=0)
     qkv_third = qkv_third.transpose(0, 2, 1).reshape(-1, qkv_third.shape[1])
 
-    merge_third, qkv_third, up_third, up_second, out_third, cells = lax.optimization_barrier(
-        (merge_third, qkv_third, up_third, up_second, out_third, cells)
-    )
     left, right = neighbours(cells[:, :, :2], cells[:, :, -2:], "lon")
+    merge_third, qkv_third, left, right = lax.optimization_barrier(
+        (merge_third, qkv_third, left, right)
+    )
 
     merge_mine, qkv_mine = [
         swap_rings(lax.dynamic_slice_in_dim(table, core * (table.shape[0] // 2), table.shape[0] // 2))
         for table in (merge_third, qkv_third)
     ]
-
-    own_rest = jnp.concatenate(
-        [
-            cut(up_third, column * 16, 16, core * 512, 512),
-            cut(up_second, column // 2 * 16, 16, core * 256 + column % 2 * 128, 128),
-            cut(out_third, column // 2 * 16, 16, column % 2 * 1024 + core * 512, 512),
-        ],
-        axis=1,
-    )
-    other_rest = swap_rings(own_rest)
-    late = in_order(ring, own_rest, other_rest, 1)
-
-    padded = jnp.pad(late, ((0, 0), (0, 4096 - late.shape[1])))
-    late_rows = lax.all_gather(
-        padded, "lat", axis=0, axis_index_groups=RINGS, tiled=True
-    )
 
     ext_rows = tile_rows + 4
     own_window = (jnp.arange(32 * 4) % tile_cols + 2) // 4
@@ -487,7 +498,6 @@
         ),
         flops=2 * 640 * 512 * 1536,
     )
-    attended = after(attended, merge_mine, qkv_mine, padded)
     tokens = attended.shape[0]
     skip_first, merged_in = call_kernel(
         skip_kernel,
@@ -504,7 +514,7 @@
     second_half, second_send = call_kernel(
         merge_kernel,
         (half_shape, half_shape),
-        (merged_in, after(swap_cores(merged_in), merge_partner, qkv_partner), merge_weights),
+        (merged_in, after(swap_cores(merged_in), merge_mine, qkv_mine), merge_weights),
         flops=2 * 192 * 2048 * 512,
     )
     second_cells, coarse_in = call_kernel(
@@ -517,19 +527,21 @@
         (pltpu.VMEM((2, own_rows, 512), jnp.bfloat16),),
         flops=2 * 96 * 96 * 1024,
     )
+    coarse_in = after(coarse_in, merge_partner, qkv_partner)
     own_count = coarse_in.shape[0]
 
     pieces, forth, back = [coarse_in], coarse_in, coarse_in
     for _ in range(3):
         forth, back = ring_shift(forth, 1), ring_shift(back, -1)
         pieces += [forth, back]
+    late = after(merge_weights, coarse_in).reshape(2, Z_RING, 10, 16, 640)[:, :, :9, :, 512:]
     late = lax.all_gather(
-        after(late_rows, pieces[1])[:, : late.shape[1]],
+        late.reshape(-1, 128),
         "lon",
         axis=0,
         axis_index_groups=[[4 * y + x for y in range(8)] for x in range(4)],
         tiled=True,
-    ).reshape(64, 16, -1)
+    ).reshape(-1, 16, 128)
     half_feats = coarse_in.shape[1] // 2
     pieces += [ring_shift(forth[:, :half_feats], 1), ring_shift(back[:, half_feats:], -1)]
     column_block = call_kernel(

time: 211 us -> 200 us (0.948)
  starting transfers between devices: 88.9 us -> 79 us
  waiting for transfers between devices: 37.3 us -> 29.2 us
  blocking collectives: 28.8 us -> 32.5 us
  local copies, waits for them, and re-layouts: 16.8 us -> 19.9 us
    all_gather x1, waiting for transfers between devices: 0.02 us -> 12.5 us  [on_device(): lax.all_gather(both_merge, 'lat', axis=1, axis_index_groups=RINGS, tiled=...]
    all_gather x2 -> x1, waiting for transfers between devices: 12.2 us -> 0.02 us  [on_device(): lax.all_gather(late.reshape(-1, 128), 'lon', axis=0, axis_index_groups=[[...]
    ppermute x5, starting transfers between devices: 26.6 us -> 16.3 us  [swap_cores(): return lax.ppermute(values, 'lon', [(i, i ^ 1) for i in range(count)])]
    unnamed x36 -> x56, local copies, waits for them, and re-layouts: 10.4 us -> 16.6 us
    ppermute x8, waiting for transfers between devices: 14.4 us -> 9.91 us  [ring_shift(): return lax.ppermute(values, 'lat', pairs)]
    all_to_all x2, blocking collectives: 28.8 us -> 32.5 us  [ring_scatter(): lax.all_to_all(blocks, 'lat', 0, 0, axis_index_groups=RINGS, tiled=True)]
    ppermute x4 -> x3, waiting for transfers between devices: 6.7 us -> 3.12 us  [swap_rings(): lax.ppermute(values, 'lat', [(i, (i + Z_RING) % count) for i in range(cou...]
    ppermute x8, starting transfers between devices: 22.9 us -> 26.4 us  [ring_shift(): return lax.ppermute(values, 'lat', pairs)]
  transfers between devices with their start and end apart: 24 -> 22, of which waited for: 15 -> 10; matrix products, arithmetic and copies ran while one was open for 4% -> 3% of each run, Pallas kernels for 7% -> 7%
where the time goes in v6:
time: 200 us; the launch traced here: 199 us
  starting transfers between devices  79 us (40%)
  blocking collectives  32.5 us (16%)
  waiting for transfers between devices  29.2 us (15%)
  Pallas kernels  20.3 us (10%)
  local copies, waits for them, and re-layouts  19.9 us (10%)
  between operations  14 us (7%)
  other arithmetic  3.03 us (2%)
    all_to_all x2, blocking collectives, ring_scatter(): lax.all_to_all(blocks, 'lat', 0, 0, axis_index_groups=RINGS, tiled=True)  32.5 us
    ppermute x8, starting transfers between devices, ring_shift(): return lax.ppermute(values, 'lat', pairs)  26.4 us
    pallas_call x8, Pallas kernels, call_kernel(): pl.pallas_call(body, out_shape=out_shape, in_specs=[pl.BlockSpec(memory_s...  20.3 us
    unnamed x56, local copies, waits for them, and re-layouts  16.6 us
    ppermute x2, starting transfers between devices, neighbours(): lax.ppermute(first, axis, [((i + 1) % count, i) for i in range(count)])  16.5 us
    ppermute x5, starting transfers between devices, swap_cores(): return lax.ppermute(values, 'lon', [(i, i ^ 1) for i in range(count)])  16.3 us
    all_gather x1, waiting for transfers between devices, on_device(): lax.all_gather(both_merge, 'lat', axis=1, axis_index_groups=RINGS, tiled=...  12.5 us
    ppermute x3, starting transfers between devices, swap_rings(): lax.ppermute(values, 'lat', [(i, (i + Z_RING) % count) for i in range(cou...  12.2 us
  transfers between devices with their start and end apart: 22, of which 10 were waited for; matrix products, arithmetic and copies ran while one was open for 3% of the time, Pallas kernels for 7%

profile of v6, /device:TPU:1, one launch (start us, length us, event | category | flops | bytes accessed | tf_op | source)
XLA Modules:
  0.0 199.0 jit_solution(13430082331482289884)
XLA Ops:
  11.9 5.5 %collective-permute-start = (bf16[1,160,640]{2,1,0:T(8,128)(2,1)S(1)}, bf16[1,160,640]{2,1,0:T(8,128)(2,1)S(1)}, u32[]{:S(2)}, u32[]{:S(2)}) collective-permute-start(bf16[1,160,640]{2,1,0:T(8,128)(2,1)S(1)} %bitcast.27), channel_id=1, source_target_pairs={{0,256},{32,288},{64,320},{96,352},{128,384},{160,416},{192,448},{... | collective-permute-start | bytes 614408 | tf_op jit(solution)/shard_map/ppermute | solution.py:384
  17.4 3.1 %collective-permute-done = bf16[1,160,640]{2,1,0:T(8,128)(2,1)S(1)} collective-permute-done((bf16[1,160,640]{2,1,0:T(8,128)(2,1)S(1)}, bf16[1,160,640]{2,1,0:T(8,128)(2,1)S(1)}, u32[]{:S(2)}, u32[]{:S(2)}) %collective-permute-start) | collective-permute-done | bytes 204832 | tf_op jit(solution)/shard_map/ppermute | solution.py:384
  24.8 5.5 %collective-permute-start.1 = (bf16[2,2,16,512]{3,2,1,0:T(8,128)(2,1)S(1)}, bf16[2,2,16,512]{3,2,1,0:T(8,128)(2,1)S(1)}, u32[]{:S(2)}, u32[]{:S(2)}) collective-permute-start(bf16[2,2,16,512]{3,2,1,0:T(8,128)(2,1)S(1)} %get-tuple-element.42), channel_id=1, source_target_pairs={{0,32},{32,64},{64,96},{96,128},{128,160},{160,192},{192,224},{224... | collective-permute-start | bytes 196616 | tf_op jit(solution)/shard_map/ppermute | solution.py:372
  30.4 11.0 %collective-permute-start.2 = (bf16[2,2,16,512]{3,2,1,0:T(8,128)(2,1)S(1)}, bf16[2,2,16,512]{3,2,1,0:T(8,128)(2,1)S(1)}, u32[]{:S(2)}, u32[]{:S(2)}) collective-permute-start(bf16[2,2,16,512]{3,2,1,0:T(8,128)(2,1)S(1)} %get-tuple-element.41), channel_id=1, source_target_pairs={{32,0},{64,32},{96,64},{128,96},{160,128},{192,160},{224,192},{256... | collective-permute-start | bytes 196616 | tf_op jit(solution)/shard_map/ppermute | solution.py:373
  42.9 5.4 %collective-permute-start.4 = (bf16[16,2,2,512]{3,2,1,0:T(2,128)(2,1)S(1)}, bf16[16,2,2,512]{3,2,1,0:T(2,128)(2,1)S(1)}, u32[]{:S(2)}, u32[]{:S(2)}) collective-permute-start(bf16[16,2,2,512]{3,2,1,0:T(2,128)(2,1)S(1)} %get-tuple-element.39), channel_id=1, source_target_pairs={{1,0},{2,1},{3,2},{4,3},{5,4},{6,5},{7,6},{8,7},{9,8},{10,9},{11,1... | collective-permute-start | bytes 196616 | tf_op jit(solution)/shard_map/ppermute | solution.py:373
  52.5 3.2 %collective-permute-start.6 = (bf16[2048,128]{1,0:T(8,128)(2,1)}, bf16[2048,128]{1,0:T(8,128)(2,1)}, u32[]{:S(2)}, u32[]{:S(2)}) collective-permute-start(bf16[2048,128]{1,0:T(8,128)(2,1)} %constant_dynamic-slice_fusion.1), channel_id=1, source_target_pairs={{0,256},{32,288},{64,320},{96,352},{128,384},{160,416},{192,448},{... | collective-permute-start | bytes 1572872 | tf_op jit(solution)/shard_map/ppermute | solution.py:384
  56.6 3.6 %collective-permute-start.7 = (bf16[96,2048]{1,0:T(8,128)(2,1)}, bf16[96,2048]{1,0:T(8,128)(2,1)}, u32[]{:S(2)}, u32[]{:S(2)}) collective-permute-start(bf16[96,2048]{1,0:T(8,128)(2,1)} %constant_dynamic-slice_fusion), channel_id=1, source_target_pairs={{0,256},{32,288},{64,320},{96,352},{128,384},{160,416},{192,448},{... | collective-permute-start | bytes 1179656 | tf_op jit(solution)/shard_map/ppermute | solution.py:384
  61.7 3.3 %shard_map.155.attended_ref = bf16[384,512]{1,0:T(8,128)(2,1)S(1)} custom-call(bf16[512,512]{1,0:T(8,128)(2,1)S(1)} %bitcast.29, bf16[64,512]{1,0:T(8,128)(2,1)S(1)} %reshape.74.left_ref, bf16[64,512]{1,0:T(8,128)(2,1)S(1)} %reshape.75.right_ref, f32[1,512]{1,0:T(1,128)S(1)} %bitcast.33, bf16[3,512,512]{2,1,0:T(8,128)(2,1)S(1)} %copy-done.24, ...), custom_call_target="tpu_custom_call" | custom-call | flops 1006632960 | bytes 2314752 | tf_op jit(solution)/shard_map/pallas_call | solution.py:20
  65.8 12.5 %all-gather.3.cloned.1.call-done.weights_ref = bf16[2,1280,640]{2,1,0:T(8,128)(2,1)} async-done(((bf16[2,160,640]{2,1,0:T(8,128)(2,1)}), bf16[2,1280,640]{2,1,0:T(8,128)(2,1)}) %all-gather.3.cloned.1.call-update) | async-done | bytes 3276816 | tf_op jit(solution)/shard_map/all_gather | solution.py:449
  84.9 2.6 %collective-permute-start.5 = (bf16[96,2048]{1,0:T(8,128)(2,1)}, bf16[96,2048]{1,0:T(8,128)(2,1)}, u32[]{:S(2)}, u32[]{:S(2)}) collective-permute-start(bf16[96,2048]{1,0:T(8,128)(2,1)} %get-tuple-element.25.own_ref), channel_id=1, source_target_pairs={{0,1},{1,0},{2,3},{3,2},{4,5},{5,4},{6,7},{7,6},{8,9},{9,8},{10,11... | collective-permute-start | bytes 1179656 | tf_op jit(solution)/shard_map/ppermute | solution.py:379
  89.5 2.4 %collective-permute-start.10 = (bf16[96,2048]{1,0:T(8,128)(2,1)}, bf16[96,2048]{1,0:T(8,128)(2,1)}, u32[]{:S(2)}, u32[]{:S(2)}) collective-permute-start(bf16[96,2048]{1,0:T(8,128)(2,1)} %collective-permute-done.7.mine_ref), channel_id=1, source_target_pairs={{0,1},{1,0},{2,3},{3,2},{4,5},{5,4},{6,7},{7,6},{8,9},{9,8},{10,11... | collective-permute-start | bytes 1179656 | tf_op jit(solution)/shard_map/ppermute | solution.py:379
  98.9 3.3 %collective-permute-start.12 = (bf16[24,4096]{1,0:T(8,128)(2,1)S(1)}, bf16[24,4096]{1,0:T(8,128)(2,1)S(1)}, u32[]{:S(2)}, u32[]{:S(2)}) collective-permute-start(bf16[24,4096]{1,0:T(8,128)(2,1)S(1)} %get-tuple-element.32.refs_0_), channel_id=1, source_target_pairs={{0,224},{32,0},{64,32},{96,64},{128,96},{160,128},{192,160},{224,1... | collective-permute-start | bytes 589832 | tf_op jit(solution)/shard_map/ppermute | solution.py:393
  104.3 2.9 %collective-permute-done.12.refs_2_ = bf16[24,4096]{1,0:T(8,128)(2,1)S(1)} collective-permute-done((bf16[24,4096]{1,0:T(8,128)(2,1)S(1)}, bf16[24,4096]{1,0:T(8,128)(2,1)S(1)}, u32[]{:S(2)}, u32[]{:S(2)}) %collective-permute-start.12) | collective-permute-done | bytes 196640 | tf_op jit(solution)/shard_map/ppermute | solution.py:393
  107.2 4.4 %collective-permute-start.14 = (bf16[24,4096]{1,0:T(8,128)(2,1)S(1)}, bf16[24,4096]{1,0:T(8,128)(2,1)S(1)}, u32[]{:S(2)}, u32[]{:S(2)}) collective-permute-start(bf16[24,4096]{1,0:T(8,128)(2,1)S(1)} %collective-permute-done.12.refs_2_), channel_id=1, source_target_pairs={{0,224},{32,0},{64,32},{96,64},{128,96},{160,128},{192,160},{224,1... | collective-permute-start | bytes 589832 | tf_op jit(solution)/shard_map/ppermute | solution.py:393
  114.8 5.4 %collective-permute-start.16 = (bf16[24,4096]{1,0:T(8,128)(2,1)S(1)}, bf16[24,4096]{1,0:T(8,128)(2,1)S(1)}, u32[]{:S(2)}, u32[]{:S(2)}) collective-permute-start(bf16[24,4096]{1,0:T(8,128)(2,1)S(1)} %collective-permute-done.14.refs_4_), channel_id=1, source_target_pairs={{0,224},{32,0},{64,32},{96,64},{128,96},{160,128},{192,160},{224,1... | collective-permute-start | bytes 589832 | tf_op jit(solution)/shard_map/ppermute | solution.py:393
  122.8 5.4 %collective-permute-start.18 = (bf16[24,2048]{1,0:T(8,128)(2,1)S(1)}, bf16[24,2048]{1,0:T(8,128)(2,1)S(1)}, u32[]{:S(2)}, u32[]{:S(2)}) collective-permute-start(bf16[24,2048]{1,0:T(8,128)(2,1)S(1)} %slice.31), channel_id=1, source_target_pairs={{0,224},{32,0},{64,32},{96,64},{128,96},{160,128},{192,160},{224,1... | collective-permute-start | bytes 294920 | tf_op jit(solution)/shard_map/ppermute | solution.py:393
  130.2 5.0 %collective-permute-done.17.refs_7_ = bf16[24,2048]{1,0:T(8,128)(2,1)S(1)} collective-permute-done((bf16[24,2048]{1,0:T(8,128)(2,1)S(1)}, bf16[24,2048]{1,0:T(8,128)(2,1)S(1)}, u32[]{:S(2)}, u32[]{:S(2)}) %collective-permute-start.17) | collective-permute-done | bytes 98336 | tf_op jit(solution)/shard_map/ppermute | solution.py:393
  136.5 2.5 %shard_map.159 = bf16[8,2,24,128]{3,2,1,0:T(8,128)(2,1)S(1)} custom-call(s32[3]{0:T(128)S(1)} %pad_add_fusion.1.core_ref.place_ref, bf16[24,4096]{1,0:T(8,128)(2,1)S(1)} %get-tuple-element.32.refs_0_, bf16[24,4096]{1,0:T(8,128)(2,1)S(1)} %collective-permute-done.11.refs_1_, bf16[24,4096]{1,0:T(8,128)(2,1)S(1)} %collective-permute-done.12.refs_2_, ...), custom_call_target="tpu_custom_call" | custom-call | flops 402653184 | bytes 3670028 | tf_op jit(solution)/shard_map/pallas_call | solution.py:20
  139.1 23.1 %all_to_all.10.x_ref = bf16[8,8,2,24,128]{4,3,2,1,0:T(8,128)(2,1)S(1)} all-to-all(bf16[8,8,2,24,128]{4,3,2,1,0:T(8,128)(2,1)S(1)} %broadcast_in_dim.46), channel_id=1, replica_groups={{0,32,64,96,128,160,192,224},{256,288,320,352,384,416,448,480},{1,33,65..., dimensions={0} | all-to-all | bytes 1572864 | tf_op jit(solution)/shard_map/all_to_all | solution.py:388
  163.3 3.8 %shard_map.160 = (bf16[8,2,24,64]{3,2,1,0:T(8,128)(2,1)S(1)}, f32[24,2048]{1,0:T(8,128)S(1)}) custom-call(s32[3]{0:T(128)S(1)} %pad_add_fusion.1.core_ref.place_ref, bf16[8,8,2,24,128]{4,3,2,1,0:T(8,128)(2,1)S(1)} %all_to_all.10.x_ref, f32[1,2048]{1,0:T(1,128)S(1)} %bitcast.32, bf16[192,2048]{1,0:T(8,128)(2,1)S(1)} %bitcast.26, ...), custom_call_target="tpu_custom_call" | custom-call | flops 301989888 | bytes 2367500 | tf_op jit(solution)/shard_map/pallas_call | solution.py:20
  167.2 7.5 %collective-permute-start.19 = (bf16[1152,16,128]{2,1,0:T(8,128)(2,1)}, bf16[1152,16,128]{2,1,0:T(8,128)(2,1)}, u32[]{:S(2)}, u32[]{:S(2)}) collective-permute-start(bf16[1152,16,128]{2,1,0:T(8,128)(2,1)} %bitcast.22), channel_id=1, source_target_pairs={{0,1},{1,0},{2,3},{3,2},{4,5},{5,4},{6,7},{7,6},{8,9},{9,8},{10,11... | collective-permute-start | bytes 14155784 | tf_op jit(solution)/shard_map/ppermute | solution.py:379
  174.8 9.4 %all_to_all.11 = bf16[8,2,1536]{2,1,0:T(2,128)(2,1)S(1)} all-to-all(bf16[8,2,1536]{2,1,0:T(2,128)(2,1)S(1)} %reshape.82), channel_id=1, replica_groups={{0,32,64,96,128,160,192,224},{256,288,320,352,384,416,448,480},{1,33,65..., dimensions={0} | all-to-all | bytes 98304 | tf_op jit(solution)/shard_map/all_to_all | solution.py:388
  184.3 2.3 %copy-done.3 = bf16[18432,128]{1,0:T(8,128)(2,1)S(1)} copy-done((bf16[18432,128]{1,0:T(8,128)(2,1)S(1)}, bf16[18432,128]{1,0:T(8,128)(2,1)}, u32[]{:S(2)}) %copy-start.3) | copy-done | bytes 4718616
  186.6 5.6 %shard_map.161 = bf16[384,512]{1,0:T(8,128)(2,1)} custom-call(s32[3]{0:T(128)S(1)} %pad_add_fusion.1.core_ref.place_ref, bf16[8,2,24,64]{3,2,1,0:T(8,128)(2,1)S(1)} %reshape.83.heads_ref, f32[24,2048]{1,0:T(8,128)S(1)} %get-tuple-element.34.own_coarse_ref, bf16[1152,16,128]{2,1,0:T(8,128)(2,1)S(1)} %bitcast.23, ...), custom_call_target="tpu_custom_call" | custom-call | flops 301989888 | bytes 10272780 | tf_op jit(solution)/shard_map/pallas_call | solution.py:20
  (117 shorter events, 46.4 us)
Async XLA Ops:
  6.5 71.7 %all-gather.3.cloned.1.call-start = ((), (), s32[]{:S(2)}) async-start(), calls=%async_computation.2 | async-start | bytes 3686400 | tf_op jit(solution)/shard_map/all_gather | solution.py:449
  11.9 8.6 %collective-permute-start = (bf16[1,160,640]{2,1,0:T(8,128)(2,1)S(1)}, bf16[1,160,640]{2,1,0:T(8,128)(2,1)S(1)}, u32[]{:S(2)}, u32[]{:S(2)}) collective-permute-start(bf16[1,160,640]{2,1,0:T(8,128)(2,1)S(1)} %bitcast.27), channel_id=1, source_target_pairs={{0,256},{32,288},{64,320},{96,352},{128,384},{160,416},{192,448},{... | collective-permute-start | bytes 614408 | tf_op jit(solution)/shard_map/ppermute | solution.py:384
  21.4 145.8 %all-gather.5.cloned.1.call-start = ((), (), s32[]{:S(2)}) async-start(), calls=%async_computation.3 | async-start | bytes 5308416 | tf_op jit(solution)/shard_map/all_gather | solution.py:538
  24.8 16.6 %collective-permute-start.1 = (bf16[2,2,16,512]{3,2,1,0:T(8,128)(2,1)S(1)}, bf16[2,2,16,512]{3,2,1,0:T(8,128)(2,1)S(1)}, u32[]{:S(2)}, u32[]{:S(2)}) collective-permute-start(bf16[2,2,16,512]{3,2,1,0:T(8,128)(2,1)S(1)} %get-tuple-element.42), channel_id=1, source_target_pairs={{0,32},{32,64},{64,96},{96,128},{128,160},{160,192},{192,224},{224... | collective-permute-start | bytes 196616 | tf_op jit(solution)/shard_map/ppermute | solution.py:372
  30.4 12.4 %collective-permute-start.2 = (bf16[2,2,16,512]{3,2,1,0:T(8,128)(2,1)S(1)}, bf16[2,2,16,512]{3,2,1,0:T(8,128)(2,1)S(1)}, u32[]{:S(2)}, u32[]{:S(2)}) collective-permute-start(bf16[2,2,16,512]{3,2,1,0:T(8,128)(2,1)S(1)} %get-tuple-element.41), channel_id=1, source_target_pairs={{32,0},{64,32},{96,64},{128,96},{160,128},{192,160},{224,192},{256... | collective-permute-start | bytes 196616 | tf_op jit(solution)/shard_map/ppermute | solution.py:373
  42.9 7.9 %collective-permute-start.4 = (bf16[16,2,2,512]{3,2,1,0:T(2,128)(2,1)S(1)}, bf16[16,2,2,512]{3,2,1,0:T(2,128)(2,1)S(1)}, u32[]{:S(2)}, u32[]{:S(2)}) collective-permute-start(bf16[16,2,2,512]{3,2,1,0:T(2,128)(2,1)S(1)} %get-tuple-element.39), channel_id=1, source_target_pairs={{1,0},{2,1},{3,2},{4,3},{5,4},{6,5},{7,6},{8,7},{9,8},{10,9},{11,1... | collective-permute-start | bytes 196616 | tf_op jit(solution)/shard_map/ppermute | solution.py:373
  48.3 3.4 %collective-permute-start.3 = (bf16[16,2,2,512]{3,2,1,0:T(2,128)(2,1)S(1)}, bf16[16,2,2,512]{3,2,1,0:T(2,128)(2,1)S(1)}, u32[]{:S(2)}, u32[]{:S(2)}) collective-permute-start(bf16[16,2,2,512]{3,2,1,0:T(2,128)(2,1)S(1)} %get-tuple-element.40), channel_id=1, source_target_pairs={{0,1},{1,2},{2,3},{3,4},{4,5},{5,6},{6,7},{7,8},{8,9},{9,10},{10,1... | collective-permute-start | bytes 196616 | tf_op jit(solution)/shard_map/ppermute | solution.py:372
  52.5 35.0 %collective-permute-start.6 = (bf16[2048,128]{1,0:T(8,128)(2,1)}, bf16[2048,128]{1,0:T(8,128)(2,1)}, u32[]{:S(2)}, u32[]{:S(2)}) collective-permute-start(bf16[2048,128]{1,0:T(8,128)(2,1)} %constant_dynamic-slice_fusion.1), channel_id=1, source_target_pairs={{0,256},{32,288},{64,320},{96,352},{128,384},{160,416},{192,448},{... | collective-permute-start | bytes 1572872 | tf_op jit(solution)/shard_map/ppermute | solution.py:384
  56.6 32.9 %collective-permute-start.7 = (bf16[96,2048]{1,0:T(8,128)(2,1)}, bf16[96,2048]{1,0:T(8,128)(2,1)}, u32[]{:S(2)}, u32[]{:S(2)}) collective-permute-start(bf16[96,2048]{1,0:T(8,128)(2,1)} %constant_dynamic-slice_fusion), channel_id=1, source_target_pairs={{0,256},{32,288},{64,320},{96,352},{128,384},{160,416},{192,448},{... | collective-permute-start | bytes 1179656 | tf_op jit(solution)/shard_map/ppermute | solution.py:384
  84.9 7.0 %collective-permute-start.5 = (bf16[96,2048]{1,0:T(8,128)(2,1)}, bf16[96,2048]{1,0:T(8,128)(2,1)}, u32[]{:S(2)}, u32[]{:S(2)}) collective-permute-start(bf16[96,2048]{1,0:T(8,128)(2,1)} %get-tuple-element.25.own_ref), channel_id=1, source_target_pairs={{0,1},{1,0},{2,3},{3,2},{4,5},{5,4},{6,7},{7,6},{8,9},{9,8},{10,11... | collective-permute-start | bytes 1179656 | tf_op jit(solution)/shard_map/ppermute | solution.py:379
  87.5 10.4 %collective-permute-start.9 = (bf16[2048,128]{1,0:T(8,128)(2,1)}, bf16[2048,128]{1,0:T(8,128)(2,1)}, u32[]{:S(2)}, u32[]{:S(2)}) collective-permute-start(bf16[2048,128]{1,0:T(8,128)(2,1)} %collective-permute-done.6.refs_10_), channel_id=1, source_target_pairs={{0,1},{1,0},{2,3},{3,2},{4,5},{5,4},{6,7},{7,6},{8,9},{9,8},{10,11... | collective-permute-start | bytes 1572872 | tf_op jit(solution)/shard_map/ppermute | solution.py:379
  89.5 8.4 %collective-permute-start.10 = (bf16[96,2048]{1,0:T(8,128)(2,1)}, bf16[96,2048]{1,0:T(8,128)(2,1)}, u32[]{:S(2)}, u32[]{:S(2)}) collective-permute-start(bf16[96,2048]{1,0:T(8,128)(2,1)} %collective-permute-done.7.mine_ref), channel_id=1, source_target_pairs={{0,1},{1,0},{2,3},{3,2},{4,5},{5,4},{6,7},{7,6},{8,9},{9,8},{10,11... | collective-permute-start | bytes 1179656 | tf_op jit(solution)/shard_map/ppermute | solution.py:379
  93.6 3.2 %collective-permute-start.8 = (bf16[96,512]{1,0:T(8,128)(2,1)S(1)}, bf16[96,512]{1,0:T(8,128)(2,1)S(1)}, u32[]{:S(2)}, u32[]{:S(2)}) collective-permute-start(bf16[96,512]{1,0:T(8,128)(2,1)S(1)} %get-tuple-element.30), channel_id=1, source_target_pairs={{0,1},{1,0},{2,3},{3,2},{4,5},{5,4},{6,7},{7,6},{8,9},{9,8},{10,11... | collective-permute-start | bytes 294920 | tf_op jit(solution)/shard_map/ppermute | solution.py:379
  98.8 85.4 %copy-start.11 = (bf16[384,512]{1,0:T(8,128)(2,1)S(1)}, bf16[384,512]{1,0:T(8,128)(2,1)}, u32[]{:S(2)}) copy-start(bf16[384,512]{1,0:T(8,128)(2,1)} %copy-done.10) | copy-start | bytes 1179652
  98.9 85.4 %copy-start.18 = (bf16[96,1024]{1,0:T(8,128)(2,1)S(1)}, bf16[96,1024]{1,0:T(8,128)(2,1)}, u32[]{:S(2)}) copy-start(bf16[96,1024]{1,0:T(8,128)(2,1)} %copy-done.17) | copy-start | bytes 589828
  98.9 8.4 %collective-permute-start.12 = (bf16[24,4096]{1,0:T(8,128)(2,1)S(1)}, bf16[24,4096]{1,0:T(8,128)(2,1)S(1)}, u32[]{:S(2)}, u32[]{:S(2)}) collective-permute-start(bf16[24,4096]{1,0:T(8,128)(2,1)S(1)} %get-tuple-element.32.refs_0_), channel_id=1, source_target_pairs={{0,224},{32,0},{64,32},{96,64},{128,96},{160,128},{192,160},{224,1... | collective-permute-start | bytes 589832 | tf_op jit(solution)/shard_map/ppermute | solution.py:393
  102.2 9.4 %collective-permute-start.11 = (bf16[24,4096]{1,0:T(8,128)(2,1)S(1)}, bf16[24,4096]{1,0:T(8,128)(2,1)S(1)}, u32[]{:S(2)}, u32[]{:S(2)}) collective-permute-start(bf16[24,4096]{1,0:T(8,128)(2,1)S(1)} %get-tuple-element.32.refs_0_), channel_id=1, source_target_pairs={{0,32},{32,64},{64,96},{96,128},{128,160},{160,192},{192,224},{224... | collective-permute-start | bytes 589832 | tf_op jit(solution)/shard_map/ppermute | solution.py:393
  107.2 7.6 %collective-permute-start.14 = (bf16[24,4096]{1,0:T(8,128)(2,1)S(1)}, bf16[24,4096]{1,0:T(8,128)(2,1)S(1)}, u32[]{:S(2)}, u32[]{:S(2)}) collective-permute-start(bf16[24,4096]{1,0:T(8,128)(2,1)S(1)} %collective-permute-done.12.refs_2_), channel_id=1, source_target_pairs={{0,224},{32,0},{64,32},{96,64},{128,96},{160,128},{192,160},{224,1... | collective-permute-start | bytes 589832 | tf_op jit(solution)/shard_map/ppermute | solution.py:393
  111.6 8.6 %collective-permute-start.13 = (bf16[24,4096]{1,0:T(8,128)(2,1)S(1)}, bf16[24,4096]{1,0:T(8,128)(2,1)S(1)}, u32[]{:S(2)}, u32[]{:S(2)}) collective-permute-start(bf16[24,4096]{1,0:T(8,128)(2,1)S(1)} %collective-permute-done.11.refs_1_), channel_id=1, source_target_pairs={{0,32},{32,64},{64,96},{96,128},{128,160},{160,192},{192,224},{224... | collective-permute-start | bytes 589832 | tf_op jit(solution)/shard_map/ppermute | solution.py:393
  114.8 8.0 %collective-permute-start.16 = (bf16[24,4096]{1,0:T(8,128)(2,1)S(1)}, bf16[24,4096]{1,0:T(8,128)(2,1)S(1)}, u32[]{:S(2)}, u32[]{:S(2)}) collective-permute-start(bf16[24,4096]{1,0:T(8,128)(2,1)S(1)} %collective-permute-done.14.refs_4_), channel_id=1, source_target_pairs={{0,224},{32,0},{64,32},{96,64},{128,96},{160,128},{192,160},{224,1... | collective-permute-start | bytes 589832 | tf_op jit(solution)/shard_map/ppermute | solution.py:393
  120.2 8.0 %collective-permute-start.15 = (bf16[24,4096]{1,0:T(8,128)(2,1)S(1)}, bf16[24,4096]{1,0:T(8,128)(2,1)S(1)}, u32[]{:S(2)}, u32[]{:S(2)}) collective-permute-start(bf16[24,4096]{1,0:T(8,128)(2,1)S(1)} %collective-permute-done.13.refs_3_), channel_id=1, source_target_pairs={{0,32},{32,64},{64,96},{96,128},{128,160},{160,192},{192,224},{224... | collective-permute-start | bytes 589832 | tf_op jit(solution)/shard_map/ppermute | solution.py:393
  122.8 7.4 %collective-permute-start.18 = (bf16[24,2048]{1,0:T(8,128)(2,1)S(1)}, bf16[24,2048]{1,0:T(8,128)(2,1)S(1)}, u32[]{:S(2)}, u32[]{:S(2)}) collective-permute-start(bf16[24,2048]{1,0:T(8,128)(2,1)S(1)} %slice.31), channel_id=1, source_target_pairs={{0,224},{32,0},{64,32},{96,64},{128,96},{160,128},{192,160},{224,1... | collective-permute-start | bytes 294920 | tf_op jit(solution)/shard_map/ppermute | solution.py:393
  128.3 7.0 %collective-permute-start.17 = (bf16[24,2048]{1,0:T(8,128)(2,1)S(1)}, bf16[24,2048]{1,0:T(8,128)(2,1)S(1)}, u32[]{:S(2)}, u32[]{:S(2)}) collective-permute-start(bf16[24,2048]{1,0:T(8,128)(2,1)S(1)} %slice.30), channel_id=1, source_target_pairs={{0,32},{32,64},{64,96},{96,128},{128,160},{160,192},{192,224},{224... | collective-permute-start | bytes 294920 | tf_op jit(solution)/shard_map/ppermute | solution.py:393
  167.2 17.1 %collective-permute-start.19 = (bf16[1152,16,128]{2,1,0:T(8,128)(2,1)}, bf16[1152,16,128]{2,1,0:T(8,128)(2,1)}, u32[]{:S(2)}, u32[]{:S(2)}) collective-permute-start(bf16[1152,16,128]{2,1,0:T(8,128)(2,1)} %bitcast.22), channel_id=1, source_target_pairs={{0,1},{1,0},{2,3},{3,2},{4,5},{5,4},{6,7},{7,6},{8,9},{9,8},{10,11... | collective-permute-start | bytes 14155784 | tf_op jit(solution)/shard_map/ppermute | solution.py:379
  (24 other events, 399.5 us)
Sparse Core Ops, SparseCore 0:
  21.5 56.7 all-gather.2
  99.0 59.6 all-gather.4

commit v7 on v6

--- a/solution.py
+++ b/solution.py
@@ -15,23 +15,31 @@
     return centred * lax.rsqrt(spread + 1e-05) * gain
 
 
-def call_kernel(body, out_shape, operands, scratch=(), flops=0):
-    smem = [operand.dtype == jnp.int32 for operand in operands]
+def call_kernel(body, out_shape, operands, scratch=(), flops=0, pulled=(), vmem_mib=48):
+    spaces = [
+        pltpu.SMEM if operand.dtype == jnp.int32 else pltpu.HBM if at in pulled else pltpu.VMEM
+        for at, operand in enumerate(operands)
+    ]
     return pl.pallas_call(
         body,
         out_shape=out_shape,
-        in_specs=[
-            pl.BlockSpec(memory_space=pltpu.SMEM if scalar else pltpu.VMEM) for scalar in smem
-        ],
+        in_specs=[pl.BlockSpec(memory_space=space) for space in spaces],
         out_specs=jax.tree.map(lambda _: pl.BlockSpec(memory_space=pltpu.VMEM), out_shape),
         scratch_shapes=list(scratch),
-        compiler_params=pltpu.CompilerParams(vmem_limit_bytes=48 * 1024 * 1024),
+        compiler_params=pltpu.CompilerParams(vmem_limit_bytes=vmem_mib * 1024 * 1024),
         cost_estimate=pl.CostEstimate(
             flops=flops,
             bytes_accessed=sum(operand.size * operand.dtype.itemsize for operand in operands),
             transcendentals=0,
         ),
     )(*operands)
+
+
+def pull(sems, *pairs):
+    copies = [pltpu.make_async_copy(src, dst, sems.at[at]) for at, (src, dst) in enumerate(pairs)]
+    for copy in copies:
+        copy.start()
+    return copies
 
 
 def dot_rows(left, right):
@@ -50,22 +58,38 @@
     )
 
 
-def pack_kernel(place_ref, merge_ref, first_ref, up_third_ref, up_second_ref, out_third_ref, out_ref):
+def pack_kernel(
+    place_ref, merge_ref, first_ref, up_third_ref, up_second_ref, out_third_ref, out_ref, sems
+):
     core, column = place_ref[0], place_ref[1]
-    out_ref[:128, :512] = merge_ref[:, pl.ds(pl.multiple_of(core * 512, 128), 512)]
-    out_ref[128:, :512] = first_ref[...]
     high, low = jnp.right_shift(column, 1), jnp.bitwise_and(column, 1)
-    rows = pl.ds(pl.multiple_of(high * 16, 16), 16)
+
+    def part(ref, row, lane, lanes=128, rows=16):
+        return ref.at[pl.ds(pl.multiple_of(row, 16), rows), pl.ds(pl.multiple_of(lane, 128), lanes)]
+
+    pairs = [
+        (part(merge_ref, 0, core * 512, 512, 128), out_ref.at[:128, :512]),
+        (first_ref, out_ref.at[128:, :512]),
+    ]
     for tile in range(4):
-        start = pl.multiple_of(core * 512 + tile * 128, 128)
-        out_ref[tile * 16 : tile * 16 + 16, 512:] = up_third_ref[
-            pl.ds(pl.multiple_of(column * 16, 16), 16), pl.ds(start, 128)
-        ]
-        start = pl.multiple_of(low * 1024 + core * 512 + tile * 128, 128)
-        out_ref[64 + tile * 16 : 80 + tile * 16, 512:] = out_third_ref[rows, pl.ds(start, 128)]
-    last = up_second_ref[rows, pl.ds(pl.multiple_of(core * 256 + low * 128, 128), 128)]
-    out_ref[128:144, 512:] = last
-    out_ref[144:, 512:] = last
+        pairs.append(
+            (
+                part(up_third_ref, column * 16, core * 512 + tile * 128),
+                out_ref.at[tile * 16 : tile * 16 + 16, 512:],
+            )
+        )
+        pairs.append(
+            (
+                part(out_third_ref, high * 16, low * 1024 + core * 512 + tile * 128),
+                out_ref.at[64 + tile * 16 : 80 + tile * 16, 512:],
+            )
+        )
+    for row in (128, 144):
+        pairs.append(
+            (part(up_second_ref, high * 16, core * 256 + low * 128), out_ref.at[row : row + 16, 512:])
+        )
+    for copy in pull(sems, *pairs):
+        copy.wait()
 
 
 def first_kernel(x_ref, left_ref, right_ref, gain_ref, qkv_ref, window_ref, lat_ref, out_ref):
@@ -132,12 +156,23 @@
         out_ref[:, here] = (part * scale * gain_ref[:, here]).astype(jnp.bfloat16)
 
 
-def skip_kernel(attended_ref, hidden_ref, weights_ref, gain_ref, skip_ref, merged_ref):
+def skip_kernel(
+    attended_ref, hidden_hbm, weights_hbm, gain_hbm, skip_ref, merged_ref,
+    hidden_ref, weights_ref, gain_ref, sems,
+):
+    copies = pull(
+        sems,
+        (weights_hbm.at[:, :, 128:160, :512], weights_ref),
+        (hidden_hbm, hidden_ref),
+        (gain_hbm, gain_ref),
+    )
+    for copy in copies:
+        copy.wait()
     total = None
     for ring in range(2):
         for z in range(0, 8, 4):
             right = jnp.concatenate(
-                [weights_ref[ring, zz * 160 + 128 : zz * 160 + 160, :512] for zz in range(z, z + 4)],
+                [weights_ref[ring, zz] for zz in range(z, z + 4)],
                 axis=0,
             )
             start = (ring * 8 + z) * 32
@@ -184,25 +219,35 @@
     )
 
 
-def columns_kernel(place_ref, *refs):
-    near, (far_low, far_high), (own_ref, *halves, out_ref) = refs[:7], refs[7:9], refs[9:]
-    rows, half = far_low.shape
+def near_kernel(place_ref, *refs):
+    near, (own_ref, *halves, out_ref) = refs[:7], refs[7:]
     left = jnp.concatenate([ref[...].astype(jnp.float32) for ref in near], axis=0)
     left = left.astype(jnp.bfloat16)
-    ring = place_ref[2]
-    own = own_ref[...]
-    for weights, shard in ((own, ring), (halves_in_order(place_ref[0], *halves), 1 - ring)):
+    rows = near[0].shape[0]
+    own, other = own_ref[...], halves_in_order(place_ref[0], *halves)
+    for weights, shard in ((own, place_ref[2]), (other, 1 - place_ref[2])):
         product = dot_rows(left, weights)
+        for at in range(len(near)):
+            out_ref[shard, at] = product[at * rows : (at + 1) * rows].astype(jnp.bfloat16)
+
+
+def far_kernel(place_ref, near_ref, low_ref, high_ref, own_ref, mine_ref, partner_ref, out_ref):
+    half = low_ref.shape[1]
+    own, other = own_ref[...], halves_in_order(place_ref[0], mine_ref, partner_ref)
+    for weights, shard in ((own, place_ref[2]), (other, 1 - place_ref[2])):
+        far = dot_rows(low_ref[...], weights[:half]) + dot_rows(high_ref[...], weights[half:])
+        out_ref[jnp.bitwise_and(place_ref[1] + 4, 7), shard] = far.astype(jnp.bfloat16)
+    for shard in range(2):
         for at, offset in enumerate(RING_ORDER):
             place = jnp.bitwise_and(place_ref[1] + (offset + 8), 7)
-            out_ref[place, shard] = product[at * rows : (at + 1) * rows].astype(jnp.bfloat16)
-        far = dot_rows(far_low[...], weights[:half]) + dot_rows(far_high[...], weights[half:])
-        out_ref[jnp.bitwise_and(place_ref[1] + 4, 7), shard] = far.astype(jnp.bfloat16)
+            out_ref[place, shard] = near_ref[shard, at]
 
 
 def third_kernel(
-    place_ref, x_ref, gain_ref, own_ref, mine_ref, partner_ref, out_ref, coarse_ref, normed_ref
+    place_ref, x_ref, gain_ref, own_hbm, mine_ref, partner_ref, out_ref, coarse_ref,
+    normed_ref, own_ref, sems,
 ):
+    (copy,) = pull(sems, (own_hbm, own_ref))
     blocks, places, shards, rows, width = x_ref.shape
     count = 1.0 / (blocks * shards * width)
     order = [(z, shard) for shard in range(shards) for z in range(blocks)]
@@ -231,6 +276,7 @@
     keep = jnp.right_shift(query_token, 5) == jnp.right_shift(key_token, 5)
     ring = place_ref[2]
     other = halves_in_order(place_ref[0], mine_ref, partner_ref)
+    copy.wait()
     for weights, shard in ((own_ref[...], ring), (other, 1 - ring)):
         triple = lax.dot_general(
             normed_ref[...],
@@ -293,7 +339,7 @@
                     axis=1,
                 ).astype(jnp.bfloat16)
             )
-    for weights_ref, origin in ((late_ref, core), (swapped_ref, 1 - core)):
+    for weights_ref, origin in ((swapped_ref, 1 - core), (late_ref, core)):
         for part in range(2):
             total = None
             for ring in range(2):
@@ -444,6 +490,9 @@
             up_second,
             out_third,
         ),
+        (pltpu.SemaphoreType.DMA((12,)),),
+        pulled=(1, 2, 3, 4, 5),
+        vmem_mib=62,
     )[None]
     both_merge = in_order(ring, own_merge, swap_rings(own_merge), 0)
     merge_weights = lax.all_gather(
@@ -505,36 +554,23 @@
             jax.ShapeDtypeStruct((tokens, feat_dim), jnp.bfloat16),
             jax.ShapeDtypeStruct((tokens // 4, 4 * feat_dim), jnp.bfloat16),
         ),
-        (attended, hidden.reshape(-1, feat_dim), merge_weights, norm_merge2[None]),
+        (
+            attended,
+            hidden.reshape(-1, feat_dim),
+            merge_weights.reshape(2, Z_RING, 160, 640),
+            norm_merge2[None],
+        ),
+        (
+            pltpu.VMEM((tokens, feat_dim), jnp.bfloat16),
+            pltpu.VMEM((2, Z_RING, 32, 512), jnp.bfloat16),
+            pltpu.VMEM((1, 4 * feat_dim), jnp.float32),
+            pltpu.SemaphoreType.DMA((3,)),
+        ),
         flops=2 * 384 * 512 * 512,
-    )
-    own_rows = merged_in.shape[0]
-    half_shape = jax.ShapeDtypeStruct((own_rows, 512), jnp.bfloat16)
-    merge_partner, qkv_partner = swap_cores(merge_mine), swap_cores(qkv_mine)
-    second_half, second_send = call_kernel(
-        merge_kernel,
-        (half_shape, half_shape),
-        (merged_in, after(swap_cores(merged_in), merge_mine, qkv_mine), merge_weights),
-        flops=2 * 192 * 2048 * 512,
-    )
-    second_cells, coarse_in = call_kernel(
-        join_kernel,
-        (
-            jax.ShapeDtypeStruct((own_rows, 1024), jnp.bfloat16),
-            jax.ShapeDtypeStruct((own_rows // 4, 4096), jnp.bfloat16),
-        ),
-        (core_place, second_half, swap_cores(second_send), norm_merge3[None]),
-        (pltpu.VMEM((2, own_rows, 512), jnp.bfloat16),),
-        flops=2 * 96 * 96 * 1024,
-    )
-    coarse_in = after(coarse_in, merge_partner, qkv_partner)
-    own_count = coarse_in.shape[0]
-
-    pieces, forth, back = [coarse_in], coarse_in, coarse_in
-    for _ in range(3):
-        forth, back = ring_shift(forth, 1), ring_shift(back, -1)
-        pieces += [forth, back]
-    late = after(merge_weights, coarse_in).reshape(2, Z_RING, 10, 16, 640)[:, :, :9, :, 512:]
+        pulled=(1, 2, 3),
+        vmem_mib=58,
+    )
+    late = after(merge_weights, merged_in).reshape(2, Z_RING, 10, 16, 640)[:, :, :9, :, 512:]
     late = lax.all_gather(
         late.reshape(-1, 128),
         "lon",
@@ -542,13 +578,47 @@
         axis_index_groups=[[4 * y + x for y in range(8)] for x in range(4)],
         tiled=True,
     ).reshape(-1, 16, 128)
+    own_rows = merged_in.shape[0]
+    half_shape = jax.ShapeDtypeStruct((own_rows, 512), jnp.bfloat16)
+    second_half, second_send = call_kernel(
+        merge_kernel,
+        (half_shape, half_shape),
+        (merged_in, after(swap_cores(merged_in), merge_mine, qkv_mine), merge_weights),
+        flops=2 * 192 * 2048 * 512,
+    )
+    second_cells, coarse_in = call_kernel(
+        join_kernel,
+        (
+            jax.ShapeDtypeStruct((own_rows, 1024), jnp.bfloat16),
+            jax.ShapeDtypeStruct((own_rows // 4, 4096), jnp.bfloat16),
+        ),
+        (core_place, second_half, swap_cores(second_send), norm_merge3[None]),
+        (pltpu.VMEM((2, own_rows, 512), jnp.bfloat16),),
+        flops=2 * 96 * 96 * 1024,
+    )
+    own_count = coarse_in.shape[0]
+
+    pieces, forth, back = [coarse_in], coarse_in, coarse_in
+    for _ in range(3):
+        forth, back = ring_shift(forth, 1), ring_shift(back, -1)
+        pieces += [forth, back]
+    merge_mine, qkv_mine = after(merge_mine, pieces[1]), after(qkv_mine, pieces[3])
+    merge_partner, qkv_partner = swap_cores(merge_mine), swap_cores(qkv_mine)
     half_feats = coarse_in.shape[1] // 2
-    pieces += [ring_shift(forth[:, :half_feats], 1), ring_shift(back[:, half_feats:], -1)]
+    forth, back = after(forth, merge_partner), after(back, qkv_partner)
+    far_low, far_high = ring_shift(forth[:, :half_feats], 1), ring_shift(back[:, half_feats:], -1)
+    tables = (merge_third, merge_mine, merge_partner)
+    near = call_kernel(
+        near_kernel,
+        jax.ShapeDtypeStruct((2, len(RING_ORDER), own_count, 128), jnp.bfloat16),
+        (core_place, *pieces, *tables),
+        flops=2 * 168 * 4096 * 256,
+    )
     column_block = call_kernel(
-        columns_kernel,
+        far_kernel,
         jax.ShapeDtypeStruct((Z_RING, 2, own_count, 128), jnp.bfloat16),
-        (core_place, *pieces, merge_third, merge_mine, merge_partner),
-        flops=2 * 192 * 4096 * 256,
+        (core_place, near, far_low, far_high, *tables),
+        flops=2 * 24 * 4096 * 256,
     )
     heads_out, own_coarse = call_kernel(
         third_kernel,
@@ -557,8 +627,13 @@
             jax.ShapeDtypeStruct((own_count, 2048), jnp.float32),
         ),
         (core_place, ring_gather(column_block), norm_third[None], qkv_third, qkv_mine, qkv_partner),
-        (pltpu.VMEM((Z_RING * own_count, 2048), jnp.bfloat16),),
+        (
+            pltpu.VMEM((Z_RING * own_count, 2048), jnp.bfloat16),
+            pltpu.VMEM(qkv_third.shape, jnp.bfloat16),
+            pltpu.SemaphoreType.DMA((1,)),
+        ),
         flops=2 * 192 * 2048 * 384,
+        pulled=(3,),
     )
 
     late_swapped = swap_cores(after(late, heads_out))

time: 200 us -> 220 us (1.10)
  waiting for transfers between devices: 29.2 us -> 47.5 us
  local copies, waits for them, and re-layouts: 19.9 us -> 10.9 us
  Pallas kernels: 20.3 us -> 26 us
  starting transfers between devices: 79 us -> 81.8 us
    ppermute x3, waiting for transfers between devices: 3.12 us -> 16.5 us  [swap_rings(): lax.ppermute(values, 'lat', [(i, (i + Z_RING) % count) for i in range(cou...]
    unnamed x56 -> x30, local copies, waits for them, and re-layouts: 16.6 us -> 4.4 us
    all_gather x1, waiting for transfers between devices: 12.5 us -> 22.5 us  [on_device(): lax.all_gather(both_merge, 'lat', axis=1, axis_index_groups=RINGS, tiled=...]
    pallas_call x8 -> x9, Pallas kernels: 20.3 us -> 26 us  [call_kernel(): pl.pallas_call(body, out_shape=out_shape, in_specs=[pl.BlockSpec(memory_s...]
    ppermute x8, waiting for transfers between devices: 9.91 us -> 5.27 us  [ring_shift(): return lax.ppermute(values, 'lat', pairs)]
  transfers between devices with their start and end apart: 22 -> 22, of which waited for: 10 -> 9; matrix products, arithmetic and copies ran while one was open for 3% -> 4% of each run, Pallas kernels for 7% -> 6%
where the time goes in v7:
time: 220 us; the launch traced here: 219 us
  starting transfers between devices  81.8 us (37%)
  waiting for transfers between devices  47.5 us (22%)
  blocking collectives  32.9 us (15%)
  Pallas kernels  26 us (12%)
  between operations  14 us (6%)
  local copies, waits for them, and re-layouts  10.9 us (5%)
  other arithmetic  4.59 us (2%)
    all_to_all x2, blocking collectives, ring_scatter(): lax.all_to_all(blocks, 'lat', 0, 0, axis_index_groups=RINGS, tiled=True)  32.9 us
    ppermute x8, starting transfers between devices, ring_shift(): return lax.ppermute(values, 'lat', pairs)  26.9 us
    pallas_call x9, Pallas kernels, call_kernel(): pl.pallas_call(body, out_shape=out_shape, in_specs=[pl.BlockSpec(memory_s...  26 us
    all_gather x1, waiting for transfers between devices, on_device(): lax.all_gather(both_merge, 'lat', axis=1, axis_index_groups=RINGS, tiled=...  22.5 us
    ppermute x5, starting transfers between devices, swap_cores(): return lax.ppermute(values, 'lon', [(i, i ^ 1) for i in range(count)])  18.4 us
    ppermute x3, waiting for transfers between devices, swap_rings(): lax.ppermute(values, 'lat', [(i, (i + Z_RING) % count) for i in range(cou...  16.5 us
    ppermute x2, starting transfers between devices, neighbours(): lax.ppermute(first, axis, [((i + 1) % count, i) for i in range(count)])  16.4 us
    ppermute x3, starting transfers between devices, swap_rings(): lax.ppermute(values, 'lat', [(i, (i + Z_RING) % count) for i in range(cou...  12.2 us
  transfers between devices with their start and end apart: 22, of which 9 were waited for; matrix products, arithmetic and copies ran while one was open for 4% of the time, Pallas kernels for 6%

profile of v7, /device:TPU:1, one launch (start us, length us, event | category | flops | bytes accessed | tf_op | source)
XLA Modules:
  0.0 218.6 jit_solution(10270059448367858737)
XLA Ops:
  9.5 5.5 %collective-permute-start = (bf16[1,160,640]{2,1,0:T(8,128)(2,1)}, bf16[1,160,640]{2,1,0:T(8,128)(2,1)S(1)}, u32[]{:S(2)}, u32[]{:S(2)}) collective-permute-start(bf16[1,160,640]{2,1,0:T(8,128)(2,1)} %bitcast.34), channel_id=1, source_target_pairs={{0,256},{32,288},{64,320},{96,352},{128,384},{160,416},{192,448},{... | collective-permute-start | bytes 614408 | tf_op jit(solution)/shard_map/ppermute | solution.py:430
  15.1 3.3 %collective-permute-done = bf16[1,160,640]{2,1,0:T(8,128)(2,1)S(1)} collective-permute-done((bf16[1,160,640]{2,1,0:T(8,128)(2,1)}, bf16[1,160,640]{2,1,0:T(8,128)(2,1)S(1)}, u32[]{:S(2)}, u32[]{:S(2)}) %collective-permute-start) | collective-permute-done | bytes 204832 | tf_op jit(solution)/shard_map/ppermute | solution.py:430
  23.3 5.6 %collective-permute-start.1 = (bf16[2,2,16,512]{3,2,1,0:T(8,128)(2,1)S(1)}, bf16[2,2,16,512]{3,2,1,0:T(8,128)(2,1)S(1)}, u32[]{:S(2)}, u32[]{:S(2)}) collective-permute-start(bf16[2,2,16,512]{3,2,1,0:T(8,128)(2,1)S(1)} %get-tuple-element.48), channel_id=1, source_target_pairs={{0,32},{32,64},{64,96},{96,128},{128,160},{160,192},{192,224},{224... | collective-permute-start | bytes 196616 | tf_op jit(solution)/shard_map/ppermute | solution.py:418
  29.2 11.0 %collective-permute-start.2 = (bf16[2,2,16,512]{3,2,1,0:T(8,128)(2,1)S(1)}, bf16[2,2,16,512]{3,2,1,0:T(8,128)(2,1)S(1)}, u32[]{:S(2)}, u32[]{:S(2)}) collective-permute-start(bf16[2,2,16,512]{3,2,1,0:T(8,128)(2,1)S(1)} %get-tuple-element.47), channel_id=1, source_target_pairs={{32,0},{64,32},{96,64},{128,96},{160,128},{192,160},{224,192},{256... | collective-permute-start | bytes 196616 | tf_op jit(solution)/shard_map/ppermute | solution.py:419
  41.7 5.3 %collective-permute-start.4 = (bf16[16,2,2,512]{3,2,1,0:T(2,128)(2,1)S(1)}, bf16[16,2,2,512]{3,2,1,0:T(2,128)(2,1)S(1)}, u32[]{:S(2)}, u32[]{:S(2)}) collective-permute-start(bf16[16,2,2,512]{3,2,1,0:T(2,128)(2,1)S(1)} %get-tuple-element.45), channel_id=1, source_target_pairs={{1,0},{2,1},{3,2},{4,3},{5,4},{6,5},{7,6},{8,7},{9,8},{10,9},{11,1... | collective-permute-start | bytes 196616 | tf_op jit(solution)/shard_map/ppermute | solution.py:419
  50.6 3.3 %shard_map.155.attended_ref = bf16[384,512]{1,0:T(8,128)(2,1)S(1)} custom-call(bf16[512,512]{1,0:T(8,128)(2,1)S(1)} %bitcast.28, bf16[64,512]{1,0:T(8,128)(2,1)S(1)} %reshape.77.left_ref, bf16[64,512]{1,0:T(8,128)(2,1)S(1)} %reshape.78.right_ref, f32[1,512]{1,0:T(1,128)S(1)} %bitcast.31, bf16[3,512,512]{2,1,0:T(8,128)(2,1)S(1)} %copy-done.10, ...), custom_call_target="tpu_custom_call" | custom-call | flops 1006632960 | bytes 2314752 | tf_op jit(solution)/shard_map/pallas_call | solution.py:23
  54.7 22.5 %all-gather.3.cloned.1.call-done.weights_ref = bf16[2,1280,640]{2,1,0:T(8,128)(2,1)} async-done(((bf16[2,160,640]{2,1,0:T(8,128)(2,1)}), bf16[2,1280,640]{2,1,0:T(8,128)(2,1)}) %all-gather.3.cloned.1.call-update) | async-done | bytes 3276816 | tf_op jit(solution)/shard_map/all_gather | solution.py:498
  77.2 4.3 %shard_map.156 = (bf16[384,512]{1,0:T(8,128)(2,1)}, bf16[96,2048]{1,0:T(8,128)(2,1)}) custom-call(bf16[384,512]{1,0:T(8,128)(2,1)} %copy-done.7, bf16[384,512]{1,0:T(8,128)(2,1)} %bitcast.32, bf16[2,8,160,640]{3,2,1,0:T(8,128)(2,1)} %bitcast.22, f32[1,2048]{1,0:T(1,128)} %bitcast.36), custom_call_target="tpu_custom_call" | custom-call | flops 201326592 | bytes 4071424 | tf_op jit(solution)/shard_map/pallas_call | solution.py:23
  85.5 4.6 %collective-permute-start.6 = (bf16[2048,128]{1,0:T(8,128)(2,1)}, bf16[2048,128]{1,0:T(8,128)(2,1)}, u32[]{:S(2)}, u32[]{:S(2)}) collective-permute-start(bf16[2048,128]{1,0:T(8,128)(2,1)} %constant_dynamic-slice_fusion.1), channel_id=1, source_target_pairs={{0,256},{32,288},{64,320},{96,352},{128,384},{160,416},{192,448},{... | collective-permute-start | bytes 1572872 | tf_op jit(solution)/shard_map/ppermute | solution.py:430
  94.0 3.1 %collective-permute-start.5 = (bf16[96,2048]{1,0:T(8,128)(2,1)}, bf16[96,2048]{1,0:T(8,128)(2,1)}, u32[]{:S(2)}, u32[]{:S(2)}) collective-permute-start(bf16[96,2048]{1,0:T(8,128)(2,1)} %get-tuple-element.28.own_ref), channel_id=1, source_target_pairs={{0,1},{1,0},{2,3},{3,2},{4,5},{5,4},{6,7},{7,6},{8,9},{9,8},{10,11... | collective-permute-start | bytes 1179656 | tf_op jit(solution)/shard_map/ppermute | solution.py:425
  97.2 13.2 %collective-permute-done.7.mine_ref = bf16[96,2048]{1,0:T(8,128)(2,1)} collective-permute-done((bf16[96,2048]{1,0:T(8,128)(2,1)}, bf16[96,2048]{1,0:T(8,128)(2,1)}, u32[]{:S(2)}, u32[]{:S(2)}) %collective-permute-start.7) | collective-permute-done | bytes 393248 | tf_op jit(solution)/shard_map/ppermute | solution.py:430
  113.0 3.6 %collective-permute-start.8 = (bf16[96,512]{1,0:T(8,128)(2,1)S(1)}, bf16[96,512]{1,0:T(8,128)(2,1)S(1)}, u32[]{:S(2)}, u32[]{:S(2)}) collective-permute-start(bf16[96,512]{1,0:T(8,128)(2,1)S(1)} %get-tuple-element.33), channel_id=1, source_target_pairs={{0,1},{1,0},{2,3},{3,2},{4,5},{5,4},{6,7},{7,6},{8,9},{9,8},{10,11... | collective-permute-start | bytes 294920 | tf_op jit(solution)/shard_map/ppermute | solution.py:425
  120.5 4.6 %collective-permute-start.10 = (bf16[24,4096]{1,0:T(8,128)(2,1)S(1)}, bf16[24,4096]{1,0:T(8,128)(2,1)S(1)}, u32[]{:S(2)}, u32[]{:S(2)}) collective-permute-start(bf16[24,4096]{1,0:T(8,128)(2,1)S(1)} %get-tuple-element.34.refs_0_), channel_id=1, source_target_pairs={{0,224},{32,0},{64,32},{96,64},{128,96},{160,128},{192,160},{224,1... | collective-permute-start | bytes 589832 | tf_op jit(solution)/shard_map/ppermute | solution.py:439
  125.1 2.8 %collective-permute-done.9.refs_1_ = bf16[24,4096]{1,0:T(8,128)(2,1)S(1)} collective-permute-done((bf16[24,4096]{1,0:T(8,128)(2,1)S(1)}, bf16[24,4096]{1,0:T(8,128)(2,1)S(1)}, u32[]{:S(2)}, u32[]{:S(2)}) %collective-permute-start.9) | collective-permute-done | bytes 196640 | tf_op jit(solution)/shard_map/ppermute | solution.py:439
  129.8 3.0 %collective-permute-start.15 = (bf16[2048,128]{1,0:T(8,128)(2,1)}, bf16[2048,128]{1,0:T(8,128)(2,1)S(1)}, u32[]{:S(2)}, u32[]{:S(2)}) collective-permute-start(bf16[2048,128]{1,0:T(8,128)(2,1)} %collective-permute-done.6.refs_8_.mine_ref), channel_id=1, source_target_pairs={{0,1},{1,0},{2,3},{3,2},{4,5},{5,4},{6,7},{7,6},{8,9},{9,8},{10,11... | collective-permute-start | bytes 1572872 | tf_op jit(solution)/shard_map/ppermute | solution.py:425
  132.9 4.9 %collective-permute-start.12 = (bf16[24,4096]{1,0:T(8,128)(2,1)S(1)}, bf16[24,4096]{1,0:T(8,128)(2,1)S(1)}, u32[]{:S(2)}, u32[]{:S(2)}) collective-permute-start(bf16[24,4096]{1,0:T(8,128)(2,1)S(1)} %collective-permute-done.10.refs_2_), channel_id=1, source_target_pairs={{0,224},{32,0},{64,32},{96,64},{128,96},{160,128},{192,160},{224,1... | collective-permute-start | bytes 589832 | tf_op jit(solution)/shard_map/ppermute | solution.py:439
  137.7 2.5 %collective-permute-start.17 = (bf16[96,2048]{1,0:T(8,128)(2,1)}, bf16[96,2048]{1,0:T(8,128)(2,1)S(1)}, u32[]{:S(2)}, u32[]{:S(2)}) collective-permute-start(bf16[96,2048]{1,0:T(8,128)(2,1)} %collective-permute-done.7.mine_ref), channel_id=1, source_target_pairs={{0,1},{1,0},{2,3},{3,2},{4,5},{5,4},{6,7},{7,6},{8,9},{9,8},{10,11... | collective-permute-start | bytes 1179656 | tf_op jit(solution)/shard_map/ppermute | solution.py:425
  142.2 5.2 %collective-permute-start.14 = (bf16[24,4096]{1,0:T(8,128)(2,1)S(1)}, bf16[24,4096]{1,0:T(8,128)(2,1)S(1)}, u32[]{:S(2)}, u32[]{:S(2)}) collective-permute-start(bf16[24,4096]{1,0:T(8,128)(2,1)S(1)} %collective-permute-done.12.refs_4_), channel_id=1, source_target_pairs={{0,224},{32,0},{64,32},{96,64},{128,96},{160,128},{192,160},{224,1... | collective-permute-start | bytes 589832 | tf_op jit(solution)/shard_map/ppermute | solution.py:439
  151.9 4.6 %collective-permute-start.18 = (bf16[24,2048]{1,0:T(8,128)(2,1)S(1)}, bf16[24,2048]{1,0:T(8,128)(2,1)S(1)}, u32[]{:S(2)}, u32[]{:S(2)}) collective-permute-start(bf16[24,2048]{1,0:T(8,128)(2,1)S(1)} %slice.26), channel_id=1, source_target_pairs={{0,224},{32,0},{64,32},{96,64},{128,96},{160,128},{192,160},{224,1... | collective-permute-start | bytes 294920 | tf_op jit(solution)/shard_map/ppermute | solution.py:439
  160.4 23.6 %all_to_all.10.x_ref = bf16[8,8,2,24,128]{4,3,2,1,0:T(8,128)(2,1)S(1)} all-to-all(bf16[8,8,2,24,128]{4,3,2,1,0:T(8,128)(2,1)S(1)} %broadcast_in_dim.46), channel_id=1, replica_groups={{0,32,64,96,128,160,192,224},{256,288,320,352,384,416,448,480},{1,33,65..., dimensions={0} | all-to-all | bytes 1572864 | tf_op jit(solution)/shard_map/all_to_all | solution.py:434
  184.0 4.0 %shard_map.161 = (bf16[8,2,24,64]{3,2,1,0:T(8,128)(2,1)S(1)}, f32[24,2048]{1,0:T(8,128)S(1)}) custom-call(s32[3]{0:T(128)S(1)} %pad_add_fusion.1.core_ref.place_ref, bf16[8,8,2,24,128]{4,3,2,1,0:T(8,128)(2,1)S(1)} %all_to_all.10.x_ref, f32[1,2048]{1,0:T(1,128)S(1)} %bitcast.30, bf16[192,2048]{1,0:T(8,128)(2,1)S(1)} %bitcast.27, ...), custom_call_target="tpu_custom_call" | custom-call | flops 301989888 | bytes 2367500 | tf_op jit(solution)/shard_map/pallas_call | solution.py:23
  188.0 6.2 %collective-permute-start.19 = (bf16[1152,16,128]{2,1,0:T(8,128)(2,1)}, bf16[1152,16,128]{2,1,0:T(8,128)(2,1)}, u32[]{:S(2)}, u32[]{:S(2)}) collective-permute-start(bf16[1152,16,128]{2,1,0:T(8,128)(2,1)} %bitcast.24), channel_id=1, source_target_pairs={{0,1},{1,0},{2,3},{3,2},{4,5},{5,4},{6,7},{7,6},{8,9},{9,8},{10,11... | collective-permute-start | bytes 14155784 | tf_op jit(solution)/shard_map/ppermute | solution.py:425
  194.3 9.4 %all_to_all.11 = bf16[8,2,1536]{2,1,0:T(2,128)(2,1)S(1)} all-to-all(bf16[8,2,1536]{2,1,0:T(2,128)(2,1)S(1)} %reshape.86), channel_id=1, replica_groups={{0,32,64,96,128,160,192,224},{256,288,320,352,384,416,448,480},{1,33,65..., dimensions={0} | all-to-all | bytes 98304 | tf_op jit(solution)/shard_map/all_to_all | solution.py:434
  206.2 5.6 %shard_map.162 = bf16[384,512]{1,0:T(8,128)(2,1)} custom-call(s32[3]{0:T(128)S(1)} %pad_add_fusion.1.core_ref.place_ref, bf16[8,2,24,64]{3,2,1,0:T(8,128)(2,1)S(1)} %reshape.87.heads_ref, f32[24,2048]{1,0:T(8,128)S(1)} %get-tuple-element.40.own_coarse_ref, bf16[1152,16,128]{2,1,0:T(8,128)(2,1)S(1)} %bitcast.25, ...), custom_call_target="tpu_custom_call" | custom-call | flops 301989888 | bytes 10272780 | tf_op jit(solution)/shard_map/pallas_call | solution.py:23
  (92 shorter events, 43.0 us)
Async XLA Ops:
  6.5 70.7 %all-gather.3.cloned.1.call-start = ((), (), s32[]{:S(2)}) async-start(), calls=%async_computation.2 | async-start | bytes 3686400 | tf_op jit(solution)/shard_map/all_gather | solution.py:498
  9.5 8.8 %collective-permute-start = (bf16[1,160,640]{2,1,0:T(8,128)(2,1)}, bf16[1,160,640]{2,1,0:T(8,128)(2,1)S(1)}, u32[]{:S(2)}, u32[]{:S(2)}) collective-permute-start(bf16[1,160,640]{2,1,0:T(8,128)(2,1)} %bitcast.34), channel_id=1, source_target_pairs={{0,256},{32,288},{64,320},{96,352},{128,384},{160,416},{192,448},{... | collective-permute-start | bytes 614408 | tf_op jit(solution)/shard_map/ppermute | solution.py:430
  20.3 167.8 %all-gather.5.cloned.1.call-start = ((), (), s32[]{:S(2)}) async-start(), calls=%async_computation.3 | async-start | bytes 5308416 | tf_op jit(solution)/shard_map/all_gather | solution.py:574
  23.3 16.9 %collective-permute-start.1 = (bf16[2,2,16,512]{3,2,1,0:T(8,128)(2,1)S(1)}, bf16[2,2,16,512]{3,2,1,0:T(8,128)(2,1)S(1)}, u32[]{:S(2)}, u32[]{:S(2)}) collective-permute-start(bf16[2,2,16,512]{3,2,1,0:T(8,128)(2,1)S(1)} %get-tuple-element.48), channel_id=1, source_target_pairs={{0,32},{32,64},{64,96},{96,128},{128,160},{160,192},{192,224},{224... | collective-permute-start | bytes 196616 | tf_op jit(solution)/shard_map/ppermute | solution.py:418
  29.2 12.4 %collective-permute-start.2 = (bf16[2,2,16,512]{3,2,1,0:T(8,128)(2,1)S(1)}, bf16[2,2,16,512]{3,2,1,0:T(8,128)(2,1)S(1)}, u32[]{:S(2)}, u32[]{:S(2)}) collective-permute-start(bf16[2,2,16,512]{3,2,1,0:T(8,128)(2,1)S(1)} %get-tuple-element.47), channel_id=1, source_target_pairs={{32,0},{64,32},{96,64},{128,96},{160,128},{192,160},{224,192},{256... | collective-permute-start | bytes 196616 | tf_op jit(solution)/shard_map/ppermute | solution.py:419
  41.7 8.0 %collective-permute-start.4 = (bf16[16,2,2,512]{3,2,1,0:T(2,128)(2,1)S(1)}, bf16[16,2,2,512]{3,2,1,0:T(2,128)(2,1)S(1)}, u32[]{:S(2)}, u32[]{:S(2)}) collective-permute-start(bf16[16,2,2,512]{3,2,1,0:T(2,128)(2,1)S(1)} %get-tuple-element.45), channel_id=1, source_target_pairs={{1,0},{2,1},{3,2},{4,3},{5,4},{6,5},{7,6},{8,7},{9,8},{10,9},{11,1... | collective-permute-start | bytes 196616 | tf_op jit(solution)/shard_map/ppermute | solution.py:419
  47.0 3.6 %collective-permute-start.3 = (bf16[16,2,2,512]{3,2,1,0:T(2,128)(2,1)S(1)}, bf16[16,2,2,512]{3,2,1,0:T(2,128)(2,1)S(1)}, u32[]{:S(2)}, u32[]{:S(2)}) collective-permute-start(bf16[16,2,2,512]{3,2,1,0:T(2,128)(2,1)S(1)} %get-tuple-element.46), channel_id=1, source_target_pairs={{0,1},{1,2},{2,3},{3,4},{4,5},{5,6},{6,7},{7,8},{8,9},{9,10},{10,1... | collective-permute-start | bytes 196616 | tf_op jit(solution)/shard_map/ppermute | solution.py:418
  85.5 24.9 %collective-permute-start.6 = (bf16[2048,128]{1,0:T(8,128)(2,1)}, bf16[2048,128]{1,0:T(8,128)(2,1)}, u32[]{:S(2)}, u32[]{:S(2)}) collective-permute-start(bf16[2048,128]{1,0:T(8,128)(2,1)} %constant_dynamic-slice_fusion.1), channel_id=1, source_target_pairs={{0,256},{32,288},{64,320},{96,352},{128,384},{160,416},{192,448},{... | collective-permute-start | bytes 1572872 | tf_op jit(solution)/shard_map/ppermute | solution.py:430
  91.8 18.5 %collective-permute-start.7 = (bf16[96,2048]{1,0:T(8,128)(2,1)}, bf16[96,2048]{1,0:T(8,128)(2,1)}, u32[]{:S(2)}, u32[]{:S(2)}) collective-permute-start(bf16[96,2048]{1,0:T(8,128)(2,1)} %constant_dynamic-slice_fusion), channel_id=1, source_target_pairs={{0,256},{32,288},{64,320},{96,352},{128,384},{160,416},{192,448},{... | collective-permute-start | bytes 1179656 | tf_op jit(solution)/shard_map/ppermute | solution.py:430
  94.0 16.4 %collective-permute-start.5 = (bf16[96,2048]{1,0:T(8,128)(2,1)}, bf16[96,2048]{1,0:T(8,128)(2,1)}, u32[]{:S(2)}, u32[]{:S(2)}) collective-permute-start(bf16[96,2048]{1,0:T(8,128)(2,1)} %get-tuple-element.28.own_ref), channel_id=1, source_target_pairs={{0,1},{1,0},{2,3},{3,2},{4,5},{5,4},{6,7},{7,6},{8,9},{9,8},{10,11... | collective-permute-start | bytes 1179656 | tf_op jit(solution)/shard_map/ppermute | solution.py:425
  113.0 71.0 %copy-start.4 = (bf16[3,2048,64]{1,2,0:T(8,128)(2,1)S(1)}, bf16[3,2048,64]{1,2,0:T(8,128)(2,1)}, u32[]{:S(2)}) copy-start(bf16[3,2048,64]{1,2,0:T(8,128)(2,1)} %param.28) | copy-start | bytes 2359300
  113.0 71.0 %copy-start.9 = (f32[2048]{0:T(1024)S(1)}, f32[2048]{0:T(1024)}, u32[]{:S(2)}) copy-start(f32[2048]{0:T(1024)} %param.27) | copy-start | bytes 24580
  113.0 4.5 %collective-permute-start.8 = (bf16[96,512]{1,0:T(8,128)(2,1)S(1)}, bf16[96,512]{1,0:T(8,128)(2,1)S(1)}, u32[]{:S(2)}, u32[]{:S(2)}) collective-permute-start(bf16[96,512]{1,0:T(8,128)(2,1)S(1)} %get-tuple-element.33), channel_id=1, source_target_pairs={{0,1},{1,0},{2,3},{3,2},{4,5},{5,4},{6,7},{7,6},{8,9},{9,8},{10,11... | collective-permute-start | bytes 294920 | tf_op jit(solution)/shard_map/ppermute | solution.py:425
  118.6 9.3 %collective-permute-start.9 = (bf16[24,4096]{1,0:T(8,128)(2,1)S(1)}, bf16[24,4096]{1,0:T(8,128)(2,1)S(1)}, u32[]{:S(2)}, u32[]{:S(2)}) collective-permute-start(bf16[24,4096]{1,0:T(8,128)(2,1)S(1)} %get-tuple-element.34.refs_0_), channel_id=1, source_target_pairs={{0,32},{32,64},{64,96},{96,128},{128,160},{160,192},{192,224},{224... | collective-permute-start | bytes 589832 | tf_op jit(solution)/shard_map/ppermute | solution.py:439
  120.5 12.3 %collective-permute-start.10 = (bf16[24,4096]{1,0:T(8,128)(2,1)S(1)}, bf16[24,4096]{1,0:T(8,128)(2,1)S(1)}, u32[]{:S(2)}, u32[]{:S(2)}) collective-permute-start(bf16[24,4096]{1,0:T(8,128)(2,1)S(1)} %get-tuple-element.34.refs_0_), channel_id=1, source_target_pairs={{0,224},{32,0},{64,32},{96,64},{128,96},{160,128},{192,160},{224,1... | collective-permute-start | bytes 589832 | tf_op jit(solution)/shard_map/ppermute | solution.py:439
  127.9 9.8 %collective-permute-start.11 = (bf16[24,4096]{1,0:T(8,128)(2,1)S(1)}, bf16[24,4096]{1,0:T(8,128)(2,1)S(1)}, u32[]{:S(2)}, u32[]{:S(2)}) collective-permute-start(bf16[24,4096]{1,0:T(8,128)(2,1)S(1)} %collective-permute-done.9.refs_1_), channel_id=1, source_target_pairs={{0,32},{32,64},{64,96},{96,128},{128,160},{160,192},{192,224},{224... | collective-permute-start | bytes 589832 | tf_op jit(solution)/shard_map/ppermute | solution.py:439
  129.8 20.0 %collective-permute-start.15 = (bf16[2048,128]{1,0:T(8,128)(2,1)}, bf16[2048,128]{1,0:T(8,128)(2,1)S(1)}, u32[]{:S(2)}, u32[]{:S(2)}) collective-permute-start(bf16[2048,128]{1,0:T(8,128)(2,1)} %collective-permute-done.6.refs_8_.mine_ref), channel_id=1, source_target_pairs={{0,1},{1,0},{2,3},{3,2},{4,5},{5,4},{6,7},{7,6},{8,9},{9,8},{10,11... | collective-permute-start | bytes 1572872 | tf_op jit(solution)/shard_map/ppermute | solution.py:425
  132.9 9.3 %collective-permute-start.12 = (bf16[24,4096]{1,0:T(8,128)(2,1)S(1)}, bf16[24,4096]{1,0:T(8,128)(2,1)S(1)}, u32[]{:S(2)}, u32[]{:S(2)}) collective-permute-start(bf16[24,4096]{1,0:T(8,128)(2,1)S(1)} %collective-permute-done.10.refs_2_), channel_id=1, source_target_pairs={{0,224},{32,0},{64,32},{96,64},{128,96},{160,128},{192,160},{224,1... | collective-permute-start | bytes 589832 | tf_op jit(solution)/shard_map/ppermute | solution.py:439
  137.7 14.1 %collective-permute-start.17 = (bf16[96,2048]{1,0:T(8,128)(2,1)}, bf16[96,2048]{1,0:T(8,128)(2,1)S(1)}, u32[]{:S(2)}, u32[]{:S(2)}) collective-permute-start(bf16[96,2048]{1,0:T(8,128)(2,1)} %collective-permute-done.7.mine_ref), channel_id=1, source_target_pairs={{0,1},{1,0},{2,3},{3,2},{4,5},{5,4},{6,7},{7,6},{8,9},{9,8},{10,11... | collective-permute-start | bytes 1179656 | tf_op jit(solution)/shard_map/ppermute | solution.py:425
  140.2 9.6 %collective-permute-start.13 = (bf16[24,4096]{1,0:T(8,128)(2,1)S(1)}, bf16[24,4096]{1,0:T(8,128)(2,1)S(1)}, u32[]{:S(2)}, u32[]{:S(2)}) collective-permute-start(bf16[24,4096]{1,0:T(8,128)(2,1)S(1)} %collective-permute-done.11.refs_3_), channel_id=1, source_target_pairs={{0,32},{32,64},{64,96},{96,128},{128,160},{160,192},{192,224},{224... | collective-permute-start | bytes 589832 | tf_op jit(solution)/shard_map/ppermute | solution.py:439
  142.2 9.6 %collective-permute-start.14 = (bf16[24,4096]{1,0:T(8,128)(2,1)S(1)}, bf16[24,4096]{1,0:T(8,128)(2,1)S(1)}, u32[]{:S(2)}, u32[]{:S(2)}) collective-permute-start(bf16[24,4096]{1,0:T(8,128)(2,1)S(1)} %collective-permute-done.12.refs_4_), channel_id=1, source_target_pairs={{0,224},{32,0},{64,32},{96,64},{128,96},{160,128},{192,160},{224,1... | collective-permute-start | bytes 589832 | tf_op jit(solution)/shard_map/ppermute | solution.py:439
  149.9 8.7 %collective-permute-start.16 = (bf16[24,2048]{1,0:T(8,128)(2,1)S(1)}, bf16[24,2048]{1,0:T(8,128)(2,1)S(1)}, u32[]{:S(2)}, u32[]{:S(2)}) collective-permute-start(bf16[24,2048]{1,0:T(8,128)(2,1)S(1)} %slice.25), channel_id=1, source_target_pairs={{0,32},{32,64},{64,96},{96,128},{128,160},{160,192},{192,224},{224... | collective-permute-start | bytes 294920 | tf_op jit(solution)/shard_map/ppermute | solution.py:439
  151.9 6.7 %collective-permute-start.18 = (bf16[24,2048]{1,0:T(8,128)(2,1)S(1)}, bf16[24,2048]{1,0:T(8,128)(2,1)S(1)}, u32[]{:S(2)}, u32[]{:S(2)}) collective-permute-start(bf16[24,2048]{1,0:T(8,128)(2,1)S(1)} %slice.26), channel_id=1, source_target_pairs={{0,224},{32,0},{64,32},{96,64},{128,96},{160,128},{192,160},{224,1... | collective-permute-start | bytes 294920 | tf_op jit(solution)/shard_map/ppermute | solution.py:439
  188.0 15.8 %collective-permute-start.19 = (bf16[1152,16,128]{2,1,0:T(8,128)(2,1)}, bf16[1152,16,128]{2,1,0:T(8,128)(2,1)}, u32[]{:S(2)}, u32[]{:S(2)}) collective-permute-start(bf16[1152,16,128]{2,1,0:T(8,128)(2,1)} %bitcast.24), channel_id=1, source_target_pairs={{0,1},{1,0},{2,3},{3,2},{4,5},{5,4},{6,7},{7,6},{8,9},{9,8},{10,11... | collective-permute-start | bytes 14155784 | tf_op jit(solution)/shard_map/ppermute | solution.py:425
  (11 other events, 308.0 us)
Sparse Core Ops, SparseCore 0:
  20.4 56.7 all-gather.2
  83.7 60.1 all-gather.4

commit v8 on v7

--- a/solution.py
+++ b/solution.py
@@ -547,6 +547,7 @@
         ),
         flops=2 * 640 * 512 * 1536,
     )
+    attended = after(attended, merge_mine, qkv_mine)
     tokens = attended.shape[0]
     skip_first, merged_in = call_kernel(
         skip_kernel,
@@ -570,7 +571,15 @@
         pulled=(1, 2, 3),
         vmem_mib=58,
     )
-    late = after(merge_weights, merged_in).reshape(2, Z_RING, 10, 16, 640)[:, :, :9, :, 512:]
+    own_rows = merged_in.shape[0]
+    half_shape = jax.ShapeDtypeStruct((own_rows, 512), jnp.bfloat16)
+    second_half, second_send = call_kernel(
+        merge_kernel,
+        (half_shape, half_shape),
+        (merged_in, swap_cores(merged_in), merge_weights),
+        flops=2 * 192 * 2048 * 512,
+    )
+    late = after(merge_weights, second_send).reshape(2, Z_RING, 10, 16, 640)[:, :, :9, :, 512:]
     late = lax.all_gather(
         late.reshape(-1, 128),
         "lon",
@@ -578,14 +587,6 @@
         axis_index_groups=[[4 * y + x for y in range(8)] for x in range(4)],
         tiled=True,
     ).reshape(-1, 16, 128)
-    own_rows = merged_in.shape[0]
-    half_shape = jax.ShapeDtypeStruct((own_rows, 512), jnp.bfloat16)
-    second_half, second_send = call_kernel(
-        merge_kernel,
-        (half_shape, half_shape),
-        (merged_in, after(swap_cores(merged_in), merge_mine, qkv_mine), merge_weights),
-        flops=2 * 192 * 2048 * 512,
-    )
     second_cells, coarse_in = call_kernel(
         join_kernel,
         (

time: 220 us -> 197 us (0.90)
  waiting for transfers between devices: 47.5 us -> 26.8 us
  Pallas kernels: 26 us -> 23.7 us
    all_gather x1, waiting for transfers between devices: 22.5 us -> 4.73 us  [on_device(): lax.all_gather(both_merge, 'lat', axis=1, axis_index_groups=RINGS, tiled=...]
    ppermute x3, waiting for transfers between devices: 16.5 us -> 11 us  [swap_rings(): lax.ppermute(values, 'lat', [(i, (i + Z_RING) % count) for i in range(cou...]
    pallas_call x9, Pallas kernels: 26 us -> 23.7 us  [call_kernel(): pl.pallas_call(body, out_shape=out_shape, in_specs=[pl.BlockSpec(memory_s...]
    ppermute x5, starting transfers between devices: 18.4 us -> 16.2 us  [swap_cores(): return lax.ppermute(values, 'lon', [(i, i ^ 1) for i in range(count)])]
    unnamed x30 -> x32, local copies, waits for them, and re-layouts: 4.4 us -> 5.82 us
  transfers between devices with their start and end apart: 22 -> 22, of which waited for: 9 -> 11; matrix products, arithmetic and copies ran while one was open for 4% -> 3% of each run, Pallas kernels for 6% -> 6%
where the time goes in v8:
time: 197 us; the launch traced here: 194 us
  starting transfers between devices  80.4 us (41%)
  blocking collectives  34.1 us (17%)
  waiting for transfers between devices  26.8 us (14%)
  Pallas kernels  23.7 us (12%)
  between operations  14 us (7%)
  local copies, waits for them, and re-layouts  9.2 us (5%)
  other arithmetic  4.66 us (2%)
    all_to_all x2, blocking collectives, ring_scatter(): lax.all_to_all(blocks, 'lat', 0, 0, axis_index_groups=RINGS, tiled=True)  34.1 us
    ppermute x8, starting transfers between devices, ring_shift(): return lax.ppermute(values, 'lat', pairs)  27.8 us
    pallas_call x9, Pallas kernels, call_kernel(): pl.pallas_call(body, out_shape=out_shape, in_specs=[pl.BlockSpec(memory_s...  23.7 us
    ppermute x2, starting transfers between devices, neighbours(): lax.ppermute(first, axis, [((i + 1) % count, i) for i in range(count)])  16.4 us
    ppermute x5, starting transfers between devices, swap_cores(): return lax.ppermute(values, 'lon', [(i, i ^ 1) for i in range(count)])  16.2 us
    ppermute x3, starting transfers between devices, swap_rings(): lax.ppermute(values, 'lat', [(i, (i + Z_RING) % count) for i in range(cou...  12.2 us
    ppermute x3, waiting for transfers between devices, swap_rings(): lax.ppermute(values, 'lat', [(i, (i + Z_RING) % count) for i in range(cou...  11 us
    ppermute x2, starting transfers between devices, neighbours(): lax.ppermute(last, axis, [(i, (i + 1) % count) for i in range(count)])  7.64 us
  transfers between devices with their start and end apart: 22, of which 11 were waited for; matrix products, arithmetic and copies ran while one was open for 3% of the time, Pallas kernels for 6%

profile of v8, /device:TPU:1, one launch (start us, length us, event | category | flops | bytes accessed | tf_op | source)
XLA Modules:
  0.0 193.8 jit_solution(2432234015890559212)
XLA Ops:
  9.6 5.5 %collective-permute-start = (bf16[1,160,640]{2,1,0:T(8,128)(2,1)}, bf16[1,160,640]{2,1,0:T(8,128)(2,1)S(1)}, u32[]{:S(2)}, u32[]{:S(2)}) collective-permute-start(bf16[1,160,640]{2,1,0:T(8,128)(2,1)} %bitcast.34), channel_id=1, source_target_pairs={{0,256},{32,288},{64,320},{96,352},{128,384},{160,416},{192,448},{... | collective-permute-start | bytes 614408 | tf_op jit(solution)/shard_map/ppermute | solution.py:430
  15.1 3.3 %collective-permute-done = bf16[1,160,640]{2,1,0:T(8,128)(2,1)S(1)} collective-permute-done((bf16[1,160,640]{2,1,0:T(8,128)(2,1)}, bf16[1,160,640]{2,1,0:T(8,128)(2,1)S(1)}, u32[]{:S(2)}, u32[]{:S(2)}) %collective-permute-start) | collective-permute-done | bytes 204832 | tf_op jit(solution)/shard_map/ppermute | solution.py:430
  23.6 5.6 %collective-permute-start.1 = (bf16[2,2,16,512]{3,2,1,0:T(8,128)(2,1)S(1)}, bf16[2,2,16,512]{3,2,1,0:T(8,128)(2,1)S(1)}, u32[]{:S(2)}, u32[]{:S(2)}) collective-permute-start(bf16[2,2,16,512]{3,2,1,0:T(8,128)(2,1)S(1)} %get-tuple-element.48), channel_id=1, source_target_pairs={{0,32},{32,64},{64,96},{96,128},{128,160},{160,192},{192,224},{224... | collective-permute-start | bytes 196616 | tf_op jit(solution)/shard_map/ppermute | solution.py:418
  29.4 11.0 %collective-permute-start.2 = (bf16[2,2,16,512]{3,2,1,0:T(8,128)(2,1)S(1)}, bf16[2,2,16,512]{3,2,1,0:T(8,128)(2,1)S(1)}, u32[]{:S(2)}, u32[]{:S(2)}) collective-permute-start(bf16[2,2,16,512]{3,2,1,0:T(8,128)(2,1)S(1)} %get-tuple-element.47), channel_id=1, source_target_pairs={{32,0},{64,32},{96,64},{128,96},{160,128},{192,160},{224,192},{256... | collective-permute-start | bytes 196616 | tf_op jit(solution)/shard_map/ppermute | solution.py:419
  41.9 5.4 %collective-permute-start.4 = (bf16[16,2,2,512]{3,2,1,0:T(2,128)(2,1)S(1)}, bf16[16,2,2,512]{3,2,1,0:T(2,128)(2,1)S(1)}, u32[]{:S(2)}, u32[]{:S(2)}) collective-permute-start(bf16[16,2,2,512]{3,2,1,0:T(2,128)(2,1)S(1)} %get-tuple-element.45), channel_id=1, source_target_pairs={{1,0},{2,1},{3,2},{4,3},{5,4},{6,5},{7,6},{8,7},{9,8},{10,9},{11,1... | collective-permute-start | bytes 196616 | tf_op jit(solution)/shard_map/ppermute | solution.py:419
  51.5 3.2 %collective-permute-start.5 = (bf16[2048,128]{1,0:T(8,128)(2,1)}, bf16[2048,128]{1,0:T(8,128)(2,1)S(1)}, u32[]{:S(2)}, u32[]{:S(2)}) collective-permute-start(bf16[2048,128]{1,0:T(8,128)(2,1)} %constant_dynamic-slice_fusion.1), channel_id=1, source_target_pairs={{0,256},{32,288},{64,320},{96,352},{128,384},{160,416},{192,448},{... | collective-permute-start | bytes 1572872 | tf_op jit(solution)/shard_map/ppermute | solution.py:430
  55.5 3.6 %collective-permute-start.6 = (bf16[96,2048]{1,0:T(8,128)(2,1)}, bf16[96,2048]{1,0:T(8,128)(2,1)}, u32[]{:S(2)}, u32[]{:S(2)}) collective-permute-start(bf16[96,2048]{1,0:T(8,128)(2,1)} %constant_dynamic-slice_fusion), channel_id=1, source_target_pairs={{0,256},{32,288},{64,320},{96,352},{128,384},{160,416},{192,448},{... | collective-permute-start | bytes 1179656 | tf_op jit(solution)/shard_map/ppermute | solution.py:430
  60.8 3.3 %shard_map.155.attended_ref = bf16[384,512]{1,0:T(8,128)(2,1)S(1)} custom-call(bf16[512,512]{1,0:T(8,128)(2,1)S(1)} %bitcast.28, bf16[64,512]{1,0:T(8,128)(2,1)S(1)} %reshape.77.left_ref, bf16[64,512]{1,0:T(8,128)(2,1)S(1)} %reshape.78.right_ref, f32[1,512]{1,0:T(1,128)S(1)} %bitcast.31, bf16[3,512,512]{2,1,0:T(8,128)(2,1)S(1)} %copy-done.10, ...), custom_call_target="tpu_custom_call" | custom-call | flops 1006632960 | bytes 2314752 | tf_op jit(solution)/shard_map/pallas_call | solution.py:23
  64.9 7.7 %collective-permute-done.6.mine_ref = bf16[96,2048]{1,0:T(8,128)(2,1)} collective-permute-done((bf16[96,2048]{1,0:T(8,128)(2,1)}, bf16[96,2048]{1,0:T(8,128)(2,1)}, u32[]{:S(2)}, u32[]{:S(2)}) %collective-permute-start.6) | collective-permute-done | bytes 393248 | tf_op jit(solution)/shard_map/ppermute | solution.py:430
  72.5 4.7 %all-gather.3.cloned.1.call-done.weights_ref = bf16[2,1280,640]{2,1,0:T(8,128)(2,1)} async-done(((bf16[2,160,640]{2,1,0:T(8,128)(2,1)}), bf16[2,1280,640]{2,1,0:T(8,128)(2,1)}) %all-gather.3.cloned.1.call-update) | async-done | bytes 3276816 | tf_op jit(solution)/shard_map/all_gather | solution.py:498
  77.3 4.3 %shard_map.156 = (bf16[384,512]{1,0:T(8,128)(2,1)}, bf16[96,2048]{1,0:T(8,128)(2,1)}) custom-call(bf16[384,512]{1,0:T(8,128)(2,1)} %copy-done.6, bf16[384,512]{1,0:T(8,128)(2,1)} %bitcast.32, bf16[2,8,160,640]{3,2,1,0:T(8,128)(2,1)} %bitcast.22, f32[1,2048]{1,0:T(1,128)} %bitcast.36), custom_call_target="tpu_custom_call" | custom-call | flops 201326592 | bytes 4071424 | tf_op jit(solution)/shard_map/pallas_call | solution.py:23
  95.1 5.4 %collective-permute-start.10 = (bf16[24,4096]{1,0:T(8,128)(2,1)S(1)}, bf16[24,4096]{1,0:T(8,128)(2,1)S(1)}, u32[]{:S(2)}, u32[]{:S(2)}) collective-permute-start(bf16[24,4096]{1,0:T(8,128)(2,1)S(1)} %get-tuple-element.34.refs_0_), channel_id=1, source_target_pairs={{0,224},{32,0},{64,32},{96,64},{128,96},{160,128},{192,160},{224,1... | collective-permute-start | bytes 589832 | tf_op jit(solution)/shard_map/ppermute | solution.py:439
  100.5 3.0 %collective-permute-done.9.refs_1_ = bf16[24,4096]{1,0:T(8,128)(2,1)S(1)} collective-permute-done((bf16[24,4096]{1,0:T(8,128)(2,1)S(1)}, bf16[24,4096]{1,0:T(8,128)(2,1)S(1)}, u32[]{:S(2)}, u32[]{:S(2)}) %collective-permute-start.9) | collective-permute-done | bytes 196640 | tf_op jit(solution)/shard_map/ppermute | solution.py:439
  105.4 2.8 %collective-permute-start.15 = (bf16[2048,128]{1,0:T(8,128)(2,1)S(1)}, bf16[2048,128]{1,0:T(8,128)(2,1)S(1)}, u32[]{:S(2)}, u32[]{:S(2)}) collective-permute-start(bf16[2048,128]{1,0:T(8,128)(2,1)S(1)} %collective-permute-done.5.refs_8_.mine_ref), channel_id=1, source_target_pairs={{0,1},{1,0},{2,3},{3,2},{4,5},{5,4},{6,7},{7,6},{8,9},{9,8},{10,11... | collective-permute-start | bytes 1572872 | tf_op jit(solution)/shard_map/ppermute | solution.py:425
  108.2 4.9 %collective-permute-start.12 = (bf16[24,4096]{1,0:T(8,128)(2,1)S(1)}, bf16[24,4096]{1,0:T(8,128)(2,1)S(1)}, u32[]{:S(2)}, u32[]{:S(2)}) collective-permute-start(bf16[24,4096]{1,0:T(8,128)(2,1)S(1)} %collective-permute-done.10.refs_2_), channel_id=1, source_target_pairs={{0,224},{32,0},{64,32},{96,64},{128,96},{160,128},{192,160},{224,1... | collective-permute-start | bytes 589832 | tf_op jit(solution)/shard_map/ppermute | solution.py:439
  113.1 2.7 %collective-permute-start.17 = (bf16[96,2048]{1,0:T(8,128)(2,1)}, bf16[96,2048]{1,0:T(8,128)(2,1)S(1)}, u32[]{:S(2)}, u32[]{:S(2)}) collective-permute-start(bf16[96,2048]{1,0:T(8,128)(2,1)} %collective-permute-done.6.mine_ref), channel_id=1, source_target_pairs={{0,1},{1,0},{2,3},{3,2},{4,5},{5,4},{6,7},{7,6},{8,9},{9,8},{10,11... | collective-permute-start | bytes 1179656 | tf_op jit(solution)/shard_map/ppermute | solution.py:425
  117.7 5.0 %collective-permute-start.14 = (bf16[24,4096]{1,0:T(8,128)(2,1)S(1)}, bf16[24,4096]{1,0:T(8,128)(2,1)S(1)}, u32[]{:S(2)}, u32[]{:S(2)}) collective-permute-start(bf16[24,4096]{1,0:T(8,128)(2,1)S(1)} %collective-permute-done.12.refs_4_), channel_id=1, source_target_pairs={{0,224},{32,0},{64,32},{96,64},{128,96},{160,128},{192,160},{224,1... | collective-permute-start | bytes 589832 | tf_op jit(solution)/shard_map/ppermute | solution.py:439
  122.8 2.7 %collective-permute-done.13.refs_5_ = bf16[24,4096]{1,0:T(8,128)(2,1)S(1)} collective-permute-done((bf16[24,4096]{1,0:T(8,128)(2,1)S(1)}, bf16[24,4096]{1,0:T(8,128)(2,1)S(1)}, u32[]{:S(2)}, u32[]{:S(2)}) %collective-permute-start.13) | collective-permute-done | bytes 196640 | tf_op jit(solution)/shard_map/ppermute | solution.py:439
  127.5 4.6 %collective-permute-start.18 = (bf16[24,2048]{1,0:T(8,128)(2,1)S(1)}, bf16[24,2048]{1,0:T(8,128)(2,1)S(1)}, u32[]{:S(2)}, u32[]{:S(2)}) collective-permute-start(bf16[24,2048]{1,0:T(8,128)(2,1)S(1)} %slice.26), channel_id=1, source_target_pairs={{0,224},{32,0},{64,32},{96,64},{128,96},{160,128},{192,160},{224,1... | collective-permute-start | bytes 294920 | tf_op jit(solution)/shard_map/ppermute | solution.py:439
  134.9 24.7 %all_to_all.10.x_ref = bf16[8,8,2,24,128]{4,3,2,1,0:T(8,128)(2,1)S(1)} all-to-all(bf16[8,8,2,24,128]{4,3,2,1,0:T(8,128)(2,1)S(1)} %broadcast_in_dim.46), channel_id=1, replica_groups={{0,32,64,96,128,160,192,224},{256,288,320,352,384,416,448,480},{1,33,65..., dimensions={0} | all-to-all | bytes 1572864 | tf_op jit(solution)/shard_map/all_to_all | solution.py:434
  159.6 4.0 %shard_map.161 = (bf16[8,2,24,64]{3,2,1,0:T(8,128)(2,1)S(1)}, f32[24,2048]{1,0:T(8,128)S(1)}) custom-call(s32[3]{0:T(128)S(1)} %pad_add_fusion.1.core_ref.place_ref, bf16[8,8,2,24,128]{4,3,2,1,0:T(8,128)(2,1)S(1)} %all_to_all.10.x_ref, f32[1,2048]{1,0:T(1,128)S(1)} %bitcast.30, bf16[192,2048]{1,0:T(8,128)(2,1)S(1)} %bitcast.27, ...), custom_call_target="tpu_custom_call" | custom-call | flops 301989888 | bytes 2367500 | tf_op jit(solution)/shard_map/pallas_call | solution.py:23
  163.7 5.8 %collective-permute-start.19 = (bf16[1152,16,128]{2,1,0:T(8,128)(2,1)}, bf16[1152,16,128]{2,1,0:T(8,128)(2,1)}, u32[]{:S(2)}, u32[]{:S(2)}) collective-permute-start(bf16[1152,16,128]{2,1,0:T(8,128)(2,1)} %bitcast.24), channel_id=1, source_target_pairs={{0,1},{1,0},{2,3},{3,2},{4,5},{5,4},{6,7},{7,6},{8,9},{9,8},{10,11... | collective-permute-start | bytes 14155784 | tf_op jit(solution)/shard_map/ppermute | solution.py:425
  169.6 9.4 %all_to_all.11 = bf16[8,2,1536]{2,1,0:T(2,128)(2,1)S(1)} all-to-all(bf16[8,2,1536]{2,1,0:T(2,128)(2,1)S(1)} %reshape.86), channel_id=1, replica_groups={{0,32,64,96,128,160,192,224},{256,288,320,352,384,416,448,480},{1,33,65..., dimensions={0} | all-to-all | bytes 98304 | tf_op jit(solution)/shard_map/all_to_all | solution.py:434
  181.4 5.6 %shard_map.162 = bf16[384,512]{1,0:T(8,128)(2,1)} custom-call(s32[3]{0:T(128)S(1)} %pad_add_fusion.1.core_ref.place_ref, bf16[8,2,24,64]{3,2,1,0:T(8,128)(2,1)S(1)} %reshape.87.heads_ref, f32[24,2048]{1,0:T(8,128)S(1)} %get-tuple-element.40.own_coarse_ref, bf16[1152,16,128]{2,1,0:T(8,128)(2,1)S(1)} %bitcast.25, ...), custom_call_target="tpu_custom_call" | custom-call | flops 301989888 | bytes 10272780 | tf_op jit(solution)/shard_map/pallas_call | solution.py:23
  (94 shorter events, 41.7 us)
Async XLA Ops:
  6.5 52.8 %copy-start.12 = (f32[512]{0:T(512)S(1)}, f32[512]{0:T(512)}, u32[]{:S(2)}) copy-start(f32[512]{0:T(512)} %param.20) | copy-start | bytes 6148
  6.5 70.7 %all-gather.3.cloned.1.call-start = ((), (), s32[]{:S(2)}) async-start(), calls=%async_computation.2 | async-start | bytes 3686400 | tf_op jit(solution)/shard_map/all_gather | solution.py:498
  9.6 8.8 %collective-permute-start = (bf16[1,160,640]{2,1,0:T(8,128)(2,1)}, bf16[1,160,640]{2,1,0:T(8,128)(2,1)S(1)}, u32[]{:S(2)}, u32[]{:S(2)}) collective-permute-start(bf16[1,160,640]{2,1,0:T(8,128)(2,1)} %bitcast.34), channel_id=1, source_target_pairs={{0,256},{32,288},{64,320},{96,352},{128,384},{160,416},{192,448},{... | collective-permute-start | bytes 614408 | tf_op jit(solution)/shard_map/ppermute | solution.py:430
  20.4 143.3 %all-gather.5.cloned.1.call-start = ((), (), s32[]{:S(2)}) async-start(), calls=%async_computation.3 | async-start | bytes 5308416 | tf_op jit(solution)/shard_map/all_gather | solution.py:583
  23.6 16.9 %collective-permute-start.1 = (bf16[2,2,16,512]{3,2,1,0:T(8,128)(2,1)S(1)}, bf16[2,2,16,512]{3,2,1,0:T(8,128)(2,1)S(1)}, u32[]{:S(2)}, u32[]{:S(2)}) collective-permute-start(bf16[2,2,16,512]{3,2,1,0:T(8,128)(2,1)S(1)} %get-tuple-element.48), channel_id=1, source_target_pairs={{0,32},{32,64},{64,96},{96,128},{128,160},{160,192},{192,224},{224... | collective-permute-start | bytes 196616 | tf_op jit(solution)/shard_map/ppermute | solution.py:418
  29.4 12.4 %collective-permute-start.2 = (bf16[2,2,16,512]{3,2,1,0:T(8,128)(2,1)S(1)}, bf16[2,2,16,512]{3,2,1,0:T(8,128)(2,1)S(1)}, u32[]{:S(2)}, u32[]{:S(2)}) collective-permute-start(bf16[2,2,16,512]{3,2,1,0:T(8,128)(2,1)S(1)} %get-tuple-element.47), channel_id=1, source_target_pairs={{32,0},{64,32},{96,64},{128,96},{160,128},{192,160},{224,192},{256... | collective-permute-start | bytes 196616 | tf_op jit(solution)/shard_map/ppermute | solution.py:419
  41.9 7.9 %collective-permute-start.4 = (bf16[16,2,2,512]{3,2,1,0:T(2,128)(2,1)S(1)}, bf16[16,2,2,512]{3,2,1,0:T(2,128)(2,1)S(1)}, u32[]{:S(2)}, u32[]{:S(2)}) collective-permute-start(bf16[16,2,2,512]{3,2,1,0:T(2,128)(2,1)S(1)} %get-tuple-element.45), channel_id=1, source_target_pairs={{1,0},{2,1},{3,2},{4,3},{5,4},{6,5},{7,6},{8,7},{9,8},{10,9},{11,1... | collective-permute-start | bytes 196616 | tf_op jit(solution)/shard_map/ppermute | solution.py:419
  47.3 3.4 %collective-permute-start.3 = (bf16[16,2,2,512]{3,2,1,0:T(2,128)(2,1)S(1)}, bf16[16,2,2,512]{3,2,1,0:T(2,128)(2,1)S(1)}, u32[]{:S(2)}, u32[]{:S(2)}) collective-permute-start(bf16[16,2,2,512]{3,2,1,0:T(2,128)(2,1)S(1)} %get-tuple-element.46), channel_id=1, source_target_pairs={{0,1},{1,2},{2,3},{3,4},{4,5},{5,6},{6,7},{7,8},{8,9},{9,10},{10,1... | collective-permute-start | bytes 196616 | tf_op jit(solution)/shard_map/ppermute | solution.py:418
  51.5 21.0 %collective-permute-start.5 = (bf16[2048,128]{1,0:T(8,128)(2,1)}, bf16[2048,128]{1,0:T(8,128)(2,1)S(1)}, u32[]{:S(2)}, u32[]{:S(2)}) collective-permute-start(bf16[2048,128]{1,0:T(8,128)(2,1)} %constant_dynamic-slice_fusion.1), channel_id=1, source_target_pairs={{0,256},{32,288},{64,320},{96,352},{128,384},{160,416},{192,448},{... | collective-permute-start | bytes 1572872 | tf_op jit(solution)/shard_map/ppermute | solution.py:430
  55.5 17.0 %collective-permute-start.6 = (bf16[96,2048]{1,0:T(8,128)(2,1)}, bf16[96,2048]{1,0:T(8,128)(2,1)}, u32[]{:S(2)}, u32[]{:S(2)}) collective-permute-start(bf16[96,2048]{1,0:T(8,128)(2,1)} %constant_dynamic-slice_fusion), channel_id=1, source_target_pairs={{0,256},{32,288},{64,320},{96,352},{128,384},{160,416},{192,448},{... | collective-permute-start | bytes 1179656 | tf_op jit(solution)/shard_map/ppermute | solution.py:430
  81.6 4.2 %collective-permute-start.7 = (bf16[96,2048]{1,0:T(8,128)(2,1)}, bf16[96,2048]{1,0:T(8,128)(2,1)S(1)}, u32[]{:S(2)}, u32[]{:S(2)}) collective-permute-start(bf16[96,2048]{1,0:T(8,128)(2,1)} %get-tuple-element.31.own_ref), channel_id=1, source_target_pairs={{0,1},{1,0},{2,3},{3,2},{4,5},{5,4},{6,7},{7,6},{8,9},{9,8},{10,11... | collective-permute-start | bytes 1179656 | tf_op jit(solution)/shard_map/ppermute | solution.py:425
  88.3 71.3 %copy-start.9 = (f32[2048]{0:T(1024)S(1)}, f32[2048]{0:T(1024)}, u32[]{:S(2)}) copy-start(f32[2048]{0:T(1024)} %param.27) | copy-start | bytes 24580
  88.3 3.4 %collective-permute-start.8 = (bf16[96,512]{1,0:T(8,128)(2,1)}, bf16[96,512]{1,0:T(8,128)(2,1)S(1)}, u32[]{:S(2)}, u32[]{:S(2)}) collective-permute-start(bf16[96,512]{1,0:T(8,128)(2,1)} %copy-done.11), channel_id=1, source_target_pairs={{0,1},{1,0},{2,3},{3,2},{4,5},{5,4},{6,7},{7,6},{8,9},{9,8},{10,11... | collective-permute-start | bytes 294920 | tf_op jit(solution)/shard_map/ppermute | solution.py:425
  92.8 10.7 %collective-permute-start.9 = (bf16[24,4096]{1,0:T(8,128)(2,1)S(1)}, bf16[24,4096]{1,0:T(8,128)(2,1)S(1)}, u32[]{:S(2)}, u32[]{:S(2)}) collective-permute-start(bf16[24,4096]{1,0:T(8,128)(2,1)S(1)} %get-tuple-element.34.refs_0_), channel_id=1, source_target_pairs={{0,32},{32,64},{64,96},{96,128},{128,160},{160,192},{192,224},{224... | collective-permute-start | bytes 589832 | tf_op jit(solution)/shard_map/ppermute | solution.py:439
  95.1 13.1 %collective-permute-start.10 = (bf16[24,4096]{1,0:T(8,128)(2,1)S(1)}, bf16[24,4096]{1,0:T(8,128)(2,1)S(1)}, u32[]{:S(2)}, u32[]{:S(2)}) collective-permute-start(bf16[24,4096]{1,0:T(8,128)(2,1)S(1)} %get-tuple-element.34.refs_0_), channel_id=1, source_target_pairs={{0,224},{32,0},{64,32},{96,64},{128,96},{160,128},{192,160},{224,1... | collective-permute-start | bytes 589832 | tf_op jit(solution)/shard_map/ppermute | solution.py:439
  103.5 9.6 %collective-permute-start.11 = (bf16[24,4096]{1,0:T(8,128)(2,1)S(1)}, bf16[24,4096]{1,0:T(8,128)(2,1)S(1)}, u32[]{:S(2)}, u32[]{:S(2)}) collective-permute-start(bf16[24,4096]{1,0:T(8,128)(2,1)S(1)} %collective-permute-done.9.refs_1_), channel_id=1, source_target_pairs={{0,32},{32,64},{64,96},{96,128},{128,160},{160,192},{192,224},{224... | collective-permute-start | bytes 589832 | tf_op jit(solution)/shard_map/ppermute | solution.py:439
  105.4 20.1 %collective-permute-start.15 = (bf16[2048,128]{1,0:T(8,128)(2,1)S(1)}, bf16[2048,128]{1,0:T(8,128)(2,1)S(1)}, u32[]{:S(2)}, u32[]{:S(2)}) collective-permute-start(bf16[2048,128]{1,0:T(8,128)(2,1)S(1)} %collective-permute-done.5.refs_8_.mine_ref), channel_id=1, source_target_pairs={{0,1},{1,0},{2,3},{3,2},{4,5},{5,4},{6,7},{7,6},{8,9},{9,8},{10,11... | collective-permute-start | bytes 1572872 | tf_op jit(solution)/shard_map/ppermute | solution.py:425
  108.2 9.5 %collective-permute-start.12 = (bf16[24,4096]{1,0:T(8,128)(2,1)S(1)}, bf16[24,4096]{1,0:T(8,128)(2,1)S(1)}, u32[]{:S(2)}, u32[]{:S(2)}) collective-permute-start(bf16[24,4096]{1,0:T(8,128)(2,1)S(1)} %collective-permute-done.10.refs_2_), channel_id=1, source_target_pairs={{0,224},{32,0},{64,32},{96,64},{128,96},{160,128},{192,160},{224,1... | collective-permute-start | bytes 589832 | tf_op jit(solution)/shard_map/ppermute | solution.py:439
  113.1 14.4 %collective-permute-start.17 = (bf16[96,2048]{1,0:T(8,128)(2,1)}, bf16[96,2048]{1,0:T(8,128)(2,1)S(1)}, u32[]{:S(2)}, u32[]{:S(2)}) collective-permute-start(bf16[96,2048]{1,0:T(8,128)(2,1)} %collective-permute-done.6.mine_ref), channel_id=1, source_target_pairs={{0,1},{1,0},{2,3},{3,2},{4,5},{5,4},{6,7},{7,6},{8,9},{9,8},{10,11... | collective-permute-start | bytes 1179656 | tf_op jit(solution)/shard_map/ppermute | solution.py:425
  115.8 9.7 %collective-permute-start.13 = (bf16[24,4096]{1,0:T(8,128)(2,1)S(1)}, bf16[24,4096]{1,0:T(8,128)(2,1)S(1)}, u32[]{:S(2)}, u32[]{:S(2)}) collective-permute-start(bf16[24,4096]{1,0:T(8,128)(2,1)S(1)} %collective-permute-done.11.refs_3_), channel_id=1, source_target_pairs={{0,32},{32,64},{64,96},{96,128},{128,160},{160,192},{192,224},{224... | collective-permute-start | bytes 589832 | tf_op jit(solution)/shard_map/ppermute | solution.py:439
  117.7 9.7 %collective-permute-start.14 = (bf16[24,4096]{1,0:T(8,128)(2,1)S(1)}, bf16[24,4096]{1,0:T(8,128)(2,1)S(1)}, u32[]{:S(2)}, u32[]{:S(2)}) collective-permute-start(bf16[24,4096]{1,0:T(8,128)(2,1)S(1)} %collective-permute-done.12.refs_4_), channel_id=1, source_target_pairs={{0,224},{32,0},{64,32},{96,64},{128,96},{160,128},{192,160},{224,1... | collective-permute-start | bytes 589832 | tf_op jit(solution)/shard_map/ppermute | solution.py:439
  125.6 8.0 %collective-permute-start.16 = (bf16[24,2048]{1,0:T(8,128)(2,1)S(1)}, bf16[24,2048]{1,0:T(8,128)(2,1)S(1)}, u32[]{:S(2)}, u32[]{:S(2)}) collective-permute-start(bf16[24,2048]{1,0:T(8,128)(2,1)S(1)} %slice.25), channel_id=1, source_target_pairs={{0,32},{32,64},{64,96},{96,128},{128,160},{160,192},{192,224},{224... | collective-permute-start | bytes 294920 | tf_op jit(solution)/shard_map/ppermute | solution.py:439
  127.5 6.2 %collective-permute-start.18 = (bf16[24,2048]{1,0:T(8,128)(2,1)S(1)}, bf16[24,2048]{1,0:T(8,128)(2,1)S(1)}, u32[]{:S(2)}, u32[]{:S(2)}) collective-permute-start(bf16[24,2048]{1,0:T(8,128)(2,1)S(1)} %slice.26), channel_id=1, source_target_pairs={{0,224},{32,0},{64,32},{96,64},{128,96},{160,128},{192,160},{224,1... | collective-permute-start | bytes 294920 | tf_op jit(solution)/shard_map/ppermute | solution.py:439
  163.7 15.4 %collective-permute-start.19 = (bf16[1152,16,128]{2,1,0:T(8,128)(2,1)}, bf16[1152,16,128]{2,1,0:T(8,128)(2,1)}, u32[]{:S(2)}, u32[]{:S(2)}) collective-permute-start(bf16[1152,16,128]{2,1,0:T(8,128)(2,1)} %bitcast.24), channel_id=1, source_target_pairs={{0,1},{1,0},{2,3},{3,2},{4,5},{5,4},{6,7},{7,6},{8,9},{9,8},{10,11... | collective-permute-start | bytes 14155784 | tf_op jit(solution)/shard_map/ppermute | solution.py:425
  (12 other events, 209.3 us)
Sparse Core Ops, SparseCore 0:
  20.5 56.7 all-gather.2
  88.5 61.4 all-gather.4

commit v9 on v8

--- a/solution.py
+++ b/solution.py
@@ -208,7 +208,7 @@
     join_quads(second, 3, 4, gain_ref, coarse_ref)
 
 
-RING_ORDER = (0, -1, 1, -2, 2, -3, 3)
+NEAR_PLACES, FAR_PLACES = (0, -1, 1, -2, 2, 4), (-3, 3)
 
 
 def halves_in_order(core, mine_ref, partner_ref):
@@ -220,7 +220,7 @@
 
 
 def near_kernel(place_ref, *refs):
-    near, (own_ref, *halves, out_ref) = refs[:7], refs[7:]
+    near, (own_ref, *halves, out_ref) = refs[:6], refs[6:]
     left = jnp.concatenate([ref[...].astype(jnp.float32) for ref in near], axis=0)
     left = left.astype(jnp.bfloat16)
     rows = near[0].shape[0]
@@ -231,14 +231,18 @@
             out_ref[shard, at] = product[at * rows : (at + 1) * rows].astype(jnp.bfloat16)
 
 
-def far_kernel(place_ref, near_ref, low_ref, high_ref, own_ref, mine_ref, partner_ref, out_ref):
-    half = low_ref.shape[1]
+def far_kernel(place_ref, near_ref, back_ref, forth_ref, own_ref, mine_ref, partner_ref, out_ref):
+    rows = back_ref.shape[0]
+    left = jnp.concatenate([back_ref[...].astype(jnp.float32), forth_ref[...].astype(jnp.float32)], axis=0)
+    left = left.astype(jnp.bfloat16)
     own, other = own_ref[...], halves_in_order(place_ref[0], mine_ref, partner_ref)
     for weights, shard in ((own, place_ref[2]), (other, 1 - place_ref[2])):
-        far = dot_rows(low_ref[...], weights[:half]) + dot_rows(high_ref[...], weights[half:])
-        out_ref[jnp.bitwise_and(place_ref[1] + 4, 7), shard] = far.astype(jnp.bfloat16)
+        far = dot_rows(left, weights)
+        for at, offset in enumerate(FAR_PLACES):
+            place = jnp.bitwise_and(place_ref[1] + (offset + 8), 7)
+            out_ref[place, shard] = far[at * rows : (at + 1) * rows].astype(jnp.bfloat16)
     for shard in range(2):
-        for at, offset in enumerate(RING_ORDER):
+        for at, offset in enumerate(NEAR_PLACES):
             place = jnp.bitwise_and(place_ref[1] + (offset + 8), 7)
             out_ref[place, shard] = near_ref[shard, at]
 
@@ -332,27 +336,26 @@
     core = core_ref[0]
     pairs = []
     for ring in range(2):
-        for z in range(0, 8, 2):
+        for z in range(0, 8, 4):
             pairs.append(
                 jnp.concatenate(
-                    [heads_ref[z, ring].astype(jnp.float32), heads_ref[z + 1, ring].astype(jnp.float32)],
-                    axis=1,
+                    [heads_ref[zz, ring].astype(jnp.float32) for zz in range(z, z + 4)], axis=1
                 ).astype(jnp.bfloat16)
             )
     for weights_ref, origin in ((swapped_ref, 1 - core), (late_ref, core)):
         for part in range(2):
             total = None
             for ring in range(2):
-                for z in range(0, 8, 2):
+                for z in range(0, 8, 4):
                     right = jnp.concatenate(
                         [
                             late_row(weights_ref, 2 * row + part, ring, zz, 4)
-                            for zz in (z, z + 1)
+                            for zz in range(z, z + 4)
                             for row in range(4)
                         ],
                         axis=0,
                     )
-                    product = dot_rows(pairs[ring * 4 + z // 2], right)
+                    product = dot_rows(pairs[ring * 2 + z // 4], right)
                     total = product if total is None else total + product
             third_ref[part, origin] = total
     level_three = []
@@ -364,12 +367,14 @@
     for weights_ref, origin in ((late_ref, core), (swapped_ref, 1 - core)):
         total = None
         for ring in range(2):
-            for z in range(8):
+            for z in range(0, 8, 2):
                 right = jnp.concatenate(
-                    [late_row(weights_ref, y, ring, z, 0) for y in range(8)],
+                    [late_row(weights_ref, y, ring, zz, 0) for zz in (z, z + 1) for y in range(8)],
                     axis=0,
                 )
-                product = dot_rows(level_three[ring * 8 + z], right)
+                start = ring * 8 + z
+                left = jnp.concatenate(level_three[start : start + 2], axis=1)
+                product = dot_rows(left, right)
                 total = product if total is None else total + product
         lift_ref[origin] = total
     lat_count, lon_count = 6, 8
@@ -382,13 +387,13 @@
     for weights_ref, origin in ((late_ref, core), (swapped_ref, 1 - core)):
         total = None
         for ring in range(2):
-            for z in range(0, 8, 2):
+            for z in range(0, 8, 4):
                 right = jnp.concatenate(
                     [
                         jnp.concatenate(
                             [
                                 late_tile(weights_ref, 2 * row + part, ring, zz, 8)
-                                for zz in (z, z + 1)
+                                for zz in range(z, z + 4)
                                 for row in range(4)
                             ],
                             axis=0,
@@ -398,7 +403,7 @@
                     axis=1,
                 )
                 start = (ring * 8 + z) * 64
-                product = dot_rows(level_ref[:, start : start + 128], right)
+                product = dot_rows(level_ref[:, start : start + 256], right)
                 total = product if total is None else total + product
         small_ref[origin] = total
     for side in range(2):
@@ -493,8 +498,10 @@
         (pltpu.SemaphoreType.DMA((12,)),),
         pulled=(1, 2, 3, 4, 5),
         vmem_mib=62,
-    )[None]
-    both_merge = in_order(ring, own_merge, swap_rings(own_merge), 0)
+    )
+    both_merge = lax.all_gather(
+        own_merge, "lat", axis_index_groups=[[z, z + Z_RING] for z in range(Z_RING)]
+    )
     merge_weights = lax.all_gather(
         both_merge, "lat", axis=1, axis_index_groups=RINGS, tiled=True
     )
@@ -511,10 +518,9 @@
     cells = jnp.concatenate([above, hidden, below], axis=0)
     qkv_third = qkv_third.transpose(0, 2, 1).reshape(-1, qkv_third.shape[1])
 
+    merge_third, cells = lax.optimization_barrier((merge_third, cells))
     left, right = neighbours(cells[:, :, :2], cells[:, :, -2:], "lon")
-    merge_third, qkv_third, left, right = lax.optimization_barrier(
-        (merge_third, qkv_third, left, right)
-    )
+    qkv_third, left, right = lax.optimization_barrier((qkv_third, left, right))
 
     merge_mine, qkv_mine = [
         swap_rings(lax.dynamic_slice_in_dim(table, core * (table.shape[0] // 2), table.shape[0] // 2))
@@ -600,27 +606,31 @@
     own_count = coarse_in.shape[0]
 
     pieces, forth, back = [coarse_in], coarse_in, coarse_in
-    for _ in range(3):
+    opposite = None
+    for _ in range(2):
         forth, back = ring_shift(forth, 1), ring_shift(back, -1)
+        opposite = ring_shift(coarse_in, 4) if opposite is None else opposite
         pieces += [forth, back]
-    merge_mine, qkv_mine = after(merge_mine, pieces[1]), after(qkv_mine, pieces[3])
+    merge_mine = after(merge_mine, pieces[1], pieces[2])
+    qkv_mine = after(qkv_mine, pieces[3])
     merge_partner, qkv_partner = swap_cores(merge_mine), swap_cores(qkv_mine)
-    half_feats = coarse_in.shape[1] // 2
-    forth, back = after(forth, merge_partner), after(back, qkv_partner)
-    far_low, far_high = ring_shift(forth[:, :half_feats], 1), ring_shift(back[:, half_feats:], -1)
+    back, merge_partner = lax.optimization_barrier((back, merge_partner))
+    pieces.append(opposite)
+    far_back, far_forth = ring_shift(forth, 1), ring_shift(back, -1)
     tables = (merge_third, merge_mine, merge_partner)
     near = call_kernel(
         near_kernel,
-        jax.ShapeDtypeStruct((2, len(RING_ORDER), own_count, 128), jnp.bfloat16),
+        jax.ShapeDtypeStruct((2, len(pieces), own_count, 128), jnp.bfloat16),
         (core_place, *pieces, *tables),
-        flops=2 * 168 * 4096 * 256,
+        flops=2 * 144 * 4096 * 256,
     )
     column_block = call_kernel(
         far_kernel,
         jax.ShapeDtypeStruct((Z_RING, 2, own_count, 128), jnp.bfloat16),
-        (core_place, near, far_low, far_high, *tables),
-        flops=2 * 24 * 4096 * 256,
-    )
+        (core_place, near, far_back, far_forth, *tables),
+        flops=2 * 48 * 4096 * 256,
+    )
+    column_block = after(column_block, qkv_partner)
     heads_out, own_coarse = call_kernel(
         third_kernel,
         (

time: 197 us -> 198 us (level)
  starting transfers between devices: 80.4 us -> 67.3 us
  blocking collectives: 34.1 us -> 44.3 us
  waiting for transfers between devices: 26.8 us -> 32.5 us
    ppermute x8 -> x7, waiting for transfers between devices: 5.91 us -> 16.1 us  [ring_shift(): return lax.ppermute(values, 'lat', pairs)]
    all_gather x0 -> x1, blocking collectives: none -> 9.31 us  [on_device(): lax.all_gather(own_merge, 'lat', axis_index_groups=[[z, z + Z_RING] for z...]
    ppermute x3 -> x2, starting transfers between devices: 12.2 us -> 6.76 us  [swap_rings(): lax.ppermute(values, 'lat', [(i, (i + Z_RING) % count) for i in range(cou...]
    ppermute x8 -> x7, starting transfers between devices: 27.8 us -> 23.6 us  [ring_shift(): return lax.ppermute(values, 'lat', pairs)]
    ppermute x2, starting transfers between devices: 16.4 us -> 14.3 us  [neighbours(): lax.ppermute(first, axis, [((i + 1) % count, i) for i in range(count)])]
    ppermute x3 -> x2, waiting for transfers between devices: 11 us -> 10.8 us  [swap_rings(): lax.ppermute(values, 'lat', [(i, (i + Z_RING) % count) for i in range(cou...]
  transfers between devices with their start and end apart: 22 -> 20, of which waited for: 11 -> 9; matrix products, arithmetic and copies ran while one was open for 3% -> 3% of each run, Pallas kernels for 6% -> 5%
where the time goes in v9:
time: 198 us; the launch traced here: 196 us
  starting transfers between devices  67.3 us (34%)
  blocking collectives  44.3 us (22%)
  waiting for transfers between devices  32.5 us (16%)
  Pallas kernels  23.7 us (12%)
  between operations  13.9 us (7%)
  local copies, waits for them, and re-layouts  10.8 us (5%)
  other arithmetic  2.8 us (1%)
    all_to_all x2, blocking collectives, ring_scatter(): lax.all_to_all(blocks, 'lat', 0, 0, axis_index_groups=RINGS, tiled=True)  35 us
    pallas_call x9, Pallas kernels, call_kernel(): pl.pallas_call(body, out_shape=out_shape, in_specs=[pl.BlockSpec(memory_s...  23.7 us
    ppermute x7, starting transfers between devices, ring_shift(): return lax.ppermute(values, 'lat', pairs)  23.6 us
    ppermute x7, waiting for transfers between devices, ring_shift(): return lax.ppermute(values, 'lat', pairs)  16.1 us
    ppermute x5, starting transfers between devices, swap_cores(): return lax.ppermute(values, 'lon', [(i, i ^ 1) for i in range(count)])  15 us
    ppermute x2, starting transfers between devices, neighbours(): lax.ppermute(first, axis, [((i + 1) % count, i) for i in range(count)])  14.3 us
    ppermute x2, waiting for transfers between devices, swap_rings(): lax.ppermute(values, 'lat', [(i, (i + Z_RING) % count) for i in range(cou...  10.8 us
    all_gather x1, blocking collectives, on_device(): lax.all_gather(own_merge, 'lat', axis_index_groups=[[z, z + Z_RING] for z...  9.31 us
  transfers between devices with their start and end apart: 20, of which 9 were waited for; matrix products, arithmetic and copies ran while one was open for 3% of the time, Pallas kernels for 5%

profile of v9, /device:TPU:1, one launch (start us, length us, event | category | flops | bytes accessed | tf_op | source)
XLA Modules:
  0.0 196.4 jit_solution(10619396095712412702)
XLA Ops:
  9.6 9.3 %all-gather = bf16[320,640]{1,0:T(8,128)(2,1)} all-gather(bf16[160,640]{1,0:T(8,128)(2,1)} %shard_map.154), channel_id=2, replica_groups={{0,256},{32,288},{64,320},{96,352},{128,384},{160,416},{192,448},{224,4..., dimensions={0}, use_global_device_ids=true | all-gather | bytes 614400 | tf_op jit(solution)/shard_map/all_gather | solution.py:502
  21.8 5.7 %collective-permute-start = (bf16[2,2,16,512]{3,2,1,0:T(8,128)(2,1)S(1)}, bf16[2,2,16,512]{3,2,1,0:T(8,128)(2,1)S(1)}, u32[]{:S(2)}, u32[]{:S(2)}) collective-permute-start(bf16[2,2,16,512]{3,2,1,0:T(8,128)(2,1)S(1)} %get-tuple-element.51), channel_id=1, source_target_pairs={{0,32},{32,64},{64,96},{96,128},{128,160},{160,192},{192,224},{224... | collective-permute-start | bytes 196616 | tf_op jit(solution)/shard_map/ppermute | solution.py:423
  27.4 9.4 %collective-permute-start.1 = (bf16[2,2,16,512]{3,2,1,0:T(8,128)(2,1)S(1)}, bf16[2,2,16,512]{3,2,1,0:T(8,128)(2,1)S(1)}, u32[]{:S(2)}, u32[]{:S(2)}) collective-permute-start(bf16[2,2,16,512]{3,2,1,0:T(8,128)(2,1)S(1)} %get-tuple-element.52), channel_id=1, source_target_pairs={{32,0},{64,32},{96,64},{128,96},{160,128},{192,160},{224,192},{256... | collective-permute-start | bytes 196616 | tf_op jit(solution)/shard_map/ppermute | solution.py:424
  38.3 4.9 %collective-permute-start.3 = (bf16[16,2,2,512]{3,2,1,0:T(2,128)(2,1)S(1)}, bf16[16,2,2,512]{3,2,1,0:T(2,128)(2,1)S(1)}, u32[]{:S(2)}, u32[]{:S(2)}) collective-permute-start(bf16[16,2,2,512]{3,2,1,0:T(2,128)(2,1)S(1)} %get-tuple-element.49), channel_id=1, source_target_pairs={{1,0},{2,1},{3,2},{4,3},{5,4},{6,5},{7,6},{8,7},{9,8},{10,9},{11,1... | collective-permute-start | bytes 196616 | tf_op jit(solution)/shard_map/ppermute | solution.py:424
  46.2 3.6 %collective-permute-start.4 = (bf16[2048,128]{1,0:T(8,128)(2,1)}, bf16[2048,128]{1,0:T(8,128)(2,1)S(1)}, u32[]{:S(2)}, u32[]{:S(2)}) collective-permute-start(bf16[2048,128]{1,0:T(8,128)(2,1)} %constant_dynamic-slice_fusion.1), channel_id=1, source_target_pairs={{0,256},{32,288},{64,320},{96,352},{128,384},{160,416},{192,448},{... | collective-permute-start | bytes 1572872 | tf_op jit(solution)/shard_map/ppermute | solution.py:435
  50.6 3.1 %collective-permute-start.5 = (bf16[96,2048]{1,0:T(8,128)(2,1)}, bf16[96,2048]{1,0:T(8,128)(2,1)}, u32[]{:S(2)}, u32[]{:S(2)}) collective-permute-start(bf16[96,2048]{1,0:T(8,128)(2,1)} %constant_dynamic-slice_fusion), channel_id=1, source_target_pairs={{0,256},{32,288},{64,320},{96,352},{128,384},{160,416},{192,448},{... | collective-permute-start | bytes 1179656 | tf_op jit(solution)/shard_map/ppermute | solution.py:435
  56.4 3.3 %shard_map.155.attended_ref = bf16[384,512]{1,0:T(8,128)(2,1)S(1)} custom-call(bf16[512,512]{1,0:T(8,128)(2,1)S(1)} %bitcast.28, bf16[64,512]{1,0:T(8,128)(2,1)S(1)} %reshape.77.left_ref, bf16[64,512]{1,0:T(8,128)(2,1)S(1)} %reshape.78.right_ref, f32[1,512]{1,0:T(1,128)S(1)} %bitcast.31, bf16[3,512,512]{2,1,0:T(8,128)(2,1)S(1)} %copy-done.11, ...), custom_call_target="tpu_custom_call" | custom-call | flops 1006632960 | bytes 2314752 | tf_op jit(solution)/shard_map/pallas_call | solution.py:23
  60.5 10.8 %collective-permute-done.5.mine_ref = bf16[96,2048]{1,0:T(8,128)(2,1)} collective-permute-done((bf16[96,2048]{1,0:T(8,128)(2,1)}, bf16[96,2048]{1,0:T(8,128)(2,1)}, u32[]{:S(2)}, u32[]{:S(2)}) %collective-permute-start.5) | collective-permute-done | bytes 393248 | tf_op jit(solution)/shard_map/ppermute | solution.py:435
  71.3 2.9 %all-gather.4.cloned.1.call-done.weights_ref = bf16[2,1280,640]{2,1,0:T(8,128)(2,1)} async-done(((bf16[2,160,640]{2,1,0:T(8,128)(2,1)}), bf16[2,1280,640]{2,1,0:T(8,128)(2,1)}) %all-gather.4.cloned.1.call-update) | async-done | bytes 3276816 | tf_op jit(solution)/shard_map/all_gather | solution.py:505
  74.2 4.3 %shard_map.156 = (bf16[384,512]{1,0:T(8,128)(2,1)}, bf16[96,2048]{1,0:T(8,128)(2,1)}) custom-call(bf16[384,512]{1,0:T(8,128)(2,1)} %copy-done.6, bf16[384,512]{1,0:T(8,128)(2,1)} %bitcast.32, bf16[2,8,160,640]{3,2,1,0:T(8,128)(2,1)} %bitcast.22, f32[1,2048]{1,0:T(1,128)} %bitcast.35), custom_call_target="tpu_custom_call" | custom-call | flops 201326592 | bytes 4071424 | tf_op jit(solution)/shard_map/pallas_call | solution.py:23
  89.7 3.9 %collective-permute-start.9 = (bf16[24,4096]{1,0:T(8,128)(2,1)S(1)}, bf16[24,4096]{1,0:T(8,128)(2,1)S(1)}, u32[]{:S(2)}, u32[]{:S(2)}) collective-permute-start(bf16[24,4096]{1,0:T(8,128)(2,1)S(1)} %get-tuple-element.37.refs_0_), channel_id=1, source_target_pairs={{0,224},{32,0},{64,32},{96,64},{128,96},{160,128},{192,160},{224,1... | collective-permute-start | bytes 589832 | tf_op jit(solution)/shard_map/ppermute | solution.py:444
  97.7 4.9 %collective-permute-done.8.refs_1_ = bf16[24,4096]{1,0:T(8,128)(2,1)S(1)} collective-permute-done((bf16[24,4096]{1,0:T(8,128)(2,1)S(1)}, bf16[24,4096]{1,0:T(8,128)(2,1)S(1)}, u32[]{:S(2)}, u32[]{:S(2)}) %collective-permute-start.8) | collective-permute-done | bytes 196640 | tf_op jit(solution)/shard_map/ppermute | solution.py:444
  102.6 3.3 %collective-permute-start.13 = (bf16[2048,128]{1,0:T(8,128)(2,1)S(1)}, bf16[2048,128]{1,0:T(8,128)(2,1)S(1)}, u32[]{:S(2)}, u32[]{:S(2)}) collective-permute-start(bf16[2048,128]{1,0:T(8,128)(2,1)S(1)} %collective-permute-done.4.refs_7_.mine_ref), channel_id=1, source_target_pairs={{0,1},{1,0},{2,3},{3,2},{4,5},{5,4},{6,7},{7,6},{8,9},{9,8},{10,11... | collective-permute-start | bytes 1572872 | tf_op jit(solution)/shard_map/ppermute | solution.py:430
  107.9 4.6 %collective-permute-start.11 = (bf16[24,4096]{1,0:T(8,128)(2,1)S(1)}, bf16[24,4096]{1,0:T(8,128)(2,1)S(1)}, u32[]{:S(2)}, u32[]{:S(2)}) collective-permute-start(bf16[24,4096]{1,0:T(8,128)(2,1)S(1)} %collective-permute-done.9.refs_2_), channel_id=1, source_target_pairs={{0,224},{32,0},{64,32},{96,64},{128,96},{160,128},{192,160},{224,1... | collective-permute-start | bytes 589832 | tf_op jit(solution)/shard_map/ppermute | solution.py:444
  112.5 3.2 %collective-permute-done.10.refs_3_ = bf16[24,4096]{1,0:T(8,128)(2,1)S(1)} collective-permute-done((bf16[24,4096]{1,0:T(8,128)(2,1)S(1)}, bf16[24,4096]{1,0:T(8,128)(2,1)S(1)}, u32[]{:S(2)}, u32[]{:S(2)}) %collective-permute-start.10) | collective-permute-done | bytes 196640 | tf_op jit(solution)/shard_map/ppermute | solution.py:444
  115.7 2.6 %collective-permute-start.16 = (bf16[96,2048]{1,0:T(8,128)(2,1)}, bf16[96,2048]{1,0:T(8,128)(2,1)S(1)}, u32[]{:S(2)}, u32[]{:S(2)}) collective-permute-start(bf16[96,2048]{1,0:T(8,128)(2,1)} %collective-permute-done.5.mine_ref), channel_id=1, source_target_pairs={{0,1},{1,0},{2,3},{3,2},{4,5},{5,4},{6,7},{7,6},{8,9},{9,8},{10,11... | collective-permute-start | bytes 1179656 | tf_op jit(solution)/shard_map/ppermute | solution.py:430
  118.3 4.8 %collective-permute-start.12 = (bf16[24,4096]{1,0:T(8,128)(2,1)S(1)}, bf16[24,4096]{1,0:T(8,128)(2,1)S(1)}, u32[]{:S(2)}, u32[]{:S(2)}) collective-permute-start(bf16[24,4096]{1,0:T(8,128)(2,1)S(1)} %get-tuple-element.37.refs_0_), channel_id=1, source_target_pairs={{0,128},{32,160},{64,192},{96,224},{128,0},{160,32},{192,64},{224,... | collective-permute-start | bytes 589832 | tf_op jit(solution)/shard_map/ppermute | solution.py:444
  125.0 4.6 %collective-permute-start.15 = (bf16[24,4096]{1,0:T(8,128)(2,1)S(1)}, bf16[24,4096]{1,0:T(8,128)(2,1)S(1)}, u32[]{:S(2)}, u32[]{:S(2)}) collective-permute-start(bf16[24,4096]{1,0:T(8,128)(2,1)S(1)} %collective-permute-done.11.refs_4_), channel_id=1, source_target_pairs={{0,224},{32,0},{64,32},{96,64},{128,96},{160,128},{192,160},{224,1... | collective-permute-start | bytes 589832 | tf_op jit(solution)/shard_map/ppermute | solution.py:444
  129.6 3.8 %collective-permute-done.12.refs_5_ = bf16[24,4096]{1,0:T(8,128)(2,1)S(1)} collective-permute-done((bf16[24,4096]{1,0:T(8,128)(2,1)S(1)}, bf16[24,4096]{1,0:T(8,128)(2,1)S(1)}, u32[]{:S(2)}, u32[]{:S(2)}) %collective-permute-start.12) | collective-permute-done | bytes 196640 | tf_op jit(solution)/shard_map/ppermute | solution.py:444
  137.9 25.6 %all_to_all.10.x_ref = bf16[8,8,2,24,128]{4,3,2,1,0:T(8,128)(2,1)S(1)} all-to-all(bf16[8,8,2,24,128]{4,3,2,1,0:T(8,128)(2,1)S(1)} %broadcast_in_dim.42), channel_id=1, replica_groups={{0,32,64,96,128,160,192,224},{256,288,320,352,384,416,448,480},{1,33,65..., dimensions={0} | all-to-all | bytes 1572864 | tf_op jit(solution)/shard_map/all_to_all | solution.py:439
  163.6 4.0 %shard_map.161 = (bf16[8,2,24,64]{3,2,1,0:T(8,128)(2,1)S(1)}, f32[24,2048]{1,0:T(8,128)S(1)}) custom-call(s32[3]{0:T(128)S(1)} %pad_add_fusion.1.core_ref.place_ref, bf16[8,8,2,24,128]{4,3,2,1,0:T(8,128)(2,1)S(1)} %all_to_all.10.x_ref, f32[1,2048]{1,0:T(1,128)S(1)} %bitcast.30, bf16[192,2048]{1,0:T(8,128)(2,1)S(1)} %bitcast.27, ...), custom_call_target="tpu_custom_call" | custom-call | flops 301989888 | bytes 2367500 | tf_op jit(solution)/shard_map/pallas_call | solution.py:23
  167.6 4.2 %collective-permute-start.17 = (bf16[1152,16,128]{2,1,0:T(8,128)(2,1)}, bf16[1152,16,128]{2,1,0:T(8,128)(2,1)}, u32[]{:S(2)}, u32[]{:S(2)}) collective-permute-start(bf16[1152,16,128]{2,1,0:T(8,128)(2,1)} %bitcast.24), channel_id=1, source_target_pairs={{0,1},{1,0},{2,3},{3,2},{4,5},{5,4},{6,7},{7,6},{8,9},{9,8},{10,11... | collective-permute-start | bytes 14155784 | tf_op jit(solution)/shard_map/ppermute | solution.py:430
  172.0 9.4 %all_to_all.11 = bf16[8,2,1536]{2,1,0:T(2,128)(2,1)S(1)} all-to-all(bf16[8,2,1536]{2,1,0:T(2,128)(2,1)S(1)} %reshape.87), channel_id=1, replica_groups={{0,32,64,96,128,160,192,224},{256,288,320,352,384,416,448,480},{1,33,65..., dimensions={0} | all-to-all | bytes 98304 | tf_op jit(solution)/shard_map/all_to_all | solution.py:439
  183.8 5.8 %shard_map.162 = bf16[384,512]{1,0:T(8,128)(2,1)} custom-call(s32[3]{0:T(128)S(1)} %pad_add_fusion.1.core_ref.place_ref, bf16[8,2,24,64]{3,2,1,0:T(8,128)(2,1)S(1)} %reshape.88.heads_ref, f32[24,2048]{1,0:T(8,128)S(1)} %get-tuple-element.44.own_coarse_ref, bf16[1152,16,128]{2,1,0:T(8,128)(2,1)S(1)} %bitcast.25, ...), custom_call_target="tpu_custom_call" | custom-call | flops 301989888 | bytes 10272780 | tf_op jit(solution)/shard_map/pallas_call | solution.py:23
  (88 shorter events, 40.6 us)
Async XLA Ops:
  6.5 43.3 %copy-start.4 = (bf16[3,2048,64]{1,2,0:T(8,128)(2,1)S(1)}, bf16[3,2048,64]{1,2,0:T(8,128)(2,1)}, u32[]{:S(2)}) copy-start(bf16[3,2048,64]{1,2,0:T(8,128)(2,1)} %param.28) | copy-start | bytes 2359300
  6.5 47.5 %copy-start.13 = (f32[512]{0:T(512)S(1)}, f32[512]{0:T(512)}, u32[]{:S(2)}) copy-start(f32[512]{0:T(512)} %param.20) | copy-start | bytes 6148
  6.5 67.7 %all-gather.4.cloned.1.call-start = ((), (), s32[]{:S(2)}) async-start(), calls=%async_computation.2 | async-start | bytes 3686400 | tf_op jit(solution)/shard_map/all_gather | solution.py:505
  18.9 148.7 %all-gather.6.cloned.1.call-start = ((), (), s32[]{:S(2)}) async-start(), calls=%async_computation.3 | async-start | bytes 5308416 | tf_op jit(solution)/shard_map/all_gather | solution.py:589
  21.8 16.4 %collective-permute-start = (bf16[2,2,16,512]{3,2,1,0:T(8,128)(2,1)S(1)}, bf16[2,2,16,512]{3,2,1,0:T(8,128)(2,1)S(1)}, u32[]{:S(2)}, u32[]{:S(2)}) collective-permute-start(bf16[2,2,16,512]{3,2,1,0:T(8,128)(2,1)S(1)} %get-tuple-element.51), channel_id=1, source_target_pairs={{0,32},{32,64},{64,96},{96,128},{128,160},{160,192},{192,224},{224... | collective-permute-start | bytes 196616 | tf_op jit(solution)/shard_map/ppermute | solution.py:423
  27.4 10.7 %collective-permute-start.1 = (bf16[2,2,16,512]{3,2,1,0:T(8,128)(2,1)S(1)}, bf16[2,2,16,512]{3,2,1,0:T(8,128)(2,1)S(1)}, u32[]{:S(2)}, u32[]{:S(2)}) collective-permute-start(bf16[2,2,16,512]{3,2,1,0:T(8,128)(2,1)S(1)} %get-tuple-element.52), channel_id=1, source_target_pairs={{32,0},{64,32},{96,64},{128,96},{160,128},{192,160},{224,192},{256... | collective-permute-start | bytes 196616 | tf_op jit(solution)/shard_map/ppermute | solution.py:424
  38.3 11.5 %collective-permute-start.3 = (bf16[16,2,2,512]{3,2,1,0:T(2,128)(2,1)S(1)}, bf16[16,2,2,512]{3,2,1,0:T(2,128)(2,1)S(1)}, u32[]{:S(2)}, u32[]{:S(2)}) collective-permute-start(bf16[16,2,2,512]{3,2,1,0:T(2,128)(2,1)S(1)} %get-tuple-element.49), channel_id=1, source_target_pairs={{1,0},{2,1},{3,2},{4,3},{5,4},{6,5},{7,6},{8,7},{9,8},{10,9},{11,1... | collective-permute-start | bytes 196616 | tf_op jit(solution)/shard_map/ppermute | solution.py:424
  43.3 6.5 %collective-permute-start.2 = (bf16[16,2,2,512]{3,2,1,0:T(2,128)(2,1)S(1)}, bf16[16,2,2,512]{3,2,1,0:T(2,128)(2,1)S(1)}, u32[]{:S(2)}, u32[]{:S(2)}) collective-permute-start(bf16[16,2,2,512]{3,2,1,0:T(2,128)(2,1)S(1)} %get-tuple-element.50), channel_id=1, source_target_pairs={{0,1},{1,2},{2,3},{3,4},{4,5},{5,6},{6,7},{7,8},{8,9},{9,10},{10,1... | collective-permute-start | bytes 196616 | tf_op jit(solution)/shard_map/ppermute | solution.py:423
  46.2 25.1 %collective-permute-start.4 = (bf16[2048,128]{1,0:T(8,128)(2,1)}, bf16[2048,128]{1,0:T(8,128)(2,1)S(1)}, u32[]{:S(2)}, u32[]{:S(2)}) collective-permute-start(bf16[2048,128]{1,0:T(8,128)(2,1)} %constant_dynamic-slice_fusion.1), channel_id=1, source_target_pairs={{0,256},{32,288},{64,320},{96,352},{128,384},{160,416},{192,448},{... | collective-permute-start | bytes 1572872 | tf_op jit(solution)/shard_map/ppermute | solution.py:435
  50.6 20.7 %collective-permute-start.5 = (bf16[96,2048]{1,0:T(8,128)(2,1)}, bf16[96,2048]{1,0:T(8,128)(2,1)}, u32[]{:S(2)}, u32[]{:S(2)}) collective-permute-start(bf16[96,2048]{1,0:T(8,128)(2,1)} %constant_dynamic-slice_fusion), channel_id=1, source_target_pairs={{0,256},{32,288},{64,320},{96,352},{128,384},{160,416},{192,448},{... | collective-permute-start | bytes 1179656 | tf_op jit(solution)/shard_map/ppermute | solution.py:435
  78.5 4.1 %collective-permute-start.6 = (bf16[96,2048]{1,0:T(8,128)(2,1)}, bf16[96,2048]{1,0:T(8,128)(2,1)S(1)}, u32[]{:S(2)}, u32[]{:S(2)}) collective-permute-start(bf16[96,2048]{1,0:T(8,128)(2,1)} %get-tuple-element.34.own_ref), channel_id=1, source_target_pairs={{0,1},{1,0},{2,3},{3,2},{4,5},{5,4},{6,7},{7,6},{8,9},{9,8},{10,11... | collective-permute-start | bytes 1179656 | tf_op jit(solution)/shard_map/ppermute | solution.py:430
  85.2 78.4 %copy-start.10 = (f32[2048]{0:T(1024)S(1)}, f32[2048]{0:T(1024)}, u32[]{:S(2)}) copy-start(f32[2048]{0:T(1024)} %param.27) | copy-start | bytes 24580
  85.2 3.4 %collective-permute-start.7 = (bf16[96,512]{1,0:T(8,128)(2,1)}, bf16[96,512]{1,0:T(8,128)(2,1)S(1)}, u32[]{:S(2)}, u32[]{:S(2)}) collective-permute-start(bf16[96,512]{1,0:T(8,128)(2,1)} %copy-done.12), channel_id=1, source_target_pairs={{0,1},{1,0},{2,3},{3,2},{4,5},{5,4},{6,7},{7,6},{8,9},{9,8},{10,11... | collective-permute-start | bytes 294920 | tf_op jit(solution)/shard_map/ppermute | solution.py:430
  89.7 8.0 %collective-permute-start.9 = (bf16[24,4096]{1,0:T(8,128)(2,1)S(1)}, bf16[24,4096]{1,0:T(8,128)(2,1)S(1)}, u32[]{:S(2)}, u32[]{:S(2)}) collective-permute-start(bf16[24,4096]{1,0:T(8,128)(2,1)S(1)} %get-tuple-element.37.refs_0_), channel_id=1, source_target_pairs={{0,224},{32,0},{64,32},{96,64},{128,96},{160,128},{192,160},{224,1... | collective-permute-start | bytes 589832 | tf_op jit(solution)/shard_map/ppermute | solution.py:444
  93.6 9.0 %collective-permute-start.8 = (bf16[24,4096]{1,0:T(8,128)(2,1)S(1)}, bf16[24,4096]{1,0:T(8,128)(2,1)S(1)}, u32[]{:S(2)}, u32[]{:S(2)}) collective-permute-start(bf16[24,4096]{1,0:T(8,128)(2,1)S(1)} %get-tuple-element.37.refs_0_), channel_id=1, source_target_pairs={{0,32},{32,64},{64,96},{96,128},{128,160},{160,192},{192,224},{224... | collective-permute-start | bytes 589832 | tf_op jit(solution)/shard_map/ppermute | solution.py:444
  102.6 22.3 %collective-permute-start.13 = (bf16[2048,128]{1,0:T(8,128)(2,1)S(1)}, bf16[2048,128]{1,0:T(8,128)(2,1)S(1)}, u32[]{:S(2)}, u32[]{:S(2)}) collective-permute-start(bf16[2048,128]{1,0:T(8,128)(2,1)S(1)} %collective-permute-done.4.refs_7_.mine_ref), channel_id=1, source_target_pairs={{0,1},{1,0},{2,3},{3,2},{4,5},{5,4},{6,7},{7,6},{8,9},{9,8},{10,11... | collective-permute-start | bytes 1572872 | tf_op jit(solution)/shard_map/ppermute | solution.py:430
  106.0 9.7 %collective-permute-start.10 = (bf16[24,4096]{1,0:T(8,128)(2,1)S(1)}, bf16[24,4096]{1,0:T(8,128)(2,1)S(1)}, u32[]{:S(2)}, u32[]{:S(2)}) collective-permute-start(bf16[24,4096]{1,0:T(8,128)(2,1)S(1)} %collective-permute-done.8.refs_1_), channel_id=1, source_target_pairs={{0,32},{32,64},{64,96},{96,128},{128,160},{160,192},{192,224},{224... | collective-permute-start | bytes 589832 | tf_op jit(solution)/shard_map/ppermute | solution.py:444
  107.9 17.1 %collective-permute-start.11 = (bf16[24,4096]{1,0:T(8,128)(2,1)S(1)}, bf16[24,4096]{1,0:T(8,128)(2,1)S(1)}, u32[]{:S(2)}, u32[]{:S(2)}) collective-permute-start(bf16[24,4096]{1,0:T(8,128)(2,1)S(1)} %collective-permute-done.9.refs_2_), channel_id=1, source_target_pairs={{0,224},{32,0},{64,32},{96,64},{128,96},{160,128},{192,160},{224,1... | collective-permute-start | bytes 589832 | tf_op jit(solution)/shard_map/ppermute | solution.py:444
  115.7 22.1 %collective-permute-start.16 = (bf16[96,2048]{1,0:T(8,128)(2,1)}, bf16[96,2048]{1,0:T(8,128)(2,1)S(1)}, u32[]{:S(2)}, u32[]{:S(2)}) collective-permute-start(bf16[96,2048]{1,0:T(8,128)(2,1)} %collective-permute-done.5.mine_ref), channel_id=1, source_target_pairs={{0,1},{1,0},{2,3},{3,2},{4,5},{5,4},{6,7},{7,6},{8,9},{9,8},{10,11... | collective-permute-start | bytes 1179656 | tf_op jit(solution)/shard_map/ppermute | solution.py:430
  118.3 15.1 %collective-permute-start.12 = (bf16[24,4096]{1,0:T(8,128)(2,1)S(1)}, bf16[24,4096]{1,0:T(8,128)(2,1)S(1)}, u32[]{:S(2)}, u32[]{:S(2)}) collective-permute-start(bf16[24,4096]{1,0:T(8,128)(2,1)S(1)} %get-tuple-element.37.refs_0_), channel_id=1, source_target_pairs={{0,128},{32,160},{64,192},{96,224},{128,0},{160,32},{192,64},{224,... | collective-permute-start | bytes 589832 | tf_op jit(solution)/shard_map/ppermute | solution.py:444
  123.0 13.7 %collective-permute-start.14 = (bf16[24,4096]{1,0:T(8,128)(2,1)S(1)}, bf16[24,4096]{1,0:T(8,128)(2,1)S(1)}, u32[]{:S(2)}, u32[]{:S(2)}) collective-permute-start(bf16[24,4096]{1,0:T(8,128)(2,1)S(1)} %collective-permute-done.10.refs_3_), channel_id=1, source_target_pairs={{0,32},{32,64},{64,96},{96,128},{128,160},{160,192},{192,224},{224... | collective-permute-start | bytes 589832 | tf_op jit(solution)/shard_map/ppermute | solution.py:444
  125.0 11.7 %collective-permute-start.15 = (bf16[24,4096]{1,0:T(8,128)(2,1)S(1)}, bf16[24,4096]{1,0:T(8,128)(2,1)S(1)}, u32[]{:S(2)}, u32[]{:S(2)}) collective-permute-start(bf16[24,4096]{1,0:T(8,128)(2,1)S(1)} %collective-permute-done.11.refs_4_), channel_id=1, source_target_pairs={{0,224},{32,0},{64,32},{96,64},{128,96},{160,128},{192,160},{224,1... | collective-permute-start | bytes 589832 | tf_op jit(solution)/shard_map/ppermute | solution.py:444
  134.7 46.8 %copy-start.5 = (bf16[384,512]{1,0:T(8,128)(2,1)S(1)}, bf16[384,512]{1,0:T(8,128)(2,1)}, u32[]{:S(2)}) copy-start(bf16[384,512]{1,0:T(8,128)(2,1)} %get-tuple-element.48.skip_ref) | copy-start | bytes 1179652
  167.6 13.8 %collective-permute-start.17 = (bf16[1152,16,128]{2,1,0:T(8,128)(2,1)}, bf16[1152,16,128]{2,1,0:T(8,128)(2,1)}, u32[]{:S(2)}, u32[]{:S(2)}) collective-permute-start(bf16[1152,16,128]{2,1,0:T(8,128)(2,1)} %bitcast.24), channel_id=1, source_target_pairs={{0,1},{1,0},{2,3},{3,2},{4,5},{5,4},{6,7},{7,6},{8,9},{9,8},{10,11... | collective-permute-start | bytes 14155784 | tf_op jit(solution)/shard_map/ppermute | solution.py:430
  (11 other events, 105.8 us)
Sparse Core Ops, SparseCore 0:
  19.0 55.1 all-gather.3
  85.3 59.8 all-gather.5

commit v10 on v8

--- a/solution.py
+++ b/solution.py
@@ -443,14 +443,6 @@
     return ring_scatter(jnp.broadcast_to(values[None], (Z_RING,) + values.shape))
 
 
-def in_order(flag, own, other, axis):
-    return jnp.where(
-        flag == 0,
-        jnp.concatenate([own, other], axis=axis),
-        jnp.concatenate([other, own], axis=axis),
-    )
-
-
 def after(values, *before):
     return lax.optimization_barrier((values,) + before)[0]
 
@@ -493,8 +485,10 @@
         (pltpu.SemaphoreType.DMA((12,)),),
         pulled=(1, 2, 3, 4, 5),
         vmem_mib=62,
-    )[None]
-    both_merge = in_order(ring, own_merge, swap_rings(own_merge), 0)
+    )
+    both_merge = lax.all_gather(
+        own_merge, "lat", axis_index_groups=[[z, z + Z_RING] for z in range(Z_RING)]
+    )
     merge_weights = lax.all_gather(
         both_merge, "lat", axis=1, axis_index_groups=RINGS, tiled=True
     )
@@ -511,10 +505,9 @@
     cells = jnp.concatenate([above, hidden, below], axis=0)
     qkv_third = qkv_third.transpose(0, 2, 1).reshape(-1, qkv_third.shape[1])
 
+    merge_third, cells = lax.optimization_barrier((merge_third, cells))
     left, right = neighbours(cells[:, :, :2], cells[:, :, -2:], "lon")
-    merge_third, qkv_third, left, right = lax.optimization_barrier(
-        (merge_third, qkv_third, left, right)
-    )
+    qkv_third, left, right = lax.optimization_barrier((qkv_third, left, right))
 
     merge_mine, qkv_mine = [
         swap_rings(lax.dynamic_slice_in_dim(table, core * (table.shape[0] // 2), table.shape[0] // 2))

time: 197 us -> 191 us (0.970)
  blocking collectives: 34.1 us -> 43.4 us
  starting transfers between devices: 80.4 us -> 72.1 us
  waiting for transfers between devices: 26.8 us -> 21.7 us
    all_gather x0 -> x1, blocking collectives: none -> 9.3 us  [on_device(): lax.all_gather(own_merge, 'lat', axis_index_groups=[[z, z + Z_RING] for z...]
    ppermute x3 -> x2, starting transfers between devices: 12.2 us -> 6.76 us  [swap_rings(): lax.ppermute(values, 'lat', [(i, (i + Z_RING) % count) for i in range(cou...]
    ppermute x2, starting transfers between devices: 16.4 us -> 14.3 us  [neighbours(): lax.ppermute(first, axis, [((i + 1) % count, i) for i in range(count)])]
    ppermute x3 -> x2, waiting for transfers between devices: 11 us -> 10.8 us  [swap_rings(): lax.ppermute(values, 'lat', [(i, (i + Z_RING) % count) for i in range(cou...]
  transfers between devices with their start and end apart: 22 -> 21, of which waited for: 11 -> 7; matrix products, arithmetic and copies ran while one was open for 3% -> 3% of each run, Pallas kernels for 6% -> 6%
where the time goes in v10:
time: 191 us; the launch traced here: 190 us
  starting transfers between devices  72.1 us (38%)
  blocking collectives  43.4 us (23%)
  Pallas kernels  23.7 us (12%)
  waiting for transfers between devices  21.7 us (11%)
  between operations  14 us (7%)
  local copies, waits for them, and re-layouts  10.9 us (6%)
  other arithmetic  2.85 us (1%)
    all_to_all x2, blocking collectives, ring_scatter(): lax.all_to_all(blocks, 'lat', 0, 0, axis_index_groups=RINGS, tiled=True)  34.1 us
    ppermute x8, starting transfers between devices, ring_shift(): return lax.ppermute(values, 'lat', pairs)  27 us
    pallas_call x9, Pallas kernels, call_kernel(): pl.pallas_call(body, out_shape=out_shape, in_specs=[pl.BlockSpec(memory_s...  23.7 us
    ppermute x5, starting transfers between devices, swap_cores(): return lax.ppermute(values, 'lon', [(i, i ^ 1) for i in range(count)])  16.3 us
    ppermute x2, starting transfers between devices, neighbours(): lax.ppermute(first, axis, [((i + 1) % count, i) for i in range(count)])  14.3 us
    ppermute x2, waiting for transfers between devices, swap_rings(): lax.ppermute(values, 'lat', [(i, (i + Z_RING) % count) for i in range(cou...  10.8 us
    all_gather x1, blocking collectives, on_device(): lax.all_gather(own_merge, 'lat', axis_index_groups=[[z, z + Z_RING] for z...  9.3 us
    ppermute x2, starting transfers between devices, neighbours(): lax.ppermute(last, axis, [(i, (i + 1) % count) for i in range(count)])  7.69 us
  transfers between devices with their start and end apart: 21, of which 7 were waited for; matrix products, arithmetic and copies ran while one was open for 3% of the time, Pallas kernels for 6%

profile of v10, /device:TPU:1, one launch (start us, length us, event | category | flops | bytes accessed | tf_op | source)
XLA Modules:
  0.0 189.6 jit_solution(11930301017968567549)
XLA Ops:
  9.6 9.3 %all-gather = bf16[320,640]{1,0:T(8,128)(2,1)} all-gather(bf16[160,640]{1,0:T(8,128)(2,1)} %shard_map.154), channel_id=2, replica_groups={{0,256},{32,288},{64,320},{96,352},{128,384},{160,416},{192,448},{224,4..., dimensions={0}, use_global_device_ids=true | all-gather | bytes 614400 | tf_op jit(solution)/shard_map/all_gather | solution.py:489
  21.8 5.7 %collective-permute-start = (bf16[2,2,16,512]{3,2,1,0:T(8,128)(2,1)S(1)}, bf16[2,2,16,512]{3,2,1,0:T(8,128)(2,1)S(1)}, u32[]{:S(2)}, u32[]{:S(2)}) collective-permute-start(bf16[2,2,16,512]{3,2,1,0:T(8,128)(2,1)S(1)} %get-tuple-element.49), channel_id=1, source_target_pairs={{0,32},{32,64},{64,96},{96,128},{128,160},{160,192},{192,224},{224... | collective-permute-start | bytes 196616 | tf_op jit(solution)/shard_map/ppermute | solution.py:418
  27.5 9.4 %collective-permute-start.1 = (bf16[2,2,16,512]{3,2,1,0:T(8,128)(2,1)S(1)}, bf16[2,2,16,512]{3,2,1,0:T(8,128)(2,1)S(1)}, u32[]{:S(2)}, u32[]{:S(2)}) collective-permute-start(bf16[2,2,16,512]{3,2,1,0:T(8,128)(2,1)S(1)} %get-tuple-element.50), channel_id=1, source_target_pairs={{32,0},{64,32},{96,64},{128,96},{160,128},{192,160},{224,192},{256... | collective-permute-start | bytes 196616 | tf_op jit(solution)/shard_map/ppermute | solution.py:419
  38.4 4.9 %collective-permute-start.3 = (bf16[16,2,2,512]{3,2,1,0:T(2,128)(2,1)S(1)}, bf16[16,2,2,512]{3,2,1,0:T(2,128)(2,1)S(1)}, u32[]{:S(2)}, u32[]{:S(2)}) collective-permute-start(bf16[16,2,2,512]{3,2,1,0:T(2,128)(2,1)S(1)} %get-tuple-element.47), channel_id=1, source_target_pairs={{1,0},{2,1},{3,2},{4,3},{5,4},{6,5},{7,6},{8,7},{9,8},{10,9},{11,1... | collective-permute-start | bytes 196616 | tf_op jit(solution)/shard_map/ppermute | solution.py:419
  46.2 3.6 %collective-permute-start.4 = (bf16[2048,128]{1,0:T(8,128)(2,1)}, bf16[2048,128]{1,0:T(8,128)(2,1)S(1)}, u32[]{:S(2)}, u32[]{:S(2)}) collective-permute-start(bf16[2048,128]{1,0:T(8,128)(2,1)} %constant_dynamic-slice_fusion.1), channel_id=1, source_target_pairs={{0,256},{32,288},{64,320},{96,352},{128,384},{160,416},{192,448},{... | collective-permute-start | bytes 1572872 | tf_op jit(solution)/shard_map/ppermute | solution.py:430
  50.7 3.2 %collective-permute-start.5 = (bf16[96,2048]{1,0:T(8,128)(2,1)}, bf16[96,2048]{1,0:T(8,128)(2,1)}, u32[]{:S(2)}, u32[]{:S(2)}) collective-permute-start(bf16[96,2048]{1,0:T(8,128)(2,1)} %constant_dynamic-slice_fusion), channel_id=1, source_target_pairs={{0,256},{32,288},{64,320},{96,352},{128,384},{160,416},{192,448},{... | collective-permute-start | bytes 1179656 | tf_op jit(solution)/shard_map/ppermute | solution.py:430
  56.5 3.3 %shard_map.155.attended_ref = bf16[384,512]{1,0:T(8,128)(2,1)S(1)} custom-call(bf16[512,512]{1,0:T(8,128)(2,1)S(1)} %bitcast.28, bf16[64,512]{1,0:T(8,128)(2,1)S(1)} %reshape.77.left_ref, bf16[64,512]{1,0:T(8,128)(2,1)S(1)} %reshape.78.right_ref, f32[1,512]{1,0:T(1,128)S(1)} %bitcast.31, bf16[3,512,512]{2,1,0:T(8,128)(2,1)S(1)} %copy-done.11, ...), custom_call_target="tpu_custom_call" | custom-call | flops 1006632960 | bytes 2314752 | tf_op jit(solution)/shard_map/pallas_call | solution.py:23
  60.6 10.8 %collective-permute-done.5.mine_ref = bf16[96,2048]{1,0:T(8,128)(2,1)} collective-permute-done((bf16[96,2048]{1,0:T(8,128)(2,1)}, bf16[96,2048]{1,0:T(8,128)(2,1)}, u32[]{:S(2)}, u32[]{:S(2)}) %collective-permute-start.5) | collective-permute-done | bytes 393248 | tf_op jit(solution)/shard_map/ppermute | solution.py:430
  71.4 2.9 %all-gather.4.cloned.1.call-done.weights_ref = bf16[2,1280,640]{2,1,0:T(8,128)(2,1)} async-done(((bf16[2,160,640]{2,1,0:T(8,128)(2,1)}), bf16[2,1280,640]{2,1,0:T(8,128)(2,1)}) %all-gather.4.cloned.1.call-update) | async-done | bytes 3276816 | tf_op jit(solution)/shard_map/all_gather | solution.py:492
  74.3 4.3 %shard_map.156 = (bf16[384,512]{1,0:T(8,128)(2,1)}, bf16[96,2048]{1,0:T(8,128)(2,1)}) custom-call(bf16[384,512]{1,0:T(8,128)(2,1)} %copy-done.6, bf16[384,512]{1,0:T(8,128)(2,1)} %bitcast.32, bf16[2,8,160,640]{3,2,1,0:T(8,128)(2,1)} %bitcast.22, f32[1,2048]{1,0:T(1,128)} %bitcast.35), custom_call_target="tpu_custom_call" | custom-call | flops 201326592 | bytes 4071424 | tf_op jit(solution)/shard_map/pallas_call | solution.py:23
  78.6 2.6 %collective-permute-start.6 = (bf16[96,2048]{1,0:T(8,128)(2,1)}, bf16[96,2048]{1,0:T(8,128)(2,1)S(1)}, u32[]{:S(2)}, u32[]{:S(2)}) collective-permute-start(bf16[96,2048]{1,0:T(8,128)(2,1)} %get-tuple-element.33.own_ref), channel_id=1, source_target_pairs={{0,1},{1,0},{2,3},{3,2},{4,5},{5,4},{6,7},{7,6},{8,9},{9,8},{10,11... | collective-permute-start | bytes 1179656 | tf_op jit(solution)/shard_map/ppermute | solution.py:425
  92.2 4.1 %collective-permute-start.9 = (bf16[24,4096]{1,0:T(8,128)(2,1)S(1)}, bf16[24,4096]{1,0:T(8,128)(2,1)S(1)}, u32[]{:S(2)}, u32[]{:S(2)}) collective-permute-start(bf16[24,4096]{1,0:T(8,128)(2,1)S(1)} %get-tuple-element.36.refs_0_), channel_id=1, source_target_pairs={{0,224},{32,0},{64,32},{96,64},{128,96},{160,128},{192,160},{224,1... | collective-permute-start | bytes 589832 | tf_op jit(solution)/shard_map/ppermute | solution.py:439
  96.3 2.7 %collective-permute-done.8.refs_1_ = bf16[24,4096]{1,0:T(8,128)(2,1)S(1)} collective-permute-done((bf16[24,4096]{1,0:T(8,128)(2,1)S(1)}, bf16[24,4096]{1,0:T(8,128)(2,1)S(1)}, u32[]{:S(2)}, u32[]{:S(2)}) %collective-permute-start.8) | collective-permute-done | bytes 196640 | tf_op jit(solution)/shard_map/ppermute | solution.py:439
  101.0 3.1 %collective-permute-start.14 = (bf16[2048,128]{1,0:T(8,128)(2,1)S(1)}, bf16[2048,128]{1,0:T(8,128)(2,1)S(1)}, u32[]{:S(2)}, u32[]{:S(2)}) collective-permute-start(bf16[2048,128]{1,0:T(8,128)(2,1)S(1)} %collective-permute-done.4.refs_8_.mine_ref), channel_id=1, source_target_pairs={{0,1},{1,0},{2,3},{3,2},{4,5},{5,4},{6,7},{7,6},{8,9},{9,8},{10,11... | collective-permute-start | bytes 1572872 | tf_op jit(solution)/shard_map/ppermute | solution.py:425
  104.1 4.9 %collective-permute-start.11 = (bf16[24,4096]{1,0:T(8,128)(2,1)S(1)}, bf16[24,4096]{1,0:T(8,128)(2,1)S(1)}, u32[]{:S(2)}, u32[]{:S(2)}) collective-permute-start(bf16[24,4096]{1,0:T(8,128)(2,1)S(1)} %collective-permute-done.9.refs_2_), channel_id=1, source_target_pairs={{0,224},{32,0},{64,32},{96,64},{128,96},{160,128},{192,160},{224,1... | collective-permute-start | bytes 589832 | tf_op jit(solution)/shard_map/ppermute | solution.py:439
  108.9 2.4 %collective-permute-start.16 = (bf16[96,2048]{1,0:T(8,128)(2,1)}, bf16[96,2048]{1,0:T(8,128)(2,1)S(1)}, u32[]{:S(2)}, u32[]{:S(2)}) collective-permute-start(bf16[96,2048]{1,0:T(8,128)(2,1)} %collective-permute-done.5.mine_ref), channel_id=1, source_target_pairs={{0,1},{1,0},{2,3},{3,2},{4,5},{5,4},{6,7},{7,6},{8,9},{9,8},{10,11... | collective-permute-start | bytes 1179656 | tf_op jit(solution)/shard_map/ppermute | solution.py:425
  113.3 5.4 %collective-permute-start.13 = (bf16[24,4096]{1,0:T(8,128)(2,1)S(1)}, bf16[24,4096]{1,0:T(8,128)(2,1)S(1)}, u32[]{:S(2)}, u32[]{:S(2)}) collective-permute-start(bf16[24,4096]{1,0:T(8,128)(2,1)S(1)} %collective-permute-done.11.refs_4_), channel_id=1, source_target_pairs={{0,224},{32,0},{64,32},{96,64},{128,96},{160,128},{192,160},{224,1... | collective-permute-start | bytes 589832 | tf_op jit(solution)/shard_map/ppermute | solution.py:439
  118.6 2.4 %collective-permute-done.12.refs_5_ = bf16[24,4096]{1,0:T(8,128)(2,1)S(1)} collective-permute-done((bf16[24,4096]{1,0:T(8,128)(2,1)S(1)}, bf16[24,4096]{1,0:T(8,128)(2,1)S(1)}, u32[]{:S(2)}, u32[]{:S(2)}) %collective-permute-start.12) | collective-permute-done | bytes 196640 | tf_op jit(solution)/shard_map/ppermute | solution.py:439
  123.1 4.6 %collective-permute-start.17 = (bf16[24,2048]{1,0:T(8,128)(2,1)S(1)}, bf16[24,2048]{1,0:T(8,128)(2,1)S(1)}, u32[]{:S(2)}, u32[]{:S(2)}) collective-permute-start(bf16[24,2048]{1,0:T(8,128)(2,1)S(1)} %slice.26), channel_id=1, source_target_pairs={{0,224},{32,0},{64,32},{96,64},{128,96},{160,128},{192,160},{224,1... | collective-permute-start | bytes 294920 | tf_op jit(solution)/shard_map/ppermute | solution.py:439
  130.4 24.8 %all_to_all.10.x_ref = bf16[8,8,2,24,128]{4,3,2,1,0:T(8,128)(2,1)S(1)} all-to-all(bf16[8,8,2,24,128]{4,3,2,1,0:T(8,128)(2,1)S(1)} %broadcast_in_dim.42), channel_id=1, replica_groups={{0,32,64,96,128,160,192,224},{256,288,320,352,384,416,448,480},{1,33,65..., dimensions={0} | all-to-all | bytes 1572864 | tf_op jit(solution)/shard_map/all_to_all | solution.py:434
  155.2 4.0 %shard_map.161 = (bf16[8,2,24,64]{3,2,1,0:T(8,128)(2,1)S(1)}, f32[24,2048]{1,0:T(8,128)S(1)}) custom-call(s32[3]{0:T(128)S(1)} %pad_add_fusion.1.core_ref.place_ref, bf16[8,8,2,24,128]{4,3,2,1,0:T(8,128)(2,1)S(1)} %all_to_all.10.x_ref, f32[1,2048]{1,0:T(1,128)S(1)} %bitcast.30, bf16[192,2048]{1,0:T(8,128)(2,1)S(1)} %bitcast.27, ...), custom_call_target="tpu_custom_call" | custom-call | flops 301989888 | bytes 2367500 | tf_op jit(solution)/shard_map/pallas_call | solution.py:23
  159.3 5.9 %collective-permute-start.18 = (bf16[1152,16,128]{2,1,0:T(8,128)(2,1)}, bf16[1152,16,128]{2,1,0:T(8,128)(2,1)}, u32[]{:S(2)}, u32[]{:S(2)}) collective-permute-start(bf16[1152,16,128]{2,1,0:T(8,128)(2,1)} %bitcast.24), channel_id=1, source_target_pairs={{0,1},{1,0},{2,3},{3,2},{4,5},{5,4},{6,7},{7,6},{8,9},{9,8},{10,11... | collective-permute-start | bytes 14155784 | tf_op jit(solution)/shard_map/ppermute | solution.py:425
  165.3 9.4 %all_to_all.11 = bf16[8,2,1536]{2,1,0:T(2,128)(2,1)S(1)} all-to-all(bf16[8,2,1536]{2,1,0:T(2,128)(2,1)S(1)} %reshape.87), channel_id=1, replica_groups={{0,32,64,96,128,160,192,224},{256,288,320,352,384,416,448,480},{1,33,65..., dimensions={0} | all-to-all | bytes 98304 | tf_op jit(solution)/shard_map/all_to_all | solution.py:434
  177.2 5.6 %shard_map.162 = bf16[384,512]{1,0:T(8,128)(2,1)} custom-call(s32[3]{0:T(128)S(1)} %pad_add_fusion.1.core_ref.place_ref, bf16[8,2,24,64]{3,2,1,0:T(8,128)(2,1)S(1)} %reshape.88.heads_ref, f32[24,2048]{1,0:T(8,128)S(1)} %get-tuple-element.42.own_coarse_ref, bf16[1152,16,128]{2,1,0:T(8,128)(2,1)S(1)} %bitcast.25, ...), custom_call_target="tpu_custom_call" | custom-call | flops 301989888 | bytes 10272780 | tf_op jit(solution)/shard_map/pallas_call | solution.py:23
  (92 shorter events, 36.5 us)
Async XLA Ops:
  6.5 47.6 %copy-start.13 = (f32[512]{0:T(512)S(1)}, f32[512]{0:T(512)}, u32[]{:S(2)}) copy-start(f32[512]{0:T(512)} %param.20) | copy-start | bytes 6148
  6.5 67.7 %all-gather.4.cloned.1.call-start = ((), (), s32[]{:S(2)}) async-start(), calls=%async_computation.2 | async-start | bytes 3686400 | tf_op jit(solution)/shard_map/all_gather | solution.py:492
  19.0 140.3 %all-gather.6.cloned.1.call-start = ((), (), s32[]{:S(2)}) async-start(), calls=%async_computation.3 | async-start | bytes 5308416 | tf_op jit(solution)/shard_map/all_gather | solution.py:576
  21.8 16.4 %collective-permute-start = (bf16[2,2,16,512]{3,2,1,0:T(8,128)(2,1)S(1)}, bf16[2,2,16,512]{3,2,1,0:T(8,128)(2,1)S(1)}, u32[]{:S(2)}, u32[]{:S(2)}) collective-permute-start(bf16[2,2,16,512]{3,2,1,0:T(8,128)(2,1)S(1)} %get-tuple-element.49), channel_id=1, source_target_pairs={{0,32},{32,64},{64,96},{96,128},{128,160},{160,192},{192,224},{224... | collective-permute-start | bytes 196616 | tf_op jit(solution)/shard_map/ppermute | solution.py:418
  27.5 10.7 %collective-permute-start.1 = (bf16[2,2,16,512]{3,2,1,0:T(8,128)(2,1)S(1)}, bf16[2,2,16,512]{3,2,1,0:T(8,128)(2,1)S(1)}, u32[]{:S(2)}, u32[]{:S(2)}) collective-permute-start(bf16[2,2,16,512]{3,2,1,0:T(8,128)(2,1)S(1)} %get-tuple-element.50), channel_id=1, source_target_pairs={{32,0},{64,32},{96,64},{128,96},{160,128},{192,160},{224,192},{256... | collective-permute-start | bytes 196616 | tf_op jit(solution)/shard_map/ppermute | solution.py:419
  38.4 11.4 %collective-permute-start.3 = (bf16[16,2,2,512]{3,2,1,0:T(2,128)(2,1)S(1)}, bf16[16,2,2,512]{3,2,1,0:T(2,128)(2,1)S(1)}, u32[]{:S(2)}, u32[]{:S(2)}) collective-permute-start(bf16[16,2,2,512]{3,2,1,0:T(2,128)(2,1)S(1)} %get-tuple-element.47), channel_id=1, source_target_pairs={{1,0},{2,1},{3,2},{4,3},{5,4},{6,5},{7,6},{8,7},{9,8},{10,9},{11,1... | collective-permute-start | bytes 196616 | tf_op jit(solution)/shard_map/ppermute | solution.py:419
  43.3 6.5 %collective-permute-start.2 = (bf16[16,2,2,512]{3,2,1,0:T(2,128)(2,1)S(1)}, bf16[16,2,2,512]{3,2,1,0:T(2,128)(2,1)S(1)}, u32[]{:S(2)}, u32[]{:S(2)}) collective-permute-start(bf16[16,2,2,512]{3,2,1,0:T(2,128)(2,1)S(1)} %get-tuple-element.48), channel_id=1, source_target_pairs={{0,1},{1,2},{2,3},{3,4},{4,5},{5,6},{6,7},{7,8},{8,9},{9,10},{10,1... | collective-permute-start | bytes 196616 | tf_op jit(solution)/shard_map/ppermute | solution.py:418
  46.2 25.2 %collective-permute-start.4 = (bf16[2048,128]{1,0:T(8,128)(2,1)}, bf16[2048,128]{1,0:T(8,128)(2,1)S(1)}, u32[]{:S(2)}, u32[]{:S(2)}) collective-permute-start(bf16[2048,128]{1,0:T(8,128)(2,1)} %constant_dynamic-slice_fusion.1), channel_id=1, source_target_pairs={{0,256},{32,288},{64,320},{96,352},{128,384},{160,416},{192,448},{... | collective-permute-start | bytes 1572872 | tf_op jit(solution)/shard_map/ppermute | solution.py:430
  50.7 20.7 %collective-permute-start.5 = (bf16[96,2048]{1,0:T(8,128)(2,1)}, bf16[96,2048]{1,0:T(8,128)(2,1)}, u32[]{:S(2)}, u32[]{:S(2)}) collective-permute-start(bf16[96,2048]{1,0:T(8,128)(2,1)} %constant_dynamic-slice_fusion), channel_id=1, source_target_pairs={{0,256},{32,288},{64,320},{96,352},{128,384},{160,416},{192,448},{... | collective-permute-start | bytes 1179656 | tf_op jit(solution)/shard_map/ppermute | solution.py:430
  78.6 4.1 %collective-permute-start.6 = (bf16[96,2048]{1,0:T(8,128)(2,1)}, bf16[96,2048]{1,0:T(8,128)(2,1)S(1)}, u32[]{:S(2)}, u32[]{:S(2)}) collective-permute-start(bf16[96,2048]{1,0:T(8,128)(2,1)} %get-tuple-element.33.own_ref), channel_id=1, source_target_pairs={{0,1},{1,0},{2,3},{3,2},{4,5},{5,4},{6,7},{7,6},{8,9},{9,8},{10,11... | collective-permute-start | bytes 1179656 | tf_op jit(solution)/shard_map/ppermute | solution.py:425
  85.3 69.9 %copy-start.10 = (f32[2048]{0:T(1024)S(1)}, f32[2048]{0:T(1024)}, u32[]{:S(2)}) copy-start(f32[2048]{0:T(1024)} %param.27) | copy-start | bytes 24580
  85.3 3.4 %collective-permute-start.7 = (bf16[96,512]{1,0:T(8,128)(2,1)}, bf16[96,512]{1,0:T(8,128)(2,1)S(1)}, u32[]{:S(2)}, u32[]{:S(2)}) collective-permute-start(bf16[96,512]{1,0:T(8,128)(2,1)} %copy-done.12), channel_id=1, source_target_pairs={{0,1},{1,0},{2,3},{3,2},{4,5},{5,4},{6,7},{7,6},{8,9},{9,8},{10,11... | collective-permute-start | bytes 294920 | tf_op jit(solution)/shard_map/ppermute | solution.py:425
  89.8 9.2 %collective-permute-start.8 = (bf16[24,4096]{1,0:T(8,128)(2,1)S(1)}, bf16[24,4096]{1,0:T(8,128)(2,1)S(1)}, u32[]{:S(2)}, u32[]{:S(2)}) collective-permute-start(bf16[24,4096]{1,0:T(8,128)(2,1)S(1)} %get-tuple-element.36.refs_0_), channel_id=1, source_target_pairs={{0,32},{32,64},{64,96},{96,128},{128,160},{160,192},{192,224},{224... | collective-permute-start | bytes 589832 | tf_op jit(solution)/shard_map/ppermute | solution.py:439
  92.2 11.9 %collective-permute-start.9 = (bf16[24,4096]{1,0:T(8,128)(2,1)S(1)}, bf16[24,4096]{1,0:T(8,128)(2,1)S(1)}, u32[]{:S(2)}, u32[]{:S(2)}) collective-permute-start(bf16[24,4096]{1,0:T(8,128)(2,1)S(1)} %get-tuple-element.36.refs_0_), channel_id=1, source_target_pairs={{0,224},{32,0},{64,32},{96,64},{128,96},{160,128},{192,160},{224,1... | collective-permute-start | bytes 589832 | tf_op jit(solution)/shard_map/ppermute | solution.py:439
  99.0 9.9 %collective-permute-start.10 = (bf16[24,4096]{1,0:T(8,128)(2,1)S(1)}, bf16[24,4096]{1,0:T(8,128)(2,1)S(1)}, u32[]{:S(2)}, u32[]{:S(2)}) collective-permute-start(bf16[24,4096]{1,0:T(8,128)(2,1)S(1)} %collective-permute-done.8.refs_1_), channel_id=1, source_target_pairs={{0,32},{32,64},{64,96},{96,128},{128,160},{160,192},{192,224},{224... | collective-permute-start | bytes 589832 | tf_op jit(solution)/shard_map/ppermute | solution.py:439
  101.0 20.1 %collective-permute-start.14 = (bf16[2048,128]{1,0:T(8,128)(2,1)S(1)}, bf16[2048,128]{1,0:T(8,128)(2,1)S(1)}, u32[]{:S(2)}, u32[]{:S(2)}) collective-permute-start(bf16[2048,128]{1,0:T(8,128)(2,1)S(1)} %collective-permute-done.4.refs_8_.mine_ref), channel_id=1, source_target_pairs={{0,1},{1,0},{2,3},{3,2},{4,5},{5,4},{6,7},{7,6},{8,9},{9,8},{10,11... | collective-permute-start | bytes 1572872 | tf_op jit(solution)/shard_map/ppermute | solution.py:425
  104.1 9.2 %collective-permute-start.11 = (bf16[24,4096]{1,0:T(8,128)(2,1)S(1)}, bf16[24,4096]{1,0:T(8,128)(2,1)S(1)}, u32[]{:S(2)}, u32[]{:S(2)}) collective-permute-start(bf16[24,4096]{1,0:T(8,128)(2,1)S(1)} %collective-permute-done.9.refs_2_), channel_id=1, source_target_pairs={{0,224},{32,0},{64,32},{96,64},{128,96},{160,128},{192,160},{224,1... | collective-permute-start | bytes 589832 | tf_op jit(solution)/shard_map/ppermute | solution.py:439
  108.9 14.1 %collective-permute-start.16 = (bf16[96,2048]{1,0:T(8,128)(2,1)}, bf16[96,2048]{1,0:T(8,128)(2,1)S(1)}, u32[]{:S(2)}, u32[]{:S(2)}) collective-permute-start(bf16[96,2048]{1,0:T(8,128)(2,1)} %collective-permute-done.5.mine_ref), channel_id=1, source_target_pairs={{0,1},{1,0},{2,3},{3,2},{4,5},{5,4},{6,7},{7,6},{8,9},{9,8},{10,11... | collective-permute-start | bytes 1179656 | tf_op jit(solution)/shard_map/ppermute | solution.py:425
  111.3 9.7 %collective-permute-start.12 = (bf16[24,4096]{1,0:T(8,128)(2,1)S(1)}, bf16[24,4096]{1,0:T(8,128)(2,1)S(1)}, u32[]{:S(2)}, u32[]{:S(2)}) collective-permute-start(bf16[24,4096]{1,0:T(8,128)(2,1)S(1)} %collective-permute-done.10.refs_3_), channel_id=1, source_target_pairs={{0,32},{32,64},{64,96},{96,128},{128,160},{160,192},{192,224},{224... | collective-permute-start | bytes 589832 | tf_op jit(solution)/shard_map/ppermute | solution.py:439
  113.3 9.7 %collective-permute-start.13 = (bf16[24,4096]{1,0:T(8,128)(2,1)S(1)}, bf16[24,4096]{1,0:T(8,128)(2,1)S(1)}, u32[]{:S(2)}, u32[]{:S(2)}) collective-permute-start(bf16[24,4096]{1,0:T(8,128)(2,1)S(1)} %collective-permute-done.11.refs_4_), channel_id=1, source_target_pairs={{0,224},{32,0},{64,32},{96,64},{128,96},{160,128},{192,160},{224,1... | collective-permute-start | bytes 589832 | tf_op jit(solution)/shard_map/ppermute | solution.py:439
  121.1 8.0 %collective-permute-start.15 = (bf16[24,2048]{1,0:T(8,128)(2,1)S(1)}, bf16[24,2048]{1,0:T(8,128)(2,1)S(1)}, u32[]{:S(2)}, u32[]{:S(2)}) collective-permute-start(bf16[24,2048]{1,0:T(8,128)(2,1)S(1)} %slice.25), channel_id=1, source_target_pairs={{0,32},{32,64},{64,96},{96,128},{128,160},{160,192},{192,224},{224... | collective-permute-start | bytes 294920 | tf_op jit(solution)/shard_map/ppermute | solution.py:439
  123.1 6.2 %collective-permute-start.17 = (bf16[24,2048]{1,0:T(8,128)(2,1)S(1)}, bf16[24,2048]{1,0:T(8,128)(2,1)S(1)}, u32[]{:S(2)}, u32[]{:S(2)}) collective-permute-start(bf16[24,2048]{1,0:T(8,128)(2,1)S(1)} %slice.26), channel_id=1, source_target_pairs={{0,224},{32,0},{64,32},{96,64},{128,96},{160,128},{192,160},{224,1... | collective-permute-start | bytes 294920 | tf_op jit(solution)/shard_map/ppermute | solution.py:439
  129.1 45.7 %copy-start.5 = (bf16[384,512]{1,0:T(8,128)(2,1)S(1)}, bf16[384,512]{1,0:T(8,128)(2,1)}, u32[]{:S(2)}) copy-start(bf16[384,512]{1,0:T(8,128)(2,1)} %get-tuple-element.46.skip_ref) | copy-start | bytes 1179652
  159.3 15.5 %collective-permute-start.18 = (bf16[1152,16,128]{2,1,0:T(8,128)(2,1)}, bf16[1152,16,128]{2,1,0:T(8,128)(2,1)}, u32[]{:S(2)}, u32[]{:S(2)}) collective-permute-start(bf16[1152,16,128]{2,1,0:T(8,128)(2,1)} %bitcast.24), channel_id=1, source_target_pairs={{0,1},{1,0},{2,3},{3,2},{4,5},{5,4},{6,7},{7,6},{8,9},{9,8},{10,11... | collective-permute-start | bytes 14155784 | tf_op jit(solution)/shard_map/ppermute | solution.py:425
  (12 other events, 149.3 us)
Sparse Core Ops, SparseCore 0:
  19.1 55.1 all-gather.3
  85.4 59.8 all-gather.5

commit v11 on v10

--- a/solution.py
+++ b/solution.py
@@ -505,9 +505,8 @@
     cells = jnp.concatenate([above, hidden, below], axis=0)
     qkv_third = qkv_third.transpose(0, 2, 1).reshape(-1, qkv_third.shape[1])
 
-    merge_third, cells = lax.optimization_barrier((merge_third, cells))
+    merge_third, qkv_third, cells = lax.optimization_barrier((merge_third, qkv_third, cells))
     left, right = neighbours(cells[:, :, :2], cells[:, :, -2:], "lon")
-    qkv_third, left, right = lax.optimization_barrier((qkv_third, left, right))
 
     merge_mine, qkv_mine = [
         swap_rings(lax.dynamic_slice_in_dim(table, core * (table.shape[0] // 2), table.shape[0] // 2))
@@ -540,7 +539,8 @@
         ),
         flops=2 * 640 * 512 * 1536,
     )
-    attended = after(attended, merge_mine, qkv_mine)
+    merge_partner, qkv_partner = swap_cores(merge_mine), swap_cores(qkv_mine)
+    attended = after(attended, merge_partner, qkv_partner)
     tokens = attended.shape[0]
     skip_first, merged_in = call_kernel(
         skip_kernel,
@@ -596,10 +596,7 @@
     for _ in range(3):
         forth, back = ring_shift(forth, 1), ring_shift(back, -1)
         pieces += [forth, back]
-    merge_mine, qkv_mine = after(merge_mine, pieces[1]), after(qkv_mine, pieces[3])
-    merge_partner, qkv_partner = swap_cores(merge_mine), swap_cores(qkv_mine)
     half_feats = coarse_in.shape[1] // 2
-    forth, back = after(forth, merge_partner), after(back, qkv_partner)
     far_low, far_high = ring_shift(forth[:, :half_feats], 1), ring_shift(back[:, half_feats:], -1)
     tables = (merge_third, merge_mine, merge_partner)
     near = call_kernel(

time: 191 us -> 205 us (1.073)
  starting transfers between devices: 72.1 us -> 88.6 us
  local copies, waits for them, and re-layouts: 10.9 us -> 16.2 us
  waiting for transfers between devices: 21.7 us -> 17.7 us
  blocking collectives: 43.4 us -> 39.7 us
    ppermute x5, starting transfers between devices: 16.3 us -> 30.7 us  [swap_cores(): return lax.ppermute(values, 'lon', [(i, i ^ 1) for i in range(count)])]
    ppermute x2, waiting for transfers between devices: 10.8 us -> 5.96 us  [swap_rings(): lax.ppermute(values, 'lat', [(i, (i + Z_RING) % count) for i in range(cou...]
    all_to_all x2, blocking collectives: 34.1 us -> 30.4 us  [ring_scatter(): lax.all_to_all(blocks, 'lat', 0, 0, axis_index_groups=RINGS, tiled=True)]
    ppermute x8, starting transfers between devices: 27 us -> 30.5 us  [ring_shift(): return lax.ppermute(values, 'lat', pairs)]
    ppermute x2, starting transfers between devices: 14.3 us -> 11.3 us  [neighbours(): lax.ppermute(first, axis, [((i + 1) % count, i) for i in range(count)])]
    all_gather x1, waiting for transfers between devices: 2.89 us -> 0.01 us  [on_device(): lax.all_gather(both_merge, 'lat', axis=1, axis_index_groups=RINGS, tiled=...]
    unnamed x32 -> x40, local copies, waits for them, and re-layouts: 6.75 us -> 9.32 us
  transfers between devices with their start and end apart: 21 -> 21, of which waited for: 7 -> 9; matrix products, arithmetic and copies ran while one was open for 3% -> 5% of each run, Pallas kernels for 6% -> 5%
where the time goes in v11:
time: 205 us; the launch traced here: 204 us
  starting transfers between devices  88.6 us (43%)
  blocking collectives  39.7 us (19%)
  Pallas kernels  23.8 us (12%)
  waiting for transfers between devices  17.7 us (9%)
  local copies, waits for them, and re-layouts  16.2 us (8%)
  between operations  14 us (7%)
  other arithmetic  2.81 us (1%)
    ppermute x5, starting transfers between devices, swap_cores(): return lax.ppermute(values, 'lon', [(i, i ^ 1) for i in range(count)])  30.7 us
    ppermute x8, starting transfers between devices, ring_shift(): return lax.ppermute(values, 'lat', pairs)  30.5 us
    all_to_all x2, blocking collectives, ring_scatter(): lax.all_to_all(blocks, 'lat', 0, 0, axis_index_groups=RINGS, tiled=True)  30.4 us
    pallas_call x9, Pallas kernels, call_kernel(): pl.pallas_call(body, out_shape=out_shape, in_specs=[pl.BlockSpec(memory_s...  23.8 us
    ppermute x2, starting transfers between devices, neighbours(): lax.ppermute(first, axis, [((i + 1) % count, i) for i in range(count)])  11.3 us
    unnamed x40, local copies, waits for them, and re-layouts  9.32 us
    ppermute x2, starting transfers between devices, neighbours(): lax.ppermute(last, axis, [(i, (i + 1) % count) for i in range(count)])  9.3 us
    all_gather x1, blocking collectives, on_device(): lax.all_gather(own_merge, 'lat', axis_index_groups=[[z, z + Z_RING] for z...  9.3 us
  transfers between devices with their start and end apart: 21, of which 9 were waited for; matrix products, arithmetic and copies ran while one was open for 5% of the time, Pallas kernels for 5%

profile of v11, /device:TPU:1, one launch (start us, length us, event | category | flops | bytes accessed | tf_op | source)
XLA Modules:
  0.0 203.6 jit_solution(11029529142512266379)
XLA Ops:
  7.2 2.4 %shard_map.154 = bf16[160,640]{1,0:T(8,128)(2,1)} custom-call(s32[2]{0:T(128)} %pad_add_fusion.2.place_ref, bf16[128,1024]{1,0:T(8,128)(2,1)} %merge_ref.1, bf16[32,512]{1,0:T(8,128)(2,1)} %first_ref.1, bf16[128,1024]{1,0:T(8,128)(2,1)} %up_third_ref.1, bf16[64,512]{1,0:T(8,128)(2,1)} %up_second_ref.1, bf16[64,2048]{1,0:T(8,128)(2,1)} %out_third_ref.1), custom_call_target="tpu_custom_call" | custom-call | bytes 884744 | tf_op jit(solution)/shard_map/pallas_call | solution.py:23
  9.6 9.3 %all-gather = bf16[320,640]{1,0:T(8,128)(2,1)} all-gather(bf16[160,640]{1,0:T(8,128)(2,1)} %shard_map.154), channel_id=2, replica_groups={{0,256},{32,288},{64,320},{96,352},{128,384},{160,416},{192,448},{224,4..., dimensions={0}, use_global_device_ids=true | all-gather | bytes 614400 | tf_op jit(solution)/shard_map/all_gather | solution.py:489
  21.8 5.7 %collective-permute-start = (bf16[2,2,16,512]{3,2,1,0:T(8,128)(2,1)S(1)}, bf16[2,2,16,512]{3,2,1,0:T(8,128)(2,1)S(1)}, u32[]{:S(2)}, u32[]{:S(2)}) collective-permute-start(bf16[2,2,16,512]{3,2,1,0:T(8,128)(2,1)S(1)} %get-tuple-element.37), channel_id=1, source_target_pairs={{0,32},{32,64},{64,96},{96,128},{128,160},{160,192},{192,224},{224... | collective-permute-start | bytes 196616 | tf_op jit(solution)/shard_map/ppermute | solution.py:418
  27.4 9.4 %collective-permute-start.1 = (bf16[2,2,16,512]{3,2,1,0:T(8,128)(2,1)S(1)}, bf16[2,2,16,512]{3,2,1,0:T(8,128)(2,1)S(1)}, u32[]{:S(2)}, u32[]{:S(2)}) collective-permute-start(bf16[2,2,16,512]{3,2,1,0:T(8,128)(2,1)S(1)} %get-tuple-element.38), channel_id=1, source_target_pairs={{32,0},{64,32},{96,64},{128,96},{160,128},{192,160},{224,192},{256... | collective-permute-start | bytes 196616 | tf_op jit(solution)/shard_map/ppermute | solution.py:419
  38.3 3.8 %collective-permute-start.4 = (bf16[2048,128]{1,0:T(8,128)(2,1)S(1)}, bf16[2048,128]{1,0:T(8,128)(2,1)S(1)}, u32[]{:S(2)}, u32[]{:S(2)}) collective-permute-start(bf16[2048,128]{1,0:T(8,128)(2,1)S(1)} %constant_dynamic-slice_fusion.1), channel_id=1, source_target_pairs={{0,256},{32,288},{64,320},{96,352},{128,384},{160,416},{192,448},{... | collective-permute-start | bytes 1572872 | tf_op jit(solution)/shard_map/ppermute | solution.py:430
  42.9 3.0 %collective-permute-start.6 = (bf16[96,2048]{1,0:T(8,128)(2,1)}, bf16[96,2048]{1,0:T(8,128)(2,1)}, u32[]{:S(2)}, u32[]{:S(2)}) collective-permute-start(bf16[96,2048]{1,0:T(8,128)(2,1)} %constant_dynamic-slice_fusion), channel_id=1, source_target_pairs={{0,256},{32,288},{64,320},{96,352},{128,384},{160,416},{192,448},{... | collective-permute-start | bytes 1179656 | tf_op jit(solution)/shard_map/ppermute | solution.py:430
  46.0 6.0 %collective-permute-done.4.refs_8_.mine_ref = bf16[2048,128]{1,0:T(8,128)(2,1)S(1)} collective-permute-done((bf16[2048,128]{1,0:T(8,128)(2,1)S(1)}, bf16[2048,128]{1,0:T(8,128)(2,1)S(1)}, u32[]{:S(2)}, u32[]{:S(2)}) %collective-permute-start.4) | collective-permute-done | bytes 524320 | tf_op jit(solution)/shard_map/ppermute | solution.py:430
  52.0 9.5 %collective-permute-start.5 = (bf16[2048,128]{1,0:T(8,128)(2,1)S(1)}, bf16[2048,128]{1,0:T(8,128)(2,1)S(1)}, u32[]{:S(2)}, u32[]{:S(2)}) collective-permute-start(bf16[2048,128]{1,0:T(8,128)(2,1)S(1)} %collective-permute-done.4.refs_8_.mine_ref), channel_id=1, source_target_pairs={{0,1},{1,0},{2,3},{3,2},{4,5},{5,4},{6,7},{7,6},{8,9},{9,8},{10,11... | collective-permute-start | bytes 1572872 | tf_op jit(solution)/shard_map/ppermute | solution.py:425
  61.8 4.6 %collective-permute-start.7 = (bf16[96,2048]{1,0:T(8,128)(2,1)}, bf16[96,2048]{1,0:T(8,128)(2,1)}, u32[]{:S(2)}, u32[]{:S(2)}) collective-permute-start(bf16[96,2048]{1,0:T(8,128)(2,1)} %collective-permute-done.6.mine_ref), channel_id=1, source_target_pairs={{0,1},{1,0},{2,3},{3,2},{4,5},{5,4},{6,7},{7,6},{8,9},{9,8},{10,11... | collective-permute-start | bytes 1179656 | tf_op jit(solution)/shard_map/ppermute | solution.py:425
  69.1 3.6 %collective-permute-start.2 = (bf16[16,2,2,512]{3,2,1,0:T(2,128)(2,1)}, bf16[16,2,2,512]{3,2,1,0:T(2,128)(2,1)}, u32[]{:S(2)}, u32[]{:S(2)}) collective-permute-start(bf16[16,2,2,512]{3,2,1,0:T(2,128)(2,1)} %get-tuple-element.36), channel_id=1, source_target_pairs={{0,1},{1,2},{2,3},{3,4},{4,5},{5,6},{6,7},{7,8},{8,9},{9,10},{10,1... | collective-permute-start | bytes 196616 | tf_op jit(solution)/shard_map/ppermute | solution.py:418
  81.3 3.3 %shard_map.155.attended_ref = bf16[384,512]{1,0:T(8,128)(2,1)S(1)} custom-call(bf16[512,512]{1,0:T(8,128)(2,1)S(1)} %bitcast.28, bf16[64,512]{1,0:T(8,128)(2,1)S(1)} %copy-done.12, bf16[64,512]{1,0:T(8,128)(2,1)S(1)} %copy-done.11, f32[1,512]{1,0:T(1,128)S(1)} %bitcast.31, bf16[3,512,512]{2,1,0:T(8,128)(2,1)S(1)} %copy-done.15, ...), custom_call_target="tpu_custom_call" | custom-call | flops 1006632960 | bytes 2314752 | tf_op jit(solution)/shard_map/pallas_call | solution.py:23
  85.3 4.3 %shard_map.156 = (bf16[384,512]{1,0:T(8,128)(2,1)}, bf16[96,2048]{1,0:T(8,128)(2,1)}) custom-call(bf16[384,512]{1,0:T(8,128)(2,1)} %copy-done.6, bf16[384,512]{1,0:T(8,128)(2,1)} %bitcast.32, bf16[2,8,160,640]{3,2,1,0:T(8,128)(2,1)} %bitcast.22, f32[1,2048]{1,0:T(1,128)} %bitcast.35), custom_call_target="tpu_custom_call" | custom-call | flops 201326592 | bytes 4071424 | tf_op jit(solution)/shard_map/pallas_call | solution.py:23
  89.6 6.9 %collective-permute-start.8 = (bf16[96,2048]{1,0:T(8,128)(2,1)}, bf16[96,2048]{1,0:T(8,128)(2,1)S(1)}, u32[]{:S(2)}, u32[]{:S(2)}) collective-permute-start(bf16[96,2048]{1,0:T(8,128)(2,1)} %get-tuple-element.25.own_ref), channel_id=1, source_target_pairs={{0,1},{1,0},{2,3},{3,2},{4,5},{5,4},{6,7},{7,6},{8,9},{9,8},{10,11... | collective-permute-start | bytes 1179656 | tf_op jit(solution)/shard_map/ppermute | solution.py:425
  106.1 6.5 %collective-permute-start.11 = (bf16[24,4096]{1,0:T(8,128)(2,1)S(1)}, bf16[24,4096]{1,0:T(8,128)(2,1)S(1)}, u32[]{:S(2)}, u32[]{:S(2)}) collective-permute-start(bf16[24,4096]{1,0:T(8,128)(2,1)S(1)} %get-tuple-element.28.refs_0_), channel_id=1, source_target_pairs={{0,224},{32,0},{64,32},{96,64},{128,96},{160,128},{192,160},{224,1... | collective-permute-start | bytes 589832 | tf_op jit(solution)/shard_map/ppermute | solution.py:439
  116.5 5.4 %collective-permute-start.13 = (bf16[24,4096]{1,0:T(8,128)(2,1)S(1)}, bf16[24,4096]{1,0:T(8,128)(2,1)S(1)}, u32[]{:S(2)}, u32[]{:S(2)}) collective-permute-start(bf16[24,4096]{1,0:T(8,128)(2,1)S(1)} %collective-permute-done.11.refs_2_), channel_id=1, source_target_pairs={{0,224},{32,0},{64,32},{96,64},{128,96},{160,128},{192,160},{224,1... | collective-permute-start | bytes 589832 | tf_op jit(solution)/shard_map/ppermute | solution.py:439
  125.0 5.4 %collective-permute-start.15 = (bf16[24,4096]{1,0:T(8,128)(2,1)S(1)}, bf16[24,4096]{1,0:T(8,128)(2,1)S(1)}, u32[]{:S(2)}, u32[]{:S(2)}) collective-permute-start(bf16[24,4096]{1,0:T(8,128)(2,1)S(1)} %collective-permute-done.13.refs_4_), channel_id=1, source_target_pairs={{0,224},{32,0},{64,32},{96,64},{128,96},{160,128},{192,160},{224,1... | collective-permute-start | bytes 589832 | tf_op jit(solution)/shard_map/ppermute | solution.py:439
  133.1 5.4 %collective-permute-start.17 = (bf16[24,2048]{1,0:T(8,128)(2,1)S(1)}, bf16[24,2048]{1,0:T(8,128)(2,1)S(1)}, u32[]{:S(2)}, u32[]{:S(2)}) collective-permute-start(bf16[24,2048]{1,0:T(8,128)(2,1)S(1)} %slice.29), channel_id=1, source_target_pairs={{0,224},{32,0},{64,32},{96,64},{128,96},{160,128},{192,160},{224,1... | collective-permute-start | bytes 294920 | tf_op jit(solution)/shard_map/ppermute | solution.py:439
  141.9 3.5 %collective-permute-done.16.low_ref = bf16[24,2048]{1,0:T(8,128)(2,1)S(1)} collective-permute-done((bf16[24,2048]{1,0:T(8,128)(2,1)S(1)}, bf16[24,2048]{1,0:T(8,128)(2,1)S(1)}, u32[]{:S(2)}, u32[]{:S(2)}) %collective-permute-start.16) | collective-permute-done | bytes 98336 | tf_op jit(solution)/shard_map/ppermute | solution.py:439
  146.7 21.0 %all_to_all.10.x_ref = bf16[8,8,2,24,128]{4,3,2,1,0:T(8,128)(2,1)S(1)} all-to-all(bf16[8,8,2,24,128]{4,3,2,1,0:T(8,128)(2,1)S(1)} %broadcast_in_dim.42), channel_id=1, replica_groups={{0,32,64,96,128,160,192,224},{256,288,320,352,384,416,448,480},{1,33,65..., dimensions={0} | all-to-all | bytes 1572864 | tf_op jit(solution)/shard_map/all_to_all | solution.py:434
  167.7 4.1 %shard_map.161 = (bf16[8,2,24,64]{3,2,1,0:T(8,128)(2,1)S(1)}, f32[24,2048]{1,0:T(8,128)S(1)}) custom-call(s32[3]{0:T(128)S(1)} %pad_add_fusion.1.core_ref.place_ref, bf16[8,8,2,24,128]{4,3,2,1,0:T(8,128)(2,1)S(1)} %all_to_all.10.x_ref, f32[1,2048]{1,0:T(1,128)S(1)} %bitcast.30, bf16[192,2048]{1,0:T(8,128)(2,1)S(1)} %bitcast.27, ...), custom_call_target="tpu_custom_call" | custom-call | flops 301989888 | bytes 2367500 | tf_op jit(solution)/shard_map/pallas_call | solution.py:23
  171.8 7.4 %collective-permute-start.18 = (bf16[1152,16,128]{2,1,0:T(8,128)(2,1)}, bf16[1152,16,128]{2,1,0:T(8,128)(2,1)}, u32[]{:S(2)}, u32[]{:S(2)}) collective-permute-start(bf16[1152,16,128]{2,1,0:T(8,128)(2,1)} %bitcast.24), channel_id=1, source_target_pairs={{0,1},{1,0},{2,3},{3,2},{4,5},{5,4},{6,7},{7,6},{8,9},{9,8},{10,11... | collective-permute-start | bytes 14155784 | tf_op jit(solution)/shard_map/ppermute | solution.py:425
  179.4 9.4 %all_to_all.11 = bf16[8,2,1536]{2,1,0:T(2,128)(2,1)S(1)} all-to-all(bf16[8,2,1536]{2,1,0:T(2,128)(2,1)S(1)} %reshape.87), channel_id=1, replica_groups={{0,32,64,96,128,160,192,224},{256,288,320,352,384,416,448,480},{1,33,65..., dimensions={0} | all-to-all | bytes 98304 | tf_op jit(solution)/shard_map/all_to_all | solution.py:434
  188.9 2.3 %copy-done.3 = bf16[18432,128]{1,0:T(8,128)(2,1)S(1)} copy-done((bf16[18432,128]{1,0:T(8,128)(2,1)S(1)}, bf16[18432,128]{1,0:T(8,128)(2,1)}, u32[]{:S(2)}) %copy-start.3) | copy-done | bytes 4718616
  191.2 5.6 %shard_map.162 = bf16[384,512]{1,0:T(8,128)(2,1)} custom-call(s32[3]{0:T(128)S(1)} %pad_add_fusion.1.core_ref.place_ref, bf16[8,2,24,64]{3,2,1,0:T(8,128)(2,1)S(1)} %reshape.88.heads_ref, f32[24,2048]{1,0:T(8,128)S(1)} %get-tuple-element.30.own_coarse_ref, bf16[1152,16,128]{2,1,0:T(8,128)(2,1)S(1)} %bitcast.25, ...), custom_call_target="tpu_custom_call" | custom-call | flops 301989888 | bytes 10272780 | tf_op jit(solution)/shard_map/pallas_call | solution.py:23
  (100 shorter events, 41.9 us)
Async XLA Ops:
  6.5 70.7 %copy-start.17 = (f32[512]{0:T(512)S(1)}, f32[512]{0:T(512)}, u32[]{:S(2)}) copy-start(f32[512]{0:T(512)} %param.20) | copy-start | bytes 6148
  6.5 78.8 %all-gather.4.cloned.1.call-start = ((), (), s32[]{:S(2)}) async-start(), calls=%async_computation.2 | async-start | bytes 3686400 | tf_op jit(solution)/shard_map/all_gather | solution.py:492
  18.9 152.9 %all-gather.6.cloned.1.call-start = ((), (), s32[]{:S(2)}) async-start(), calls=%async_computation.3 | async-start | bytes 5308416 | tf_op jit(solution)/shard_map/all_gather | solution.py:576
  21.8 15.1 %collective-permute-start = (bf16[2,2,16,512]{3,2,1,0:T(8,128)(2,1)S(1)}, bf16[2,2,16,512]{3,2,1,0:T(8,128)(2,1)S(1)}, u32[]{:S(2)}, u32[]{:S(2)}) collective-permute-start(bf16[2,2,16,512]{3,2,1,0:T(8,128)(2,1)S(1)} %get-tuple-element.37), channel_id=1, source_target_pairs={{0,32},{32,64},{64,96},{96,128},{128,160},{160,192},{192,224},{224... | collective-permute-start | bytes 196616 | tf_op jit(solution)/shard_map/ppermute | solution.py:418
  27.4 10.7 %collective-permute-start.1 = (bf16[2,2,16,512]{3,2,1,0:T(8,128)(2,1)S(1)}, bf16[2,2,16,512]{3,2,1,0:T(8,128)(2,1)S(1)}, u32[]{:S(2)}, u32[]{:S(2)}) collective-permute-start(bf16[2,2,16,512]{3,2,1,0:T(8,128)(2,1)S(1)} %get-tuple-element.38), channel_id=1, source_target_pairs={{32,0},{64,32},{96,64},{128,96},{160,128},{192,160},{224,192},{256... | collective-permute-start | bytes 196616 | tf_op jit(solution)/shard_map/ppermute | solution.py:419
  38.3 13.7 %collective-permute-start.4 = (bf16[2048,128]{1,0:T(8,128)(2,1)S(1)}, bf16[2048,128]{1,0:T(8,128)(2,1)S(1)}, u32[]{:S(2)}, u32[]{:S(2)}) collective-permute-start(bf16[2048,128]{1,0:T(8,128)(2,1)S(1)} %constant_dynamic-slice_fusion.1), channel_id=1, source_target_pairs={{0,256},{32,288},{64,320},{96,352},{128,384},{160,416},{192,448},{... | collective-permute-start | bytes 1572872 | tf_op jit(solution)/shard_map/ppermute | solution.py:430
  42.9 19.0 %collective-permute-start.6 = (bf16[96,2048]{1,0:T(8,128)(2,1)}, bf16[96,2048]{1,0:T(8,128)(2,1)}, u32[]{:S(2)}, u32[]{:S(2)}) collective-permute-start(bf16[96,2048]{1,0:T(8,128)(2,1)} %constant_dynamic-slice_fusion), channel_id=1, source_target_pairs={{0,256},{32,288},{64,320},{96,352},{128,384},{160,416},{192,448},{... | collective-permute-start | bytes 1179656 | tf_op jit(solution)/shard_map/ppermute | solution.py:430
  52.0 33.3 %collective-permute-start.5 = (bf16[2048,128]{1,0:T(8,128)(2,1)S(1)}, bf16[2048,128]{1,0:T(8,128)(2,1)S(1)}, u32[]{:S(2)}, u32[]{:S(2)}) collective-permute-start(bf16[2048,128]{1,0:T(8,128)(2,1)S(1)} %collective-permute-done.4.refs_8_.mine_ref), channel_id=1, source_target_pairs={{0,1},{1,0},{2,3},{3,2},{4,5},{5,4},{6,7},{7,6},{8,9},{9,8},{10,11... | collective-permute-start | bytes 1572872 | tf_op jit(solution)/shard_map/ppermute | solution.py:425
  61.8 23.5 %collective-permute-start.7 = (bf16[96,2048]{1,0:T(8,128)(2,1)}, bf16[96,2048]{1,0:T(8,128)(2,1)}, u32[]{:S(2)}, u32[]{:S(2)}) collective-permute-start(bf16[96,2048]{1,0:T(8,128)(2,1)} %collective-permute-done.6.mine_ref), channel_id=1, source_target_pairs={{0,1},{1,0},{2,3},{3,2},{4,5},{5,4},{6,7},{7,6},{8,9},{9,8},{10,11... | collective-permute-start | bytes 1179656 | tf_op jit(solution)/shard_map/ppermute | solution.py:425
  67.2 6.6 %collective-permute-start.3 = (bf16[16,2,2,512]{3,2,1,0:T(2,128)(2,1)}, bf16[16,2,2,512]{3,2,1,0:T(2,128)(2,1)}, u32[]{:S(2)}, u32[]{:S(2)}) collective-permute-start(bf16[16,2,2,512]{3,2,1,0:T(2,128)(2,1)} %get-tuple-element.35), channel_id=1, source_target_pairs={{1,0},{2,1},{3,2},{4,3},{5,4},{6,5},{7,6},{8,7},{9,8},{10,9},{11,1... | collective-permute-start | bytes 196616 | tf_op jit(solution)/shard_map/ppermute | solution.py:419
  69.1 6.6 %collective-permute-start.2 = (bf16[16,2,2,512]{3,2,1,0:T(2,128)(2,1)}, bf16[16,2,2,512]{3,2,1,0:T(2,128)(2,1)}, u32[]{:S(2)}, u32[]{:S(2)}) collective-permute-start(bf16[16,2,2,512]{3,2,1,0:T(2,128)(2,1)} %get-tuple-element.36), channel_id=1, source_target_pairs={{0,1},{1,2},{2,3},{3,4},{4,5},{5,6},{6,7},{7,8},{8,9},{9,10},{10,1... | collective-permute-start | bytes 196616 | tf_op jit(solution)/shard_map/ppermute | solution.py:418
  89.6 8.5 %collective-permute-start.8 = (bf16[96,2048]{1,0:T(8,128)(2,1)}, bf16[96,2048]{1,0:T(8,128)(2,1)S(1)}, u32[]{:S(2)}, u32[]{:S(2)}) collective-permute-start(bf16[96,2048]{1,0:T(8,128)(2,1)} %get-tuple-element.25.own_ref), channel_id=1, source_target_pairs={{0,1},{1,0},{2,3},{3,2},{4,5},{5,4},{6,7},{7,6},{8,9},{9,8},{10,11... | collective-permute-start | bytes 1179656 | tf_op jit(solution)/shard_map/ppermute | solution.py:425
  100.7 67.0 %copy-start.14 = (f32[2048]{0:T(1024)S(1)}, f32[2048]{0:T(1024)}, u32[]{:S(2)}) copy-start(f32[2048]{0:T(1024)} %param.27) | copy-start | bytes 24580
  100.7 3.4 %collective-permute-start.9 = (bf16[96,512]{1,0:T(8,128)(2,1)}, bf16[96,512]{1,0:T(8,128)(2,1)S(1)}, u32[]{:S(2)}, u32[]{:S(2)}) collective-permute-start(bf16[96,512]{1,0:T(8,128)(2,1)} %copy-done.16), channel_id=1, source_target_pairs={{0,1},{1,0},{2,3},{3,2},{4,5},{5,4},{6,7},{7,6},{8,9},{9,8},{10,11... | collective-permute-start | bytes 294920 | tf_op jit(solution)/shard_map/ppermute | solution.py:425
  106.1 10.4 %collective-permute-start.11 = (bf16[24,4096]{1,0:T(8,128)(2,1)S(1)}, bf16[24,4096]{1,0:T(8,128)(2,1)S(1)}, u32[]{:S(2)}, u32[]{:S(2)}) collective-permute-start(bf16[24,4096]{1,0:T(8,128)(2,1)S(1)} %get-tuple-element.28.refs_0_), channel_id=1, source_target_pairs={{0,224},{32,0},{64,32},{96,64},{128,96},{160,128},{192,160},{224,1... | collective-permute-start | bytes 589832 | tf_op jit(solution)/shard_map/ppermute | solution.py:439
  112.6 9.3 %collective-permute-start.10 = (bf16[24,4096]{1,0:T(8,128)(2,1)S(1)}, bf16[24,4096]{1,0:T(8,128)(2,1)S(1)}, u32[]{:S(2)}, u32[]{:S(2)}) collective-permute-start(bf16[24,4096]{1,0:T(8,128)(2,1)S(1)} %get-tuple-element.28.refs_0_), channel_id=1, source_target_pairs={{0,32},{32,64},{64,96},{96,128},{128,160},{160,192},{192,224},{224... | collective-permute-start | bytes 589832 | tf_op jit(solution)/shard_map/ppermute | solution.py:439
  116.5 8.5 %collective-permute-start.13 = (bf16[24,4096]{1,0:T(8,128)(2,1)S(1)}, bf16[24,4096]{1,0:T(8,128)(2,1)S(1)}, u32[]{:S(2)}, u32[]{:S(2)}) collective-permute-start(bf16[24,4096]{1,0:T(8,128)(2,1)S(1)} %collective-permute-done.11.refs_2_), channel_id=1, source_target_pairs={{0,224},{32,0},{64,32},{96,64},{128,96},{160,128},{192,160},{224,1... | collective-permute-start | bytes 589832 | tf_op jit(solution)/shard_map/ppermute | solution.py:439
  122.0 8.5 %collective-permute-start.12 = (bf16[24,4096]{1,0:T(8,128)(2,1)S(1)}, bf16[24,4096]{1,0:T(8,128)(2,1)S(1)}, u32[]{:S(2)}, u32[]{:S(2)}) collective-permute-start(bf16[24,4096]{1,0:T(8,128)(2,1)S(1)} %collective-permute-done.10.refs_1_), channel_id=1, source_target_pairs={{0,32},{32,64},{64,96},{96,128},{128,160},{160,192},{192,224},{224... | collective-permute-start | bytes 589832 | tf_op jit(solution)/shard_map/ppermute | solution.py:439
  125.0 8.0 %collective-permute-start.15 = (bf16[24,4096]{1,0:T(8,128)(2,1)S(1)}, bf16[24,4096]{1,0:T(8,128)(2,1)S(1)}, u32[]{:S(2)}, u32[]{:S(2)}) collective-permute-start(bf16[24,4096]{1,0:T(8,128)(2,1)S(1)} %collective-permute-done.13.refs_4_), channel_id=1, source_target_pairs={{0,224},{32,0},{64,32},{96,64},{128,96},{160,128},{192,160},{224,1... | collective-permute-start | bytes 589832 | tf_op jit(solution)/shard_map/ppermute | solution.py:439
  130.5 8.0 %collective-permute-start.14 = (bf16[24,4096]{1,0:T(8,128)(2,1)S(1)}, bf16[24,4096]{1,0:T(8,128)(2,1)S(1)}, u32[]{:S(2)}, u32[]{:S(2)}) collective-permute-start(bf16[24,4096]{1,0:T(8,128)(2,1)S(1)} %collective-permute-done.12.refs_3_), channel_id=1, source_target_pairs={{0,32},{32,64},{64,96},{96,128},{128,160},{160,192},{192,224},{224... | collective-permute-start | bytes 589832 | tf_op jit(solution)/shard_map/ppermute | solution.py:439
  133.1 8.9 %collective-permute-start.17 = (bf16[24,2048]{1,0:T(8,128)(2,1)S(1)}, bf16[24,2048]{1,0:T(8,128)(2,1)S(1)}, u32[]{:S(2)}, u32[]{:S(2)}) collective-permute-start(bf16[24,2048]{1,0:T(8,128)(2,1)S(1)} %slice.29), channel_id=1, source_target_pairs={{0,224},{32,0},{64,32},{96,64},{128,96},{160,128},{192,160},{224,1... | collective-permute-start | bytes 294920 | tf_op jit(solution)/shard_map/ppermute | solution.py:439
  138.5 7.0 %collective-permute-start.16 = (bf16[24,2048]{1,0:T(8,128)(2,1)S(1)}, bf16[24,2048]{1,0:T(8,128)(2,1)S(1)}, u32[]{:S(2)}, u32[]{:S(2)}) collective-permute-start(bf16[24,2048]{1,0:T(8,128)(2,1)S(1)} %slice.28), channel_id=1, source_target_pairs={{0,32},{32,64},{64,96},{96,128},{128,160},{160,192},{192,224},{224... | collective-permute-start | bytes 294920 | tf_op jit(solution)/shard_map/ppermute | solution.py:439
  141.9 46.9 %copy-start.5 = (bf16[384,512]{1,0:T(8,128)(2,1)S(1)}, bf16[384,512]{1,0:T(8,128)(2,1)}, u32[]{:S(2)}) copy-start(bf16[384,512]{1,0:T(8,128)(2,1)} %get-tuple-element.34.skip_ref) | copy-start | bytes 1179652
  171.8 17.0 %collective-permute-start.18 = (bf16[1152,16,128]{2,1,0:T(8,128)(2,1)}, bf16[1152,16,128]{2,1,0:T(8,128)(2,1)}, u32[]{:S(2)}, u32[]{:S(2)}) collective-permute-start(bf16[1152,16,128]{2,1,0:T(8,128)(2,1)} %bitcast.24), channel_id=1, source_target_pairs={{0,1},{1,0},{2,3},{3,2},{4,5},{5,4},{6,7},{7,6},{8,9},{9,8},{10,11... | collective-permute-start | bytes 14155784 | tf_op jit(solution)/shard_map/ppermute | solution.py:425
  (16 other events, 139.3 us)
Sparse Core Ops, SparseCore 0:
  19.0 55.1 all-gather.3
  100.8 58.1 all-gather.5
